TPU v7x, 256 devices: a whole 4x4x8 slice. The times are simulated.
256 devices in a mesh: wide: 64 (over y, z_hi, x, core), narrow: 4 (over z_lo).
Axes of the slice: x: 4, y: 4, z: 8 (z_hi: 2, z_lo: 4; z = z_hi * 4 + z_lo), core: 2. Of those that a mesh axis runs over, the one named last changes fastest.
Arguments:
- image_raw: float32 [12288, 1152], P(('wide', 'narrow')), may hold values from -3 to 3
- text_raw: float32 [12288, 1152], P(('wide', 'narrow')), may hold values from -3 to 3
- image_ids: int32 [12288], replicated, may hold values from 0 to 3071, as said below
- text_ids: int32 [12288], replicated, may hold values from 0 to 3071, as said below
- log_temp: float32 [1], replicated, may hold values from 2.3 to 3.7
- bias: float32 [1], replicated, may hold values from -12 to -8
Outputs:
- loss: float32 [1], replicated
- image_grad: float32 [12288, 1152], P(('wide', 'narrow'))
- text_grad: float32 [12288, 1152], P(('wide', 'narrow'))
- temp_grad: float32 [1], replicated
- bias_grad: float32 [1], replicated
Inputs may be any that keep to these rules, and one draw needn't show every extreme that they name: `image_ids`: each pair id names exactly 4 images. `text_ids`: each pair id names exactly 4 texts; a text and an image with the same id form a positive pair.
All inputs are finite; a program needn't handle non-finite values.
Results may differ from a plain program's by a relative error of at most 0.0029.
Values may be sent and summed in bfloat16 or wider, within the bound.
No kernel may reach another device: no remote copies, remote signals or barrier semaphores. Data moves between devices by JAX's collectives and lax.ppermute only.
A program may use at most 128 MiB of HBM per device.

v0:
```python
import math

import jax
import jax.numpy as jnp
from jax import lax
from jax.sharding import PartitionSpec as P


def unit(rows):
    scale = jnp.sqrt(jnp.mean(rows * rows, axis=-1, keepdims=True) + 1e-06)
    return rows / (scale * math.sqrt(rows.shape[-1]))


def body(image_raw, text_raw, image_ids, text_ids, log_temp, bias):
    pairs = image_raw.shape[0]
    wide_count = lax.axis_size("wide")
    narrow_count = lax.axis_size("narrow")
    total = pairs * wide_count * narrow_count
    image_float, image_back = jax.vjp(unit, image_raw)
    text_float, text_back = jax.vjp(unit, text_raw)
    image_unit = image_float.astype(jnp.bfloat16)
    text_unit = text_float.astype(jnp.bfloat16)
    image_cols = lax.all_gather(image_unit, "wide", axis=0, tiled=True)
    text_block = lax.all_gather(text_unit, "narrow", axis=0, tiled=True)
    col_ids = lax.dynamic_slice_in_dim(
        image_ids.reshape(wide_count, narrow_count, pairs), lax.axis_index("narrow"), 1, 1
    ).reshape(-1)
    row_ids = lax.dynamic_slice_in_dim(
        text_ids.reshape(wide_count, narrow_count * pairs), lax.axis_index("wide"), 1, 0
    ).reshape(-1)
    temp = jnp.exp(log_temp[0])
    offset = bias[0]
    cosine = lax.dot_general(
        text_block, image_cols, (((1,), (1,)), ((), ())), preferred_element_type=jnp.float32
    )
    logits = temp * cosine + offset
    label = jnp.where(row_ids[:, None] == col_ids[None, :], 1.0, -1.0).astype(jnp.float32)
    loss_part = jnp.sum(jax.nn.softplus(-label * logits)) / total
    scaled = -label * jax.nn.sigmoid(-label * logits)
    bias_part = jnp.sum(scaled) / total
    temp_part = jnp.sum(scaled * temp * cosine) / total
    loss_sum, bias_sum, temp_sum = lax.psum((loss_part, bias_part, temp_part), ("wide", "narrow"))
    scaled_low = scaled.astype(jnp.bfloat16)
    text_term = temp * jnp.dot(scaled_low, image_cols, preferred_element_type=jnp.float32)
    text_unit_grad = lax.psum_scatter(text_term, "narrow", scatter_dimension=0, tiled=True)
    image_unit_grad = lax.psum_scatter(
        temp
        * lax.dot_general(
            scaled_low, text_block, (((0,), (0,)), ((), ())), preferred_element_type=jnp.float32
        ),
        "wide",
        scatter_dimension=0,
        tiled=True,
    )
    image_grad = image_back(image_unit_grad)[0]
    text_grad = text_back(text_unit_grad)[0]
    return (loss_sum.reshape(1), image_grad, text_grad, temp_sum.reshape(1), bias_sum.reshape(1))


def solution(mesh):
    return jax.shard_map(
        body,
        mesh=mesh,
        in_specs=(P(("wide", "narrow"), None), P(("wide", "narrow"), None), P(), P(), P(), P()),
        out_specs=(P(), P(("wide", "narrow"), None), P(("wide", "narrow"), None), P(), P()),
        check_vma=False,
    )
```

profile of v0, /device:TPU:6, one launch (start us, length us, event | category | flops | bytes accessed | tf_op | source)
XLA Modules:
  0.0 410.5 jit_solution(14858176188084494500)
XLA Ops:
  7.2 0.0 all-gather.2.cloned.1.call-start
  7.2 1.1 multiply_reduce_fusion.3
  8.3 1.7 divide_convert_fusion
  10.0 0.0 all-gather.2.cloned.1.call-update
  10.0 0.0 reduce-scatter.5.cloned.1.call-start
  11.4 0.9 reshape.78
  12.3 1.0 reshape.79
  13.2 0.1 dynamic-slice_reduce_fusion
  13.3 0.1 eq.19
  13.4 1.1 multiply_reduce_fusion.4
  14.5 1.0 divide_convert_fusion.1
  15.5 16.3 %all_gather.6 = bf16[192,1152]{1,0:T(8,128)(2,1)S(1)} all-gather(bf16[48,1152]{1,0:T(8,128)(2,1)S(1)} %divide_convert_fusion.1), channel_id=1, replica_groups=mesh['wide'=64,'narrow'=4] {'narrow'}, dimensions={0}, use_global_device_ids=true | all-gather | bytes 552960 | tf_op jit(solution)/shard_map/all_gather | solution.py:24
  31.8 88.3 %all-gather.2.cloned.1.call-done = bf16[3072,1152]{1,0:T(8,128)(2,1)} async-done(((bf16[48,1152]{1,0:T(8,128)(2,1)}), bf16[3072,1152]{1,0:T(8,128)(2,1)}) %all-gather.2.cloned.1.call-update) | async-done | bytes 7077904 | tf_op jit(solution)/shard_map/all_gather | solution.py:23
  120.1 0.0 copy-start.2
  120.1 7.8 %fusion.3 = (f32[]{:T(128)}, f32[]{:T(128)}, f32[]{:T(128)}, f32[192,3072]{1,0:T(8,128)S(1)}) fusion(f32[]{:T(128)} %bitcast.11, f32[]{:T(128)} %bitcast.1, s32[3072]{0:T(1024)S(1)} %eq.19, s32[192]{0:T(256)S(1)} %bitcast.13, bf16[192,1152]{1,0:T(8,128)(2,1)S(1)} %all_gather.6, bf16[3072,1152]{1,0:T(8,128)(2,1)} %all-gather.2.cloned.1.call-done), kind=kOutput, calls=%fused_computation.28 | convolution fusion | flops 1371340800 | bytes 9892628 | tf_op jit(solution)/shard_map/dot_general | solution.py:33
  127.9 0.0 copy-done.2
  127.9 3.1 convolution_multiply_fusion.1
  131.0 0.0 reduce-scatter.5.cloned.1.call-update
  131.0 0.0 reduce-scatter.3.cloned.1.call-start
  131.1 8.2 %convolution_multiply_fusion = f32[3072,1152]{1,0:T(8,128)} fusion(bf16[192,1152]{1,0:T(8,128)(2,1)S(1)} %all_gather.6, f32[]{:T(128)} %bitcast.1, f32[192,3072]{1,0:T(8,128)S(1)} %get-tuple-element.15, f32[]{:T(128)} %bitcast.10, s32[3072]{0:T(1024)S(1)} %eq.19, s32[192]{0:T(256)S(1)} %bitcast.15), kind=kOutput, calls=%fused_computation | convolution fusion | flops 1368981504 | bytes 16970504 | tf_op jit(solution)/shard_map/dot_general | solution.py:48
  139.3 0.0 copy-start
  139.3 0.0 copy-start.1
  139.3 0.0 reduce-scatter.3.cloned.1.call-update
  141.3 76.2 %all-reduce = (f32[1]{0:T(128)}, f32[1]{0:T(128)}, f32[1]{0:T(128)}) all-reduce(f32[1]{0:T(128)} %bitcast.3, f32[1]{0:T(128)} %bitcast.4, f32[1]{0:T(128)} %bitcast.5), channel_id=1, replica_groups=mesh['wide'=64,'narrow'=4] {'wide','narrow'}, use_global_device_ids=true, to_apply=%region_3.4 | all-reduce | flops 3 | bytes 24 | tf_op jit(solution)/shard_map/psum | solution.py:42
  217.5 0.0 reduce-scatter.5.cloned.1.call-done
  217.5 0.0 copy-done
  217.5 1.1 multiply_reduce_fusion.1
  218.7 1.7 add_add_fusion
  220.4 180.7 %reduce-scatter.3.cloned.1.call-done = f32[48,1152]{1,0:T(8,128)} async-done(((f32[3072,1152]{1,0:T(8,128)}), f32[48,1152]{1,0:T(8,128)}) %reduce-scatter.3.cloned.1.call-update) | async-done | bytes 221200 | tf_op jit(solution)/shard_map/reduce_scatter | solution.py:46
  401.1 0.0 copy-done.1
  401.1 1.1 multiply_reduce_fusion.2
  402.2 1.7 add_add_fusion.1
  (5 shorter events, 0.1 us)
Async XLA Ops:
  7.2 112.9 %all-gather.2.cloned.1.call-start = ((), (), s32[]{:S(2)}) async-start(), calls=%async_computation.2 | async-start | bytes 7188480 | tf_op jit(solution)/shard_map/all_gather | solution.py:23
  10.0 207.5 %reduce-scatter.5.cloned.1.call-start = ((), (), s32[]{:S(2)}) async-start(), calls=%async_computation.4 | async-start | bytes 1105920 | tf_op jit(solution)/shard_map/reduce_scatter | solution.py:45
  120.1 7.8 %copy-start.2 = (bf16[3072,1152]{1,0:T(8,128)(2,1)S(1)}, bf16[3072,1152]{1,0:T(8,128)(2,1)}, u32[]{:S(2)}) copy-start(bf16[3072,1152]{1,0:T(8,128)(2,1)} %all-gather.2.cloned.1.call-done) | copy-start | bytes 21233668
  131.0 270.0 %reduce-scatter.3.cloned.1.call-start = ((), (), s32[]{:S(2)}) async-start(), calls=%async_computation.3 | async-start | bytes 14376960 | tf_op jit(solution)/shard_map/reduce_scatter | solution.py:46
  139.3 78.2 %copy-start = (f32[48,1152]{1,0:T(8,128)S(1)}, f32[48,1152]{1,0:T(8,128)}, u32[]{:S(2)}) copy-start(f32[48,1152]{1,0:T(8,128)} %param.7) | copy-start | bytes 663556
  139.3 261.8 %copy-start.1 = (f32[48,1152]{1,0:T(8,128)S(1)}, f32[48,1152]{1,0:T(8,128)}, u32[]{:S(2)}) copy-start(f32[48,1152]{1,0:T(8,128)} %param.6) | copy-start | bytes 663556
Sparse Core Ops, SparseCore 0:
  12.1 107.9 all-gather.1
  131.2 25.3 reduce-scatter.4
  163.0 238.0 reduce-scatter.2
where the time goes:
time: 412 us; the launch traced here: 411 us
  waiting for transfers between devices  269 us (65%)
  blocking collectives  92.5 us (22%)
  matrix products  19.1 us (5%)
  between operations  17.1 us (4%)
  other arithmetic  10.7 us (3%)
    reduce_scatter x1, waiting for transfers between devices, body(): lax.psum_scatter(temp * lax.dot_general(scaled_low, text_block, (((0,), (...  181 us
    all_gather x1, waiting for transfers between devices, body(): image_cols = lax.all_gather(image_unit, 'wide', axis=0, tiled=True)  88.3 us
    psum x1, blocking collectives, body(): lax.psum((loss_part, bias_part, temp_part), ('wide', 'narrow'))  76.2 us
    all_gather x1, blocking collectives, body(): text_block = lax.all_gather(text_unit, 'narrow', axis=0, tiled=True)  16.3 us
  transfers between devices with their start and end apart: 3, of which 2 were waited for; matrix products, arithmetic and copies ran while one was open for 4% of the time, Pallas kernels for 0%

commit v1 on v0

v1 whole, which is shorter than its diff:
```python
import math

import jax
import jax.numpy as jnp
import numpy as np
from jax import lax
from jax.experimental import pallas as pl
from jax.experimental.pallas import tpu as pltpu
from jax.sharding import Mesh
from jax.sharding import PartitionSpec as P

SIZES = (4, 2, 4, 2, 4)
AXES = ("y", "zh", "x", "core", "zl")
ROWS = 48
OFFSETS = (1, 3, 2)
ZOFFSETS = (2, 6, 4)
VMEM = pl.BlockSpec(memory_space=pltpu.VMEM)
SMEM = pl.BlockSpec(memory_space=pltpu.SMEM)


def flat(x, y, z, c):
    return (((y * 2 + z // 4) * 4 + x) * 2 + c) * 4 + z % 4


def send(value, where):
    pairs = []
    for y, zh, x, c, zl in np.ndindex(*SIZES):
        z = zh * 4 + zl
        tx, ty, tz, tc = where(x, y, z, c)
        pairs.append((flat(x, y, z, c), flat(tx % 4, ty % 4, tz % 8, tc % 2)))
    return lax.ppermute(value, AXES, pairs)


def along_first(k):
    return lambda x, y, z, c: (x + k, y, z, c) if c == 0 else (x, y + k, z, c)


def along_second(k):
    return lambda x, y, z, c: (x, y + k, z, c) if c == 0 else (x + k, y, z, c)


def along_z(k):
    return lambda x, y, z, c: (x, y, z + k, c)


def pair_up(sign):
    return lambda x, y, z, c: (x, y, z + sign, c) if c == 0 else (x, y, z - sign, c)


def swap(x, y, z, c):
    return (x, y, z, 1 - c)


def unit_kernel(image_ref, text_ref, image_out, text_out):
    for src, dst in ((image_ref, image_out), (text_ref, text_out)):
        rows = src[...]
        scale = jnp.sqrt(jnp.mean(rows * rows, axis=-1, keepdims=True) + 1e-06)
        dst[...] = (rows / (scale * math.sqrt(rows.shape[-1]))).astype(jnp.bfloat16)


def grid_kernel(
    scalars, rows_id, cols_id, t0, t1, i0, i1, i2, i3,
    text_own, text_other, image_own, image_1, image_2, image_3, sums,
    text, image, scaled,
):
    temp = scalars[0]
    offset = scalars[1]
    for n, src in enumerate((t0, t1)):
        text[384 * n : 384 * (n + 1), :] = src[...]
    for n, src in enumerate((i0, i1, i2, i3)):
        image[192 * n : 192 * (n + 1), :] = src[...]
    cols = cols_id[...]
    totals = [jnp.zeros((8, 768), jnp.float32)] * 3
    for tile in range(3):
        at = slice(256 * tile, 256 * (tile + 1))
        cosine = lax.dot_general(
            text[at, :], image[...], (((1,), (1,)), ((), ())), preferred_element_type=jnp.float32
        )
        logits = temp * cosine + offset
        same = rows_id[at, :] == cols
        margin = jnp.where(same, -logits, logits)
        decay = jnp.exp(-jnp.abs(margin))
        inverse = 1.0 / (1.0 + decay)
        sigmoid = jnp.where(margin >= 0, inverse, decay * inverse)
        grad = jnp.where(same, -sigmoid, sigmoid)
        loss = jnp.maximum(margin, 0.0) + jnp.log1p(decay)
        scaled[at, :] = grad.astype(jnp.bfloat16)
        for n, value in enumerate((loss, grad, grad * cosine)):
            totals[n] = totals[n] + jnp.sum(value.reshape(32, 8, 768), axis=0)
    lane = lax.broadcasted_iota(jnp.int32, (8, 128), 1)
    out = jnp.zeros((8, 128), jnp.float32)
    for n in range(3):
        out = jnp.where(lane == n, jnp.sum(totals[n]), out)
    sums[...] = out
    for tile in range(3):
        at = slice(256 * tile, 256 * (tile + 1))
        part = jnp.dot(scaled[at, :], image[...], preferred_element_type=jnp.float32)
        for n in range(2):
            low, high = max(256 * tile, 384 * n), min(256 * (tile + 1), 384 * (n + 1))
            if low < high:
                piece = part[low - 256 * tile : high - 256 * tile, :]
                dst = (text_own, text_other)[n]
                dst[low - 384 * n : high - 384 * n, :] = piece.astype(dst.dtype)
    for n, dst in enumerate((image_own, image_1, image_2, image_3)):
        part = lax.dot_general(
            scaled[:, 192 * n : 192 * (n + 1)], text[...], (((0,), (0,)), ((), ())),
            preferred_element_type=jnp.float32,
        )
        dst[...] = part.astype(dst.dtype)


def finish_kernel(scalars, raw, own, r1, r2, r3, out):
    rows = raw[...]
    width = rows.shape[-1]
    grad = own[...] + r1[...].astype(jnp.float32) + r2[...].astype(jnp.float32) + r3[...].astype(jnp.float32)
    grad = grad * scalars[0]
    square = jnp.mean(rows * rows, axis=-1, keepdims=True) + 1e-06
    inner = jnp.sum(rows * grad, axis=-1, keepdims=True)
    out[...] = (grad - rows * (inner / (square * width))) / (jnp.sqrt(square) * math.sqrt(width))


def f32(*shape):
    return jax.ShapeDtypeStruct(shape, jnp.float32)


def b16(*shape):
    return jax.ShapeDtypeStruct(shape, jnp.bfloat16)


def body(image_raw, text_raw, image_ids, text_ids, log_temp, bias):
    pairs, width = image_raw.shape
    total = pairs * 256
    x, y, c = lax.axis_index("x"), lax.axis_index("y"), lax.axis_index("core")
    z = lax.axis_index("zh") * 4 + lax.axis_index("zl")
    image_unit, text_unit = pl.pallas_call(
        unit_kernel,
        out_shape=(b16(pairs, width), b16(pairs, width)),
        in_specs=[VMEM] * 2,
        out_specs=(VMEM, VMEM),
    )(image_raw, text_raw)

    line = [image_unit] + [send(image_unit, along_first(k)) for k in OFFSETS]
    ring = [text_unit] + [send(text_unit, along_z(k)) for k in ZOFFSETS]
    line = jnp.concatenate(line, 0)
    ring = jnp.concatenate(ring, 0)
    ring_next = send(ring, pair_up(1))
    plane = [line] + [send(line, along_second(k)) for k in OFFSETS]
    column = jnp.concatenate([ring, ring_next], 0)
    column_other = send(column, swap)

    back = (0,) + OFFSETS
    zback = (0,) + ZOFFSETS
    cols_from = []
    for k in back:
        for j in back:
            sx = jnp.where(c == 0, x - j, x - k) % 4
            sy = jnp.where(c == 0, y - k, y - j) % 4
            cols_from.append(flat(sx, sy, z, c))
    rows_from = []
    for core in (c, 1 - c):
        for step in (0, 1):
            start = z + jnp.where(core == 0, -step, step)
            for k in zback:
                rows_from.append(flat(x, y, (start - k) % 8, core))
    cols_id = image_ids.reshape(256, pairs)[jnp.stack(cols_from)].reshape(1, 16 * pairs)
    rows_id = text_ids.reshape(256, pairs)[jnp.stack(rows_from)].reshape(16 * pairs, 1)

    temp = jnp.exp(log_temp[0])
    scalars = jnp.stack([temp, bias[0]])
    text_own, text_far, image_own, image_1, image_2, image_3, sums = pl.pallas_call(
        grid_kernel,
        out_shape=(
            f32(384, width), b16(384, width), f32(192, width), b16(192, width), b16(192, width), b16(192, width),
            f32(8, 128),
        ),
        in_specs=[SMEM] + [VMEM] * 8,
        out_specs=(VMEM,) * 7,
        scratch_shapes=[
            pltpu.VMEM((768, width), jnp.bfloat16),
            pltpu.VMEM((768, width), jnp.bfloat16),
            pltpu.VMEM((768, 768), jnp.bfloat16),
        ],
        compiler_params=pltpu.CompilerParams(vmem_limit_bytes=48 * 1024 * 1024),
    )(scalars, rows_id, cols_id, column, column_other, *plane)

    text_sum = text_own + send(text_far, swap).astype(jnp.float32)
    image_parts = [send(p, along_second(-k)) for p, k in zip((image_1, image_2, image_3), OFFSETS)]
    near = text_sum[:192] + send(text_sum[192:].astype(jnp.bfloat16), pair_up(-1)).astype(jnp.float32)
    image_sum = image_own + sum(p.astype(jnp.float32) for p in image_parts)
    near_low = near.astype(jnp.bfloat16)
    image_low = image_sum.astype(jnp.bfloat16)
    text_parts = [send(near_low[48 * n : 48 * n + 48], along_z(-k)) for n, k in enumerate(ZOFFSETS, 1)]
    image_parts = [send(image_low[48 * n : 48 * n + 48], along_first(-k)) for n, k in enumerate(OFFSETS, 1)]

    for where in (
        swap, along_z(1), along_z(2), along_z(4), along_first(1), along_first(2), along_second(1), along_second(2),
    ):
        sums = sums + send(sums, where)

    finish = pl.pallas_call(
        finish_kernel,
        out_shape=f32(pairs, width),
        in_specs=[SMEM] + [VMEM] * 5,
        out_specs=VMEM,
    )
    image_grad = finish(scalars, image_raw, image_sum[:48], *image_parts)
    text_grad = finish(scalars, text_raw, near[:48], *text_parts)
    return (sums[0, 0:1] / total, image_grad, text_grad, sums[0, 2:3] * temp / total, sums[0, 1:2] / total)


def solution(mesh):
    fine = Mesh(mesh.devices.reshape(SIZES), AXES)
    rows = P(AXES, None)
    return jax.shard_map(
        body,
        mesh=fine,
        in_specs=(rows, rows, P(), P(), P(), P()),
        out_specs=(P(), rows, rows, P(), P()),
        check_vma=False,
    )
```

time: 412 us -> 137 us (0.33)
  waiting for transfers between devices: 269 us -> 60.6 us
  blocking collectives: 92.5 us -> 0 us
  starting transfers between devices: 0.12 us -> 42 us
  matrix products: 19.1 us -> 0 us
  Pallas kernels: 0 us -> 13.9 us
  other arithmetic: 10.7 us -> 0.61 us
  between operations: 17.1 us -> 8.82 us
  local copies, waits for them, and re-layouts: 2.02 us -> 9.71 us
    reduce_scatter x2 -> x0, waiting for transfers between devices: 181 us -> none  [the longest x1 181 us: body(): lax.psum_scatter(temp * lax.dot_general(scaled_low, text_block, (((0,), (...]
    all_gather x1 -> x0, waiting for transfers between devices: 88.3 us -> none  [body(): image_cols = lax.all_gather(image_unit, 'wide', axis=0, tiled=True)]
    psum x1 -> x0, blocking collectives: 76.2 us -> none  [body(): lax.psum((loss_part, bias_part, temp_part), ('wide', 'narrow'))]
    ppermute x0 -> x30, waiting for transfers between devices: none -> 60.6 us  [send(): return lax.ppermute(value, AXES, pairs)]
    ppermute x0 -> x30, starting transfers between devices: none -> 42 us  [send(): return lax.ppermute(value, AXES, pairs)]
    dot_general x3 -> x0, matrix products: 19.1 us -> none  [the longest x1 8.19 us: body(): lax.dot_general(scaled_low, text_block, (((0,), (0,)), ((), ())), preferr...]
    all_gather x1 -> x0, blocking collectives: 16.3 us -> none  [body(): text_block = lax.all_gather(text_unit, 'narrow', axis=0, tiled=True)]
    pallas_call x0 -> x4, Pallas kernels: none -> 13.9 us  [the longest x1 7.93 us: body(): pl.pallas_call(grid_kernel, out_shape=(f32(384, width), b16(384, width),...]
  transfers between devices with their start and end apart: 3 -> 30, of which waited for: 2 -> 15; matrix products, arithmetic and copies ran while one was open for 4% -> 5% of each run, Pallas kernels for 0% -> 2%
where the time goes in v1:
time: 137 us; the launch traced here: 136 us
  waiting for transfers between devices  60.6 us (44%)
  starting transfers between devices  42 us (31%)
  Pallas kernels  13.9 us (10%)
  local copies, waits for them, and re-layouts  9.71 us (7%)
  between operations  8.82 us (6%)
    ppermute x30, waiting for transfers between devices, send(): return lax.ppermute(value, AXES, pairs)  60.6 us
    ppermute x30, starting transfers between devices, send(): return lax.ppermute(value, AXES, pairs)  42 us
    pallas_call x1, Pallas kernels, body(): pl.pallas_call(grid_kernel, out_shape=(f32(384, width), b16(384, width),...  7.93 us
    unnamed x31, local copies, waits for them, and re-layouts  5.75 us
  transfers between devices with their start and end apart: 30, of which 15 were waited for; matrix products, arithmetic and copies ran while one was open for 5% of the time, Pallas kernels for 2%

profile of v1, /device:TPU:6, one launch (start us, length us, event | category | flops | bytes accessed | tf_op | source)
XLA Modules:
  0.0 135.6 jit_solution(10344489485724656422)
XLA Ops:
  0.6 1.9 %shard_map.101 = (bf16[48,1152]{1,0:T(8,128)(2,1)}, bf16[48,1152]{1,0:T(8,128)(2,1)}) custom-call(f32[48,1152]{1,0:T(8,128)} %raw.2, f32[48,1152]{1,0:T(8,128)} %raw.3), custom_call_target="tpu_custom_call" | custom-call | tf_op jit(solution)/shard_map/pallas_call | solution.py:135
  2.5 1.4 %collective-permute-start.7 = (bf16[48,1152]{1,0:T(8,128)(2,1)}, bf16[48,1152]{1,0:T(8,128)(2,1)S(1)}, u32[]{:S(2)}, u32[]{:S(2)}) collective-permute-start(bf16[48,1152]{1,0:T(8,128)(2,1)} %get-tuple-element.15), channel_id=1, source_target_pairs={{0,16},{1,17},{2,18},{3,19},{4,132},{5,133},{6,134},{7,135},{8,24}... | collective-permute-start | bytes 331784 | tf_op jit(solution)/shard_map/ppermute | solution.py:31
  3.9 1.7 %collective-permute-start.6 = (bf16[48,1152]{1,0:T(8,128)(2,1)}, bf16[48,1152]{1,0:T(8,128)(2,1)S(1)}, u32[]{:S(2)}, u32[]{:S(2)}) collective-permute-start(bf16[48,1152]{1,0:T(8,128)(2,1)} %get-tuple-element.15), channel_id=1, source_target_pairs={{0,24},{1,25},{2,26},{3,27},{4,196},{5,197},{6,198},{7,199},{8,0},... | collective-permute-start | bytes 331784 | tf_op jit(solution)/shard_map/ppermute | solution.py:31
  5.6 5.5 %collective-permute-start.2 = (bf16[48,1152]{1,0:T(8,128)(2,1)}, bf16[48,1152]{1,0:T(8,128)(2,1)S(1)}, u32[]{:S(2)}, u32[]{:S(2)}) collective-permute-start(bf16[48,1152]{1,0:T(8,128)(2,1)} %get-tuple-element.14), channel_id=1, source_target_pairs={{0,32},{1,33},{2,34},{3,35},{4,36},{5,37},{6,38},{7,39},{8,40},{9,... | collective-permute-start | bytes 331784 | tf_op jit(solution)/shard_map/ppermute | solution.py:31
  11.1 2.9 %collective-permute-start = (bf16[48,1152]{1,0:T(8,128)(2,1)}, bf16[48,1152]{1,0:T(8,128)(2,1)S(1)}, u32[]{:S(2)}, u32[]{:S(2)}) collective-permute-start(bf16[48,1152]{1,0:T(8,128)(2,1)} %get-tuple-element.14), channel_id=1, source_target_pairs={{0,2},{1,3},{2,32},{3,33},{4,6},{5,7},{6,36},{7,37},{8,10},{9,11},... | collective-permute-start | bytes 331784 | tf_op jit(solution)/shard_map/ppermute | solution.py:31
  14.0 0.9 constant_dynamic-update-slice_fusion.8
  14.9 0.9 constant_dynamic-update-slice_fusion.4
  18.8 3.3 %collective-permute-start.5 = (bf16[48,1152]{1,0:T(8,128)(2,1)S(1)}, bf16[48,1152]{1,0:T(8,128)(2,1)S(1)}, u32[]{:S(2)}, u32[]{:S(2)}) collective-permute-start(bf16[48,1152]{1,0:T(8,128)(2,1)S(1)} %copy-done.9), channel_id=1, source_target_pairs={{0,8},{1,9},{2,10},{3,11},{4,68},{5,69},{6,70},{7,71},{8,16},{9,17... | collective-permute-start | bytes 331784 | tf_op jit(solution)/shard_map/ppermute | solution.py:31
  22.1 1.0 collective-permute-done.1
  23.7 0.8 collective-permute-done.5
  24.4 8.2 %collective-permute-done.3 = bf16[192,1152]{1,0:T(8,128)(2,1)S(1)} collective-permute-done((bf16[192,1152]{1,0:T(8,128)(2,1)S(1)}, bf16[192,1152]{1,0:T(8,128)(2,1)S(1)}, u32[]{:S(2)}, u32[]{:S(2)}) %collective-permute-start.3) | collective-permute-done | bytes 442400 | tf_op jit(solution)/shard_map/ppermute | solution.py:31
  32.9 3.0 %collective-permute-start.10 = (bf16[192,1152]{1,0:T(8,128)(2,1)S(1)}, bf16[192,1152]{1,0:T(8,128)(2,1)S(1)}, u32[]{:S(2)}, u32[]{:S(2)}) collective-permute-start(bf16[192,1152]{1,0:T(8,128)(2,1)S(1)} %constant_dynamic-update-slice_fusion.5.i0), channel_id=1, source_target_pairs={{0,128},{1,129},{2,130},{3,131},{4,20},{5,21},{6,22},{7,23},{8,136... | collective-permute-start | bytes 1327112 | tf_op jit(solution)/shard_map/ppermute | solution.py:31
  35.9 1.1 collective-permute-start.9
  37.1 0.9 collective-permute-start.8
  38.0 0.6 gather_fusion.1
  38.7 0.6 gather_fusion
  39.6 3.3 %collective-permute-done.10.i3 = bf16[192,1152]{1,0:T(8,128)(2,1)S(1)} collective-permute-done((bf16[192,1152]{1,0:T(8,128)(2,1)S(1)}, bf16[192,1152]{1,0:T(8,128)(2,1)S(1)}, u32[]{:S(2)}, u32[]{:S(2)}) %collective-permute-start.10) | collective-permute-done | bytes 442400 | tf_op jit(solution)/shard_map/ppermute | solution.py:31
  42.9 4.1 %collective-permute-done.9.i2 = bf16[192,1152]{1,0:T(8,128)(2,1)S(1)} collective-permute-done((bf16[192,1152]{1,0:T(8,128)(2,1)S(1)}, bf16[192,1152]{1,0:T(8,128)(2,1)S(1)}, u32[]{:S(2)}, u32[]{:S(2)}) %collective-permute-start.9) | collective-permute-done | bytes 442400 | tf_op jit(solution)/shard_map/ppermute | solution.py:31
  47.0 0.6 collective-permute-done.8.i1
  47.5 7.9 %shard_map.102 = (f32[384,1152]{1,0:T(8,128)}, bf16[384,1152]{1,0:T(8,128)(2,1)S(1)}, f32[192,1152]{1,0:T(8,128)S(1)}, bf16[192,1152]{1,0:T(8,128)(2,1)S(1)}, bf...) custom-call(f32[2]{0:T(128)S(1)} %pad_maximum_fusion.1.scalars, ...), custom_call_target="tpu_custom_call" | custom-call | tf_op jit(solution)/shard_map/pallas_call | solution.py:170
  55.5 2.2 %collective-permute-start.19 = (bf16[192,1152]{1,0:T(8,128)(2,1)S(1)}, bf16[192,1152]{1,0:T(8,128)(2,1)S(1)}, u32[]{:S(2)}, u32[]{:S(2)}) collective-permute-start(bf16[192,1152]{1,0:T(8,128)(2,1)S(1)} %get-tuple-element.18), channel_id=1, source_target_pairs={{0,192},{1,193},{2,194},{3,195},{4,28},{5,29},{6,30},{7,31},{8,200... | collective-permute-start | bytes 1327112 | tf_op jit(solution)/shard_map/ppermute | solution.py:31
  57.6 2.9 %collective-permute-start.21 = (bf16[192,1152]{1,0:T(8,128)(2,1)S(1)}, bf16[192,1152]{1,0:T(8,128)(2,1)S(1)}, u32[]{:S(2)}, u32[]{:S(2)}) collective-permute-start(bf16[192,1152]{1,0:T(8,128)(2,1)S(1)} %get-tuple-element.20), channel_id=1, source_target_pairs={{0,128},{1,129},{2,130},{3,131},{4,20},{5,21},{6,22},{7,23},{8,136... | collective-permute-start | bytes 1327112 | tf_op jit(solution)/shard_map/ppermute | solution.py:31
  61.1 1.9 %collective-permute-done.11 = f32[8,128]{1,0:T(8,128)S(1)} collective-permute-done((f32[8,128]{1,0:T(8,128)S(1)}, f32[8,128]{1,0:T(8,128)S(1)}, u32[]{:S(2)}, u32[]{:S(2)}) %collective-permute-start.11) | collective-permute-done | bytes 4128 | tf_op jit(solution)/shard_map/ppermute | solution.py:31
  63.0 4.8 %collective-permute-done.12 = f32[8,128]{1,0:T(8,128)S(1)} collective-permute-done((f32[8,128]{1,0:T(8,128)S(1)}, f32[8,128]{1,0:T(8,128)S(1)}, u32[]{:S(2)}, u32[]{:S(2)}) %collective-permute-start.12) | collective-permute-done | bytes 4128 | tf_op jit(solution)/shard_map/ppermute | solution.py:31
  67.8 5.7 %collective-permute-done.13 = f32[8,128]{1,0:T(8,128)S(1)} collective-permute-done((f32[8,128]{1,0:T(8,128)S(1)}, f32[8,128]{1,0:T(8,128)S(1)}, u32[]{:S(2)}, u32[]{:S(2)}) %collective-permute-start.13) | collective-permute-done | bytes 4128 | tf_op jit(solution)/shard_map/ppermute | solution.py:31
  73.5 2.2 %collective-permute-start.14 = (f32[8,128]{1,0:T(8,128)S(1)}, f32[8,128]{1,0:T(8,128)S(1)}, u32[]{:S(2)}, u32[]{:S(2)}) collective-permute-start(f32[8,128]{1,0:T(8,128)S(1)} %add.852), channel_id=1, source_target_pairs={{0,32},{1,33},{2,34},{3,35},{4,36},{5,37},{6,38},{7,39},{8,40},{9,... | collective-permute-start | bytes 12296 | tf_op jit(solution)/shard_map/ppermute | solution.py:31
  75.8 5.3 %collective-permute-done.14 = f32[8,128]{1,0:T(8,128)S(1)} collective-permute-done((f32[8,128]{1,0:T(8,128)S(1)}, f32[8,128]{1,0:T(8,128)S(1)}, u32[]{:S(2)}, u32[]{:S(2)}) %collective-permute-start.14) | collective-permute-done | bytes 4128 | tf_op jit(solution)/shard_map/ppermute | solution.py:31
  81.6 3.1 %collective-permute-done.15 = f32[8,128]{1,0:T(8,128)S(1)} collective-permute-done((f32[8,128]{1,0:T(8,128)S(1)}, f32[8,128]{1,0:T(8,128)S(1)}, u32[]{:S(2)}, u32[]{:S(2)}) %collective-permute-start.15) | collective-permute-done | bytes 4128 | tf_op jit(solution)/shard_map/ppermute | solution.py:31
  84.7 1.5 %collective-permute-start.16 = (f32[8,128]{1,0:T(8,128)S(1)}, f32[8,128]{1,0:T(8,128)S(1)}, u32[]{:S(2)}, u32[]{:S(2)}) collective-permute-start(f32[8,128]{1,0:T(8,128)S(1)} %add.854), channel_id=1, source_target_pairs={{0,16},{1,17},{2,18},{3,19},{4,132},{5,133},{6,134},{7,135},{8,24}... | collective-permute-start | bytes 12296 | tf_op jit(solution)/shard_map/ppermute | solution.py:31
  86.2 3.6 %collective-permute-done.16 = f32[8,128]{1,0:T(8,128)S(1)} collective-permute-done((f32[8,128]{1,0:T(8,128)S(1)}, f32[8,128]{1,0:T(8,128)S(1)}, u32[]{:S(2)}, u32[]{:S(2)}) %collective-permute-start.16) | collective-permute-done | bytes 4128 | tf_op jit(solution)/shard_map/ppermute | solution.py:31
  89.8 1.2 collective-permute-start.17
  91.0 3.6 %collective-permute-done.17 = f32[8,128]{1,0:T(8,128)S(1)} collective-permute-done((f32[8,128]{1,0:T(8,128)S(1)}, f32[8,128]{1,0:T(8,128)S(1)}, u32[]{:S(2)}, u32[]{:S(2)}) %collective-permute-start.17) | collective-permute-done | bytes 4128 | tf_op jit(solution)/shard_map/ppermute | solution.py:31
  94.6 5.2 %collective-permute-done.18 = f32[8,128]{1,0:T(8,128)S(1)} collective-permute-done((f32[8,128]{1,0:T(8,128)S(1)}, f32[8,128]{1,0:T(8,128)S(1)}, u32[]{:S(2)}, u32[]{:S(2)}) %collective-permute-start.18) | collective-permute-done | bytes 4128 | tf_op jit(solution)/shard_map/ppermute | solution.py:31
  100.1 1.2 copy-done.1
  101.7 1.6 %collective-permute-start.24 = (bf16[48,1152]{1,0:T(8,128)(2,1)S(1)}, bf16[48,1152]{1,0:T(8,128)(2,1)S(1)}, u32[]{:S(2)}, u32[]{:S(2)}) collective-permute-start(bf16[48,1152]{1,0:T(8,128)(2,1)S(1)} %get-tuple-element.30), channel_id=1, source_target_pairs={{0,16},{1,17},{2,18},{3,19},{4,132},{5,133},{6,134},{7,135},{8,24}... | collective-permute-start | bytes 331784 | tf_op jit(solution)/shard_map/ppermute | solution.py:31
  103.3 1.9 %collective-permute-start.23 = (bf16[48,1152]{1,0:T(8,128)(2,1)S(1)}, bf16[48,1152]{1,0:T(8,128)(2,1)S(1)}, u32[]{:S(2)}, u32[]{:S(2)}) collective-permute-start(bf16[48,1152]{1,0:T(8,128)(2,1)S(1)} %get-tuple-element.31), channel_id=1, source_target_pairs={{0,8},{1,9},{2,10},{3,11},{4,68},{5,69},{6,70},{7,71},{8,16},{9,17... | collective-permute-start | bytes 331784 | tf_op jit(solution)/shard_map/ppermute | solution.py:31
  105.3 9.3 %collective-permute-done.26 = bf16[192,1152]{1,0:T(8,128)(2,1)S(1)} collective-permute-done((bf16[192,1152]{1,0:T(8,128)(2,1)S(1)}, bf16[192,1152]{1,0:T(8,128)(2,1)S(1)}, u32[]{:S(2)}, u32[]{:S(2)}) %collective-permute-start.26) | collective-permute-done | bytes 442400 | tf_op jit(solution)/shard_map/ppermute | solution.py:31
  114.8 2.6 %collective-permute-start.29 = (bf16[48,1152]{1,0:T(8,128)(2,1)S(1)}, bf16[48,1152]{1,0:T(8,128)(2,1)S(1)}, u32[]{:S(2)}, u32[]{:S(2)}) collective-permute-start(bf16[48,1152]{1,0:T(8,128)(2,1)S(1)} %get-tuple-element.27), channel_id=1, source_target_pairs={{0,32},{1,33},{2,34},{3,35},{4,36},{5,37},{6,38},{7,39},{8,40},{9,... | collective-permute-start | bytes 331784 | tf_op jit(solution)/shard_map/ppermute | solution.py:31
  117.4 4.1 %collective-permute-start.27 = (bf16[48,1152]{1,0:T(8,128)(2,1)S(1)}, bf16[48,1152]{1,0:T(8,128)(2,1)S(1)}, u32[]{:S(2)}, u32[]{:S(2)}) collective-permute-start(bf16[48,1152]{1,0:T(8,128)(2,1)S(1)} %get-tuple-element.29), channel_id=1, source_target_pairs={{0,34},{1,35},{2,0},{3,1},{4,38},{5,39},{6,4},{7,5},{8,42},{9,43},... | collective-permute-start | bytes 331784 | tf_op jit(solution)/shard_map/ppermute | solution.py:31
  121.5 0.6 fusion.6
  124.0 0.7 slice.57.own
  124.8 0.6 copy-done.4
  125.4 0.6 copy-done.6
  126.0 2.1 %shard_map.103 = f32[48,1152]{1,0:T(8,128)} custom-call(f32[2]{0:T(128)} %copy-done, f32[48,1152]{1,0:T(8,128)} %raw.2, f32[48,1152]{1,0:T(8,128)} %slice.57.own, bf16[48,1152]{1,0:T(8,128)(2,1)} %copy-done.6, bf16[48,1152]{1,0:T(8,128)(2,1)} %copy-done.4, bf16[48,1152]{1,0:T(8,128)(2,1)} %copy-done.3), custom_call_target="tpu_custom_call" | custom-call | tf_op jit(solution)/shard_map/pallas_call | solution.py:206
  128.1 0.7 slice.63.own
  128.9 0.6 copy-done.5
  129.5 0.6 copy-done.8
  130.2 2.1 %shard_map.104 = f32[48,1152]{1,0:T(8,128)} custom-call(f32[2]{0:T(128)} %copy-done, f32[48,1152]{1,0:T(8,128)} %raw.3, f32[48,1152]{1,0:T(8,128)} %slice.63.own, bf16[48,1152]{1,0:T(8,128)(2,1)} %copy-done.8, bf16[48,1152]{1,0:T(8,128)(2,1)} %copy-done.7, bf16[48,1152]{1,0:T(8,128)(2,1)} %copy-done.5), custom_call_target="tpu_custom_call" | custom-call | tf_op jit(solution)/shard_map/pallas_call | solution.py:207
  (79 shorter events, 3.5 us)
Async XLA Ops:
  0.6 17.8 %copy-start.10 = (s32[12288]{0:T(1024)S(1)}, s32[12288]{0:T(1024)}, u32[]{:S(2)}) copy-start(s32[12288]{0:T(1024)} %param.8) | copy-start | bytes 147460
  2.5 16.3 %copy-start.9 = (bf16[48,1152]{1,0:T(8,128)(2,1)S(1)}, bf16[48,1152]{1,0:T(8,128)(2,1)}, u32[]{:S(2)}) copy-start(bf16[48,1152]{1,0:T(8,128)(2,1)} %get-tuple-element.15) | copy-start | bytes 331780
  2.5 20.6 %copy-start.2 = (bf16[48,1152]{1,0:T(8,128)(2,1)S(1)}, bf16[48,1152]{1,0:T(8,128)(2,1)}, u32[]{:S(2)}) copy-start(bf16[48,1152]{1,0:T(8,128)(2,1)} %get-tuple-element.14) | copy-start | bytes 331780
  2.5 30.4 %collective-permute-start.7 = (bf16[48,1152]{1,0:T(8,128)(2,1)}, bf16[48,1152]{1,0:T(8,128)(2,1)S(1)}, u32[]{:S(2)}, u32[]{:S(2)}) collective-permute-start(bf16[48,1152]{1,0:T(8,128)(2,1)} %get-tuple-element.15), channel_id=1, source_target_pairs={{0,16},{1,17},{2,18},{3,19},{4,132},{5,133},{6,134},{7,135},{8,24}... | collective-permute-start | bytes 331784 | tf_op jit(solution)/shard_map/ppermute | solution.py:31
  3.9 28.9 %collective-permute-start.6 = (bf16[48,1152]{1,0:T(8,128)(2,1)}, bf16[48,1152]{1,0:T(8,128)(2,1)S(1)}, u32[]{:S(2)}, u32[]{:S(2)}) collective-permute-start(bf16[48,1152]{1,0:T(8,128)(2,1)} %get-tuple-element.15), channel_id=1, source_target_pairs={{0,24},{1,25},{2,26},{3,27},{4,196},{5,197},{6,198},{7,199},{8,0},... | collective-permute-start | bytes 331784 | tf_op jit(solution)/shard_map/ppermute | solution.py:31
  5.6 13.2 %collective-permute-start.2 = (bf16[48,1152]{1,0:T(8,128)(2,1)}, bf16[48,1152]{1,0:T(8,128)(2,1)S(1)}, u32[]{:S(2)}, u32[]{:S(2)}) collective-permute-start(bf16[48,1152]{1,0:T(8,128)(2,1)} %get-tuple-element.14), channel_id=1, source_target_pairs={{0,32},{1,33},{2,34},{3,35},{4,36},{5,37},{6,38},{7,39},{8,40},{9,... | collective-permute-start | bytes 331784 | tf_op jit(solution)/shard_map/ppermute | solution.py:31
  11.1 11.9 %collective-permute-start.1 = (bf16[48,1152]{1,0:T(8,128)(2,1)}, bf16[48,1152]{1,0:T(8,128)(2,1)S(1)}, u32[]{:S(2)}, u32[]{:S(2)}) collective-permute-start(bf16[48,1152]{1,0:T(8,128)(2,1)} %get-tuple-element.14), channel_id=1, source_target_pairs={{0,34},{1,35},{2,0},{3,1},{4,38},{5,39},{6,4},{7,5},{8,42},{9,43},... | collective-permute-start | bytes 331784 | tf_op jit(solution)/shard_map/ppermute | solution.py:31
  11.1 11.9 %collective-permute-start = (bf16[48,1152]{1,0:T(8,128)(2,1)}, bf16[48,1152]{1,0:T(8,128)(2,1)S(1)}, u32[]{:S(2)}, u32[]{:S(2)}) collective-permute-start(bf16[48,1152]{1,0:T(8,128)(2,1)} %get-tuple-element.14), channel_id=1, source_target_pairs={{0,2},{1,3},{2,32},{3,33},{4,6},{5,7},{6,36},{7,37},{8,10},{9,11},... | collective-permute-start | bytes 331784 | tf_op jit(solution)/shard_map/ppermute | solution.py:31
  17.0 21.6 %copy-start.11 = (s32[12288]{0:T(1024)S(1)}, s32[12288]{0:T(1024)}, u32[]{:S(2)}) copy-start(s32[12288]{0:T(1024)} %param.9) | copy-start | bytes 147460
  18.8 5.6 %collective-permute-start.5 = (bf16[48,1152]{1,0:T(8,128)(2,1)S(1)}, bf16[48,1152]{1,0:T(8,128)(2,1)S(1)}, u32[]{:S(2)}, u32[]{:S(2)}) collective-permute-start(bf16[48,1152]{1,0:T(8,128)(2,1)S(1)} %copy-done.9), channel_id=1, source_target_pairs={{0,8},{1,9},{2,10},{3,11},{4,68},{5,69},{6,70},{7,71},{8,16},{9,17... | collective-permute-start | bytes 331784 | tf_op jit(solution)/shard_map/ppermute | solution.py:31
  23.1 9.6 %collective-permute-start.3 = (bf16[192,1152]{1,0:T(8,128)(2,1)S(1)}, bf16[192,1152]{1,0:T(8,128)(2,1)S(1)}, u32[]{:S(2)}, u32[]{:S(2)}) collective-permute-start(bf16[192,1152]{1,0:T(8,128)(2,1)S(1)} %pad_maximum_fusion), channel_id=1, source_target_pairs={{0,1},{1,2},{2,3},{3,32},{4,39},{5,4},{6,5},{7,6},{8,9},{9,10},{10... | collective-permute-start | bytes 1327112 | tf_op jit(solution)/shard_map/ppermute | solution.py:31
  32.7 14.8 %collective-permute-start.4 = (bf16[384,1152]{1,0:T(8,128)(2,1)S(1)}, bf16[384,1152]{1,0:T(8,128)(2,1)}, u32[]{:S(2)}, u32[]{:S(2)}) collective-permute-start(bf16[384,1152]{1,0:T(8,128)(2,1)S(1)} %constant_dynamic-update-slice_fusion.t0), channel_id=1, source_target_pairs={{0,4},{1,5},{2,6},{3,7},{4,0},{5,1},{6,2},{7,3},{8,12},{9,13},{10,... | collective-permute-start | bytes 2654216 | tf_op jit(solution)/shard_map/ppermute | solution.py:31
  32.9 10.0 %collective-permute-start.10 = (bf16[192,1152]{1,0:T(8,128)(2,1)S(1)}, bf16[192,1152]{1,0:T(8,128)(2,1)S(1)}, u32[]{:S(2)}, u32[]{:S(2)}) collective-permute-start(bf16[192,1152]{1,0:T(8,128)(2,1)S(1)} %constant_dynamic-update-slice_fusion.5.i0), channel_id=1, source_target_pairs={{0,128},{1,129},{2,130},{3,131},{4,20},{5,21},{6,22},{7,23},{8,136... | collective-permute-start | bytes 1327112 | tf_op jit(solution)/shard_map/ppermute | solution.py:31
  35.9 11.0 %collective-permute-start.9 = (bf16[192,1152]{1,0:T(8,128)(2,1)S(1)}, bf16[192,1152]{1,0:T(8,128)(2,1)S(1)}, u32[]{:S(2)}, u32[]{:S(2)}) collective-permute-start(bf16[192,1152]{1,0:T(8,128)(2,1)S(1)} %constant_dynamic-update-slice_fusion.5.i0), channel_id=1, source_target_pairs={{0,192},{1,193},{2,194},{3,195},{4,28},{5,29},{6,30},{7,31},{8,200... | collective-permute-start | bytes 1327112 | tf_op jit(solution)/shard_map/ppermute | solution.py:31
  37.1 10.5 %collective-permute-start.8 = (bf16[192,1152]{1,0:T(8,128)(2,1)S(1)}, bf16[192,1152]{1,0:T(8,128)(2,1)S(1)}, u32[]{:S(2)}, u32[]{:S(2)}) collective-permute-start(bf16[192,1152]{1,0:T(8,128)(2,1)S(1)} %constant_dynamic-update-slice_fusion.5.i0), channel_id=1, source_target_pairs={{0,64},{1,65},{2,66},{3,67},{4,12},{5,13},{6,14},{7,15},{8,72},{9,... | collective-permute-start | bytes 1327112 | tf_op jit(solution)/shard_map/ppermute | solution.py:31
  39.6 15.9 %copy-start = (f32[2]{0:T(128)}, f32[2]{0:T(128)S(1)}, u32[]{:S(2)}) copy-start(f32[2]{0:T(128)S(1)} %pad_maximum_fusion.1.scalars) | copy-start | bytes 28
  55.5 44.3 %collective-permute-start.19 = (bf16[192,1152]{1,0:T(8,128)(2,1)S(1)}, bf16[192,1152]{1,0:T(8,128)(2,1)S(1)}, u32[]{:S(2)}, u32[]{:S(2)}) collective-permute-start(bf16[192,1152]{1,0:T(8,128)(2,1)S(1)} %get-tuple-element.18), channel_id=1, source_target_pairs={{0,192},{1,193},{2,194},{3,195},{4,28},{5,29},{6,30},{7,31},{8,200... | collective-permute-start | bytes 1327112 | tf_op jit(solution)/shard_map/ppermute | solution.py:31
  57.6 42.2 %collective-permute-start.20 = (bf16[192,1152]{1,0:T(8,128)(2,1)S(1)}, bf16[192,1152]{1,0:T(8,128)(2,1)S(1)}, u32[]{:S(2)}, u32[]{:S(2)}) collective-permute-start(bf16[192,1152]{1,0:T(8,128)(2,1)S(1)} %get-tuple-element.19), channel_id=1, source_target_pairs={{0,64},{1,65},{2,66},{3,67},{4,12},{5,13},{6,14},{7,15},{8,72},{9,... | collective-permute-start | bytes 1327112 | tf_op jit(solution)/shard_map/ppermute | solution.py:31
  57.6 42.2 %collective-permute-start.21 = (bf16[192,1152]{1,0:T(8,128)(2,1)S(1)}, bf16[192,1152]{1,0:T(8,128)(2,1)S(1)}, u32[]{:S(2)}, u32[]{:S(2)}) collective-permute-start(bf16[192,1152]{1,0:T(8,128)(2,1)S(1)} %get-tuple-element.20), channel_id=1, source_target_pairs={{0,128},{1,129},{2,130},{3,131},{4,20},{5,21},{6,22},{7,23},{8,136... | collective-permute-start | bytes 1327112 | tf_op jit(solution)/shard_map/ppermute | solution.py:31
  60.6 39.5 %collective-permute-start.25 = (bf16[384,1152]{1,0:T(8,128)(2,1)S(1)}, bf16[384,1152]{1,0:T(8,128)(2,1)S(1)}, u32[]{:S(2)}, u32[]{:S(2)}) collective-permute-start(bf16[384,1152]{1,0:T(8,128)(2,1)S(1)} %get-tuple-element.22), channel_id=1, source_target_pairs={{0,4},{1,5},{2,6},{3,7},{4,0},{5,1},{6,2},{7,3},{8,12},{9,13},{10,... | collective-permute-start | bytes 2654216 | tf_op jit(solution)/shard_map/ppermute | solution.py:31
  60.6 2.4 %collective-permute-start.11 = (f32[8,128]{1,0:T(8,128)S(1)}, f32[8,128]{1,0:T(8,128)S(1)}, u32[]{:S(2)}, u32[]{:S(2)}) collective-permute-start(f32[8,128]{1,0:T(8,128)S(1)} %get-tuple-element.16), channel_id=1, source_target_pairs={{0,4},{1,5},{2,6},{3,7},{4,0},{5,1},{6,2},{7,3},{8,12},{9,13},{10,... | collective-permute-start | bytes 12296 | tf_op jit(solution)/shard_map/ppermute | solution.py:31
  63.0 4.8 %collective-permute-start.12 = (f32[8,128]{1,0:T(8,128)S(1)}, f32[8,128]{1,0:T(8,128)S(1)}, u32[]{:S(2)}, u32[]{:S(2)}) collective-permute-start(f32[8,128]{1,0:T(8,128)S(1)} %add.850), channel_id=1, source_target_pairs={{0,1},{1,2},{2,3},{3,32},{4,5},{5,6},{6,7},{7,36},{8,9},{9,10},{10... | collective-permute-start | bytes 12296 | tf_op jit(solution)/shard_map/ppermute | solution.py:31
  67.8 5.7 %collective-permute-start.13 = (f32[8,128]{1,0:T(8,128)S(1)}, f32[8,128]{1,0:T(8,128)S(1)}, u32[]{:S(2)}, u32[]{:S(2)}) collective-permute-start(f32[8,128]{1,0:T(8,128)S(1)} %add.851), channel_id=1, source_target_pairs={{0,2},{1,3},{2,32},{3,33},{4,6},{5,7},{6,36},{7,37},{8,10},{9,11},... | collective-permute-start | bytes 12296 | tf_op jit(solution)/shard_map/ppermute | solution.py:31
  73.5 7.5 %collective-permute-start.14 = (f32[8,128]{1,0:T(8,128)S(1)}, f32[8,128]{1,0:T(8,128)S(1)}, u32[]{:S(2)}, u32[]{:S(2)}) collective-permute-start(f32[8,128]{1,0:T(8,128)S(1)} %add.852), channel_id=1, source_target_pairs={{0,32},{1,33},{2,34},{3,35},{4,36},{5,37},{6,38},{7,39},{8,40},{9,... | collective-permute-start | bytes 12296 | tf_op jit(solution)/shard_map/ppermute | solution.py:31
  81.1 3.6 %collective-permute-start.15 = (f32[8,128]{1,0:T(8,128)S(1)}, f32[8,128]{1,0:T(8,128)S(1)}, u32[]{:S(2)}, u32[]{:S(2)}) collective-permute-start(f32[8,128]{1,0:T(8,128)S(1)} %add.853), channel_id=1, source_target_pairs={{0,8},{1,9},{2,10},{3,11},{4,68},{5,69},{6,70},{7,71},{8,16},{9,17... | collective-permute-start | bytes 12296 | tf_op jit(solution)/shard_map/ppermute | solution.py:31
  84.7 5.1 %collective-permute-start.16 = (f32[8,128]{1,0:T(8,128)S(1)}, f32[8,128]{1,0:T(8,128)S(1)}, u32[]{:S(2)}, u32[]{:S(2)}) collective-permute-start(f32[8,128]{1,0:T(8,128)S(1)} %add.854), channel_id=1, source_target_pairs={{0,16},{1,17},{2,18},{3,19},{4,132},{5,133},{6,134},{7,135},{8,24}... | collective-permute-start | bytes 12296 | tf_op jit(solution)/shard_map/ppermute | solution.py:31
  89.8 4.8 %collective-permute-start.17 = (f32[8,128]{1,0:T(8,128)S(1)}, f32[8,128]{1,0:T(8,128)S(1)}, u32[]{:S(2)}, u32[]{:S(2)}) collective-permute-start(f32[8,128]{1,0:T(8,128)S(1)} %add.855), channel_id=1, source_target_pairs={{0,64},{1,65},{2,66},{3,67},{4,12},{5,13},{6,14},{7,15},{8,72},{9,... | collective-permute-start | bytes 12296 | tf_op jit(solution)/shard_map/ppermute | solution.py:31
  94.6 5.2 %collective-permute-start.18 = (f32[8,128]{1,0:T(8,128)S(1)}, f32[8,128]{1,0:T(8,128)S(1)}, u32[]{:S(2)}, u32[]{:S(2)}) collective-permute-start(f32[8,128]{1,0:T(8,128)S(1)} %add.856), channel_id=1, source_target_pairs={{0,128},{1,129},{2,130},{3,131},{4,20},{5,21},{6,22},{7,23},{8,136... | collective-permute-start | bytes 12296 | tf_op jit(solution)/shard_map/ppermute | solution.py:31
  99.9 1.5 %copy-start.1 = (f32[384,1152]{1,0:T(8,128)S(1)}, f32[384,1152]{1,0:T(8,128)}, u32[]{:S(2)}) copy-start(f32[384,1152]{1,0:T(8,128)} %get-tuple-element.21) | copy-start | bytes 5308420
  101.5 13.1 %collective-permute-start.26 = (bf16[192,1152]{1,0:T(8,128)(2,1)S(1)}, bf16[192,1152]{1,0:T(8,128)(2,1)S(1)}, u32[]{:S(2)}, u32[]{:S(2)}) collective-permute-start(bf16[192,1152]{1,0:T(8,128)(2,1)S(1)} %slice.69), channel_id=1, source_target_pairs={{0,35},{1,0},{2,1},{3,2},{4,5},{5,6},{6,7},{7,36},{8,43},{9,8},{10... | collective-permute-start | bytes 1327112 | tf_op jit(solution)/shard_map/ppermute | solution.py:31
  101.7 15.7 %collective-permute-start.24 = (bf16[48,1152]{1,0:T(8,128)(2,1)S(1)}, bf16[48,1152]{1,0:T(8,128)(2,1)S(1)}, u32[]{:S(2)}, u32[]{:S(2)}) collective-permute-start(bf16[48,1152]{1,0:T(8,128)(2,1)S(1)} %get-tuple-element.30), channel_id=1, source_target_pairs={{0,16},{1,17},{2,18},{3,19},{4,132},{5,133},{6,134},{7,135},{8,24}... | collective-permute-start | bytes 331784 | tf_op jit(solution)/shard_map/ppermute | solution.py:31
  103.3 21.5 %collective-permute-start.23 = (bf16[48,1152]{1,0:T(8,128)(2,1)S(1)}, bf16[48,1152]{1,0:T(8,128)(2,1)S(1)}, u32[]{:S(2)}, u32[]{:S(2)}) collective-permute-start(bf16[48,1152]{1,0:T(8,128)(2,1)S(1)} %get-tuple-element.31), channel_id=1, source_target_pairs={{0,8},{1,9},{2,10},{3,11},{4,68},{5,69},{6,70},{7,71},{8,16},{9,17... | collective-permute-start | bytes 331784 | tf_op jit(solution)/shard_map/ppermute | solution.py:31
  105.2 19.5 %collective-permute-start.22 = (bf16[48,1152]{1,0:T(8,128)(2,1)S(1)}, bf16[48,1152]{1,0:T(8,128)(2,1)S(1)}, u32[]{:S(2)}, u32[]{:S(2)}) collective-permute-start(bf16[48,1152]{1,0:T(8,128)(2,1)S(1)} %get-tuple-element.32), channel_id=1, source_target_pairs={{0,24},{1,25},{2,26},{3,27},{4,196},{5,197},{6,198},{7,199},{8,0},... | collective-permute-start | bytes 331784 | tf_op jit(solution)/shard_map/ppermute | solution.py:31
  114.8 14.0 %collective-permute-start.29 = (bf16[48,1152]{1,0:T(8,128)(2,1)S(1)}, bf16[48,1152]{1,0:T(8,128)(2,1)S(1)}, u32[]{:S(2)}, u32[]{:S(2)}) collective-permute-start(bf16[48,1152]{1,0:T(8,128)(2,1)S(1)} %get-tuple-element.27), channel_id=1, source_target_pairs={{0,32},{1,33},{2,34},{3,35},{4,36},{5,37},{6,38},{7,39},{8,40},{9,... | collective-permute-start | bytes 331784 | tf_op jit(solution)/shard_map/ppermute | solution.py:31
  117.3 11.5 %collective-permute-start.28 = (bf16[48,1152]{1,0:T(8,128)(2,1)S(1)}, bf16[48,1152]{1,0:T(8,128)(2,1)S(1)}, u32[]{:S(2)}, u32[]{:S(2)}) collective-permute-start(bf16[48,1152]{1,0:T(8,128)(2,1)S(1)} %get-tuple-element.28), channel_id=1, source_target_pairs={{0,2},{1,3},{2,32},{3,33},{4,6},{5,7},{6,36},{7,37},{8,10},{9,11},... | collective-permute-start | bytes 331784 | tf_op jit(solution)/shard_map/ppermute | solution.py:31
  117.4 7.4 %copy-start.3 = (bf16[48,1152]{1,0:T(8,128)(2,1)}, bf16[48,1152]{1,0:T(8,128)(2,1)S(1)}, u32[]{:S(2)}) copy-start(bf16[48,1152]{1,0:T(8,128)(2,1)S(1)} %collective-permute-done.24.r3) | copy-start | bytes 331780
  117.4 11.5 %collective-permute-start.27 = (bf16[48,1152]{1,0:T(8,128)(2,1)S(1)}, bf16[48,1152]{1,0:T(8,128)(2,1)S(1)}, u32[]{:S(2)}, u32[]{:S(2)}) collective-permute-start(bf16[48,1152]{1,0:T(8,128)(2,1)S(1)} %get-tuple-element.29), channel_id=1, source_target_pairs={{0,34},{1,35},{2,0},{3,1},{4,38},{5,39},{6,4},{7,5},{8,42},{9,43},... | collective-permute-start | bytes 331784 | tf_op jit(solution)/shard_map/ppermute | solution.py:31
  124.7 0.7 copy-start.4
  125.4 0.6 copy-start.6
  128.8 0.6 copy-start.5
  128.8 0.7 copy-start.7
  129.5 0.6 copy-start.8

commit v2 on v1

v2 whole, which is shorter than its diff:
```python
import math

import jax
import jax.numpy as jnp
import numpy as np
from jax import lax
from jax.experimental import pallas as pl
from jax.experimental.pallas import tpu as pltpu
from jax.sharding import Mesh
from jax.sharding import PartitionSpec as P

SIZES = (4, 2, 4, 2, 4)
AXES = ("y", "zh", "x", "core", "zl")
ROWS = 48
OFFSETS = (1, 3, 2)
ZOFFSETS = (2, 6, 4)
VMEM = pl.BlockSpec(memory_space=pltpu.VMEM)
SMEM = pl.BlockSpec(memory_space=pltpu.SMEM)


def flat(x, y, z, c):
    return (((y * 2 + z // 4) * 4 + x) * 2 + c) * 4 + z % 4


def send(value, where, name="move"):
    pairs = []
    for y, zh, x, c, zl in np.ndindex(*SIZES):
        z = zh * 4 + zl
        tx, ty, tz, tc = where(x, y, z, c)
        pairs.append((flat(x, y, z, c), flat(tx % 4, ty % 4, tz % 8, tc % 2)))
    with jax.named_scope(name):
        return lax.ppermute(value, AXES, pairs)


def along_first(k):
    return lambda x, y, z, c: (x + k, y, z, c) if c == 0 else (x, y + k, z, c)


def along_second(k):
    return lambda x, y, z, c: (x, y + k, z, c) if c == 0 else (x + k, y, z, c)


def along_z(k):
    return lambda x, y, z, c: (x, y, z + k, c)


def pair_up(sign):
    return lambda x, y, z, c: (x, y, z + sign, c) if c == 0 else (x, y, z - sign, c)


def swap(x, y, z, c):
    return (x, y, z, 1 - c)


def unit_kernel(image_ref, text_ref, image_out, text_out):
    for src, dst in ((image_ref, image_out), (text_ref, text_out)):
        rows = src[...]
        scale = jnp.sqrt(jnp.mean(rows * rows, axis=-1, keepdims=True) + 1e-06)
        dst[...] = (rows / (scale * math.sqrt(rows.shape[-1]))).astype(jnp.bfloat16)


def join_kernel(*refs):
    *sources, out = refs
    rows = sources[0].shape[0]
    for n, src in enumerate(sources):
        out[rows * n : rows * (n + 1), :] = src[...]


def join(*pieces):
    rows, width = pieces[0].shape
    return pl.pallas_call(
        join_kernel,
        out_shape=b16(rows * len(pieces), width),
        in_specs=[VMEM] * len(pieces),
        out_specs=VMEM,
    )(*pieces)


def terms_kernel(scalars, rows_id, cols_id, before, t0, t1, i0, i1, i2, i3, *refs):
    *far, scaled, sums, text, image = refs
    temp = scalars[0]
    offset = scalars[1]
    for n, src in enumerate((t0, t1)):
        text[192 * n : 192 * (n + 1), :] = src[...]
    for n, src in enumerate((i0, i1, i2, i3)):
        image[192 * n : 192 * (n + 1), :] = src[...]
    totals = [before[n] for n in range(3)]
    cols = cols_id[...]
    for tile in range(2):
        at = slice(192 * tile, 192 * (tile + 1))
        cosine = lax.dot_general(
            text[at, :], image[...], (((1,), (1,)), ((), ())), preferred_element_type=jnp.float32
        )
        logits = temp * cosine + offset
        same = rows_id[at, :] == cols
        margin = jnp.where(same, -logits, logits)
        decay = jnp.exp(-jnp.abs(margin))
        inverse = 1.0 / (1.0 + decay)
        sigmoid = jnp.where(margin >= 0, inverse, decay * inverse)
        grad = jnp.where(same, -sigmoid, sigmoid)
        loss = jnp.maximum(margin, 0.0) + jnp.log1p(decay)
        scaled[at, :] = grad.astype(jnp.bfloat16)
        for n, value in enumerate((loss, grad, grad * cosine)):
            totals[n] = totals[n] + jnp.sum(value.reshape(24, 8, 768), axis=0)
    if not far:
        for n in range(3):
            sums[n] = totals[n]
        return
    lane = lax.broadcasted_iota(jnp.int32, (8, 128), 1)
    out = jnp.zeros((8, 128), jnp.float32)
    for n in range(3):
        out = jnp.where(lane == n, jnp.sum(totals[n]), out)
    sums[...] = out
    part = lax.dot_general(
        scaled[...], text[...], (((0,), (0,)), ((), ())), preferred_element_type=jnp.float32
    )
    for n, dst in enumerate(far):
        dst[...] = part[192 * n : 192 * (n + 1)].astype(dst.dtype)


def text_kernel(scaled_own, scaled_far, i0, i1, i2, i3, j0, j1, j2, j3, own, next_low, image):
    total = None
    for scaled, parts in ((scaled_own, (i0, i1, i2, i3)), (scaled_far, (j0, j1, j2, j3))):
        for n, src in enumerate(parts):
            image[192 * n : 192 * (n + 1), :] = src[...]
        part = jnp.dot(scaled[...], image[...], preferred_element_type=jnp.float32)
        total = part if total is None else total + part
    own[...] = total[:192]
    next_low[...] = total[192:].astype(next_low.dtype)


def image_kernel(scaled, t0, t1, b0, b1, b2, b3, sums, own, low1, low2, low3, sums_out, text):
    for n, src in enumerate((t0, t1)):
        text[192 * n : 192 * (n + 1), :] = src[...]
    part = lax.dot_general(
        scaled[...], text[...], (((0,), (0,)), ((), ())), preferred_element_type=jnp.float32
    )
    for n, (back, dst) in enumerate(zip((b0, b1, b2, b3), (own, low1, low2, low3))):
        dst[...] = (part[192 * n : 192 * (n + 1)] + back[...].astype(jnp.float32)).astype(dst.dtype)
    sums_out[...] = sums[...]


def add_kernel(own, r1, r2, r3, sums, out_own, low1, low2, low3, sums_out):
    total = own[...] + r1[...].astype(jnp.float32) + r2[...].astype(jnp.float32) + r3[...].astype(jnp.float32)
    out_own[...] = total[:48]
    for n, dst in enumerate((low1, low2, low3), 1):
        dst[...] = total[48 * n : 48 * (n + 1)].astype(dst.dtype)
    sums_out[...] = sums[...]


def near_kernel(own, r1, out_own, low1, low2, low3):
    total = own[...] + r1[...].astype(jnp.float32)
    out_own[...] = total[:48]
    for n, dst in enumerate((low1, low2, low3), 1):
        dst[...] = total[48 * n : 48 * (n + 1)].astype(dst.dtype)


def local(kernel, out_shape, *args, scratch=()):
    return pl.pallas_call(
        kernel,
        out_shape=out_shape,
        in_specs=[SMEM if a.shape == (2,) else VMEM for a in args],
        out_specs=tuple(VMEM for _ in out_shape),
        scratch_shapes=list(scratch),
        compiler_params=pltpu.CompilerParams(vmem_limit_bytes=48 * 1024 * 1024),
    )(*args)


def finish_kernel(scalars, raw, own, r1, r2, r3, out):
    rows = raw[...]
    width = rows.shape[-1]
    grad = own[...] + r1[...].astype(jnp.float32) + r2[...].astype(jnp.float32) + r3[...].astype(jnp.float32)
    grad = grad * scalars[0]
    square = jnp.mean(rows * rows, axis=-1, keepdims=True) + 1e-06
    inner = jnp.sum(rows * grad, axis=-1, keepdims=True)
    out[...] = (grad - rows * (inner / (square * width))) / (jnp.sqrt(square) * math.sqrt(width))


def f32(*shape):
    return jax.ShapeDtypeStruct(shape, jnp.float32)


def b16(*shape):
    return jax.ShapeDtypeStruct(shape, jnp.bfloat16)


def body(image_raw, text_raw, image_ids, text_ids, log_temp, bias):
    pairs, width = image_raw.shape
    total = pairs * 256
    x, y, c = lax.axis_index("x"), lax.axis_index("y"), lax.axis_index("core")
    z = lax.axis_index("zh") * 4 + lax.axis_index("zl")
    image_unit, text_unit = pl.pallas_call(
        unit_kernel,
        out_shape=(b16(pairs, width), b16(pairs, width)),
        in_specs=[VMEM] * 2,
        out_specs=(VMEM, VMEM),
    )(image_raw, text_raw)

    line = join(image_unit, *[send(image_unit, along_first(k), "first") for k in OFFSETS])
    ring = join(text_unit, *[send(text_unit, along_z(k), "zq") for k in ZOFFSETS])
    plane = [line] + [send(line, along_second(k), "second") for k in OFFSETS]
    ring_next = send(ring, pair_up(1), "za")
    plane_far = [send(p, swap, "swap") for p in plane]

    back = (0,) + OFFSETS
    zback = (0,) + ZOFFSETS
    cols_from = []
    for core in (c, 1 - c):
        for k in back:
            for j in back:
                sx = jnp.where(core == 0, x - j, x - k) % 4
                sy = jnp.where(core == 0, y - k, y - j) % 4
                cols_from.append(flat(sx, sy, z, core))
    rows_from = []
    for step in (0, 1):
        start = z + jnp.where(c == 0, -step, step)
        for k in zback:
            rows_from.append(flat(x, y, (start - k) % 8, c))
    cols_id = image_ids.reshape(256, pairs)[jnp.stack(cols_from)].reshape(1, 32 * pairs)
    rows_id = text_ids.reshape(256, pairs)[jnp.stack(rows_from)].reshape(8 * pairs, 1)

    temp = jnp.exp(log_temp[0])
    scalars = jnp.stack([temp, bias[0]])
    text = (ring, ring_next)
    copies = (pltpu.VMEM((384, width), jnp.bfloat16), pltpu.VMEM((768, width), jnp.bfloat16))
    scaled_own, sums = local(
        terms_kernel, (b16(384, 768), f32(3, 8, 768)),
        scalars, rows_id, cols_id[:, :768], jnp.zeros((3, 8, 768), jnp.float32), *text, *plane, scratch=copies,
    )
    *far, scaled_far, sums = local(
        terms_kernel, (b16(192, width),) * 4 + (b16(384, 768), f32(8, 128)),
        scalars, rows_id, cols_id[:, 768:], sums, *text, *plane_far, scratch=copies,
    )
    back = [send(p, swap, "rswap") for p in far]
    text_own, text_next = local(
        text_kernel, (f32(192, width), b16(192, width)), scaled_own, scaled_far, *plane, *plane_far, scratch=copies[1:],
    )
    text_back = send(text_next, pair_up(-1), "rza")
    image_own, *lows, sums = local(
        image_kernel, (f32(192, width),) + (b16(192, width),) * 3 + (f32(8, 128),),
        scaled_own, *text, *back, sums, scratch=copies[:1],
    )
    image_parts = [send(p, along_second(-k), "rsecond") for p, k in zip(lows, OFFSETS)]
    text_own, *lows = local(
        near_kernel, (f32(pairs, width),) + (b16(pairs, width),) * 3, text_own, text_back,
    )
    text_parts = [send(p, along_z(-k), "rzq") for p, k in zip(lows, ZOFFSETS)]

    def spread(sums, axes, count):
        with jax.named_scope("terms"):
            return lax.all_to_all(jnp.broadcast_to(sums[None], (count, 8, 128)), axes, 0, 0, tiled=True).sum(0)

    sums = spread(sums, ("y", "x", "core"), 32)
    image_own, *lows, sums = local(
        add_kernel, (f32(pairs, width),) + (b16(pairs, width),) * 3 + (f32(8, 128),), image_own, *image_parts, sums,
    )
    image_parts = [send(p, along_first(-k), "rfirst") for p, k in zip(lows, OFFSETS)]
    sums = spread(sums, ("zh", "zl"), 8)

    finish = pl.pallas_call(
        finish_kernel,
        out_shape=f32(pairs, width),
        in_specs=[SMEM] + [VMEM] * 5,
        out_specs=VMEM,
    )
    image_grad = finish(scalars, image_raw, image_own, *image_parts)
    text_grad = finish(scalars, text_raw, text_own, *text_parts)
    return (sums[0, 0:1] / total, image_grad, text_grad, sums[0, 2:3] * temp / total, sums[0, 1:2] / total)


def solution(mesh):
    fine = Mesh(mesh.devices.reshape(SIZES), AXES)
    rows = P(AXES, None)
    return jax.shard_map(
        body,
        mesh=fine,
        in_specs=(rows, rows, P(), P(), P(), P()),
        out_specs=(P(), rows, rows, P(), P()),
        check_vma=False,
    )
```

time: 137 us -> 111 us (0.81)
  waiting for transfers between devices: 60.6 us -> 14.4 us
  Pallas kernels: 13.9 us -> 23.2 us
  starting transfers between devices: 42 us -> 50.1 us
  local copies, waits for them, and re-layouts: 9.71 us -> 12.9 us
    ppermute x30 -> x28, waiting for transfers between devices: 60.6 us -> 14.4 us  [send(): return lax.ppermute(value, AXES, pairs)]
    all_to_all x0 -> x2, starting transfers between devices: none -> 11.2 us  [spread(): lax.all_to_all(jnp.broadcast_to(sums[None], (count, 8, 128)), axes, 0, 0,...]
    pallas_call x3 -> x10, Pallas kernels: 12.1 us -> 21.4 us  [the longest x6 13.5 us: local(): pl.pallas_call(kernel, out_shape=out_shape, in_specs=[SMEM if a.shape ==...]
    ppermute x30 -> x28, starting transfers between devices: 42 us -> 38.8 us  [send(): return lax.ppermute(value, AXES, pairs)]
    slice x5 -> x1, local copies, waits for them, and re-layouts: 1.52 us -> 0.01 us  [body(): cols_id[:, 768:]]
    unnamed x31 -> x50, local copies, waits for them, and re-layouts: 5.75 us -> 7.02 us
  transfers between devices with their start and end apart: 30 -> 30, of which waited for: 15 -> 5; matrix products, arithmetic and copies ran while one was open for 5% -> 6% of each run, Pallas kernels for 2% -> 14%
where the time goes in v2:
time: 111 us; the launch traced here: 110 us
  starting transfers between devices  50.1 us (45%)
  Pallas kernels  23.2 us (21%)
  waiting for transfers between devices  14.4 us (13%)
  local copies, waits for them, and re-layouts  12.9 us (12%)
  between operations  7.89 us (7%)
    ppermute x28, starting transfers between devices, send(): return lax.ppermute(value, AXES, pairs)  38.8 us
    ppermute x28, waiting for transfers between devices, send(): return lax.ppermute(value, AXES, pairs)  14.4 us
    pallas_call x6, Pallas kernels, local(): pl.pallas_call(kernel, out_shape=out_shape, in_specs=[SMEM if a.shape ==...  13.5 us
    all_to_all x2, starting transfers between devices, spread(): lax.all_to_all(jnp.broadcast_to(sums[None], (count, 8, 128)), axes, 0, 0,...  11.2 us
    unnamed x50, local copies, waits for them, and re-layouts  7.02 us
    pallas_call x2, Pallas kernels, join(): pl.pallas_call(join_kernel, out_shape=b16(rows * len(pieces), width), in_...  3.72 us
  transfers between devices with their start and end apart: 30, of which 5 were waited for; matrix products, arithmetic and copies ran while one was open for 6% of the time, Pallas kernels for 14%

profile of v2, /device:TPU:6, one launch (start us, length us, event | category | flops | bytes accessed | tf_op | source)
XLA Modules:
  0.0 109.6 jit_solution(7665089091028747964)
XLA Ops:
  0.6 1.8 %shard_map.101 = (bf16[48,1152]{1,0:T(8,128)(2,1)}, bf16[48,1152]{1,0:T(8,128)(2,1)}) custom-call(f32[48,1152]{1,0:T(8,128)} %raw.2, f32[48,1152]{1,0:T(8,128)} %raw.3), custom_call_target="tpu_custom_call" | custom-call | tf_op jit(solution)/shard_map/pallas_call | solution.py:192
  2.5 1.4 %collective-permute-start.6 = (bf16[48,1152]{1,0:T(8,128)(2,1)}, bf16[48,1152]{1,0:T(8,128)(2,1)S(1)}, u32[]{:S(2)}, u32[]{:S(2)}) collective-permute-start(bf16[48,1152]{1,0:T(8,128)(2,1)} %get-tuple-element.32.refs_0_), channel_id=1, source_target_pairs={{0,16},{1,17},{2,18},{3,19},{4,132},{5,133},{6,134},{7,135},{8,24}... | collective-permute-start | bytes 331784 | tf_op jit(solution)/shard_map/first/ppermute | solution.py:32
  3.9 1.7 %collective-permute-start.5 = (bf16[48,1152]{1,0:T(8,128)(2,1)}, bf16[48,1152]{1,0:T(8,128)(2,1)S(1)}, u32[]{:S(2)}, u32[]{:S(2)}) collective-permute-start(bf16[48,1152]{1,0:T(8,128)(2,1)} %get-tuple-element.32.refs_0_), channel_id=1, source_target_pairs={{0,24},{1,25},{2,26},{3,27},{4,196},{5,197},{6,198},{7,199},{8,0},... | collective-permute-start | bytes 331784 | tf_op jit(solution)/shard_map/first/ppermute | solution.py:32
  5.5 1.6 %collective-permute-start.4 = (bf16[48,1152]{1,0:T(8,128)(2,1)}, bf16[48,1152]{1,0:T(8,128)(2,1)S(1)}, u32[]{:S(2)}, u32[]{:S(2)}) collective-permute-start(bf16[48,1152]{1,0:T(8,128)(2,1)} %get-tuple-element.32.refs_0_), channel_id=1, source_target_pairs={{0,8},{1,9},{2,10},{3,11},{4,68},{5,69},{6,70},{7,71},{8,16},{9,17... | collective-permute-start | bytes 331784 | tf_op jit(solution)/shard_map/first/ppermute | solution.py:32
  7.1 7.2 %collective-permute-start.2 = (bf16[48,1152]{1,0:T(8,128)(2,1)}, bf16[48,1152]{1,0:T(8,128)(2,1)S(1)}, u32[]{:S(2)}, u32[]{:S(2)}) collective-permute-start(bf16[48,1152]{1,0:T(8,128)(2,1)} %get-tuple-element.31.refs_0_), channel_id=1, source_target_pairs={{0,32},{1,33},{2,34},{3,35},{4,36},{5,37},{6,38},{7,39},{8,40},{9,... | collective-permute-start | bytes 331784 | tf_op jit(solution)/shard_map/zq/ppermute | solution.py:32
  14.5 0.6 copy-done.19
  15.1 0.6 copy-done.21
  15.7 1.8 %shard_map.103.i0 = bf16[192,1152]{1,0:T(8,128)(2,1)} custom-call(bf16[48,1152]{1,0:T(8,128)(2,1)} %get-tuple-element.32.refs_0_, bf16[48,1152]{1,0:T(8,128)(2,1)} %copy-done.21, bf16[48,1152]{1,0:T(8,128)(2,1)} %copy-done.20, bf16[48,1152]{1,0:T(8,128)(2,1)} %copy-done.19), custom_call_target="tpu_custom_call" | custom-call | tf_op jit(solution)/shard_map/pallas_call | solution.py:71
  17.6 3.2 %collective-permute-start.9 = (bf16[192,1152]{1,0:T(8,128)(2,1)}, bf16[192,1152]{1,0:T(8,128)(2,1)S(1)}, u32[]{:S(2)}, u32[]{:S(2)}) collective-permute-start(bf16[192,1152]{1,0:T(8,128)(2,1)} %shard_map.103.i0), channel_id=1, source_target_pairs={{0,128},{1,129},{2,130},{3,131},{4,20},{5,21},{6,22},{7,23},{8,136... | collective-permute-start | bytes 1327112 | tf_op jit(solution)/shard_map/second/ppermute | solution.py:32
  20.8 1.1 collective-permute-start.8
  21.8 1.0 collective-permute-start.7
  24.7 3.0 %collective-permute-start = (bf16[48,1152]{1,0:T(8,128)(2,1)S(1)}, bf16[48,1152]{1,0:T(8,128)(2,1)S(1)}, u32[]{:S(2)}, u32[]{:S(2)}) collective-permute-start(bf16[48,1152]{1,0:T(8,128)(2,1)S(1)} %copy-done.16), channel_id=1, source_target_pairs={{0,2},{1,3},{2,32},{3,33},{4,6},{5,7},{6,36},{7,37},{8,10},{9,11},... | collective-permute-start | bytes 331784 | tf_op jit(solution)/shard_map/zq/ppermute | solution.py:32
  28.5 0.8 reshape.1568
  29.4 3.1 %collective-permute-done.refs_1_ = bf16[48,1152]{1,0:T(8,128)(2,1)S(1)} collective-permute-done((bf16[48,1152]{1,0:T(8,128)(2,1)S(1)}, bf16[48,1152]{1,0:T(8,128)(2,1)S(1)}, u32[]{:S(2)}, u32[]{:S(2)}) %collective-permute-start) | collective-permute-done | bytes 110624 | tf_op jit(solution)/shard_map/zq/ppermute | solution.py:32
  32.5 0.6 copy-done.22
  33.1 1.9 %shard_map.102.t0 = bf16[192,1152]{1,0:T(8,128)(2,1)} custom-call(bf16[48,1152]{1,0:T(8,128)(2,1)} %get-tuple-element.31.refs_0_, bf16[48,1152]{1,0:T(8,128)(2,1)} %copy-done.22, bf16[48,1152]{1,0:T(8,128)(2,1)} %copy-done.18, bf16[48,1152]{1,0:T(8,128)(2,1)} %copy-done.17), custom_call_target="tpu_custom_call" | custom-call | tf_op jit(solution)/shard_map/pallas_call | solution.py:71
  35.0 1.8 %collective-permute-start.3 = (bf16[192,1152]{1,0:T(8,128)(2,1)}, bf16[192,1152]{1,0:T(8,128)(2,1)S(1)}, u32[]{:S(2)}, u32[]{:S(2)}) collective-permute-start(bf16[192,1152]{1,0:T(8,128)(2,1)} %shard_map.102.t0), channel_id=1, source_target_pairs={{0,1},{1,2},{2,3},{3,32},{4,39},{5,4},{6,5},{7,6},{8,9},{9,10},{10... | collective-permute-start | bytes 1327112 | tf_op jit(solution)/shard_map/za/ppermute | solution.py:32
  37.6 1.5 %gather_fusion = s32[8,48]{1,0:T(8,128)S(1)} fusion(s32[256,48]{1,0:T(8,128)} %reshape.1568, s32[1024]{0:T(1024)S(1)} %pad_clamp_fusion.1), kind=kCustom, calls=%fused_computation | custom fusion | bytes 3104 | tf_op jit(solution)/shard_map/gather | solution.py:220
  39.1 0.8 reshape.1588.rows_id
  39.9 4.8 %collective-permute-done.3.t1 = bf16[192,1152]{1,0:T(8,128)(2,1)S(1)} collective-permute-done((bf16[192,1152]{1,0:T(8,128)(2,1)}, bf16[192,1152]{1,0:T(8,128)(2,1)S(1)}, u32[]{:S(2)}, u32[]{:S(2)}) %collective-permute-start.3) | collective-permute-done | bytes 442400 | tf_op jit(solution)/shard_map/za/ppermute | solution.py:32
  44.7 1.0 copy-done
  45.7 0.9 copy-done.3
  46.7 2.8 %shard_map.104 = (bf16[384,768]{1,0:T(8,128)(2,1)S(1)}, f32[3,8,768]{2,1,0:T(8,128)S(1)}) custom-call(f32[2]{0:T(128)S(1)} %pad_maximum_fusion.scalars, s32[384,1]{1,0:T(8,128)S(1)} %copy-done.3, s32[1,768]{1,0:T(1,128)S(1)} %get-tuple-element.58.cols_id, f32[3,8,768]{2,1,0:T(8,128)S(1)} %broadcast_in_dim.6.before, bf16[192,1152]{1,0:T(8,128)(2,1)S(1)} %copy-done, ...), custom_call_target="tpu_custom_call" | custom-call | tf_op jit(solution)/shard_map/pallas_call | solution.py:159
  49.5 4.0 %shard_map.105 = (bf16[192,1152]{1,0:T(8,128)(2,1)S(1)}, bf16[192,1152]{1,0:T(8,128)(2,1)S(1)}, bf16[192,1152]{1,0:T(8,128)(2,1)S(1)}, bf16[192,1152]{1,0:T(8,12...) custom-call(f32[2]{0:T(128)S(1)} %pad_maximum_fusion.scalars, s32[384,1]{1,0:T(8,128)S(1)} %copy-done.4, ...), custom_call_target="tpu_custom_call" | custom-call | tf_op jit(solution)/shard_map/pallas_call | solution.py:159
  54.7 3.5 %shard_map.109 = (f32[192,1152]{1,0:T(8,128)S(1)}, bf16[192,1152]{1,0:T(8,128)(2,1)}) custom-call(bf16[384,768]{1,0:T(8,128)(2,1)S(1)} %get-tuple-element.33.scaled.scaled_own, bf16[384,768]{1,0:T(8,128)(2,1)S(1)} %get-tuple-element.50.scaled_far, bf16[192,1152]{1,0:T(8,128)(2,1)S(1)} %copy-done.2, bf16[192,1152]{1,0:T(8,128)(2,1)S(1)} %collective-permute-done.7.i1, ...), custom_call_target="tpu_custom_call" | custom-call | tf_op jit(solution)/shard_map/pallas_call | solution.py:159
  58.2 0.9 copy-done.5
  59.2 2.2 %shard_map.106 = (f32[192,1152]{1,0:T(8,128)S(1)}, bf16[192,1152]{1,0:T(8,128)(2,1)}, bf16[192,1152]{1,0:T(8,128)(2,1)}, bf16[192,1152]{1,0:T(8,128)(2,1)}, f32[8,128]{1,0:T(8,128)S(1)}) custom-call(bf16[384,768]{1,0:T(8,128)(2,1)S(1)} %get-tuple-element.33.scaled.scaled_own, bf16[192,1152]{1,0:T(8,128)(2,1)S(1)} %copy-done.1, ...), custom_call_target="tpu_custom_call" | custom-call | tf_op jit(solution)/shard_map/pallas_call | solution.py:159
  61.4 2.3 %collective-permute-start.18 = (bf16[192,1152]{1,0:T(8,128)(2,1)}, bf16[192,1152]{1,0:T(8,128)(2,1)S(1)}, u32[]{:S(2)}, u32[]{:S(2)}) collective-permute-start(bf16[192,1152]{1,0:T(8,128)(2,1)} %get-tuple-element.41), channel_id=1, source_target_pairs={{0,192},{1,193},{2,194},{3,195},{4,28},{5,29},{6,30},{7,31},{8,200... | collective-permute-start | bytes 1327112 | tf_op jit(solution)/shard_map/rsecond/ppermute | solution.py:32
  63.7 1.5 %collective-permute-start.20 = (bf16[192,1152]{1,0:T(8,128)(2,1)}, bf16[192,1152]{1,0:T(8,128)(2,1)S(1)}, u32[]{:S(2)}, u32[]{:S(2)}) collective-permute-start(bf16[192,1152]{1,0:T(8,128)(2,1)} %get-tuple-element.43), channel_id=1, source_target_pairs={{0,128},{1,129},{2,130},{3,131},{4,20},{5,21},{6,22},{7,23},{8,136... | collective-permute-start | bytes 1327112 | tf_op jit(solution)/shard_map/rsecond/ppermute | solution.py:32
  65.1 0.7 broadcast_in_dim.7
  65.8 6.8 %all-to-all-start = ((f32[32,8,128]{2,1,0:T(8,128)}), f32[32,8,128]{2,1,0:T(8,128)}, u32[]{:S(2)}, u32[]{:S(2)}) async-start(f32[32,8,128]{2,1,0:T(8,128)} %broadcast_in_dim.7), calls=%async_computation | async-start | bytes 262144 | tf_op jit(solution)/shard_map/terms/all_to_all | solution.py:251
  72.6 0.8 shard_map.110
  73.4 0.7 copy-done.8
  74.1 4.3 %collective-permute-start.25 = (bf16[48,1152]{1,0:T(8,128)(2,1)}, bf16[48,1152]{1,0:T(8,128)(2,1)S(1)}, u32[]{:S(2)}, u32[]{:S(2)}) collective-permute-start(bf16[48,1152]{1,0:T(8,128)(2,1)} %get-tuple-element.54), channel_id=1, source_target_pairs={{0,34},{1,35},{2,0},{3,1},{4,38},{5,39},{6,4},{7,5},{8,42},{9,43},... | collective-permute-start | bytes 331784 | tf_op jit(solution)/shard_map/rzq/ppermute | solution.py:32
  78.4 3.5 %collective-permute-start.27 = (bf16[48,1152]{1,0:T(8,128)(2,1)}, bf16[48,1152]{1,0:T(8,128)(2,1)S(1)}, u32[]{:S(2)}, u32[]{:S(2)}) collective-permute-start(bf16[48,1152]{1,0:T(8,128)(2,1)} %get-tuple-element.56), channel_id=1, source_target_pairs={{0,32},{1,33},{2,34},{3,35},{4,36},{5,37},{6,38},{7,39},{8,40},{9,... | collective-permute-start | bytes 331784 | tf_op jit(solution)/shard_map/rzq/ppermute | solution.py:32
  81.9 0.9 reduce_sum.18.sums
  83.1 0.7 broadcast_in_dim.8
  83.7 4.5 %all-to-all-start.1 = ((f32[8,8,128]{2,1,0:T(8,128)}), f32[8,8,128]{2,1,0:T(8,128)S(1)}, u32[]{:S(2)}, u32[]{:S(2)}) async-start(f32[8,8,128]{2,1,0:T(8,128)} %broadcast_in_dim.8), calls=%async_computation.1 | async-start | bytes 65536 | tf_op jit(solution)/shard_map/terms/all_to_all | solution.py:251
  88.2 3.1 %collective-permute-done.26.r2 = bf16[48,1152]{1,0:T(8,128)(2,1)S(1)} collective-permute-done((bf16[48,1152]{1,0:T(8,128)(2,1)}, bf16[48,1152]{1,0:T(8,128)(2,1)S(1)}, u32[]{:S(2)}, u32[]{:S(2)}) %collective-permute-start.26) | collective-permute-done | bytes 110624 | tf_op jit(solution)/shard_map/rzq/ppermute | solution.py:32
  91.3 0.6 copy-done.11
  92.0 2.1 %shard_map.111 = f32[48,1152]{1,0:T(8,128)} custom-call(f32[2]{0:T(128)} %copy-done.9, f32[48,1152]{1,0:T(8,128)} %raw.3, f32[48,1152]{1,0:T(8,128)} %copy-done.8, bf16[48,1152]{1,0:T(8,128)(2,1)} %copy-done.10, bf16[48,1152]{1,0:T(8,128)(2,1)} %copy-done.11, bf16[48,1152]{1,0:T(8,128)(2,1)} %copy-done.12), custom_call_target="tpu_custom_call" | custom-call | tf_op jit(solution)/shard_map/pallas_call | solution.py:267
  94.1 0.9 collective-permute-start.21
  94.9 2.4 %collective-permute-start.22 = (bf16[48,1152]{1,0:T(8,128)(2,1)S(1)}, bf16[48,1152]{1,0:T(8,128)(2,1)S(1)}, u32[]{:S(2)}, u32[]{:S(2)}) collective-permute-start(bf16[48,1152]{1,0:T(8,128)(2,1)S(1)} %get-tuple-element.48), channel_id=1, source_target_pairs={{0,8},{1,9},{2,10},{3,11},{4,68},{5,69},{6,70},{7,71},{8,16},{9,17... | collective-permute-start | bytes 331784 | tf_op jit(solution)/shard_map/rfirst/ppermute | solution.py:32
  97.6 0.6 fusion.3
  100.1 0.7 collective-permute-done.22.r2
  100.8 2.8 %collective-permute-done.23.r3 = bf16[48,1152]{1,0:T(8,128)(2,1)S(1)} collective-permute-done((bf16[48,1152]{1,0:T(8,128)(2,1)S(1)}, bf16[48,1152]{1,0:T(8,128)(2,1)S(1)}, u32[]{:S(2)}, u32[]{:S(2)}) %collective-permute-start.23) | collective-permute-done | bytes 110624 | tf_op jit(solution)/shard_map/rfirst/ppermute | solution.py:32
  103.6 0.6 copy-done.15
  104.2 2.1 %shard_map.108 = f32[48,1152]{1,0:T(8,128)} custom-call(f32[2]{0:T(128)} %copy-done.9, f32[48,1152]{1,0:T(8,128)} %raw.2, f32[48,1152]{1,0:T(8,128)} %copy-done.7, bf16[48,1152]{1,0:T(8,128)(2,1)} %copy-done.13, bf16[48,1152]{1,0:T(8,128)(2,1)} %copy-done.14, bf16[48,1152]{1,0:T(8,128)(2,1)} %copy-done.15), custom_call_target="tpu_custom_call" | custom-call | tf_op jit(solution)/shard_map/pallas_call | solution.py:266
  (93 shorter events, 3.9 us)
Async XLA Ops:
  2.5 11.9 %collective-permute-start.6 = (bf16[48,1152]{1,0:T(8,128)(2,1)}, bf16[48,1152]{1,0:T(8,128)(2,1)S(1)}, u32[]{:S(2)}, u32[]{:S(2)}) collective-permute-start(bf16[48,1152]{1,0:T(8,128)(2,1)} %get-tuple-element.32.refs_0_), channel_id=1, source_target_pairs={{0,16},{1,17},{2,18},{3,19},{4,132},{5,133},{6,134},{7,135},{8,24}... | collective-permute-start | bytes 331784 | tf_op jit(solution)/shard_map/first/ppermute | solution.py:32
  3.9 10.5 %collective-permute-start.5 = (bf16[48,1152]{1,0:T(8,128)(2,1)}, bf16[48,1152]{1,0:T(8,128)(2,1)S(1)}, u32[]{:S(2)}, u32[]{:S(2)}) collective-permute-start(bf16[48,1152]{1,0:T(8,128)(2,1)} %get-tuple-element.32.refs_0_), channel_id=1, source_target_pairs={{0,24},{1,25},{2,26},{3,27},{4,196},{5,197},{6,198},{7,199},{8,0},... | collective-permute-start | bytes 331784 | tf_op jit(solution)/shard_map/first/ppermute | solution.py:32
  5.5 8.9 %collective-permute-start.4 = (bf16[48,1152]{1,0:T(8,128)(2,1)}, bf16[48,1152]{1,0:T(8,128)(2,1)S(1)}, u32[]{:S(2)}, u32[]{:S(2)}) collective-permute-start(bf16[48,1152]{1,0:T(8,128)(2,1)} %get-tuple-element.32.refs_0_), channel_id=1, source_target_pairs={{0,8},{1,9},{2,10},{3,11},{4,68},{5,69},{6,70},{7,71},{8,16},{9,17... | collective-permute-start | bytes 331784 | tf_op jit(solution)/shard_map/first/ppermute | solution.py:32
  7.1 17.6 %collective-permute-start.2 = (bf16[48,1152]{1,0:T(8,128)(2,1)}, bf16[48,1152]{1,0:T(8,128)(2,1)S(1)}, u32[]{:S(2)}, u32[]{:S(2)}) collective-permute-start(bf16[48,1152]{1,0:T(8,128)(2,1)} %get-tuple-element.31.refs_0_), channel_id=1, source_target_pairs={{0,32},{1,33},{2,34},{3,35},{4,36},{5,37},{6,38},{7,39},{8,40},{9,... | collective-permute-start | bytes 331784 | tf_op jit(solution)/shard_map/zq/ppermute | solution.py:32
  14.3 15.0 %collective-permute-start.1 = (bf16[48,1152]{1,0:T(8,128)(2,1)}, bf16[48,1152]{1,0:T(8,128)(2,1)S(1)}, u32[]{:S(2)}, u32[]{:S(2)}) collective-permute-start(bf16[48,1152]{1,0:T(8,128)(2,1)} %get-tuple-element.31.refs_0_), channel_id=1, source_target_pairs={{0,34},{1,35},{2,0},{3,1},{4,38},{5,39},{6,4},{7,5},{8,42},{9,43},... | collective-permute-start | bytes 331784 | tf_op jit(solution)/shard_map/zq/ppermute | solution.py:32
  17.6 19.2 %collective-permute-start.9 = (bf16[192,1152]{1,0:T(8,128)(2,1)}, bf16[192,1152]{1,0:T(8,128)(2,1)S(1)}, u32[]{:S(2)}, u32[]{:S(2)}) collective-permute-start(bf16[192,1152]{1,0:T(8,128)(2,1)} %shard_map.103.i0), channel_id=1, source_target_pairs={{0,128},{1,129},{2,130},{3,131},{4,20},{5,21},{6,22},{7,23},{8,136... | collective-permute-start | bytes 1327112 | tf_op jit(solution)/shard_map/second/ppermute | solution.py:32
  20.8 16.0 %collective-permute-start.8 = (bf16[192,1152]{1,0:T(8,128)(2,1)}, bf16[192,1152]{1,0:T(8,128)(2,1)S(1)}, u32[]{:S(2)}, u32[]{:S(2)}) collective-permute-start(bf16[192,1152]{1,0:T(8,128)(2,1)} %shard_map.103.i0), channel_id=1, source_target_pairs={{0,192},{1,193},{2,194},{3,195},{4,28},{5,29},{6,30},{7,31},{8,200... | collective-permute-start | bytes 1327112 | tf_op jit(solution)/shard_map/second/ppermute | solution.py:32
  21.8 15.5 %collective-permute-start.7 = (bf16[192,1152]{1,0:T(8,128)(2,1)}, bf16[192,1152]{1,0:T(8,128)(2,1)S(1)}, u32[]{:S(2)}, u32[]{:S(2)}) collective-permute-start(bf16[192,1152]{1,0:T(8,128)(2,1)} %shard_map.103.i0), channel_id=1, source_target_pairs={{0,64},{1,65},{2,66},{3,67},{4,12},{5,13},{6,14},{7,15},{8,72},{9,... | collective-permute-start | bytes 1327112 | tf_op jit(solution)/shard_map/second/ppermute | solution.py:32
  22.8 1.7 %copy-start.23 = (s32[12288]{0:T(1024)S(1)}, s32[12288]{0:T(1024)}, u32[]{:S(2)}) copy-start(s32[12288]{0:T(1024)} %param.8) | copy-start | bytes 147460
  22.8 1.9 %copy-start.16 = (bf16[48,1152]{1,0:T(8,128)(2,1)S(1)}, bf16[48,1152]{1,0:T(8,128)(2,1)}, u32[]{:S(2)}) copy-start(bf16[48,1152]{1,0:T(8,128)(2,1)} %get-tuple-element.31.refs_0_) | copy-start | bytes 331780
  22.8 6.4 %copy-start.2 = (bf16[192,1152]{1,0:T(8,128)(2,1)S(1)}, bf16[192,1152]{1,0:T(8,128)(2,1)}, u32[]{:S(2)}) copy-start(bf16[192,1152]{1,0:T(8,128)(2,1)} %shard_map.103.i0) | copy-start | bytes 1327108
  24.7 4.6 %copy-start.17 = (bf16[48,1152]{1,0:T(8,128)(2,1)}, bf16[48,1152]{1,0:T(8,128)(2,1)S(1)}, u32[]{:S(2)}) copy-start(bf16[48,1152]{1,0:T(8,128)(2,1)S(1)} %collective-permute-done.2.refs_3_) | copy-start | bytes 331780
  24.7 7.8 %collective-permute-start = (bf16[48,1152]{1,0:T(8,128)(2,1)S(1)}, bf16[48,1152]{1,0:T(8,128)(2,1)S(1)}, u32[]{:S(2)}, u32[]{:S(2)}) collective-permute-start(bf16[48,1152]{1,0:T(8,128)(2,1)S(1)} %copy-done.16), channel_id=1, source_target_pairs={{0,2},{1,3},{2,32},{3,33},{4,6},{5,7},{6,36},{7,37},{8,10},{9,11},... | collective-permute-start | bytes 331784 | tf_op jit(solution)/shard_map/zq/ppermute | solution.py:32
  27.7 0.8 copy-start.24
  29.3 3.2 %copy-start.18 = (bf16[48,1152]{1,0:T(8,128)(2,1)}, bf16[48,1152]{1,0:T(8,128)(2,1)S(1)}, u32[]{:S(2)}) copy-start(bf16[48,1152]{1,0:T(8,128)(2,1)S(1)} %collective-permute-done.1.refs_2_) | copy-start | bytes 331780
  29.3 20.2 %collective-permute-start.10 = (bf16[192,1152]{1,0:T(8,128)(2,1)S(1)}, bf16[192,1152]{1,0:T(8,128)(2,1)S(1)}, u32[]{:S(2)}, u32[]{:S(2)}) collective-permute-start(bf16[192,1152]{1,0:T(8,128)(2,1)S(1)} %copy-done.2), channel_id=1, source_target_pairs={{0,4},{1,5},{2,6},{3,7},{4,0},{5,1},{6,2},{7,3},{8,12},{9,13},{10,... | collective-permute-start | bytes 1327112 | tf_op jit(solution)/shard_map/swap/ppermute | solution.py:32
  35.0 9.7 %collective-permute-start.3 = (bf16[192,1152]{1,0:T(8,128)(2,1)}, bf16[192,1152]{1,0:T(8,128)(2,1)S(1)}, u32[]{:S(2)}, u32[]{:S(2)}) collective-permute-start(bf16[192,1152]{1,0:T(8,128)(2,1)} %shard_map.102.t0), channel_id=1, source_target_pairs={{0,1},{1,2},{2,3},{3,32},{4,39},{5,4},{6,5},{7,6},{8,9},{9,10},{10... | collective-permute-start | bytes 1327112 | tf_op jit(solution)/shard_map/za/ppermute | solution.py:32
  36.8 12.7 %collective-permute-start.13 = (bf16[192,1152]{1,0:T(8,128)(2,1)S(1)}, bf16[192,1152]{1,0:T(8,128)(2,1)S(1)}, u32[]{:S(2)}, u32[]{:S(2)}) collective-permute-start(bf16[192,1152]{1,0:T(8,128)(2,1)S(1)} %collective-permute-done.9.i3), channel_id=1, source_target_pairs={{0,4},{1,5},{2,6},{3,7},{4,0},{5,1},{6,2},{7,3},{8,12},{9,13},{10,... | collective-permute-start | bytes 1327112 | tf_op jit(solution)/shard_map/swap/ppermute | solution.py:32
  36.8 12.7 %collective-permute-start.12 = (bf16[192,1152]{1,0:T(8,128)(2,1)S(1)}, bf16[192,1152]{1,0:T(8,128)(2,1)S(1)}, u32[]{:S(2)}, u32[]{:S(2)}) collective-permute-start(bf16[192,1152]{1,0:T(8,128)(2,1)S(1)} %collective-permute-done.8.i2), channel_id=1, source_target_pairs={{0,4},{1,5},{2,6},{3,7},{4,0},{5,1},{6,2},{7,3},{8,12},{9,13},{10,... | collective-permute-start | bytes 1327112 | tf_op jit(solution)/shard_map/swap/ppermute | solution.py:32
  37.3 12.2 %collective-permute-start.11 = (bf16[192,1152]{1,0:T(8,128)(2,1)S(1)}, bf16[192,1152]{1,0:T(8,128)(2,1)}, u32[]{:S(2)}, u32[]{:S(2)}) collective-permute-start(bf16[192,1152]{1,0:T(8,128)(2,1)S(1)} %collective-permute-done.7.i1), channel_id=1, source_target_pairs={{0,4},{1,5},{2,6},{3,7},{4,0},{5,1},{6,2},{7,3},{8,12},{9,13},{10,... | collective-permute-start | bytes 1327112 | tf_op jit(solution)/shard_map/swap/ppermute | solution.py:32
  39.9 9.6 %copy-start.9 = (f32[2]{0:T(128)}, f32[2]{0:T(128)S(1)}, u32[]{:S(2)}) copy-start(f32[2]{0:T(128)S(1)} %pad_maximum_fusion.scalars) | copy-start | bytes 28
  44.7 1.0 copy-start
  45.7 0.9 copy-start.3
  46.7 2.9 %copy-start.1 = (bf16[192,1152]{1,0:T(8,128)(2,1)S(1)}, bf16[192,1152]{1,0:T(8,128)(2,1)}, u32[]{:S(2)}) copy-start(bf16[192,1152]{1,0:T(8,128)(2,1)} %shard_map.102.t0) | copy-start | bytes 1327108
  46.7 2.9 %copy-start.4 = (s32[384,1]{1,0:T(8,128)S(1)}, s32[384,1]{1,0:T(8,128)}, u32[]{:S(2)}) copy-start(s32[384,1]{1,0:T(8,128)} %reshape.1588.rows_id) | copy-start | bytes 4612
  53.6 5.6 %collective-permute-start.14 = (bf16[192,1152]{1,0:T(8,128)(2,1)S(1)}, bf16[192,1152]{1,0:T(8,128)(2,1)S(1)}, u32[]{:S(2)}, u32[]{:S(2)}) collective-permute-start(bf16[192,1152]{1,0:T(8,128)(2,1)S(1)} %get-tuple-element.35), channel_id=1, source_target_pairs={{0,4},{1,5},{2,6},{3,7},{4,0},{5,1},{6,2},{7,3},{8,12},{9,13},{10,... | collective-permute-start | bytes 1327112 | tf_op jit(solution)/shard_map/rswap/ppermute | solution.py:32
  53.7 5.5 %collective-permute-start.15 = (bf16[192,1152]{1,0:T(8,128)(2,1)S(1)}, bf16[192,1152]{1,0:T(8,128)(2,1)S(1)}, u32[]{:S(2)}, u32[]{:S(2)}) collective-permute-start(bf16[192,1152]{1,0:T(8,128)(2,1)S(1)} %get-tuple-element.36), channel_id=1, source_target_pairs={{0,4},{1,5},{2,6},{3,7},{4,0},{5,1},{6,2},{7,3},{8,12},{9,13},{10,... | collective-permute-start | bytes 1327112 | tf_op jit(solution)/shard_map/rswap/ppermute | solution.py:32
  54.2 5.0 %collective-permute-start.16 = (bf16[192,1152]{1,0:T(8,128)(2,1)S(1)}, bf16[192,1152]{1,0:T(8,128)(2,1)S(1)}, u32[]{:S(2)}, u32[]{:S(2)}) collective-permute-start(bf16[192,1152]{1,0:T(8,128)(2,1)S(1)} %get-tuple-element.37), channel_id=1, source_target_pairs={{0,4},{1,5},{2,6},{3,7},{4,0},{5,1},{6,2},{7,3},{8,12},{9,13},{10,... | collective-permute-start | bytes 1327112 | tf_op jit(solution)/shard_map/rswap/ppermute | solution.py:32
  54.3 4.9 %collective-permute-start.17 = (bf16[192,1152]{1,0:T(8,128)(2,1)S(1)}, bf16[192,1152]{1,0:T(8,128)(2,1)S(1)}, u32[]{:S(2)}, u32[]{:S(2)}) collective-permute-start(bf16[192,1152]{1,0:T(8,128)(2,1)S(1)} %get-tuple-element.38), channel_id=1, source_target_pairs={{0,4},{1,5},{2,6},{3,7},{4,0},{5,1},{6,2},{7,3},{8,12},{9,13},{10,... | collective-permute-start | bytes 1327112 | tf_op jit(solution)/shard_map/rswap/ppermute | solution.py:32
  58.2 0.9 copy-start.5
  59.1 13.5 %collective-permute-start.24 = (bf16[192,1152]{1,0:T(8,128)(2,1)}, bf16[192,1152]{1,0:T(8,128)(2,1)S(1)}, u32[]{:S(2)}, u32[]{:S(2)}) collective-permute-start(bf16[192,1152]{1,0:T(8,128)(2,1)} %get-tuple-element.52), channel_id=1, source_target_pairs={{0,35},{1,0},{2,1},{3,2},{4,5},{5,6},{6,7},{7,36},{8,43},{9,8},{10... | collective-permute-start | bytes 1327112 | tf_op jit(solution)/shard_map/rza/ppermute | solution.py:32
  59.2 13.4 %copy-start.6 = (f32[192,1152]{1,0:T(8,128)S(1)}, f32[192,1152]{1,0:T(8,128)}, u32[]{:S(2)}) copy-start(f32[192,1152]{1,0:T(8,128)} %copy-done.5) | copy-start | bytes 2654212
  61.4 17.0 %collective-permute-start.18 = (bf16[192,1152]{1,0:T(8,128)(2,1)}, bf16[192,1152]{1,0:T(8,128)(2,1)S(1)}, u32[]{:S(2)}, u32[]{:S(2)}) collective-permute-start(bf16[192,1152]{1,0:T(8,128)(2,1)} %get-tuple-element.41), channel_id=1, source_target_pairs={{0,192},{1,193},{2,194},{3,195},{4,28},{5,29},{6,30},{7,31},{8,200... | collective-permute-start | bytes 1327112 | tf_op jit(solution)/shard_map/rsecond/ppermute | solution.py:32
  63.7 19.2 %collective-permute-start.19 = (bf16[192,1152]{1,0:T(8,128)(2,1)}, bf16[192,1152]{1,0:T(8,128)(2,1)S(1)}, u32[]{:S(2)}, u32[]{:S(2)}) collective-permute-start(bf16[192,1152]{1,0:T(8,128)(2,1)} %get-tuple-element.42), channel_id=1, source_target_pairs={{0,64},{1,65},{2,66},{3,67},{4,12},{5,13},{6,14},{7,15},{8,72},{9,... | collective-permute-start | bytes 1327112 | tf_op jit(solution)/shard_map/rsecond/ppermute | solution.py:32
  63.7 19.2 %collective-permute-start.20 = (bf16[192,1152]{1,0:T(8,128)(2,1)}, bf16[192,1152]{1,0:T(8,128)(2,1)S(1)}, u32[]{:S(2)}, u32[]{:S(2)}) collective-permute-start(bf16[192,1152]{1,0:T(8,128)(2,1)} %get-tuple-element.43), channel_id=1, source_target_pairs={{0,128},{1,129},{2,130},{3,131},{4,20},{5,21},{6,22},{7,23},{8,136... | collective-permute-start | bytes 1327112 | tf_op jit(solution)/shard_map/rsecond/ppermute | solution.py:32
  65.8 16.1 %all-to-all-start = ((f32[32,8,128]{2,1,0:T(8,128)}), f32[32,8,128]{2,1,0:T(8,128)}, u32[]{:S(2)}, u32[]{:S(2)}) async-start(f32[32,8,128]{2,1,0:T(8,128)} %broadcast_in_dim.7), calls=%async_computation | async-start | bytes 262144 | tf_op jit(solution)/shard_map/terms/all_to_all | solution.py:251
  74.1 14.1 %collective-permute-start.25 = (bf16[48,1152]{1,0:T(8,128)(2,1)}, bf16[48,1152]{1,0:T(8,128)(2,1)S(1)}, u32[]{:S(2)}, u32[]{:S(2)}) collective-permute-start(bf16[48,1152]{1,0:T(8,128)(2,1)} %get-tuple-element.54), channel_id=1, source_target_pairs={{0,34},{1,35},{2,0},{3,1},{4,38},{5,39},{6,4},{7,5},{8,42},{9,43},... | collective-permute-start | bytes 331784 | tf_op jit(solution)/shard_map/rzq/ppermute | solution.py:32
  78.4 12.9 %collective-permute-start.26 = (bf16[48,1152]{1,0:T(8,128)(2,1)}, bf16[48,1152]{1,0:T(8,128)(2,1)S(1)}, u32[]{:S(2)}, u32[]{:S(2)}) collective-permute-start(bf16[48,1152]{1,0:T(8,128)(2,1)} %get-tuple-element.55), channel_id=1, source_target_pairs={{0,2},{1,3},{2,32},{3,33},{4,6},{5,7},{6,36},{7,37},{8,10},{9,11},... | collective-permute-start | bytes 331784 | tf_op jit(solution)/shard_map/rzq/ppermute | solution.py:32
  78.4 12.9 %collective-permute-start.27 = (bf16[48,1152]{1,0:T(8,128)(2,1)}, bf16[48,1152]{1,0:T(8,128)(2,1)S(1)}, u32[]{:S(2)}, u32[]{:S(2)}) collective-permute-start(bf16[48,1152]{1,0:T(8,128)(2,1)} %get-tuple-element.56), channel_id=1, source_target_pairs={{0,32},{1,33},{2,34},{3,35},{4,36},{5,37},{6,38},{7,39},{8,40},{9,... | collective-permute-start | bytes 331784 | tf_op jit(solution)/shard_map/rzq/ppermute | solution.py:32
  83.0 11.0 %copy-start.7 = (f32[48,1152]{1,0:T(8,128)}, f32[48,1152]{1,0:T(8,128)S(1)}, u32[]{:S(2)}) copy-start(f32[48,1152]{1,0:T(8,128)S(1)} %get-tuple-element.46.own) | copy-start | bytes 663556
  83.7 13.8 %all-to-all-start.1 = ((f32[8,8,128]{2,1,0:T(8,128)}), f32[8,8,128]{2,1,0:T(8,128)S(1)}, u32[]{:S(2)}, u32[]{:S(2)}) async-start(f32[8,8,128]{2,1,0:T(8,128)} %broadcast_in_dim.8), calls=%async_computation.1 | async-start | bytes 65536 | tf_op jit(solution)/shard_map/terms/all_to_all | solution.py:251
  88.2 3.1 %copy-start.10 = (bf16[48,1152]{1,0:T(8,128)(2,1)}, bf16[48,1152]{1,0:T(8,128)(2,1)S(1)}, u32[]{:S(2)}) copy-start(bf16[48,1152]{1,0:T(8,128)(2,1)S(1)} %collective-permute-done.25.r1) | copy-start | bytes 331780
  91.3 0.7 copy-start.12
  94.1 6.0 %collective-permute-start.21 = (bf16[48,1152]{1,0:T(8,128)(2,1)S(1)}, bf16[48,1152]{1,0:T(8,128)(2,1)S(1)}, u32[]{:S(2)}, u32[]{:S(2)}) collective-permute-start(bf16[48,1152]{1,0:T(8,128)(2,1)S(1)} %get-tuple-element.47), channel_id=1, source_target_pairs={{0,24},{1,25},{2,26},{3,27},{4,196},{5,197},{6,198},{7,199},{8,0},... | collective-permute-start | bytes 331784 | tf_op jit(solution)/shard_map/rfirst/ppermute | solution.py:32
  94.9 5.8 %collective-permute-start.22 = (bf16[48,1152]{1,0:T(8,128)(2,1)S(1)}, bf16[48,1152]{1,0:T(8,128)(2,1)S(1)}, u32[]{:S(2)}, u32[]{:S(2)}) collective-permute-start(bf16[48,1152]{1,0:T(8,128)(2,1)S(1)} %get-tuple-element.48), channel_id=1, source_target_pairs={{0,8},{1,9},{2,10},{3,11},{4,68},{5,69},{6,70},{7,71},{8,16},{9,17... | collective-permute-start | bytes 331784 | tf_op jit(solution)/shard_map/rfirst/ppermute | solution.py:32
  97.3 6.3 %collective-permute-start.23 = (bf16[48,1152]{1,0:T(8,128)(2,1)S(1)}, bf16[48,1152]{1,0:T(8,128)(2,1)S(1)}, u32[]{:S(2)}, u32[]{:S(2)}) collective-permute-start(bf16[48,1152]{1,0:T(8,128)(2,1)S(1)} %get-tuple-element.49), channel_id=1, source_target_pairs={{0,16},{1,17},{2,18},{3,19},{4,132},{5,133},{6,134},{7,135},{8,24}... | collective-permute-start | bytes 331784 | tf_op jit(solution)/shard_map/rfirst/ppermute | solution.py:32
  100.1 3.4 %copy-start.13 = (bf16[48,1152]{1,0:T(8,128)(2,1)}, bf16[48,1152]{1,0:T(8,128)(2,1)S(1)}, u32[]{:S(2)}) copy-start(bf16[48,1152]{1,0:T(8,128)(2,1)S(1)} %collective-permute-done.21.r1) | copy-start | bytes 331780
  100.8 2.8 %copy-start.14 = (bf16[48,1152]{1,0:T(8,128)(2,1)}, bf16[48,1152]{1,0:T(8,128)(2,1)S(1)}, u32[]{:S(2)}) copy-start(bf16[48,1152]{1,0:T(8,128)(2,1)S(1)} %collective-permute-done.22.r2) | copy-start | bytes 331780
  (7 other events, 4.6 us)

commit v3 on v2

v3 whole, which is shorter than its diff:
```python
import math

import jax
import jax.numpy as jnp
import numpy as np
from jax import lax
from jax.experimental import pallas as pl
from jax.experimental.pallas import tpu as pltpu
from jax.sharding import Mesh
from jax.sharding import PartitionSpec as P

SIZES = (4, 2, 4, 2, 4)
AXES = ("y", "zh", "x", "core", "zl")
ROWS = 48
OFFSETS = (1, 3, 2)
ANY = pl.BlockSpec(memory_space=pl.ANY)
VMEM = pl.BlockSpec(memory_space=pltpu.VMEM)
SMEM = pl.BlockSpec(memory_space=pltpu.SMEM)


def flat(x, y, z, c):
    return (((y * 2 + z // 4) * 4 + x) * 2 + c) * 4 + z % 4


def send(value, where, name="move"):
    pairs = []
    for y, zh, x, c, zl in np.ndindex(*SIZES):
        z = zh * 4 + zl
        tx, ty, tz, tc = where(x, y, z, c)
        pairs.append((flat(x, y, z, c), flat(tx % 4, ty % 4, tz % 8, tc % 2)))
    with jax.named_scope(name):
        return lax.ppermute(value, AXES, pairs)


def along_first(k):
    return lambda x, y, z, c: (x + k, y, z, c) if c == 0 else (x, y + k, z, c)


def along_second(k):
    return lambda x, y, z, c: (x, y + k, z, c) if c == 0 else (x + k, y, z, c)


def along_z(k):
    return lambda x, y, z, c: (x, y, z + k, c)


def apart(k):
    return lambda x, y, z, c: (x, y, z + k, c) if c == 0 else (x, y, z - k, c)


def across():
    groups = {}
    for y, zh, x, c, zl in np.ndindex(*SIZES):
        groups.setdefault((c, y if c else x), []).append(flat(x, y, zh * 4 + zl, c))
    return list(groups.values())


def swap(x, y, z, c):
    return (x, y, z, 1 - c)


def unit_kernel(image_ref, text_ref, image_out, text_out):
    for src, dst in ((image_ref, image_out), (text_ref, text_out)):
        rows = src[...]
        scale = jnp.sqrt(jnp.mean(rows * rows, axis=-1, keepdims=True) + 1e-06)
        dst[...] = (rows / (scale * math.sqrt(rows.shape[-1]))).astype(jnp.bfloat16)


def stack(out, sources):
    row = 0
    for src in sources:
        out[row : row + src.shape[0], :] = src[...]
        row += src.shape[0]


def line_kernel(i0, i1, i2, i3, t0, t1, line, pair):
    stack(line, (i0, i1, i2, i3))
    stack(pair, (t0, t1))


def ring_kernel(pair, pair_2, own, opposite, message, kept):
    stack(message, (pair, pair_2))
    stack(kept, (own, opposite, pair_2))


def terms_kernel(scalars, rows_id, cols_id, before, *refs):
    pieces, (*far, scaled, sums, text, image) = refs[:6], refs[6:]
    temp = scalars[0]
    offset = scalars[1]
    stack(text, pieces[:2])
    stack(image, pieces[2:])
    totals = [before[n] for n in range(3)]
    cols = cols_id[...]
    for tile in range(2):
        at = slice(192 * tile, 192 * (tile + 1))
        cosine = lax.dot_general(
            text[at, :], image[...], (((1,), (1,)), ((), ())), preferred_element_type=jnp.float32
        )
        logits = temp * cosine + offset
        same = rows_id[at, :] == cols
        margin = jnp.where(same, -logits, logits)
        decay = jnp.exp(-jnp.abs(margin))
        inverse = 1.0 / (1.0 + decay)
        sigmoid = jnp.where(margin >= 0, inverse, decay * inverse)
        grad = jnp.where(same, -sigmoid, sigmoid)
        loss = jnp.maximum(margin, 0.0) + jnp.log1p(decay)
        scaled[at, :] = grad.astype(jnp.bfloat16)
        for n, value in enumerate((loss, grad, grad * cosine)):
            totals[n] = totals[n] + jnp.sum(value.reshape(24, 8, 768), axis=0)
    if not far:
        for n in range(3):
            sums[n] = totals[n]
        return
    lane = lax.broadcasted_iota(jnp.int32, (8, 128), 1)
    out = jnp.zeros((8, 128), jnp.float32)
    for n in range(3):
        out = jnp.where(lane == n, jnp.sum(totals[n]), out)
    sums[...] = out
    far[0][...] = lax.dot_general(
        scaled[...], text[...], (((0,), (0,)), ((), ())), preferred_element_type=jnp.float32
    ).astype(jnp.bfloat16)


def text_kernel(scaled_own, scaled_far, *refs):
    pieces, (own, opposite, pair, last, image) = refs[:8], refs[8:]
    stack(image, pieces[:4])
    total = jnp.dot(scaled_own[...], image[...], preferred_element_type=jnp.float32)
    stack(image, pieces[4:])
    total = total + jnp.dot(scaled_far[...], image[...], preferred_element_type=jnp.float32)
    row = 0
    for dst in (own, opposite, pair, last):
        dst[...] = total[row : row + dst.shape[0]].astype(dst.dtype)
        row += dst.shape[0]


def image_kernel(scaled, sums, more, t0, t1, back, own, low1, low2, low3, sums_out, text):
    stack(text, (t0, t1))
    part = lax.dot_general(
        scaled[...], text[...], (((0,), (0,)), ((), ())), preferred_element_type=jnp.float32
    )
    for n, dst in enumerate((own, low1, low2, low3)):
        at = slice(192 * n, 192 * (n + 1))
        dst[...] = (part[at] + back[at].astype(jnp.float32)).astype(dst.dtype)
    sums_out[...] = jnp.broadcast_to((sums[...] + more[...])[None], sums_out.shape)


def near_kernel(own, pair, back, opposite, out_own, out_far, low):
    out_own[...] = own[...] + back[:48].astype(jnp.float32) + opposite[...].astype(jnp.float32)
    out_far[...] = back[48:96].astype(jnp.float32)
    low[...] = (pair[...] + back[96:].astype(jnp.float32)).astype(low.dtype)


def add_kernel(own, r1, r2, r3, terms, out_own, low1, low2, low3, sums):
    total = own[...] + r1[...].astype(jnp.float32) + r2[...].astype(jnp.float32) + r3[...].astype(jnp.float32)
    out_own[...] = total[:48]
    value = jnp.sum(terms[...], axis=0)
    sums[...] = value
    high = value[0:1].astype(jnp.bfloat16)
    rest = value[0:1] - high.astype(jnp.float32)
    mid = rest.astype(jnp.bfloat16)
    low = (rest - mid.astype(jnp.float32)).astype(jnp.bfloat16)
    row = lax.broadcasted_iota(jnp.int32, (16, 128), 0)
    parts = [jnp.broadcast_to(v.astype(jnp.float32), (16, 128)) for v in (high, mid, low)]
    extra = jnp.where(row == 0, parts[0], jnp.where(row == 1, parts[1], jnp.where(row == 2, parts[2], 0.0)))
    for n, dst in enumerate((low1, low2, low3), 1):
        dst[:48, :] = total[48 * n : 48 * (n + 1)].astype(dst.dtype)
        dst[48:, :] = jnp.zeros((16, dst.shape[1]), dst.dtype)
        dst[48:, :128] = extra.astype(dst.dtype)


def far_kernel(own, far, back, after, out_own, low):
    out_own[...] = own[...] + back[:48].astype(jnp.float32)
    low[...] = (far[...] + back[48:].astype(jnp.float32)).astype(low.dtype)


def finish_kernel(scalars, image_raw, image_own, i1, i2, i3, text_raw, text_own, t1, sums, image_out, text_out, sums_out):
    for raw, own, parts, out in (
        (image_raw, image_own, (i1, i2, i3), image_out), (text_raw, text_own, (t1,), text_out),
    ):
        rows = raw[...]
        width = rows.shape[-1]
        grad = own[...]
        for part in parts:
            grad = grad + part[:48].astype(jnp.float32)
        grad = grad * scalars[0]
        square = jnp.mean(rows * rows, axis=-1, keepdims=True) + 1e-06
        inner = jnp.sum(rows * grad, axis=-1, keepdims=True)
        out[...] = (grad - rows * (inner / (square * width))) / (jnp.sqrt(square) * math.sqrt(width))
    values = [sums[0:1]]
    for part in (i1, i2, i3):
        extra = part[48:64, :128].astype(jnp.float32)
        values.append((extra[2:3] + extra[1:2]) + extra[0:1])
    sums_out[...] = jnp.broadcast_to((values[0] + values[3]) + (values[1] + values[2]), sums_out.shape)


def f32(*shape):
    return jax.ShapeDtypeStruct(shape, jnp.float32)


def b16(*shape):
    return jax.ShapeDtypeStruct(shape, jnp.bfloat16)


def local(kernel, out_shape, *args, after=(), scratch=()):
    return pl.pallas_call(
        kernel,
        out_shape=out_shape,
        in_specs=[SMEM if a.shape == (2,) else VMEM for a in args] + [ANY] * len(after),
        out_specs=tuple(VMEM for _ in out_shape),
        scratch_shapes=list(scratch),
        compiler_params=pltpu.CompilerParams(vmem_limit_bytes=48 * 1024 * 1024),
    )(*args, *after)


def body(image_raw, text_raw, image_ids, text_ids, log_temp, bias):
    pairs, width = image_raw.shape
    total = pairs * 256
    x, y, c = lax.axis_index("x"), lax.axis_index("y"), lax.axis_index("core")
    z = lax.axis_index("zh") * 4 + lax.axis_index("zl")
    image_unit, text_unit = pl.pallas_call(
        unit_kernel,
        out_shape=(b16(pairs, width), b16(pairs, width)),
        in_specs=[VMEM] * 2,
        out_specs=(VMEM, VMEM),
    )(image_raw, text_raw)

    parts = [send(image_unit, along_first(k), "first") for k in OFFSETS]
    other = send(text_unit, swap, "pair")
    opposite = send(text_unit, along_z(4), "z4")
    line, pair = local(
        line_kernel, (b16(4 * pairs, width), b16(2 * pairs, width)), image_unit, *parts, text_unit, other,
    )
    plane = [line] + [send(line, along_second(k), "second") for k in OFFSETS]
    message, kept = local(
        ring_kernel, (b16(4 * pairs, width),) * 2, pair, send(pair, apart(2), "z2"), text_unit, opposite,
    )
    text = (kept, send(message, apart(1), "z1"))
    plane_far = [send(p, swap, "swap") for p in plane]

    back = (0,) + OFFSETS
    cols_from = []
    for core in (c, 1 - c):
        for k in back:
            for j in back:
                sx = jnp.where(core == 0, x - j, x - k) % 4
                sy = jnp.where(core == 0, y - k, y - j) % 4
                cols_from.append(flat(sx, sy, z, core))
    step = jnp.where(c == 0, 1, -1)
    rows_from = [flat(x, y, z, c), flat(x, y, (z + 4) % 8, c)]
    for k in (2, 1, 3):
        rows_from += [flat(x, y, (z - k * step) % 8, core) for core in (c, 1 - c)]
    cols_id = image_ids.reshape(256, pairs)[jnp.stack(cols_from)].reshape(1, 32 * pairs)
    rows_id = text_ids.reshape(256, pairs)[jnp.stack(rows_from)].reshape(8 * pairs, 1)

    temp = jnp.exp(log_temp[0])
    scalars = jnp.stack([temp, bias[0]])
    copies = (pltpu.VMEM((384, width), jnp.bfloat16), pltpu.VMEM((768, width), jnp.bfloat16))
    scaled_own, sums = local(
        terms_kernel, (b16(384, 768), f32(3, 8, 768)),
        scalars, rows_id, cols_id[:, :768], jnp.zeros((3, 8, 768), jnp.float32), *text, *plane, scratch=copies,
    )
    far, scaled_far, sums = local(
        terms_kernel, (b16(768, width), b16(384, 768), f32(8, 128)),
        scalars, rows_id, cols_id[:, 768:], sums, *text, *plane_far, scratch=copies,
    )
    back = send(far, swap, "rswap")
    sums_core = send(sums, swap, "sums")
    text_own, opposite_low, text_pair, last = local(
        text_kernel, (f32(pairs, width), b16(pairs, width), f32(2 * pairs, width), b16(4 * pairs, width)),
        scaled_own, scaled_far, *plane, *plane_far, scratch=copies[1:],
    )
    last = send(last, apart(-1), "rz1")
    opposite_back = send(opposite_low, along_z(4), "rz4")
    image_own, *lows, spread = local(
        image_kernel, (f32(192, width),) + (b16(192, width),) * 3 + (f32(32, 8, 128),),
        scaled_own, sums, sums_core, *text, back, scratch=copies[:1],
    )
    image_parts = [send(p, along_second(-k), "rsecond") for p, k in zip(lows, OFFSETS)]
    text_own, text_far, low = local(
        near_kernel, (f32(pairs, width), f32(pairs, width), b16(2 * pairs, width)),
        text_own, text_pair, last, opposite_back,
    )
    back = send(low, apart(-2), "rz2")
    with jax.named_scope("terms"):
        spread = lax.all_to_all(spread, AXES, 0, 0, tiled=True, axis_index_groups=across())
    image_own, *lows, sums = local(
        add_kernel, (f32(pairs, width),) + (b16(pairs + 16, width),) * 3 + (f32(8, 128),),
        image_own, *image_parts, spread,
    )
    image_parts = [send(p, along_first(-k), "rfirst") for p, k in zip(lows, OFFSETS)]
    text_own, far_low = local(
        far_kernel, (f32(pairs, width), b16(pairs, width)), text_own, text_far, back, after=(image_own,),
    )
    image_grad, text_grad, sums = local(
        finish_kernel, (f32(pairs, width),) * 2 + (f32(8, 128),),
        scalars, image_raw, image_own, *image_parts, text_raw, text_own, send(far_low, swap, "rpair"), sums,
    )
    return (sums[0, 0:1] / total, image_grad, text_grad, sums[0, 2:3] * temp / total, sums[0, 1:2] / total)


def solution(mesh):
    fine = Mesh(mesh.devices.reshape(SIZES), AXES)
    rows = P(AXES, None)
    return jax.shard_map(
        body,
        mesh=fine,
        in_specs=(rows, rows, P(), P(), P(), P()),
        out_specs=(P(), rows, rows, P(), P()),
        check_vma=False,
    )
```

time: 111 us -> 103 us (0.928)
  waiting for transfers between devices: 14.4 us -> 21.5 us
  starting transfers between devices: 50.1 us -> 43.9 us
  Pallas kernels: 23.2 us -> 19.2 us
  local copies, waits for them, and re-layouts: 12.9 us -> 9.72 us
    pallas_call x4 -> x0, Pallas kernels: 7.85 us -> none  [the longest x2 3.72 us: join(): pl.pallas_call(join_kernel, out_shape=b16(rows * len(pieces), width), in_...]
    all_to_all x2 -> x1, starting transfers between devices: 11.2 us -> 6.72 us  [body(): lax.all_to_all(spread, AXES, 0, 0, tiled=True, axis_index_groups=across())]
    all_to_all x2 -> x1, waiting for transfers between devices: 0.01 us -> 4.23 us  [body(): lax.all_to_all(spread, AXES, 0, 0, tiled=True, axis_index_groups=across())]
    pallas_call x6 -> x10, Pallas kernels: 13.5 us -> 17.3 us  [local(): pl.pallas_call(kernel, out_shape=out_shape, in_specs=[SMEM if a.shape ==...]
    ppermute x28 -> x26, waiting for transfers between devices: 14.4 us -> 17.3 us  [send(): return lax.ppermute(value, AXES, pairs)]
    unnamed x50 -> x30, local copies, waits for them, and re-layouts: 7.02 us -> 5.13 us
    ppermute x28 -> x26, starting transfers between devices: 38.8 us -> 37.2 us  [send(): return lax.ppermute(value, AXES, pairs)]
    broadcast_in_dim x2 -> x0, local copies, waits for them, and re-layouts: 1.33 us -> none  [spread(): jnp.broadcast_to(sums[None], (count, 8, 128))]
  transfers between devices with their start and end apart: 30 -> 27, of which waited for: 5 -> 8; matrix products, arithmetic and copies ran while one was open for 6% -> 4% of each run, Pallas kernels for 14% -> 11%
where the time goes in v3:
time: 103 us; the launch traced here: 102 us
  starting transfers between devices  43.9 us (43%)
  waiting for transfers between devices  21.5 us (21%)
  Pallas kernels  19.2 us (19%)
  local copies, waits for them, and re-layouts  9.72 us (9%)
  between operations  7.51 us (7%)
    ppermute x26, starting transfers between devices, send(): return lax.ppermute(value, AXES, pairs)  37.2 us
    pallas_call x10, Pallas kernels, local(): pl.pallas_call(kernel, out_shape=out_shape, in_specs=[SMEM if a.shape ==...  17.3 us
    ppermute x26, waiting for transfers between devices, send(): return lax.ppermute(value, AXES, pairs)  17.3 us
    all_to_all x1, starting transfers between devices, body(): lax.all_to_all(spread, AXES, 0, 0, tiled=True, axis_index_groups=across())  6.72 us
    unnamed x30, local copies, waits for them, and re-layouts  5.13 us
    all_to_all x1, waiting for transfers between devices, body(): lax.all_to_all(spread, AXES, 0, 0, tiled=True, axis_index_groups=across())  4.23 us
  transfers between devices with their start and end apart: 27, of which 8 were waited for; matrix products, arithmetic and copies ran while one was open for 4% of the time, Pallas kernels for 11%

profile of v3, /device:TPU:6, one launch (start us, length us, event | category | flops | bytes accessed | tf_op | source)
XLA Modules:
  0.0 101.9 jit_solution(12769283976723350994)
XLA Ops:
  0.6 1.9 %shard_map.101 = (bf16[48,1152]{1,0:T(8,128)(2,1)}, bf16[48,1152]{1,0:T(8,128)(2,1)}) custom-call(f32[48,1152]{1,0:T(8,128)} %image_raw.1, f32[48,1152]{1,0:T(8,128)} %text_raw.1), custom_call_target="tpu_custom_call" | custom-call | tf_op jit(solution)/shard_map/pallas_call | solution.py:220
  2.5 1.4 %collective-permute-start.2 = (bf16[48,1152]{1,0:T(8,128)(2,1)}, bf16[48,1152]{1,0:T(8,128)(2,1)S(1)}, u32[]{:S(2)}, u32[]{:S(2)}) collective-permute-start(bf16[48,1152]{1,0:T(8,128)(2,1)} %get-tuple-element.38.i0), channel_id=1, source_target_pairs={{0,16},{1,17},{2,18},{3,19},{4,132},{5,133},{6,134},{7,135},{8,24}... | collective-permute-start | bytes 331784 | tf_op jit(solution)/shard_map/first/ppermute | solution.py:32
  3.9 1.7 %collective-permute-start.1 = (bf16[48,1152]{1,0:T(8,128)(2,1)}, bf16[48,1152]{1,0:T(8,128)(2,1)S(1)}, u32[]{:S(2)}, u32[]{:S(2)}) collective-permute-start(bf16[48,1152]{1,0:T(8,128)(2,1)} %get-tuple-element.38.i0), channel_id=1, source_target_pairs={{0,24},{1,25},{2,26},{3,27},{4,196},{5,197},{6,198},{7,199},{8,0},... | collective-permute-start | bytes 331784 | tf_op jit(solution)/shard_map/first/ppermute | solution.py:32
  5.6 1.6 %collective-permute-start = (bf16[48,1152]{1,0:T(8,128)(2,1)}, bf16[48,1152]{1,0:T(8,128)(2,1)S(1)}, u32[]{:S(2)}, u32[]{:S(2)}) collective-permute-start(bf16[48,1152]{1,0:T(8,128)(2,1)} %get-tuple-element.38.i0), channel_id=1, source_target_pairs={{0,8},{1,9},{2,10},{3,11},{4,68},{5,69},{6,70},{7,71},{8,16},{9,17... | collective-permute-start | bytes 331784 | tf_op jit(solution)/shard_map/first/ppermute | solution.py:32
  7.1 7.2 %collective-permute-start.5 = (bf16[48,1152]{1,0:T(8,128)(2,1)}, bf16[48,1152]{1,0:T(8,128)(2,1)S(1)}, u32[]{:S(2)}, u32[]{:S(2)}) collective-permute-start(bf16[48,1152]{1,0:T(8,128)(2,1)} %get-tuple-element.39.t0.own), channel_id=1, source_target_pairs={{0,32},{1,33},{2,34},{3,35},{4,36},{5,37},{6,38},{7,39},{8,40},{9,... | collective-permute-start | bytes 331784 | tf_op jit(solution)/shard_map/z4/ppermute | solution.py:32
  14.5 0.9 copy-done.5
  15.4 0.9 copy-done.12
  16.3 3.3 %collective-permute-start.9 = (bf16[192,1152]{1,0:T(8,128)(2,1)S(1)}, bf16[192,1152]{1,0:T(8,128)(2,1)S(1)}, u32[]{:S(2)}, u32[]{:S(2)}) collective-permute-start(bf16[192,1152]{1,0:T(8,128)(2,1)S(1)} %get-tuple-element.43.refs_2_.refs_0_), channel_id=1, source_target_pairs={{0,128},{1,129},{2,130},{3,131},{4,20},{5,21},{6,22},{7,23},{8,136... | collective-permute-start | bytes 1327112 | tf_op jit(solution)/shard_map/second/ppermute | solution.py:32
  19.6 1.1 %collective-permute-start.8 = (bf16[192,1152]{1,0:T(8,128)(2,1)S(1)}, bf16[192,1152]{1,0:T(8,128)(2,1)S(1)}, u32[]{:S(2)}, u32[]{:S(2)}) collective-permute-start(bf16[192,1152]{1,0:T(8,128)(2,1)S(1)} %get-tuple-element.43.refs_2_.refs_0_), channel_id=1, source_target_pairs={{0,192},{1,193},{2,194},{3,195},{4,28},{5,29},{6,30},{7,31},{8,200... | collective-permute-start | bytes 1327112 | tf_op jit(solution)/shard_map/second/ppermute | solution.py:32
  20.7 1.0 collective-permute-start.7
  21.8 1.5 %collective-permute-start.4 = (bf16[96,1152]{1,0:T(8,128)(2,1)S(1)}, bf16[96,1152]{1,0:T(8,128)(2,1)S(1)}, u32[]{:S(2)}, u32[]{:S(2)}) collective-permute-start(bf16[96,1152]{1,0:T(8,128)(2,1)S(1)} %get-tuple-element.40.pair), channel_id=1, source_target_pairs={{0,2},{1,3},{2,32},{3,33},{4,38},{5,39},{6,4},{7,5},{8,10},{9,11},... | collective-permute-start | bytes 663560 | tf_op jit(solution)/shard_map/z2/ppermute | solution.py:32
  24.8 0.6 gather_fusion.1
  25.5 0.8 reshape.1566
  26.2 5.1 %collective-permute-done.4.pair_2 = bf16[96,1152]{1,0:T(8,128)(2,1)S(1)} collective-permute-done((bf16[96,1152]{1,0:T(8,128)(2,1)S(1)}, bf16[96,1152]{1,0:T(8,128)(2,1)S(1)}, u32[]{:S(2)}, u32[]{:S(2)}) %collective-permute-start.4) | collective-permute-done | bytes 221216 | tf_op jit(solution)/shard_map/z2/ppermute | solution.py:32
  31.3 0.8 shard_map.103
  32.2 2.0 %collective-permute-start.6 = (bf16[192,1152]{1,0:T(8,128)(2,1)}, bf16[192,1152]{1,0:T(8,128)(2,1)S(1)}, u32[]{:S(2)}, u32[]{:S(2)}) collective-permute-start(bf16[192,1152]{1,0:T(8,128)(2,1)} %get-tuple-element.42), channel_id=1, source_target_pairs={{0,1},{1,2},{2,3},{3,32},{4,39},{5,4},{6,5},{7,6},{8,9},{9,10},{10... | collective-permute-start | bytes 1327112 | tf_op jit(solution)/shard_map/z1/ppermute | solution.py:32
  34.1 0.5 collective-permute-start.12
  34.6 0.3 collective-permute-start.11
  34.9 1.5 %gather_fusion = s32[8,48]{1,0:T(8,128)S(1)} fusion(s32[256,48]{1,0:T(8,128)} %reshape.1566, s32[1024]{0:T(1024)S(1)} %pad_clamp_fusion.1), kind=kCustom, calls=%fused_computation | custom fusion | bytes 3104 | tf_op jit(solution)/shard_map/gather | solution.py:253
  36.4 0.8 reshape.1586.rows_id
  37.3 4.6 %collective-permute-done.6.refs_1_.t1 = bf16[192,1152]{1,0:T(8,128)(2,1)S(1)} collective-permute-done((bf16[192,1152]{1,0:T(8,128)(2,1)}, bf16[192,1152]{1,0:T(8,128)(2,1)S(1)}, u32[]{:S(2)}, u32[]{:S(2)}) %collective-permute-start.6) | collective-permute-done | bytes 442400 | tf_op jit(solution)/shard_map/z1/ppermute | solution.py:32
  41.9 0.9 copy-done
  42.8 2.8 %shard_map.104 = (bf16[384,768]{1,0:T(8,128)(2,1)S(1)}, f32[3,8,768]{2,1,0:T(8,128)S(1)}) custom-call(f32[2]{0:T(128)S(1)} %pad_maximum_fusion.scalars, s32[384,1]{1,0:T(8,128)S(1)} %copy-done, s32[1,768]{1,0:T(1,128)S(1)} %get-tuple-element.72.cols_id, f32[3,8,768]{2,1,0:T(8,128)S(1)} %broadcast_in_dim.2.before, ...), custom_call_target="tpu_custom_call" | custom-call | tf_op jit(solution)/shard_map/pallas_call | solution.py:205
  45.7 4.2 %shard_map.105 = (bf16[768,1152]{1,0:T(8,128)(2,1)S(1)}, bf16[384,768]{1,0:T(8,128)(2,1)S(1)}, f32[8,128]{1,0:T(8,128)S(1)}) custom-call(f32[2]{0:T(128)S(1)} %pad_maximum_fusion.scalars, s32[384,1]{1,0:T(8,128)S(1)} %copy-done, s32[1,768]{1,0:T(1,128)S(1)} %get-tuple-element.71.cols_id, f32[3,8,768]{2,1,0:T(8,128)S(1)} %get-tuple-element.45.before, ...), custom_call_target="tpu_custom_call" | custom-call | tf_op jit(solution)/shard_map/pallas_call | solution.py:205
  50.0 3.7 %shard_map.108 = (f32[48,1152]{1,0:T(8,128)S(1)}, bf16[48,1152]{1,0:T(8,128)(2,1)}, f32[96,1152]{1,0:T(8,128)S(1)}, bf16[192,1152]{1,0:T(8,128)(2,1)}) custom-call(bf16[384,768]{1,0:T(8,128)(2,1)S(1)} %get-tuple-element.44.scaled.scaled_own, bf16[384,768]{1,0:T(8,128)(2,1)S(1)} %get-tuple-element.57.scaled_far, ...), custom_call_target="tpu_custom_call" | custom-call | tf_op jit(solution)/shard_map/pallas_call | solution.py:205
  53.7 0.8 copy-done.3
  54.5 0.9 collective-permute-start.14
  55.4 0.8 collective-permute-done.14.more
  56.2 2.2 %shard_map.106 = (f32[192,1152]{1,0:T(8,128)S(1)}, bf16[192,1152]{1,0:T(8,128)(2,1)}, bf16[192,1152]{1,0:T(8,128)(2,1)}, bf16[192,1152]{1,0:T(8,128)(2,1)}, f32[32,8,128]{2,1,0:T(8,128)S(1)}) custom-call(bf16[384,768]{1,0:T(8,128)(2,1)S(1)} %get-tuple-element.44.scaled.scaled_own, f32[8,128]{1,0:T(8,128)S(1)} %get-tuple-element.46.sums, ...), custom_call_target="tpu_custom_call" | custom-call | tf_op jit(solution)/shard_map/pallas_call | solution.py:205
  58.5 2.3 %collective-permute-start.16 = (bf16[192,1152]{1,0:T(8,128)(2,1)}, bf16[192,1152]{1,0:T(8,128)(2,1)S(1)}, u32[]{:S(2)}, u32[]{:S(2)}) collective-permute-start(bf16[192,1152]{1,0:T(8,128)(2,1)} %get-tuple-element.49), channel_id=1, source_target_pairs={{0,192},{1,193},{2,194},{3,195},{4,28},{5,29},{6,30},{7,31},{8,200... | collective-permute-start | bytes 1327112 | tf_op jit(solution)/shard_map/rsecond/ppermute | solution.py:32
  60.7 1.5 %collective-permute-start.18 = (bf16[192,1152]{1,0:T(8,128)(2,1)}, bf16[192,1152]{1,0:T(8,128)(2,1)}, u32[]{:S(2)}, u32[]{:S(2)}) collective-permute-start(bf16[192,1152]{1,0:T(8,128)(2,1)} %get-tuple-element.51), channel_id=1, source_target_pairs={{0,128},{1,129},{2,130},{3,131},{4,20},{5,21},{6,22},{7,23},{8,136... | collective-permute-start | bytes 1327112 | tf_op jit(solution)/shard_map/rsecond/ppermute | solution.py:32
  62.3 2.9 %collective-permute-start.23 = (bf16[48,1152]{1,0:T(8,128)(2,1)}, bf16[48,1152]{1,0:T(8,128)(2,1)S(1)}, u32[]{:S(2)}, u32[]{:S(2)}) collective-permute-start(bf16[48,1152]{1,0:T(8,128)(2,1)} %get-tuple-element.61), channel_id=1, source_target_pairs={{0,32},{1,33},{2,34},{3,35},{4,36},{5,37},{6,38},{7,39},{8,40},{9,... | collective-permute-start | bytes 331784 | tf_op jit(solution)/shard_map/rz4/ppermute | solution.py:32
  65.1 6.7 %all-to-all-start = ((f32[32,8,128]{2,1,0:T(8,128)}), f32[32,8,128]{2,1,0:T(8,128)S(1)}, u32[]{:S(2)}, u32[]{:S(2)}) async-start(f32[32,8,128]{2,1,0:T(8,128)} %copy-done.11), calls=%async_computation | async-start | bytes 262144 | tf_op jit(solution)/shard_map/terms/all_to_all | solution.py:285
  71.9 1.6 %collective-permute-done.23.opposite = bf16[48,1152]{1,0:T(8,128)(2,1)S(1)} collective-permute-done((bf16[48,1152]{1,0:T(8,128)(2,1)}, bf16[48,1152]{1,0:T(8,128)(2,1)S(1)}, u32[]{:S(2)}, u32[]{:S(2)}) %collective-permute-start.23) | collective-permute-done | bytes 110624 | tf_op jit(solution)/shard_map/rz4/ppermute | solution.py:32
  73.5 0.9 copy-done.10
  74.4 0.7 shard_map.109
  75.1 0.7 copy-done.7
  75.8 2.3 %collective-permute-start.24 = (bf16[96,1152]{1,0:T(8,128)(2,1)}, bf16[96,1152]{1,0:T(8,128)(2,1)S(1)}, u32[]{:S(2)}, u32[]{:S(2)}) collective-permute-start(bf16[96,1152]{1,0:T(8,128)(2,1)} %get-tuple-element.64), channel_id=1, source_target_pairs={{0,34},{1,35},{2,0},{3,1},{4,6},{5,7},{6,36},{7,37},{8,42},{9,43},... | collective-permute-start | bytes 663560 | tf_op jit(solution)/shard_map/rz2/ppermute | solution.py:32
  78.2 4.2 %all-to-all-done.terms = f32[32,8,128]{2,1,0:T(8,128)S(1)} async-done(((f32[32,8,128]{2,1,0:T(8,128)}), f32[32,8,128]{2,1,0:T(8,128)S(1)}, u32[]{:S(2)}, u32[]{:S(2)}) %all-to-all-start) | async-done | bytes 131104 | tf_op jit(solution)/shard_map/terms/all_to_all | solution.py:285
  82.4 1.2 %shard_map.107 = (f32[48,1152]{1,0:T(8,128)S(1)}, bf16[64,1152]{1,0:T(8,128)(2,1)S(1)}, bf16[64,1152]{1,0:T(8,128)(2,1)S(1)}, bf16[64,1152]{1,0:T(8,128)(2,1)S(1)}, f32[8,128]{1,0:T(8,128)S(1)}) custom-call(f32[192,1152]{1,0:T(8,128)S(1)} %get-tuple-element.48.own, bf16[192,1152]{1,0:T(8,128)(2,1)S(1)} %collective-permute-done.16.r1, ...), custom_call_target="tpu_custom_call" | custom-call | tf_op jit(solution)/shard_map/pallas_call | solution.py:205
  83.6 0.7 collective-permute-start.19
  84.4 3.5 %collective-permute-start.20 = (bf16[64,1152]{1,0:T(8,128)(2,1)S(1)}, bf16[64,1152]{1,0:T(8,128)(2,1)S(1)}, u32[]{:S(2)}, u32[]{:S(2)}) collective-permute-start(bf16[64,1152]{1,0:T(8,128)(2,1)S(1)} %get-tuple-element.55), channel_id=1, source_target_pairs={{0,8},{1,9},{2,10},{3,11},{4,68},{5,69},{6,70},{7,71},{8,16},{9,17... | collective-permute-start | bytes 442376 | tf_op jit(solution)/shard_map/rfirst/ppermute | solution.py:32
  87.9 1.4 %collective-permute-start.21 = (bf16[64,1152]{1,0:T(8,128)(2,1)S(1)}, bf16[64,1152]{1,0:T(8,128)(2,1)S(1)}, u32[]{:S(2)}, u32[]{:S(2)}) collective-permute-start(bf16[64,1152]{1,0:T(8,128)(2,1)S(1)} %get-tuple-element.56), channel_id=1, source_target_pairs={{0,16},{1,17},{2,18},{3,19},{4,132},{5,133},{6,134},{7,135},{8,24}... | collective-permute-start | bytes 442376 | tf_op jit(solution)/shard_map/rfirst/ppermute | solution.py:32
  89.4 1.3 %collective-permute-done.25.t1 = bf16[48,1152]{1,0:T(8,128)(2,1)S(1)} collective-permute-done((bf16[48,1152]{1,0:T(8,128)(2,1)S(1)}, bf16[48,1152]{1,0:T(8,128)(2,1)S(1)}, u32[]{:S(2)}, u32[]{:S(2)}) %collective-permute-start.25) | collective-permute-done | bytes 110624 | tf_op jit(solution)/shard_map/rpair/ppermute | solution.py:32
  90.7 0.2 collective-permute-done.19.i1
  90.9 3.6 %collective-permute-done.21.i3 = bf16[64,1152]{1,0:T(8,128)(2,1)S(1)} collective-permute-done((bf16[64,1152]{1,0:T(8,128)(2,1)S(1)}, bf16[64,1152]{1,0:T(8,128)(2,1)S(1)}, u32[]{:S(2)}, u32[]{:S(2)}) %collective-permute-start.21) | collective-permute-done | bytes 147488 | tf_op jit(solution)/shard_map/rfirst/ppermute | solution.py:32
  94.5 1.5 %shard_map.111 = (f32[48,1152]{1,0:T(8,128)}, f32[48,1152]{1,0:T(8,128)}, f32[8,128]{1,0:T(8,128)S(1)}) custom-call(f32[2]{0:T(128)S(1)} %pad_maximum_fusion.scalars, f32[48,1152]{1,0:T(8,128)S(1)} %copy-done.1, f32[48,1152]{1,0:T(8,128)S(1)} %get-tuple-element.53.after.image_own, bf16[64,1152]{1,0:T(8,128)(2,1)S(1)} %collective-permute-done.19.i1, ...), custom_call_target="tpu_custom_call" | custom-call | tf_op jit(solution)/shard_map/pallas_call | solution.py:205
  96.0 0.6 fusion.3
  (63 shorter events, 1.0 us)
Async XLA Ops:
  0.6 24.0 %copy-start.13 = (s32[12288]{0:T(1024)S(1)}, s32[12288]{0:T(1024)}, u32[]{:S(2)}) copy-start(s32[12288]{0:T(1024)} %param.8) | copy-start | bytes 147460
  2.5 23.0 %copy-start.14 = (s32[12288]{0:T(1024)S(1)}, s32[12288]{0:T(1024)}, u32[]{:S(2)}) copy-start(s32[12288]{0:T(1024)} %param.9) | copy-start | bytes 147460
  2.5 28.8 %copy-start.6 = (bf16[48,1152]{1,0:T(8,128)(2,1)S(1)}, bf16[48,1152]{1,0:T(8,128)(2,1)}, u32[]{:S(2)}) copy-start(bf16[48,1152]{1,0:T(8,128)(2,1)} %get-tuple-element.39.t0.own) | copy-start | bytes 331780
  2.5 11.9 %collective-permute-start.2 = (bf16[48,1152]{1,0:T(8,128)(2,1)}, bf16[48,1152]{1,0:T(8,128)(2,1)S(1)}, u32[]{:S(2)}, u32[]{:S(2)}) collective-permute-start(bf16[48,1152]{1,0:T(8,128)(2,1)} %get-tuple-element.38.i0), channel_id=1, source_target_pairs={{0,16},{1,17},{2,18},{3,19},{4,132},{5,133},{6,134},{7,135},{8,24}... | collective-permute-start | bytes 331784 | tf_op jit(solution)/shard_map/first/ppermute | solution.py:32
  3.9 10.5 %collective-permute-start.1 = (bf16[48,1152]{1,0:T(8,128)(2,1)}, bf16[48,1152]{1,0:T(8,128)(2,1)S(1)}, u32[]{:S(2)}, u32[]{:S(2)}) collective-permute-start(bf16[48,1152]{1,0:T(8,128)(2,1)} %get-tuple-element.38.i0), channel_id=1, source_target_pairs={{0,24},{1,25},{2,26},{3,27},{4,196},{5,197},{6,198},{7,199},{8,0},... | collective-permute-start | bytes 331784 | tf_op jit(solution)/shard_map/first/ppermute | solution.py:32
  5.6 8.9 %collective-permute-start = (bf16[48,1152]{1,0:T(8,128)(2,1)}, bf16[48,1152]{1,0:T(8,128)(2,1)S(1)}, u32[]{:S(2)}, u32[]{:S(2)}) collective-permute-start(bf16[48,1152]{1,0:T(8,128)(2,1)} %get-tuple-element.38.i0), channel_id=1, source_target_pairs={{0,8},{1,9},{2,10},{3,11},{4,68},{5,69},{6,70},{7,71},{8,16},{9,17... | collective-permute-start | bytes 331784 | tf_op jit(solution)/shard_map/first/ppermute | solution.py:32
  7.1 7.3 %collective-permute-start.3 = (bf16[48,1152]{1,0:T(8,128)(2,1)}, bf16[48,1152]{1,0:T(8,128)(2,1)S(1)}, u32[]{:S(2)}, u32[]{:S(2)}) collective-permute-start(bf16[48,1152]{1,0:T(8,128)(2,1)} %get-tuple-element.39.t0.own), channel_id=1, source_target_pairs={{0,4},{1,5},{2,6},{3,7},{4,0},{5,1},{6,2},{7,3},{8,12},{9,13},{10,... | collective-permute-start | bytes 331784 | tf_op jit(solution)/shard_map/pair/ppermute | solution.py:32
  7.1 19.1 %collective-permute-start.5 = (bf16[48,1152]{1,0:T(8,128)(2,1)}, bf16[48,1152]{1,0:T(8,128)(2,1)S(1)}, u32[]{:S(2)}, u32[]{:S(2)}) collective-permute-start(bf16[48,1152]{1,0:T(8,128)(2,1)} %get-tuple-element.39.t0.own), channel_id=1, source_target_pairs={{0,32},{1,33},{2,34},{3,35},{4,36},{5,37},{6,38},{7,39},{8,40},{9,... | collective-permute-start | bytes 331784 | tf_op jit(solution)/shard_map/z4/ppermute | solution.py:32
  14.5 0.9 copy-start.5
  15.4 0.9 copy-start.12
  16.3 17.8 %collective-permute-start.9 = (bf16[192,1152]{1,0:T(8,128)(2,1)S(1)}, bf16[192,1152]{1,0:T(8,128)(2,1)S(1)}, u32[]{:S(2)}, u32[]{:S(2)}) collective-permute-start(bf16[192,1152]{1,0:T(8,128)(2,1)S(1)} %get-tuple-element.43.refs_2_.refs_0_), channel_id=1, source_target_pairs={{0,128},{1,129},{2,130},{3,131},{4,20},{5,21},{6,22},{7,23},{8,136... | collective-permute-start | bytes 1327112 | tf_op jit(solution)/shard_map/second/ppermute | solution.py:32
  19.6 14.5 %collective-permute-start.8 = (bf16[192,1152]{1,0:T(8,128)(2,1)S(1)}, bf16[192,1152]{1,0:T(8,128)(2,1)S(1)}, u32[]{:S(2)}, u32[]{:S(2)}) collective-permute-start(bf16[192,1152]{1,0:T(8,128)(2,1)S(1)} %get-tuple-element.43.refs_2_.refs_0_), channel_id=1, source_target_pairs={{0,192},{1,193},{2,194},{3,195},{4,28},{5,29},{6,30},{7,31},{8,200... | collective-permute-start | bytes 1327112 | tf_op jit(solution)/shard_map/second/ppermute | solution.py:32
  20.7 14.0 %collective-permute-start.7 = (bf16[192,1152]{1,0:T(8,128)(2,1)S(1)}, bf16[192,1152]{1,0:T(8,128)(2,1)S(1)}, u32[]{:S(2)}, u32[]{:S(2)}) collective-permute-start(bf16[192,1152]{1,0:T(8,128)(2,1)S(1)} %get-tuple-element.43.refs_2_.refs_0_), channel_id=1, source_target_pairs={{0,64},{1,65},{2,66},{3,67},{4,12},{5,13},{6,14},{7,15},{8,72},{9,... | collective-permute-start | bytes 1327112 | tf_op jit(solution)/shard_map/second/ppermute | solution.py:32
  21.8 9.6 %collective-permute-start.4 = (bf16[96,1152]{1,0:T(8,128)(2,1)S(1)}, bf16[96,1152]{1,0:T(8,128)(2,1)S(1)}, u32[]{:S(2)}, u32[]{:S(2)}) collective-permute-start(bf16[96,1152]{1,0:T(8,128)(2,1)S(1)} %get-tuple-element.40.pair), channel_id=1, source_target_pairs={{0,2},{1,3},{2,32},{3,33},{4,38},{5,39},{6,4},{7,5},{8,10},{9,11},... | collective-permute-start | bytes 663560 | tf_op jit(solution)/shard_map/z2/ppermute | solution.py:32
  26.2 19.4 %collective-permute-start.10 = (bf16[192,1152]{1,0:T(8,128)(2,1)S(1)}, bf16[192,1152]{1,0:T(8,128)(2,1)S(1)}, u32[]{:S(2)}, u32[]{:S(2)}) collective-permute-start(bf16[192,1152]{1,0:T(8,128)(2,1)S(1)} %get-tuple-element.43.refs_2_.refs_0_), channel_id=1, source_target_pairs={{0,4},{1,5},{2,6},{3,7},{4,0},{5,1},{6,2},{7,3},{8,12},{9,13},{10,... | collective-permute-start | bytes 1327112 | tf_op jit(solution)/shard_map/swap/ppermute | solution.py:32
  32.2 9.7 %collective-permute-start.6 = (bf16[192,1152]{1,0:T(8,128)(2,1)}, bf16[192,1152]{1,0:T(8,128)(2,1)S(1)}, u32[]{:S(2)}, u32[]{:S(2)}) collective-permute-start(bf16[192,1152]{1,0:T(8,128)(2,1)} %get-tuple-element.42), channel_id=1, source_target_pairs={{0,1},{1,2},{2,3},{3,32},{4,39},{5,4},{6,5},{7,6},{8,9},{9,10},{10... | collective-permute-start | bytes 1327112 | tf_op jit(solution)/shard_map/z1/ppermute | solution.py:32
  34.1 11.5 %collective-permute-start.13 = (bf16[192,1152]{1,0:T(8,128)(2,1)S(1)}, bf16[192,1152]{1,0:T(8,128)(2,1)S(1)}, u32[]{:S(2)}, u32[]{:S(2)}) collective-permute-start(bf16[192,1152]{1,0:T(8,128)(2,1)S(1)} %collective-permute-done.9.refs_5_.refs_3_), channel_id=1, source_target_pairs={{0,4},{1,5},{2,6},{3,7},{4,0},{5,1},{6,2},{7,3},{8,12},{9,13},{10,... | collective-permute-start | bytes 1327112 | tf_op jit(solution)/shard_map/swap/ppermute | solution.py:32
  34.1 11.5 %collective-permute-start.12 = (bf16[192,1152]{1,0:T(8,128)(2,1)S(1)}, bf16[192,1152]{1,0:T(8,128)(2,1)}, u32[]{:S(2)}, u32[]{:S(2)}) collective-permute-start(bf16[192,1152]{1,0:T(8,128)(2,1)S(1)} %collective-permute-done.8.refs_4_.refs_2_), channel_id=1, source_target_pairs={{0,4},{1,5},{2,6},{3,7},{4,0},{5,1},{6,2},{7,3},{8,12},{9,13},{10,... | collective-permute-start | bytes 1327112 | tf_op jit(solution)/shard_map/swap/ppermute | solution.py:32
  34.6 11.0 %collective-permute-start.11 = (bf16[192,1152]{1,0:T(8,128)(2,1)S(1)}, bf16[192,1152]{1,0:T(8,128)(2,1)}, u32[]{:S(2)}, u32[]{:S(2)}) collective-permute-start(bf16[192,1152]{1,0:T(8,128)(2,1)S(1)} %collective-permute-done.7.refs_3_.refs_1_), channel_id=1, source_target_pairs={{0,4},{1,5},{2,6},{3,7},{4,0},{5,1},{6,2},{7,3},{8,12},{9,13},{10,... | collective-permute-start | bytes 1327112 | tf_op jit(solution)/shard_map/swap/ppermute | solution.py:32
  41.9 0.9 copy-start
  49.9 6.4 %collective-permute-start.15 = (bf16[768,1152]{1,0:T(8,128)(2,1)S(1)}, bf16[768,1152]{1,0:T(8,128)(2,1)S(1)}, u32[]{:S(2)}, u32[]{:S(2)}) collective-permute-start(bf16[768,1152]{1,0:T(8,128)(2,1)S(1)} %get-tuple-element.47), channel_id=1, source_target_pairs={{0,4},{1,5},{2,6},{3,7},{4,0},{5,1},{6,2},{7,3},{8,12},{9,13},{10,... | collective-permute-start | bytes 5308424 | tf_op jit(solution)/shard_map/rswap/ppermute | solution.py:32
  53.7 0.8 copy-start.3
  54.4 6.3 %copy-start.9 = (f32[48,1152]{1,0:T(8,128)}, f32[48,1152]{1,0:T(8,128)S(1)}, u32[]{:S(2)}) copy-start(f32[48,1152]{1,0:T(8,128)S(1)} %get-tuple-element.58.own) | copy-start | bytes 663556
  54.4 19.0 %copy-start.4 = (f32[96,1152]{1,0:T(8,128)S(1)}, f32[96,1152]{1,0:T(8,128)}, u32[]{:S(2)}) copy-start(f32[96,1152]{1,0:T(8,128)} %copy-done.3) | copy-start | bytes 1327108
  54.4 19.0 %collective-permute-start.22 = (bf16[192,1152]{1,0:T(8,128)(2,1)}, bf16[192,1152]{1,0:T(8,128)(2,1)S(1)}, u32[]{:S(2)}, u32[]{:S(2)}) collective-permute-start(bf16[192,1152]{1,0:T(8,128)(2,1)} %get-tuple-element.60), channel_id=1, source_target_pairs={{0,35},{1,0},{2,1},{3,2},{4,5},{5,6},{6,7},{7,36},{8,43},{9,8},{10... | collective-permute-start | bytes 1327112 | tf_op jit(solution)/shard_map/rz1/ppermute | solution.py:32
  54.5 1.7 %collective-permute-start.14 = (f32[8,128]{1,0:T(8,128)S(1)}, f32[8,128]{1,0:T(8,128)S(1)}, u32[]{:S(2)}, u32[]{:S(2)}) collective-permute-start(f32[8,128]{1,0:T(8,128)S(1)} %get-tuple-element.46.sums), channel_id=1, source_target_pairs={{0,4},{1,5},{2,6},{3,7},{4,0},{5,1},{6,2},{7,3},{8,12},{9,13},{10,... | collective-permute-start | bytes 12296 | tf_op jit(solution)/shard_map/sums/ppermute | solution.py:32
  58.5 6.7 %copy-start.11 = (f32[32,8,128]{2,1,0:T(8,128)}, f32[32,8,128]{2,1,0:T(8,128)S(1)}, u32[]{:S(2)}) copy-start(f32[32,8,128]{2,1,0:T(8,128)S(1)} %get-tuple-element.52) | copy-start | bytes 393220
  58.5 24.0 %collective-permute-start.16 = (bf16[192,1152]{1,0:T(8,128)(2,1)}, bf16[192,1152]{1,0:T(8,128)(2,1)S(1)}, u32[]{:S(2)}, u32[]{:S(2)}) collective-permute-start(bf16[192,1152]{1,0:T(8,128)(2,1)} %get-tuple-element.49), channel_id=1, source_target_pairs={{0,192},{1,193},{2,194},{3,195},{4,28},{5,29},{6,30},{7,31},{8,200... | collective-permute-start | bytes 1327112 | tf_op jit(solution)/shard_map/rsecond/ppermute | solution.py:32
  60.7 21.7 %collective-permute-start.17 = (bf16[192,1152]{1,0:T(8,128)(2,1)}, bf16[192,1152]{1,0:T(8,128)(2,1)S(1)}, u32[]{:S(2)}, u32[]{:S(2)}) collective-permute-start(bf16[192,1152]{1,0:T(8,128)(2,1)} %get-tuple-element.50), channel_id=1, source_target_pairs={{0,64},{1,65},{2,66},{3,67},{4,12},{5,13},{6,14},{7,15},{8,72},{9,... | collective-permute-start | bytes 1327112 | tf_op jit(solution)/shard_map/rsecond/ppermute | solution.py:32
  60.7 21.7 %collective-permute-start.18 = (bf16[192,1152]{1,0:T(8,128)(2,1)}, bf16[192,1152]{1,0:T(8,128)(2,1)}, u32[]{:S(2)}, u32[]{:S(2)}) collective-permute-start(bf16[192,1152]{1,0:T(8,128)(2,1)} %get-tuple-element.51), channel_id=1, source_target_pairs={{0,128},{1,129},{2,130},{3,131},{4,20},{5,21},{6,22},{7,23},{8,136... | collective-permute-start | bytes 1327112 | tf_op jit(solution)/shard_map/rsecond/ppermute | solution.py:32
  62.3 11.2 %collective-permute-start.23 = (bf16[48,1152]{1,0:T(8,128)(2,1)}, bf16[48,1152]{1,0:T(8,128)(2,1)S(1)}, u32[]{:S(2)}, u32[]{:S(2)}) collective-permute-start(bf16[48,1152]{1,0:T(8,128)(2,1)} %get-tuple-element.61), channel_id=1, source_target_pairs={{0,32},{1,33},{2,34},{3,35},{4,36},{5,37},{6,38},{7,39},{8,40},{9,... | collective-permute-start | bytes 331784 | tf_op jit(solution)/shard_map/rz4/ppermute | solution.py:32
  65.1 17.3 %all-to-all-start = ((f32[32,8,128]{2,1,0:T(8,128)}), f32[32,8,128]{2,1,0:T(8,128)S(1)}, u32[]{:S(2)}, u32[]{:S(2)}) async-start(f32[32,8,128]{2,1,0:T(8,128)} %copy-done.11), calls=%async_computation | async-start | bytes 262144 | tf_op jit(solution)/shard_map/terms/all_to_all | solution.py:285
  73.5 0.9 copy-start.10
  75.1 0.7 copy-start.7
  75.8 18.7 %copy-start.1 = (f32[48,1152]{1,0:T(8,128)S(1)}, f32[48,1152]{1,0:T(8,128)}, u32[]{:S(2)}) copy-start(f32[48,1152]{1,0:T(8,128)} %image_raw.1) | copy-start | bytes 663556
  75.8 18.7 %copy-start.2 = (f32[48,1152]{1,0:T(8,128)S(1)}, f32[48,1152]{1,0:T(8,128)}, u32[]{:S(2)}) copy-start(f32[48,1152]{1,0:T(8,128)} %text_raw.1) | copy-start | bytes 663556
  75.8 13.4 %copy-start.8 = (f32[48,1152]{1,0:T(8,128)S(1)}, f32[48,1152]{1,0:T(8,128)}, u32[]{:S(2)}) copy-start(f32[48,1152]{1,0:T(8,128)} %copy-done.7) | copy-start | bytes 663556
  75.8 13.4 %collective-permute-start.24 = (bf16[96,1152]{1,0:T(8,128)(2,1)}, bf16[96,1152]{1,0:T(8,128)(2,1)S(1)}, u32[]{:S(2)}, u32[]{:S(2)}) collective-permute-start(bf16[96,1152]{1,0:T(8,128)(2,1)} %get-tuple-element.64), channel_id=1, source_target_pairs={{0,34},{1,35},{2,0},{3,1},{4,6},{5,7},{6,36},{7,37},{8,42},{9,43},... | collective-permute-start | bytes 663560 | tf_op jit(solution)/shard_map/rz2/ppermute | solution.py:32
  83.6 7.3 %collective-permute-start.19 = (bf16[64,1152]{1,0:T(8,128)(2,1)S(1)}, bf16[64,1152]{1,0:T(8,128)(2,1)S(1)}, u32[]{:S(2)}, u32[]{:S(2)}) collective-permute-start(bf16[64,1152]{1,0:T(8,128)(2,1)S(1)} %get-tuple-element.54), channel_id=1, source_target_pairs={{0,24},{1,25},{2,26},{3,27},{4,196},{5,197},{6,198},{7,199},{8,0},... | collective-permute-start | bytes 442376 | tf_op jit(solution)/shard_map/rfirst/ppermute | solution.py:32
  84.4 6.5 %collective-permute-start.20 = (bf16[64,1152]{1,0:T(8,128)(2,1)S(1)}, bf16[64,1152]{1,0:T(8,128)(2,1)S(1)}, u32[]{:S(2)}, u32[]{:S(2)}) collective-permute-start(bf16[64,1152]{1,0:T(8,128)(2,1)S(1)} %get-tuple-element.55), channel_id=1, source_target_pairs={{0,8},{1,9},{2,10},{3,11},{4,68},{5,69},{6,70},{7,71},{8,16},{9,17... | collective-permute-start | bytes 442376 | tf_op jit(solution)/shard_map/rfirst/ppermute | solution.py:32
  87.9 6.6 %collective-permute-start.21 = (bf16[64,1152]{1,0:T(8,128)(2,1)S(1)}, bf16[64,1152]{1,0:T(8,128)(2,1)S(1)}, u32[]{:S(2)}, u32[]{:S(2)}) collective-permute-start(bf16[64,1152]{1,0:T(8,128)(2,1)S(1)} %get-tuple-element.56), channel_id=1, source_target_pairs={{0,16},{1,17},{2,18},{3,19},{4,132},{5,133},{6,134},{7,135},{8,24}... | collective-permute-start | bytes 442376 | tf_op jit(solution)/shard_map/rfirst/ppermute | solution.py:32
  89.3 1.4 %collective-permute-start.25 = (bf16[48,1152]{1,0:T(8,128)(2,1)S(1)}, bf16[48,1152]{1,0:T(8,128)(2,1)S(1)}, u32[]{:S(2)}, u32[]{:S(2)}) collective-permute-start(bf16[48,1152]{1,0:T(8,128)(2,1)S(1)} %get-tuple-element.66), channel_id=1, source_target_pairs={{0,4},{1,5},{2,6},{3,7},{4,0},{5,1},{6,2},{7,3},{8,12},{9,13},{10,... | collective-permute-start | bytes 331784 | tf_op jit(solution)/shard_map/rpair/ppermute | solution.py:32

commit v4 on v3

v4 whole, which is shorter than its diff:
```python
import math

import jax
import jax.numpy as jnp
import numpy as np
from jax import lax
from jax.experimental import pallas as pl
from jax.experimental.pallas import tpu as pltpu
from jax.sharding import Mesh
from jax.sharding import PartitionSpec as P

SIZES = (4, 2, 4, 2, 4)
AXES = ("y", "zh", "x", "core", "zl")
ROWS = 48
OFFSETS = (1, 3, 2)
ANY = pl.BlockSpec(memory_space=pl.ANY)
VMEM = pl.BlockSpec(memory_space=pltpu.VMEM)
SMEM = pl.BlockSpec(memory_space=pltpu.SMEM)


def flat(x, y, z, c):
    return (((y * 2 + z // 4) * 4 + x) * 2 + c) * 4 + z % 4


def send(value, where, name="move"):
    pairs = []
    for y, zh, x, c, zl in np.ndindex(*SIZES):
        z = zh * 4 + zl
        tx, ty, tz, tc = where(x, y, z, c)
        pairs.append((flat(x, y, z, c), flat(tx % 4, ty % 4, tz % 8, tc % 2)))
    with jax.named_scope(name):
        return lax.ppermute(value, AXES, pairs)


def along_first(k):
    return lambda x, y, z, c: (x + k, y, z, c) if c == 0 else (x, y + k, z, c)


def along_second(k):
    return lambda x, y, z, c: (x, y + k, z, c) if c == 0 else (x + k, y, z, c)


def along_z(k):
    return lambda x, y, z, c: (x, y, z + k, c)


def apart(k):
    return lambda x, y, z, c: (x, y, z + k, c) if c == 0 else (x, y, z - k, c)


def across():
    groups = {}
    for y, zh, x, c, zl in np.ndindex(*SIZES):
        groups.setdefault((c, y if c else x), []).append(flat(x, y, zh * 4 + zl, c))
    return list(groups.values())


def swap(x, y, z, c):
    return (x, y, z, 1 - c)


def unit(rows):
    scale = jnp.sqrt(jnp.mean(rows * rows, axis=-1, keepdims=True) + 1e-06)
    return (rows / (scale * math.sqrt(rows.shape[-1]))).astype(jnp.bfloat16)


def text_unit_kernel(raw, out, kept):
    out[...] = unit(raw[...])
    kept[...] = out[...]


def image_unit_kernel(raw, text, text_far, out, kept, pair, pair_kept):
    out[...] = unit(raw[...])
    kept[...] = out[...]
    stack(pair, (text, text_far))
    stack(pair_kept, (text, text_far))


def stack(out, sources):
    row = 0
    for src in sources:
        out[row : row + src.shape[0], :] = src[...]
        row += src.shape[0]


def gather_kernel(i0, i1, i2, i3, own, pair, pair_2, after, line, message, hop, kept):
    stack(line, (i0, i1, i2, i3))
    stack(message, (pair, pair_2))
    hop[...] = pair_2[:48]
    stack(kept, (own, pair_2))


def flag_kernel(*refs):
    refs[-1][...] = jnp.zeros_like(refs[-1])


def copy_kernel(src, after, out):
    out[...] = src[...]


def ride(out, row, value):
    high = value.astype(jnp.bfloat16).astype(jnp.float32)
    mid = (value - high).astype(jnp.bfloat16).astype(jnp.float32)
    low = value - high - mid
    at = lax.broadcasted_iota(jnp.int32, (16, 128), 0)
    extra = jnp.where(at == 0, high, jnp.where(at == 1, mid, jnp.where(at == 2, low, 0.0)))
    out[row:, :] = jnp.zeros((16, out.shape[1]), out.dtype)
    out[row:, :128] = extra.astype(out.dtype)


def alight(part, row):
    extra = part[row : row + 16, :128].astype(jnp.float32)
    return (extra[2:3] + extra[1:2]) + extra[0:1]


def terms_kernel(scalars, rows_id, cols_id, before, *refs):
    pieces, (*far, scaled, sums, text, image) = refs[:7], refs[7:]
    temp = scalars[0]
    offset = scalars[1]
    stack(text, pieces[:3])
    stack(image, pieces[3:])
    totals = [before[n] for n in range(3)]
    cols = cols_id[...]
    rows = jnp.transpose(jnp.broadcast_to(rows_id[...].astype(jnp.float32), (128, 384)))[:, :1].astype(jnp.int32)
    for tile in range(2):
        at = slice(192 * tile, 192 * (tile + 1))
        cosine = lax.dot_general(
            text[at, :], image[...], (((1,), (1,)), ((), ())), preferred_element_type=jnp.float32
        )
        logits = temp * cosine + offset
        same = rows[at, :] == cols
        margin = jnp.where(same, -logits, logits)
        decay = jnp.exp(-jnp.abs(margin))
        inverse = 1.0 / (1.0 + decay)
        sigmoid = jnp.where(margin >= 0, inverse, decay * inverse)
        grad = jnp.where(same, -sigmoid, sigmoid)
        loss = jnp.maximum(margin, 0.0) + jnp.log1p(decay)
        scaled[at, :] = grad.astype(jnp.bfloat16)
        for n, value in enumerate((loss, grad, grad * cosine)):
            totals[n] = totals[n] + jnp.sum(value.reshape(24, 8, 768), axis=0)
    if not far:
        for n in range(3):
            sums[n] = totals[n]
        return
    lane = lax.broadcasted_iota(jnp.int32, (1, 128), 1)
    out = jnp.zeros((1, 128), jnp.float32)
    for n in range(3):
        out = jnp.where(lane == n, jnp.sum(totals[n]), out)
    sums[...] = jnp.broadcast_to(out, sums.shape)
    far[0][:768, :] = lax.dot_general(
        scaled[...], text[...], (((0,), (0,)), ((), ())), preferred_element_type=jnp.float32
    ).astype(jnp.bfloat16)
    ride(far[0], 768, out)


def text_kernel(scaled_own, scaled_far, *refs):
    pieces, (own, pair, opposite, last, image) = refs[:8], refs[8:]
    stack(image, pieces[:4])
    total = jnp.dot(scaled_own[...], image[...], preferred_element_type=jnp.float32)
    stack(image, pieces[4:])
    total = total + jnp.dot(scaled_far[...], image[...], preferred_element_type=jnp.float32)
    row = 0
    for dst in (own, pair, opposite, last):
        dst[...] = total[row : row + dst.shape[0]].astype(dst.dtype)
        row += dst.shape[0]


def image_kernel(scaled, sums, t0, t1, t2, back, own, low1, low2, low3, sums_out, text):
    stack(text, (t0, t1, t2))
    part = lax.dot_general(
        scaled[...], text[...], (((0,), (0,)), ((), ())), preferred_element_type=jnp.float32
    )
    for n, dst in enumerate((own, low1, low2, low3)):
        at = slice(192 * n, 192 * (n + 1))
        dst[...] = (part[at] + back[at].astype(jnp.float32)).astype(dst.dtype)
    sums_out[...] = jnp.broadcast_to((sums[...] + alight(back, 768))[None], sums_out.shape)


def near_kernel(own, pair, back, hop, out_own, out_far, low):
    out_own[...] = own[...] + back[:48].astype(jnp.float32)
    out_far[...] = back[48:96].astype(jnp.float32)
    total = pair[...] + back[96:].astype(jnp.float32)
    low[:48] = (total[:48] + hop[...].astype(jnp.float32)).astype(low.dtype)
    low[48:] = total[48:].astype(low.dtype)


def add_kernel(own, r1, r2, r3, terms, out_own, low1, low2, low3, sums):
    total = own[...] + r1[...].astype(jnp.float32) + r2[...].astype(jnp.float32) + r3[...].astype(jnp.float32)
    out_own[...] = total[:48]
    value = jnp.sum(terms[...], axis=0)
    sums[...] = value
    for n, dst in enumerate((low1, low2, low3), 1):
        dst[:48, :] = total[48 * n : 48 * (n + 1)].astype(dst.dtype)
        ride(dst, 48, value[:1])


def far_kernel(own, far, back, after, out_own, low):
    out_own[...] = own[...] + back[:48].astype(jnp.float32)
    low[...] = (far[...] + back[48:].astype(jnp.float32)).astype(low.dtype)


def finish_kernel(scalars, image_raw, image_own, i1, i2, i3, text_raw, text_own, t1, sums,
                  image_out, text_out, loss, bias_grad, temp_grad):
    for raw, own, parts, out in (
        (image_raw, image_own, (i1, i2, i3), image_out), (text_raw, text_own, (t1,), text_out),
    ):
        rows = raw[...]
        width = rows.shape[-1]
        grad = own[...]
        for part in parts:
            grad = grad + part[:48].astype(jnp.float32)
        grad = grad * scalars[0]
        square = jnp.mean(rows * rows, axis=-1, keepdims=True) + 1e-06
        inner = jnp.sum(rows * grad, axis=-1, keepdims=True)
        out[...] = (grad - rows * (inner / (square * width))) / (jnp.sqrt(square) * math.sqrt(width))
    values = [sums[0:1]] + [alight(part, 48) for part in (i1, i2, i3)]
    total = (values[0] + values[3]) + (values[1] + values[2])
    lane = lax.broadcasted_iota(jnp.int32, total.shape, 1)
    for n, (out, factor) in enumerate(((loss, 1.0), (bias_grad, 1.0), (temp_grad, scalars[0]))):
        out[0] = jnp.sum(jnp.where(lane == n, total, 0.0)) * factor / (48 * 256)


def f32(*shape):
    return jax.ShapeDtypeStruct(shape, jnp.float32)


def b16(*shape):
    return jax.ShapeDtypeStruct(shape, jnp.bfloat16)


def local(kernel, out_shape, *args, after=(), scratch=(), grant=8):
    return pl.pallas_call(
        kernel,
        out_shape=out_shape,
        in_specs=[SMEM if a.shape == (2,) else VMEM for a in args] + [ANY] * len(after),
        out_specs=tuple(SMEM if o.shape == (1,) else VMEM for o in out_shape),
        scratch_shapes=list(scratch),
        compiler_params=pltpu.CompilerParams(vmem_limit_bytes=grant * 1024 * 1024),
    )(*args, *after)


def body(image_raw, text_raw, image_ids, text_ids, log_temp, bias):
    pairs, width = image_raw.shape
    x, y, c = lax.axis_index("x"), lax.axis_index("y"), lax.axis_index("core")
    z = lax.axis_index("zh") * 4 + lax.axis_index("zl")
    text_unit, text_kept = local(text_unit_kernel, (b16(pairs, width),) * 2, text_raw)
    image_unit, image_kept, pair, pair_kept = local(
        image_unit_kernel, (b16(pairs, width),) * 2 + (b16(2 * pairs, width),) * 2,
        image_raw, text_kept, send(text_unit, swap, "pair"),
    )

    parts = [send(image_unit, along_first(k), "first") for k in OFFSETS]
    pair_2 = send(pair, apart(2), "z2")
    (flag,) = local(flag_kernel, (f32(8, 128),), after=parts)
    flag = send(flag, swap, "flag")
    line, message, hop, kept = local(
        gather_kernel, (b16(4 * pairs, width),) * 2 + (b16(pairs, width), b16(3 * pairs, width)),
        image_kept, *parts, text_kept, pair_kept, pair_2, after=(flag,),
    )

    plane = [line] + [send(line, along_second(k), "second") for k in OFFSETS]
    text = (kept, send(hop, apart(2), "z4"), send(message, apart(1), "z1"))
    (line_kept,) = local(copy_kernel, (b16(4 * pairs, width),), line, after=(plane[1],))
    plane_far = [send(p, swap, "swap") for p in [line_kept] + plane[1:]]

    back = (0,) + OFFSETS
    cols_from = []
    for core in (c, 1 - c):
        for k in back:
            for j in back:
                sx = jnp.where(core == 0, x - j, x - k) % 4
                sy = jnp.where(core == 0, y - k, y - j) % 4
                cols_from.append(flat(sx, sy, z, core))
    step = jnp.where(c == 0, 1, -1)
    rows_from = [flat(x, y, z, c)]
    for k in (2, 4, 1, 3):
        rows_from += [flat(x, y, (z - k * step) % 8, core) for core in ((c,) if k == 4 else (c, 1 - c))]
    cols_id = image_ids.reshape(256, pairs)[jnp.stack(cols_from)].reshape(1, 32 * pairs)
    rows_id = text_ids.reshape(256, pairs)[jnp.stack(rows_from)].reshape(1, 8 * pairs)

    temp = jnp.exp(log_temp[0])
    scalars = jnp.stack([temp, bias[0]])
    copies = (pltpu.VMEM((384, width), jnp.bfloat16), pltpu.VMEM((768, width), jnp.bfloat16))
    scaled_own, sums = local(
        terms_kernel, (b16(384, 768), f32(3, 8, 768)),
        scalars, rows_id, cols_id[:, :768], jnp.zeros((3, 8, 768), jnp.float32), *text, *plane, scratch=copies, grant=16,
    )
    far, scaled_far, sums = local(
        terms_kernel, (b16(784, width), b16(384, 768), f32(8, 128)),
        scalars, rows_id, cols_id[:, 768:], sums, *text, *plane_far, scratch=copies, grant=16,
    )
    back = send(far, swap, "rswap")
    text_own, text_pair, hop, last = local(
        text_kernel, (f32(pairs, width), f32(2 * pairs, width), b16(pairs, width), b16(4 * pairs, width)),
        scaled_own, scaled_far, *plane, *plane_far, scratch=copies[1:], grant=16,
    )
    last = send(last, apart(-1), "rz1")
    hop = send(hop, apart(-2), "rz4")
    image_own, *lows, spread = local(
        image_kernel, (f32(192, width),) + (b16(192, width),) * 3 + (f32(32, 8, 128),),
        scaled_own, sums, *text, back, scratch=copies[:1], grant=16,
    )
    image_parts = [send(p, along_second(-k), "rsecond") for p, k in zip(lows, OFFSETS)]
    text_own, text_far, low = local(
        near_kernel, (f32(pairs, width), f32(pairs, width), b16(2 * pairs, width)),
        text_own, text_pair, last, hop,
    )
    back = send(low, apart(-2), "rz2")
    with jax.named_scope("terms"):
        spread = lax.all_to_all(spread, AXES, 0, 0, tiled=True, axis_index_groups=across())
    image_own, *lows, sums = local(
        add_kernel, (f32(pairs, width),) + (b16(pairs + 16, width),) * 3 + (f32(8, 128),),
        image_own, *image_parts, spread,
    )
    image_parts = [send(p, along_first(-k), "rfirst") for p, k in zip(lows, OFFSETS)]
    text_own, far_low = local(
        far_kernel, (f32(pairs, width), b16(pairs, width)), text_own, text_far, back, after=(image_own,),
    )
    image_grad, text_grad, loss, bias_grad, temp_grad = local(
        finish_kernel, (f32(pairs, width),) * 2 + (f32(1),) * 3,
        scalars, image_raw, image_own, *image_parts, text_raw, text_own, send(far_low, swap, "rpair"), sums,
    )
    return (loss, image_grad, text_grad, temp_grad, bias_grad)


def solution(mesh):
    fine = Mesh(mesh.devices.reshape(SIZES), AXES)
    rows = P(AXES, None)
    return jax.shard_map(
        body,
        mesh=fine,
        in_specs=(rows, rows, P(), P(), P(), P()),
        out_specs=(P(), rows, rows, P(), P()),
        check_vma=False,
    )
```

time: 103 us -> 91.6 us (0.89)
  the two profiles are of different devices: /device:TPU:6 before, /device:TPU:1 now
where the time goes in v4:
time: 91.6 us; the launch traced here: 91.2 us
  starting transfers between devices  41.5 us (45%)
  Pallas kernels  19.5 us (21%)
  waiting for transfers between devices  18.8 us (21%)
  local copies, waits for them, and re-layouts  8.95 us (10%)
  between operations  2.36 us (3%)
    ppermute x26, starting transfers between devices, send(): return lax.ppermute(value, AXES, pairs)  33.2 us
    pallas_call x13, Pallas kernels, local(): pl.pallas_call(kernel, out_shape=out_shape, in_specs=[SMEM if a.shape ==...  19.5 us
    ppermute x26, waiting for transfers between devices, send(): return lax.ppermute(value, AXES, pairs)  14.3 us
    all_to_all x1, starting transfers between devices, body(): lax.all_to_all(spread, AXES, 0, 0, tiled=True, axis_index_groups=across())  8.34 us
    unnamed x30, local copies, waits for them, and re-layouts  5.66 us
    all_to_all x1, waiting for transfers between devices, body(): lax.all_to_all(spread, AXES, 0, 0, tiled=True, axis_index_groups=across())  4.49 us
  transfers between devices with their start and end apart: 27, of which 9 were waited for; matrix products, arithmetic and copies ran while one was open for 4% of the time, Pallas kernels for 14%

profile of v4, /device:TPU:1, one launch (start us, length us, event | category | flops | bytes accessed | tf_op | source)
XLA Modules:
  0.0 91.2 jit_solution(13590621579555849673)
XLA Ops:
  0.6 0.9 %copy-done.2 = f32[48,1152]{1,0:T(8,128)S(1)} copy-done((f32[48,1152]{1,0:T(8,128)S(1)}, f32[48,1152]{1,0:T(8,128)}, u32[]{:S(2)}) %copy-start.2) | copy-done | bytes 221208
  1.7 3.3 %collective-permute-start = (bf16[48,1152]{1,0:T(8,128)(2,1)S(1)}, bf16[48,1152]{1,0:T(8,128)(2,1)S(1)}, u32[]{:S(2)}, u32[]{:S(2)}) collective-permute-start(bf16[48,1152]{1,0:T(8,128)(2,1)S(1)} %get-tuple-element.45), channel_id=1, source_target_pairs={{0,4},{1,5},{2,6},{3,7},{4,0},{5,1},{6,2},{7,3},{8,12},{9,13},{10,... | collective-permute-start | bytes 331784 | tf_op jit(solution)/shard_map/pair/ppermute | solution.py:32
  5.0 1.0 %collective-permute-done.text_far = bf16[48,1152]{1,0:T(8,128)(2,1)S(1)} collective-permute-done((bf16[48,1152]{1,0:T(8,128)(2,1)S(1)}, bf16[48,1152]{1,0:T(8,128)(2,1)S(1)}, u32[]{:S(2)}, u32[]{:S(2)}) %collective-permute-start) | collective-permute-done | bytes 110624 | tf_op jit(solution)/shard_map/pair/ppermute | solution.py:32
  6.0 0.9 %copy-done = f32[48,1152]{1,0:T(8,128)S(1)} copy-done((f32[48,1152]{1,0:T(8,128)S(1)}, f32[48,1152]{1,0:T(8,128)}, u32[]{:S(2)}) %copy-start) | copy-done | bytes 221208
  7.1 4.4 %collective-permute-start.4 = (bf16[96,1152]{1,0:T(8,128)(2,1)S(1)}, bf16[96,1152]{1,0:T(8,128)(2,1)S(1)}, u32[]{:S(2)}, u32[]{:S(2)}) collective-permute-start(bf16[96,1152]{1,0:T(8,128)(2,1)S(1)} %get-tuple-element.49), channel_id=1, source_target_pairs={{0,2},{1,3},{2,32},{3,33},{4,38},{5,39},{6,4},{7,5},{8,10},{9,11},... | collective-permute-start | bytes 663560 | tf_op jit(solution)/shard_map/z2/ppermute | solution.py:32
  11.4 2.9 %collective-permute-start.3 = (bf16[48,1152]{1,0:T(8,128)(2,1)S(1)}, bf16[48,1152]{1,0:T(8,128)(2,1)S(1)}, u32[]{:S(2)}, u32[]{:S(2)}) collective-permute-start(bf16[48,1152]{1,0:T(8,128)(2,1)S(1)} %get-tuple-element.47), channel_id=1, source_target_pairs={{0,16},{1,17},{2,18},{3,19},{4,132},{5,133},{6,134},{7,135},{8,24}... | collective-permute-start | bytes 331784 | tf_op jit(solution)/shard_map/first/ppermute | solution.py:32
  14.3 0.8 collective-permute-start.2
  15.1 0.7 collective-permute-start.1
  15.8 0.7 collective-permute-done.3.refs_2_.i3
  16.5 1.8 %collective-permute-done.2.refs_1_.i2 = bf16[48,1152]{1,0:T(8,128)(2,1)S(1)} collective-permute-done((bf16[48,1152]{1,0:T(8,128)(2,1)S(1)}, bf16[48,1152]{1,0:T(8,128)(2,1)S(1)}, u32[]{:S(2)}, u32[]{:S(2)}) %collective-permute-start.2) | collective-permute-done | bytes 110624 | tf_op jit(solution)/shard_map/first/ppermute | solution.py:32
  18.4 1.6 %collective-permute-done.1.refs_0_.i1 = bf16[48,1152]{1,0:T(8,128)(2,1)S(1)} collective-permute-done((bf16[48,1152]{1,0:T(8,128)(2,1)S(1)}, bf16[48,1152]{1,0:T(8,128)(2,1)S(1)}, u32[]{:S(2)}, u32[]{:S(2)}) %collective-permute-start.1) | collective-permute-done | bytes 110624 | tf_op jit(solution)/shard_map/first/ppermute | solution.py:32
  20.0 1.1 %collective-permute-done.5.after = f32[8,128]{1,0:T(8,128)S(1)} collective-permute-done((f32[8,128]{1,0:T(8,128)S(1)}, f32[8,128]{1,0:T(8,128)S(1)}, u32[]{:S(2)}, u32[]{:S(2)}) %collective-permute-start.5) | collective-permute-done | bytes 4128 | tf_op jit(solution)/shard_map/flag/ppermute | solution.py:32
  21.1 0.9 shard_map.104
  22.0 2.7 %collective-permute-start.10 = (bf16[192,1152]{1,0:T(8,128)(2,1)S(1)}, bf16[192,1152]{1,0:T(8,128)(2,1)S(1)}, u32[]{:S(2)}, u32[]{:S(2)}) collective-permute-start(bf16[192,1152]{1,0:T(8,128)(2,1)S(1)} %get-tuple-element.53.refs_3_.src.refs_0_), channel_id=1, source_target_pairs={{0,128},{1,129},{2,130},{3,131},{4,20},{5,21},{6,22},{7,23},{8,136... | collective-permute-start | bytes 1327112 | tf_op jit(solution)/shard_map/second/ppermute | solution.py:32
  24.7 0.9 collective-permute-start.9
  25.6 0.6 collective-permute-start.8
  27.8 1.2 %collective-permute-start.6 = (bf16[48,1152]{1,0:T(8,128)(2,1)S(1)}, bf16[48,1152]{1,0:T(8,128)(2,1)S(1)}, u32[]{:S(2)}, u32[]{:S(2)}) collective-permute-start(bf16[48,1152]{1,0:T(8,128)(2,1)S(1)} %get-tuple-element.51), channel_id=1, source_target_pairs={{0,2},{1,3},{2,32},{3,33},{4,38},{5,39},{6,4},{7,5},{8,10},{9,11},... | collective-permute-start | bytes 331784 | tf_op jit(solution)/shard_map/z4/ppermute | solution.py:32
  29.0 0.6 gather_fusion.1
  29.7 0.8 reshape.1562
  30.7 4.9 %collective-permute-done.8.refs_4_.after.refs_1_ = bf16[192,1152]{1,0:T(8,128)(2,1)S(1)} collective-permute-done((bf16[192,1152]{1,0:T(8,128)(2,1)S(1)}, bf16[192,1152]{1,0:T(8,128)(2,1)S(1)}, u32[]{:S(2)}, u32[]{:S(2)}) %collective-permute-start.8) | collective-permute-done | bytes 442400 | tf_op jit(solution)/shard_map/second/ppermute | solution.py:32
  35.7 0.8 shard_map.106
  36.5 1.0 %collective-permute-start.11 = (bf16[192,1152]{1,0:T(8,128)(2,1)}, bf16[192,1152]{1,0:T(8,128)(2,1)S(1)}, u32[]{:S(2)}, u32[]{:S(2)}) collective-permute-start(bf16[192,1152]{1,0:T(8,128)(2,1)} %shard_map.106), channel_id=1, source_target_pairs={{0,4},{1,5},{2,6},{3,7},{4,0},{5,1},{6,2},{7,3},{8,12},{9,13},{10,... | collective-permute-start | bytes 1327112 | tf_op jit(solution)/shard_map/swap/ppermute | solution.py:32
  37.5 0.5 collective-permute-start.14
  38.0 0.3 collective-permute-start.13
  38.3 1.5 %gather_fusion = s32[8,48]{1,0:T(8,128)S(1)} fusion(s32[256,48]{1,0:T(8,128)} %reshape.1562, s32[1024]{0:T(1024)S(1)} %pad_clamp_fusion.1), kind=kCustom, calls=%fused_computation | custom fusion | bytes 3104 | tf_op jit(solution)/shard_map/gather | solution.py:279
  39.9 2.8 %shard_map.105 = (bf16[384,768]{1,0:T(8,128)(2,1)S(1)}, f32[3,8,768]{2,1,0:T(8,128)S(1)}) custom-call(f32[2]{0:T(128)S(1)} %pad_maximum_fusion.scalars, s32[1,384]{1,0:T(1,128)S(1)} %reshape.1563.rows_id, s32[1,768]{1,0:T(1,128)S(1)} %get-tuple-element.84.cols_id, f32[3,8,768]{2,1,0:T(8,128)S(1)} %broadcast_in_dim.2.before, ...), custom_call_target="tpu_custom_call" | custom-call | tf_op jit(solution)/shard_map/pallas_call | solution.py:232
  42.8 4.3 %shard_map.107 = (bf16[784,1152]{1,0:T(8,128)(2,1)S(1)}, bf16[384,768]{1,0:T(8,128)(2,1)S(1)}, f32[8,128]{1,0:T(8,128)S(1)}) custom-call(f32[2]{0:T(128)S(1)} %pad_maximum_fusion.scalars, s32[1,384]{1,0:T(1,128)S(1)} %reshape.1563.rows_id, s32[1,768]{1,0:T(1,128)S(1)} %get-tuple-element.83.cols_id, f32[3,8,768]{2,1,0:T(8,128)S(1)} %get-tuple-element.55.before, ...), custom_call_target="tpu_custom_call" | custom-call | tf_op jit(solution)/shard_map/pallas_call | solution.py:232
  47.1 3.9 %collective-permute-start.15 = (bf16[784,1152]{1,0:T(8,128)(2,1)S(1)}, bf16[784,1152]{1,0:T(8,128)(2,1)S(1)}, u32[]{:S(2)}, u32[]{:S(2)}) collective-permute-start(bf16[784,1152]{1,0:T(8,128)(2,1)S(1)} %get-tuple-element.57), channel_id=1, source_target_pairs={{0,4},{1,5},{2,6},{3,7},{4,0},{5,1},{6,2},{7,3},{8,12},{9,13},{10,... | collective-permute-start | bytes 5419016 | tf_op jit(solution)/shard_map/rswap/ppermute | solution.py:32
  51.0 3.7 %shard_map.110 = (f32[48,1152]{1,0:T(8,128)S(1)}, f32[96,1152]{1,0:T(8,128)S(1)}, bf16[48,1152]{1,0:T(8,128)(2,1)}, bf16[192,1152]{1,0:T(8,128)(2,1)}) custom-call(bf16[384,768]{1,0:T(8,128)(2,1)S(1)} %get-tuple-element.54.scaled.scaled_own, bf16[384,768]{1,0:T(8,128)(2,1)S(1)} %get-tuple-element.67.scaled_far, ...), custom_call_target="tpu_custom_call" | custom-call | tf_op jit(solution)/shard_map/pallas_call | solution.py:232
  54.7 0.8 copy-done.4
  55.5 0.7 copy-done.10
  56.2 2.3 %shard_map.108 = (f32[192,1152]{1,0:T(8,128)S(1)}, bf16[192,1152]{1,0:T(8,128)(2,1)}, bf16[192,1152]{1,0:T(8,128)(2,1)}, bf16[192,1152]{1,0:T(8,128)(2,1)}, f32[32,8,128]{2,1,0:T(8,128)S(1)}) custom-call(bf16[384,768]{1,0:T(8,128)(2,1)S(1)} %get-tuple-element.54.scaled.scaled_own, f32[8,128]{1,0:T(8,128)S(1)} %get-tuple-element.56.sums, ...), custom_call_target="tpu_custom_call" | custom-call | tf_op jit(solution)/shard_map/pallas_call | solution.py:232
  58.5 1.5 %collective-permute-start.17 = (bf16[192,1152]{1,0:T(8,128)(2,1)}, bf16[192,1152]{1,0:T(8,128)(2,1)S(1)}, u32[]{:S(2)}, u32[]{:S(2)}) collective-permute-start(bf16[192,1152]{1,0:T(8,128)(2,1)} %get-tuple-element.60), channel_id=1, source_target_pairs={{0,64},{1,65},{2,66},{3,67},{4,12},{5,13},{6,14},{7,15},{8,72},{9,... | collective-permute-start | bytes 1327112 | tf_op jit(solution)/shard_map/rsecond/ppermute | solution.py:32
  60.0 0.7 collective-permute-start.23
  60.7 8.3 %all-to-all-start = ((f32[32,8,128]{2,1,0:T(8,128)}), f32[32,8,128]{2,1,0:T(8,128)S(1)}, u32[]{:S(2)}, u32[]{:S(2)}) async-start(f32[32,8,128]{2,1,0:T(8,128)} %copy-done.12), calls=%async_computation | async-start | bytes 262144 | tf_op jit(solution)/shard_map/terms/all_to_all | solution.py:310
  69.1 0.9 %copy-done.11 = f32[48,1152]{1,0:T(8,128)S(1)} copy-done((f32[48,1152]{1,0:T(8,128)S(1)}, f32[48,1152]{1,0:T(8,128)}, u32[]{:S(2)}) %copy-start.11) | copy-done | bytes 221208
  70.0 1.8 %shard_map.111 = (f32[48,1152]{1,0:T(8,128)S(1)}, f32[48,1152]{1,0:T(8,128)S(1)}, bf16[96,1152]{1,0:T(8,128)(2,1)}) custom-call(f32[48,1152]{1,0:T(8,128)S(1)} %copy-done.11, f32[96,1152]{1,0:T(8,128)S(1)} %copy-done.5, bf16[192,1152]{1,0:T(8,128)(2,1)} %collective-permute-done.22.back, bf16[48,1152]{1,0:T(8,128)(2,1)S(1)} %collective-permute-done.23.hop), custom_call_target="tpu_custom_call" | custom-call | tf_op jit(solution)/shard_map/pallas_call | solution.py:232
  71.8 0.7 copy-done.6
  72.5 0.7 copy-done.8
  73.2 2.4 %collective-permute-start.24 = (bf16[96,1152]{1,0:T(8,128)(2,1)}, bf16[96,1152]{1,0:T(8,128)(2,1)}, u32[]{:S(2)}, u32[]{:S(2)}) collective-permute-start(bf16[96,1152]{1,0:T(8,128)(2,1)} %get-tuple-element.74), channel_id=1, source_target_pairs={{0,34},{1,35},{2,0},{3,1},{4,6},{5,7},{6,36},{7,37},{8,42},{9,43},... | collective-permute-start | bytes 663560 | tf_op jit(solution)/shard_map/rz2/ppermute | solution.py:32
  75.6 4.5 %all-to-all-done.terms = f32[32,8,128]{2,1,0:T(8,128)S(1)} async-done(((f32[32,8,128]{2,1,0:T(8,128)}), f32[32,8,128]{2,1,0:T(8,128)S(1)}, u32[]{:S(2)}, u32[]{:S(2)}) %all-to-all-start) | async-done | bytes 131104 | tf_op jit(solution)/shard_map/terms/all_to_all | solution.py:310
  80.3 2.1 %collective-permute-start.19 = (bf16[64,1152]{1,0:T(8,128)(2,1)S(1)}, bf16[64,1152]{1,0:T(8,128)(2,1)S(1)}, u32[]{:S(2)}, u32[]{:S(2)}) collective-permute-start(bf16[64,1152]{1,0:T(8,128)(2,1)S(1)} %get-tuple-element.64), channel_id=1, source_target_pairs={{0,24},{1,25},{2,26},{3,27},{4,196},{5,197},{6,198},{7,199},{8,0},... | collective-permute-start | bytes 442376 | tf_op jit(solution)/shard_map/rfirst/ppermute | solution.py:32
  82.4 1.3 %collective-permute-start.21 = (bf16[64,1152]{1,0:T(8,128)(2,1)S(1)}, bf16[64,1152]{1,0:T(8,128)(2,1)S(1)}, u32[]{:S(2)}, u32[]{:S(2)}) collective-permute-start(bf16[64,1152]{1,0:T(8,128)(2,1)S(1)} %get-tuple-element.66), channel_id=1, source_target_pairs={{0,16},{1,17},{2,18},{3,19},{4,132},{5,133},{6,134},{7,135},{8,24}... | collective-permute-start | bytes 442376 | tf_op jit(solution)/shard_map/rfirst/ppermute | solution.py:32
  83.7 1.0 %shard_map.112 = (f32[48,1152]{1,0:T(8,128)S(1)}, bf16[48,1152]{1,0:T(8,128)(2,1)S(1)}) custom-call(f32[48,1152]{1,0:T(8,128)S(1)} %copy-done.7, f32[48,1152]{1,0:T(8,128)S(1)} %copy-done.9, bf16[96,1152]{1,0:T(8,128)(2,1)} %collective-permute-done.24.back, f32[48,1152]{1,0:T(8,128)S(1)} %get-tuple-element.63.after.image_own), custom_call_target="tpu_custom_call" | custom-call | tf_op jit(solution)/shard_map/pallas_call | solution.py:232
  84.6 1.7 %collective-permute-start.25 = (bf16[48,1152]{1,0:T(8,128)(2,1)S(1)}, bf16[48,1152]{1,0:T(8,128)(2,1)S(1)}, u32[]{:S(2)}, u32[]{:S(2)}) collective-permute-start(bf16[48,1152]{1,0:T(8,128)(2,1)S(1)} %get-tuple-element.76), channel_id=1, source_target_pairs={{0,4},{1,5},{2,6},{3,7},{4,0},{5,1},{6,2},{7,3},{8,12},{9,13},{10,... | collective-permute-start | bytes 331784 | tf_op jit(solution)/shard_map/rpair/ppermute | solution.py:32
  86.3 1.0 %collective-permute-done.25.t1 = bf16[48,1152]{1,0:T(8,128)(2,1)S(1)} collective-permute-done((bf16[48,1152]{1,0:T(8,128)(2,1)S(1)}, bf16[48,1152]{1,0:T(8,128)(2,1)S(1)}, u32[]{:S(2)}, u32[]{:S(2)}) %collective-permute-start.25) | collective-permute-done | bytes 110624 | tf_op jit(solution)/shard_map/rpair/ppermute | solution.py:32
  87.3 2.2 %collective-permute-done.20.i2 = bf16[64,1152]{1,0:T(8,128)(2,1)S(1)} collective-permute-done((bf16[64,1152]{1,0:T(8,128)(2,1)S(1)}, bf16[64,1152]{1,0:T(8,128)(2,1)S(1)}, u32[]{:S(2)}, u32[]{:S(2)}) %collective-permute-start.20) | collective-permute-done | bytes 147488 | tf_op jit(solution)/shard_map/rfirst/ppermute | solution.py:32
  89.5 1.5 %shard_map.113 = (f32[48,1152]{1,0:T(8,128)}, f32[48,1152]{1,0:T(8,128)}, f32[1]{0:T(128)}, f32[1]{0:T(128)}, f32[1]{0:T(128)}) custom-call(f32[2]{0:T(128)S(1)} %pad_maximum_fusion.scalars, f32[48,1152]{1,0:T(8,128)S(1)} %copy-done.1, f32[48,1152]{1,0:T(8,128)S(1)} %get-tuple-element.63.after.image_own, bf16[64,1152]{1,0:T(8,128)(2,1)S(1)} %collective-permute-done.19.i1, ...), custom_call_target="tpu_custom_call" | custom-call | tf_op jit(solution)/shard_map/pallas_call | solution.py:232
  (64 shorter events, 1.5 us)
Async XLA Ops:
  0.6 0.9 %copy-start.2 = (f32[48,1152]{1,0:T(8,128)S(1)}, f32[48,1152]{1,0:T(8,128)}, u32[]{:S(2)}) copy-start(f32[48,1152]{1,0:T(8,128)} %text_raw.1) | copy-start | bytes 663556
  1.7 4.3 %collective-permute-start = (bf16[48,1152]{1,0:T(8,128)(2,1)S(1)}, bf16[48,1152]{1,0:T(8,128)(2,1)S(1)}, u32[]{:S(2)}, u32[]{:S(2)}) collective-permute-start(bf16[48,1152]{1,0:T(8,128)(2,1)S(1)} %get-tuple-element.45), channel_id=1, source_target_pairs={{0,4},{1,5},{2,6},{3,7},{4,0},{5,1},{6,2},{7,3},{8,12},{9,13},{10,... | collective-permute-start | bytes 331784 | tf_op jit(solution)/shard_map/pair/ppermute | solution.py:32
  6.0 0.9 %copy-start = (f32[48,1152]{1,0:T(8,128)S(1)}, f32[48,1152]{1,0:T(8,128)}, u32[]{:S(2)}) copy-start(f32[48,1152]{1,0:T(8,128)} %image_raw.1) | copy-start | bytes 663556
  7.1 20.5 %copy-start.13 = (s32[12288]{0:T(1024)S(1)}, s32[12288]{0:T(1024)}, u32[]{:S(2)}) copy-start(s32[12288]{0:T(1024)} %param.8) | copy-start | bytes 147460
  7.1 14.0 %collective-permute-start.4 = (bf16[96,1152]{1,0:T(8,128)(2,1)S(1)}, bf16[96,1152]{1,0:T(8,128)(2,1)S(1)}, u32[]{:S(2)}, u32[]{:S(2)}) collective-permute-start(bf16[96,1152]{1,0:T(8,128)(2,1)S(1)} %get-tuple-element.49), channel_id=1, source_target_pairs={{0,2},{1,3},{2,32},{3,33},{4,38},{5,39},{6,4},{7,5},{8,10},{9,11},... | collective-permute-start | bytes 663560 | tf_op jit(solution)/shard_map/z2/ppermute | solution.py:32
  11.4 5.1 %collective-permute-start.3 = (bf16[48,1152]{1,0:T(8,128)(2,1)S(1)}, bf16[48,1152]{1,0:T(8,128)(2,1)S(1)}, u32[]{:S(2)}, u32[]{:S(2)}) collective-permute-start(bf16[48,1152]{1,0:T(8,128)(2,1)S(1)} %get-tuple-element.47), channel_id=1, source_target_pairs={{0,16},{1,17},{2,18},{3,19},{4,132},{5,133},{6,134},{7,135},{8,24}... | collective-permute-start | bytes 331784 | tf_op jit(solution)/shard_map/first/ppermute | solution.py:32
  14.3 4.0 %collective-permute-start.2 = (bf16[48,1152]{1,0:T(8,128)(2,1)S(1)}, bf16[48,1152]{1,0:T(8,128)(2,1)S(1)}, u32[]{:S(2)}, u32[]{:S(2)}) collective-permute-start(bf16[48,1152]{1,0:T(8,128)(2,1)S(1)} %get-tuple-element.47), channel_id=1, source_target_pairs={{0,24},{1,25},{2,26},{3,27},{4,196},{5,197},{6,198},{7,199},{8,0},... | collective-permute-start | bytes 331784 | tf_op jit(solution)/shard_map/first/ppermute | solution.py:32
  15.1 4.8 %collective-permute-start.1 = (bf16[48,1152]{1,0:T(8,128)(2,1)S(1)}, bf16[48,1152]{1,0:T(8,128)(2,1)S(1)}, u32[]{:S(2)}, u32[]{:S(2)}) collective-permute-start(bf16[48,1152]{1,0:T(8,128)(2,1)S(1)} %get-tuple-element.47), channel_id=1, source_target_pairs={{0,8},{1,9},{2,10},{3,11},{4,68},{5,69},{6,70},{7,71},{8,16},{9,17... | collective-permute-start | bytes 331784 | tf_op jit(solution)/shard_map/first/ppermute | solution.py:32
  15.8 13.9 %copy-start.14 = (s32[12288]{0:T(1024)S(1)}, s32[12288]{0:T(1024)}, u32[]{:S(2)}) copy-start(s32[12288]{0:T(1024)} %param.9) | copy-start | bytes 147460
  19.9 1.2 %collective-permute-start.5 = (f32[8,128]{1,0:T(8,128)S(1)}, f32[8,128]{1,0:T(8,128)S(1)}, u32[]{:S(2)}, u32[]{:S(2)}) collective-permute-start(f32[8,128]{1,0:T(8,128)S(1)} %shard_map.103), channel_id=1, source_target_pairs={{0,4},{1,5},{2,6},{3,7},{4,0},{5,1},{6,2},{7,3},{8,12},{9,13},{10,... | collective-permute-start | bytes 12296 | tf_op jit(solution)/shard_map/flag/ppermute | solution.py:32
  22.0 15.5 %collective-permute-start.10 = (bf16[192,1152]{1,0:T(8,128)(2,1)S(1)}, bf16[192,1152]{1,0:T(8,128)(2,1)S(1)}, u32[]{:S(2)}, u32[]{:S(2)}) collective-permute-start(bf16[192,1152]{1,0:T(8,128)(2,1)S(1)} %get-tuple-element.53.refs_3_.src.refs_0_), channel_id=1, source_target_pairs={{0,128},{1,129},{2,130},{3,131},{4,20},{5,21},{6,22},{7,23},{8,136... | collective-permute-start | bytes 1327112 | tf_op jit(solution)/shard_map/second/ppermute | solution.py:32
  24.7 13.3 %collective-permute-start.9 = (bf16[192,1152]{1,0:T(8,128)(2,1)S(1)}, bf16[192,1152]{1,0:T(8,128)(2,1)S(1)}, u32[]{:S(2)}, u32[]{:S(2)}) collective-permute-start(bf16[192,1152]{1,0:T(8,128)(2,1)S(1)} %get-tuple-element.53.refs_3_.src.refs_0_), channel_id=1, source_target_pairs={{0,192},{1,193},{2,194},{3,195},{4,28},{5,29},{6,30},{7,31},{8,200... | collective-permute-start | bytes 1327112 | tf_op jit(solution)/shard_map/second/ppermute | solution.py:32
  25.6 10.1 %collective-permute-start.8 = (bf16[192,1152]{1,0:T(8,128)(2,1)S(1)}, bf16[192,1152]{1,0:T(8,128)(2,1)S(1)}, u32[]{:S(2)}, u32[]{:S(2)}) collective-permute-start(bf16[192,1152]{1,0:T(8,128)(2,1)S(1)} %get-tuple-element.53.refs_3_.src.refs_0_), channel_id=1, source_target_pairs={{0,64},{1,65},{2,66},{3,67},{4,12},{5,13},{6,14},{7,15},{8,72},{9,... | collective-permute-start | bytes 1327112 | tf_op jit(solution)/shard_map/second/ppermute | solution.py:32
  27.8 9.7 %collective-permute-start.6 = (bf16[48,1152]{1,0:T(8,128)(2,1)S(1)}, bf16[48,1152]{1,0:T(8,128)(2,1)S(1)}, u32[]{:S(2)}, u32[]{:S(2)}) collective-permute-start(bf16[48,1152]{1,0:T(8,128)(2,1)S(1)} %get-tuple-element.51), channel_id=1, source_target_pairs={{0,2},{1,3},{2,32},{3,33},{4,38},{5,39},{6,4},{7,5},{8,10},{9,11},... | collective-permute-start | bytes 331784 | tf_op jit(solution)/shard_map/z4/ppermute | solution.py:32
  30.5 9.4 %collective-permute-start.7 = (bf16[192,1152]{1,0:T(8,128)(2,1)}, bf16[192,1152]{1,0:T(8,128)(2,1)S(1)}, u32[]{:S(2)}, u32[]{:S(2)}) collective-permute-start(bf16[192,1152]{1,0:T(8,128)(2,1)} %get-tuple-element.52), channel_id=1, source_target_pairs={{0,1},{1,2},{2,3},{3,32},{4,39},{5,4},{6,5},{7,6},{8,9},{9,10},{10... | collective-permute-start | bytes 1327112 | tf_op jit(solution)/shard_map/z1/ppermute | solution.py:32
  36.5 6.3 %collective-permute-start.11 = (bf16[192,1152]{1,0:T(8,128)(2,1)}, bf16[192,1152]{1,0:T(8,128)(2,1)S(1)}, u32[]{:S(2)}, u32[]{:S(2)}) collective-permute-start(bf16[192,1152]{1,0:T(8,128)(2,1)} %shard_map.106), channel_id=1, source_target_pairs={{0,4},{1,5},{2,6},{3,7},{4,0},{5,1},{6,2},{7,3},{8,12},{9,13},{10,... | collective-permute-start | bytes 1327112 | tf_op jit(solution)/shard_map/swap/ppermute | solution.py:32
  37.5 5.3 %collective-permute-start.12 = (bf16[192,1152]{1,0:T(8,128)(2,1)S(1)}, bf16[192,1152]{1,0:T(8,128)(2,1)S(1)}, u32[]{:S(2)}, u32[]{:S(2)}) collective-permute-start(bf16[192,1152]{1,0:T(8,128)(2,1)S(1)} %collective-permute-done.8.refs_4_.after.refs_1_), channel_id=1, source_target_pairs={{0,4},{1,5},{2,6},{3,7},{4,0},{5,1},{6,2},{7,3},{8,12},{9,13},{10,... | collective-permute-start | bytes 1327112 | tf_op jit(solution)/shard_map/swap/ppermute | solution.py:32
  37.5 5.3 %collective-permute-start.14 = (bf16[192,1152]{1,0:T(8,128)(2,1)S(1)}, bf16[192,1152]{1,0:T(8,128)(2,1)}, u32[]{:S(2)}, u32[]{:S(2)}) collective-permute-start(bf16[192,1152]{1,0:T(8,128)(2,1)S(1)} %collective-permute-done.10.refs_6_.refs_3_), channel_id=1, source_target_pairs={{0,4},{1,5},{2,6},{3,7},{4,0},{5,1},{6,2},{7,3},{8,12},{9,13},{10,... | collective-permute-start | bytes 1327112 | tf_op jit(solution)/shard_map/swap/ppermute | solution.py:32
  38.0 4.8 %collective-permute-start.13 = (bf16[192,1152]{1,0:T(8,128)(2,1)S(1)}, bf16[192,1152]{1,0:T(8,128)(2,1)}, u32[]{:S(2)}, u32[]{:S(2)}) collective-permute-start(bf16[192,1152]{1,0:T(8,128)(2,1)S(1)} %collective-permute-done.9.refs_5_.refs_2_), channel_id=1, source_target_pairs={{0,4},{1,5},{2,6},{3,7},{4,0},{5,1},{6,2},{7,3},{8,12},{9,13},{10,... | collective-permute-start | bytes 1327112 | tf_op jit(solution)/shard_map/swap/ppermute | solution.py:32
  47.1 9.1 %collective-permute-start.15 = (bf16[784,1152]{1,0:T(8,128)(2,1)S(1)}, bf16[784,1152]{1,0:T(8,128)(2,1)S(1)}, u32[]{:S(2)}, u32[]{:S(2)}) collective-permute-start(bf16[784,1152]{1,0:T(8,128)(2,1)S(1)} %get-tuple-element.57), channel_id=1, source_target_pairs={{0,4},{1,5},{2,6},{3,7},{4,0},{5,1},{6,2},{7,3},{8,12},{9,13},{10,... | collective-permute-start | bytes 5419016 | tf_op jit(solution)/shard_map/rswap/ppermute | solution.py:32
  54.7 0.8 copy-start.4
  55.5 0.7 copy-start.10
  56.2 12.9 %copy-start.5 = (f32[96,1152]{1,0:T(8,128)S(1)}, f32[96,1152]{1,0:T(8,128)}, u32[]{:S(2)}) copy-start(f32[96,1152]{1,0:T(8,128)} %copy-done.4) | copy-start | bytes 1327108
  56.2 12.9 %collective-permute-start.22 = (bf16[192,1152]{1,0:T(8,128)(2,1)}, bf16[192,1152]{1,0:T(8,128)(2,1)}, u32[]{:S(2)}, u32[]{:S(2)}) collective-permute-start(bf16[192,1152]{1,0:T(8,128)(2,1)} %get-tuple-element.70), channel_id=1, source_target_pairs={{0,35},{1,0},{2,1},{3,2},{4,5},{5,6},{6,7},{7,36},{8,43},{9,8},{10... | collective-permute-start | bytes 1327112 | tf_op jit(solution)/shard_map/rz1/ppermute | solution.py:32
  58.5 2.2 %copy-start.12 = (f32[32,8,128]{2,1,0:T(8,128)}, f32[32,8,128]{2,1,0:T(8,128)S(1)}, u32[]{:S(2)}) copy-start(f32[32,8,128]{2,1,0:T(8,128)S(1)} %get-tuple-element.62) | copy-start | bytes 393220
  58.5 21.6 %collective-permute-start.16 = (bf16[192,1152]{1,0:T(8,128)(2,1)}, bf16[192,1152]{1,0:T(8,128)(2,1)S(1)}, u32[]{:S(2)}, u32[]{:S(2)}) collective-permute-start(bf16[192,1152]{1,0:T(8,128)(2,1)} %get-tuple-element.59), channel_id=1, source_target_pairs={{0,192},{1,193},{2,194},{3,195},{4,28},{5,29},{6,30},{7,31},{8,200... | collective-permute-start | bytes 1327112 | tf_op jit(solution)/shard_map/rsecond/ppermute | solution.py:32
  58.5 21.6 %collective-permute-start.17 = (bf16[192,1152]{1,0:T(8,128)(2,1)}, bf16[192,1152]{1,0:T(8,128)(2,1)S(1)}, u32[]{:S(2)}, u32[]{:S(2)}) collective-permute-start(bf16[192,1152]{1,0:T(8,128)(2,1)} %get-tuple-element.60), channel_id=1, source_target_pairs={{0,64},{1,65},{2,66},{3,67},{4,12},{5,13},{6,14},{7,15},{8,72},{9,... | collective-permute-start | bytes 1327112 | tf_op jit(solution)/shard_map/rsecond/ppermute | solution.py:32
  59.9 20.2 %collective-permute-start.18 = (bf16[192,1152]{1,0:T(8,128)(2,1)}, bf16[192,1152]{1,0:T(8,128)(2,1)S(1)}, u32[]{:S(2)}, u32[]{:S(2)}) collective-permute-start(bf16[192,1152]{1,0:T(8,128)(2,1)} %get-tuple-element.61), channel_id=1, source_target_pairs={{0,128},{1,129},{2,130},{3,131},{4,20},{5,21},{6,22},{7,23},{8,136... | collective-permute-start | bytes 1327112 | tf_op jit(solution)/shard_map/rsecond/ppermute | solution.py:32
  60.0 9.1 %collective-permute-start.23 = (bf16[48,1152]{1,0:T(8,128)(2,1)}, bf16[48,1152]{1,0:T(8,128)(2,1)S(1)}, u32[]{:S(2)}, u32[]{:S(2)}) collective-permute-start(bf16[48,1152]{1,0:T(8,128)(2,1)} %get-tuple-element.71), channel_id=1, source_target_pairs={{0,34},{1,35},{2,0},{3,1},{4,6},{5,7},{6,36},{7,37},{8,42},{9,43},... | collective-permute-start | bytes 331784 | tf_op jit(solution)/shard_map/rz4/ppermute | solution.py:32
  60.7 19.4 %all-to-all-start = ((f32[32,8,128]{2,1,0:T(8,128)}), f32[32,8,128]{2,1,0:T(8,128)S(1)}, u32[]{:S(2)}, u32[]{:S(2)}) async-start(f32[32,8,128]{2,1,0:T(8,128)} %copy-done.12), calls=%async_computation | async-start | bytes 262144 | tf_op jit(solution)/shard_map/terms/all_to_all | solution.py:310
  69.1 0.9 %copy-start.11 = (f32[48,1152]{1,0:T(8,128)S(1)}, f32[48,1152]{1,0:T(8,128)}, u32[]{:S(2)}) copy-start(f32[48,1152]{1,0:T(8,128)} %copy-done.10) | copy-start | bytes 663556
  71.8 0.7 copy-start.6
  72.5 0.7 copy-start.8
  73.1 16.3 %copy-start.1 = (f32[48,1152]{1,0:T(8,128)S(1)}, f32[48,1152]{1,0:T(8,128)}, u32[]{:S(2)}) copy-start(f32[48,1152]{1,0:T(8,128)} %image_raw.1) | copy-start | bytes 663556
  73.1 16.3 %copy-start.3 = (f32[48,1152]{1,0:T(8,128)S(1)}, f32[48,1152]{1,0:T(8,128)}, u32[]{:S(2)}) copy-start(f32[48,1152]{1,0:T(8,128)} %text_raw.1) | copy-start | bytes 663556
  73.1 10.5 %copy-start.7 = (f32[48,1152]{1,0:T(8,128)S(1)}, f32[48,1152]{1,0:T(8,128)}, u32[]{:S(2)}) copy-start(f32[48,1152]{1,0:T(8,128)} %copy-done.6) | copy-start | bytes 663556
  73.1 10.5 %copy-start.9 = (f32[48,1152]{1,0:T(8,128)S(1)}, f32[48,1152]{1,0:T(8,128)}, u32[]{:S(2)}) copy-start(f32[48,1152]{1,0:T(8,128)} %copy-done.8) | copy-start | bytes 663556
  73.2 10.5 %collective-permute-start.24 = (bf16[96,1152]{1,0:T(8,128)(2,1)}, bf16[96,1152]{1,0:T(8,128)(2,1)}, u32[]{:S(2)}, u32[]{:S(2)}) collective-permute-start(bf16[96,1152]{1,0:T(8,128)(2,1)} %get-tuple-element.74), channel_id=1, source_target_pairs={{0,34},{1,35},{2,0},{3,1},{4,6},{5,7},{6,36},{7,37},{8,42},{9,43},... | collective-permute-start | bytes 663560 | tf_op jit(solution)/shard_map/rz2/ppermute | solution.py:32
  80.3 7.0 %collective-permute-start.19 = (bf16[64,1152]{1,0:T(8,128)(2,1)S(1)}, bf16[64,1152]{1,0:T(8,128)(2,1)S(1)}, u32[]{:S(2)}, u32[]{:S(2)}) collective-permute-start(bf16[64,1152]{1,0:T(8,128)(2,1)S(1)} %get-tuple-element.64), channel_id=1, source_target_pairs={{0,24},{1,25},{2,26},{3,27},{4,196},{5,197},{6,198},{7,199},{8,0},... | collective-permute-start | bytes 442376 | tf_op jit(solution)/shard_map/rfirst/ppermute | solution.py:32
  82.4 7.1 %collective-permute-start.20 = (bf16[64,1152]{1,0:T(8,128)(2,1)S(1)}, bf16[64,1152]{1,0:T(8,128)(2,1)S(1)}, u32[]{:S(2)}, u32[]{:S(2)}) collective-permute-start(bf16[64,1152]{1,0:T(8,128)(2,1)S(1)} %get-tuple-element.65), channel_id=1, source_target_pairs={{0,8},{1,9},{2,10},{3,11},{4,68},{5,69},{6,70},{7,71},{8,16},{9,17... | collective-permute-start | bytes 442376 | tf_op jit(solution)/shard_map/rfirst/ppermute | solution.py:32
  82.4 7.1 %collective-permute-start.21 = (bf16[64,1152]{1,0:T(8,128)(2,1)S(1)}, bf16[64,1152]{1,0:T(8,128)(2,1)S(1)}, u32[]{:S(2)}, u32[]{:S(2)}) collective-permute-start(bf16[64,1152]{1,0:T(8,128)(2,1)S(1)} %get-tuple-element.66), channel_id=1, source_target_pairs={{0,16},{1,17},{2,18},{3,19},{4,132},{5,133},{6,134},{7,135},{8,24}... | collective-permute-start | bytes 442376 | tf_op jit(solution)/shard_map/rfirst/ppermute | solution.py:32
  84.6 2.6 %collective-permute-start.25 = (bf16[48,1152]{1,0:T(8,128)(2,1)S(1)}, bf16[48,1152]{1,0:T(8,128)(2,1)S(1)}, u32[]{:S(2)}, u32[]{:S(2)}) collective-permute-start(bf16[48,1152]{1,0:T(8,128)(2,1)S(1)} %get-tuple-element.76), channel_id=1, source_target_pairs={{0,4},{1,5},{2,6},{3,7},{4,0},{5,1},{6,2},{7,3},{8,12},{9,13},{10,... | collective-permute-start | bytes 331784 | tf_op jit(solution)/shard_map/rpair/ppermute | solution.py:32

commit v5 on v4

--- a/solution.py
+++ b/solution.py
@@ -69,11 +69,14 @@
     kept[...] = out[...]
 
 
-def image_unit_kernel(raw, text, text_far, out, kept, pair, pair_kept):
+def image_unit_kernel(raw, after, far_after, out, kept):
     out[...] = unit(raw[...])
     kept[...] = out[...]
+
+
+def pair_kernel(text, text_far, after, pair, kept):
     stack(pair, (text, text_far))
-    stack(pair_kept, (text, text_far))
+    stack(kept, (text, text_far))
 
 
 def stack(out, sources):
@@ -83,7 +86,7 @@
         row += src.shape[0]
 
 
-def gather_kernel(i0, i1, i2, i3, own, pair, pair_2, after, line, message, hop, kept):
+def gather_kernel(i0, i1, i2, i3, own, pair, pair_2, after, cols_after, rows_after, line, message, hop, kept):
     stack(line, (i0, i1, i2, i3))
     stack(message, (pair, pair_2))
     hop[...] = pair_2[:48]
@@ -244,25 +247,14 @@
     x, y, c = lax.axis_index("x"), lax.axis_index("y"), lax.axis_index("core")
     z = lax.axis_index("zh") * 4 + lax.axis_index("zl")
     text_unit, text_kept = local(text_unit_kernel, (b16(pairs, width),) * 2, text_raw)
-    image_unit, image_kept, pair, pair_kept = local(
-        image_unit_kernel, (b16(pairs, width),) * 2 + (b16(2 * pairs, width),) * 2,
-        image_raw, text_kept, send(text_unit, swap, "pair"),
+    text_far = send(text_unit, swap, "pair")
+    image_unit, image_kept = local(image_unit_kernel, (b16(pairs, width),) * 2, image_raw, after=(text_kept, text_far))
+    pair, pair_kept = local(
+        pair_kernel, (b16(2 * pairs, width),) * 2, text_kept, text_far, after=(image_kept,),
     )
 
     parts = [send(image_unit, along_first(k), "first") for k in OFFSETS]
     pair_2 = send(pair, apart(2), "z2")
-    (flag,) = local(flag_kernel, (f32(8, 128),), after=parts)
-    flag = send(flag, swap, "flag")
-    line, message, hop, kept = local(
-        gather_kernel, (b16(4 * pairs, width),) * 2 + (b16(pairs, width), b16(3 * pairs, width)),
-        image_kept, *parts, text_kept, pair_kept, pair_2, after=(flag,),
-    )
-
-    plane = [line] + [send(line, along_second(k), "second") for k in OFFSETS]
-    text = (kept, send(hop, apart(2), "z4"), send(message, apart(1), "z1"))
-    (line_kept,) = local(copy_kernel, (b16(4 * pairs, width),), line, after=(plane[1],))
-    plane_far = [send(p, swap, "swap") for p in [line_kept] + plane[1:]]
-
     back = (0,) + OFFSETS
     cols_from = []
     for core in (c, 1 - c):
@@ -278,6 +270,18 @@
     cols_id = image_ids.reshape(256, pairs)[jnp.stack(cols_from)].reshape(1, 32 * pairs)
     rows_id = text_ids.reshape(256, pairs)[jnp.stack(rows_from)].reshape(1, 8 * pairs)
 
+    (flag,) = local(flag_kernel, (f32(8, 128),), after=parts)
+    flag = send(flag, swap, "flag")
+    line, message, hop, kept = local(
+        gather_kernel, (b16(4 * pairs, width),) * 2 + (b16(pairs, width), b16(3 * pairs, width)),
+        image_kept, *parts, text_kept, pair_kept, pair_2, after=(flag, cols_id, rows_id),
+    )
+
+    plane = [line] + [send(line, along_second(k), "second") for k in OFFSETS]
+    text = (kept, send(hop, apart(2), "z4"), send(message, apart(1), "z1"))
+    (line_kept,) = local(copy_kernel, (b16(4 * pairs, width),), line, after=(plane[1],))
+    plane_far = [send(p, swap, "swap") for p in [line_kept] + plane[1:]]
+
     temp = jnp.exp(log_temp[0])
     scalars = jnp.stack([temp, bias[0]])
     copies = (pltpu.VMEM((384, width), jnp.bfloat16), pltpu.VMEM((768, width), jnp.bfloat16))

time: 91.6 us -> 87.2 us (0.952)
  the two profiles are of different devices: /device:TPU:1 before, /device:TPU:6 now
where the time goes in v5:
time: 87.2 us; the launch traced here: 86.9 us
  starting transfers between devices  42 us (48%)
  waiting for transfers between devices  19.5 us (22%)
  Pallas kernels  15.3 us (18%)
  local copies, waits for them, and re-layouts  5.89 us (7%)
  between operations  4.11 us (5%)
    ppermute x26, starting transfers between devices, send(): return lax.ppermute(value, AXES, pairs)  36.9 us
    ppermute x26, waiting for transfers between devices, send(): return lax.ppermute(value, AXES, pairs)  18 us
    pallas_call x14, Pallas kernels, local(): pl.pallas_call(kernel, out_shape=out_shape, in_specs=[SMEM if a.shape ==...  15.3 us
    all_to_all x1, starting transfers between devices, body(): lax.all_to_all(spread, AXES, 0, 0, tiled=True, axis_index_groups=across())  5.12 us
    unnamed x22, local copies, waits for them, and re-layouts  4.15 us
  transfers between devices with their start and end apart: 27, of which 10 were waited for; matrix products, arithmetic and copies ran while one was open for 2% of the time, Pallas kernels for 11%

profile of v5, /device:TPU:6, one launch (start us, length us, event | category | flops | bytes accessed | tf_op | source)
XLA Modules:
  0.0 86.9 jit_solution(1029079597352574132)
XLA Ops:
  0.7 1.0 %copy-done.1 = f32[48,1152]{1,0:T(8,128)S(1)} copy-done((f32[48,1152]{1,0:T(8,128)S(1)}, f32[48,1152]{1,0:T(8,128)}, u32[]{:S(2)}) %copy-start.1) | copy-done | bytes 221208
  1.6 0.1 shard_map.101
  3.6 0.1 stack.139
  3.7 0.1 stack.172
  3.8 0.1 shard_map.102
  4.0 1.5 %collective-permute-start.3 = (bf16[48,1152]{1,0:T(8,128)(2,1)S(1)}, bf16[48,1152]{1,0:T(8,128)(2,1)S(1)}, u32[]{:S(2)}, u32[]{:S(2)}) collective-permute-start(bf16[48,1152]{1,0:T(8,128)(2,1)S(1)} %get-tuple-element.47), channel_id=1, source_target_pairs={{0,16},{1,17},{2,18},{3,19},{4,132},{5,133},{6,134},{7,135},{8,24}... | collective-permute-start | bytes 331784 | tf_op jit(solution)/shard_map/first/ppermute | solution.py:32
  5.5 1.7 %collective-permute-start.2 = (bf16[48,1152]{1,0:T(8,128)(2,1)S(1)}, bf16[48,1152]{1,0:T(8,128)(2,1)S(1)}, u32[]{:S(2)}, u32[]{:S(2)}) collective-permute-start(bf16[48,1152]{1,0:T(8,128)(2,1)S(1)} %get-tuple-element.47), channel_id=1, source_target_pairs={{0,24},{1,25},{2,26},{3,27},{4,196},{5,197},{6,198},{7,199},{8,0},... | collective-permute-start | bytes 331784 | tf_op jit(solution)/shard_map/first/ppermute | solution.py:32
  7.1 1.6 %collective-permute-start.1 = (bf16[48,1152]{1,0:T(8,128)(2,1)S(1)}, bf16[48,1152]{1,0:T(8,128)(2,1)S(1)}, u32[]{:S(2)}, u32[]{:S(2)}) collective-permute-start(bf16[48,1152]{1,0:T(8,128)(2,1)S(1)} %get-tuple-element.47), channel_id=1, source_target_pairs={{0,8},{1,9},{2,10},{3,11},{4,68},{5,69},{6,70},{7,71},{8,16},{9,17... | collective-permute-start | bytes 331784 | tf_op jit(solution)/shard_map/first/ppermute | solution.py:32
  8.7 3.3 %collective-permute-start.4 = (bf16[96,1152]{1,0:T(8,128)(2,1)S(1)}, bf16[96,1152]{1,0:T(8,128)(2,1)S(1)}, u32[]{:S(2)}, u32[]{:S(2)}) collective-permute-start(bf16[96,1152]{1,0:T(8,128)(2,1)S(1)} %get-tuple-element.49), channel_id=1, source_target_pairs={{0,2},{1,3},{2,32},{3,33},{4,38},{5,39},{6,4},{7,5},{8,10},{9,11},... | collective-permute-start | bytes 663560 | tf_op jit(solution)/shard_map/z2/ppermute | solution.py:32
  12.1 2.4 %collective-permute-start.5 = (f32[8,128]{1,0:T(8,128)S(1)}, f32[8,128]{1,0:T(8,128)S(1)}, u32[]{:S(2)}, u32[]{:S(2)}) collective-permute-start(f32[8,128]{1,0:T(8,128)S(1)} %shard_map.104), channel_id=1, source_target_pairs={{0,4},{1,5},{2,6},{3,7},{4,0},{5,1},{6,2},{7,3},{8,12},{9,13},{10,... | collective-permute-start | bytes 12296 | tf_op jit(solution)/shard_map/flag/ppermute | solution.py:32
  14.6 0.6 gather_fusion.1
  15.4 0.6 gather_fusion
  16.1 3.6 %collective-permute-done.4.pair_2 = bf16[96,1152]{1,0:T(8,128)(2,1)S(1)} collective-permute-done((bf16[96,1152]{1,0:T(8,128)(2,1)S(1)}, bf16[96,1152]{1,0:T(8,128)(2,1)S(1)}, u32[]{:S(2)}, u32[]{:S(2)}) %collective-permute-start.4) | collective-permute-done | bytes 221216 | tf_op jit(solution)/shard_map/z2/ppermute | solution.py:32
  19.7 1.7 %collective-permute-start.8 = (bf16[192,1152]{1,0:T(8,128)(2,1)S(1)}, bf16[192,1152]{1,0:T(8,128)(2,1)S(1)}, u32[]{:S(2)}, u32[]{:S(2)}) collective-permute-start(bf16[192,1152]{1,0:T(8,128)(2,1)S(1)} %get-tuple-element.53.refs_3_.src.refs_0_), channel_id=1, source_target_pairs={{0,64},{1,65},{2,66},{3,67},{4,12},{5,13},{6,14},{7,15},{8,72},{9,... | collective-permute-start | bytes 1327112 | tf_op jit(solution)/shard_map/second/ppermute | solution.py:32
  21.4 2.9 %collective-permute-start.10 = (bf16[192,1152]{1,0:T(8,128)(2,1)S(1)}, bf16[192,1152]{1,0:T(8,128)(2,1)S(1)}, u32[]{:S(2)}, u32[]{:S(2)}) collective-permute-start(bf16[192,1152]{1,0:T(8,128)(2,1)S(1)} %get-tuple-element.53.refs_3_.src.refs_0_), channel_id=1, source_target_pairs={{0,128},{1,129},{2,130},{3,131},{4,20},{5,21},{6,22},{7,23},{8,136... | collective-permute-start | bytes 1327112 | tf_op jit(solution)/shard_map/second/ppermute | solution.py:32
  24.3 1.3 %collective-permute-start.9 = (bf16[192,1152]{1,0:T(8,128)(2,1)S(1)}, bf16[192,1152]{1,0:T(8,128)(2,1)S(1)}, u32[]{:S(2)}, u32[]{:S(2)}) collective-permute-start(bf16[192,1152]{1,0:T(8,128)(2,1)S(1)} %get-tuple-element.53.refs_3_.src.refs_0_), channel_id=1, source_target_pairs={{0,192},{1,193},{2,194},{3,195},{4,28},{5,29},{6,30},{7,31},{8,200... | collective-permute-start | bytes 1327112 | tf_op jit(solution)/shard_map/second/ppermute | solution.py:32
  25.6 2.7 %collective-permute-start.6 = (bf16[48,1152]{1,0:T(8,128)(2,1)S(1)}, bf16[48,1152]{1,0:T(8,128)(2,1)S(1)}, u32[]{:S(2)}, u32[]{:S(2)}) collective-permute-start(bf16[48,1152]{1,0:T(8,128)(2,1)S(1)} %get-tuple-element.51), channel_id=1, source_target_pairs={{0,2},{1,3},{2,32},{3,33},{4,38},{5,39},{6,4},{7,5},{8,10},{9,11},... | collective-permute-start | bytes 331784 | tf_op jit(solution)/shard_map/z4/ppermute | solution.py:32
  28.3 0.5 collective-permute-start.7
  28.8 0.6 collective-permute-done.8.refs_4_.after.refs_1_
  29.4 5.8 %collective-permute-done.10.refs_6_.refs_3_ = bf16[192,1152]{1,0:T(8,128)(2,1)S(1)} collective-permute-done((bf16[192,1152]{1,0:T(8,128)(2,1)S(1)}, bf16[192,1152]{1,0:T(8,128)(2,1)S(1)}, u32[]{:S(2)}, u32[]{:S(2)}) %collective-permute-start.10) | collective-permute-done | bytes 442400 | tf_op jit(solution)/shard_map/second/ppermute | solution.py:32
  35.3 0.5 collective-permute-start.13
  35.8 0.3 collective-permute-start.12
  37.5 1.5 %collective-permute-done.7.refs_2_.t2 = bf16[192,1152]{1,0:T(8,128)(2,1)S(1)} collective-permute-done((bf16[192,1152]{1,0:T(8,128)(2,1)S(1)}, bf16[192,1152]{1,0:T(8,128)(2,1)S(1)}, u32[]{:S(2)}, u32[]{:S(2)}) %collective-permute-start.7) | collective-permute-done | bytes 442400 | tf_op jit(solution)/shard_map/z1/ppermute | solution.py:32
  39.0 2.8 %shard_map.106 = (bf16[384,768]{1,0:T(8,128)(2,1)S(1)}, f32[3,8,768]{2,1,0:T(8,128)S(1)}) custom-call(f32[2]{0:T(128)S(1)} %pad_maximum_fusion.scalars, s32[1,384]{1,0:T(1,128)S(1)} %reshape.1563.rows_after.rows_id, s32[1,768]{1,0:T(1,128)S(1)} %get-tuple-element.84.cols_id, f32[3,8,768]{2,1,0:T(8,128)S(1)} %broadcast_in_dim.2.before, ...), custom_call_target="tpu_custom_call" | custom-call | tf_op jit(solution)/shard_map/pallas_call | solution.py:235
  41.9 3.7 %shard_map.108 = (bf16[784,1152]{1,0:T(8,128)(2,1)S(1)}, bf16[384,768]{1,0:T(8,128)(2,1)S(1)}, f32[8,128]{1,0:T(8,128)S(1)}) custom-call(f32[2]{0:T(128)S(1)} %pad_maximum_fusion.scalars, s32[1,384]{1,0:T(1,128)S(1)} %reshape.1563.rows_after.rows_id, s32[1,768]{1,0:T(1,128)S(1)} %get-tuple-element.83.cols_id, f32[3,8,768]{2,1,0:T(8,128)S(1)} %get-tuple-element.55.before, ...), custom_call_target="tpu_custom_call" | custom-call | tf_op jit(solution)/shard_map/pallas_call | solution.py:235
  45.7 2.6 %shard_map.111 = (f32[48,1152]{1,0:T(8,128)S(1)}, f32[96,1152]{1,0:T(8,128)S(1)}, bf16[48,1152]{1,0:T(8,128)(2,1)S(1)}, bf16[192,1152]{1,0:T(8,128)(2,1)}) custom-call(bf16[384,768]{1,0:T(8,128)(2,1)S(1)} %get-tuple-element.54.scaled.scaled_own, bf16[384,768]{1,0:T(8,128)(2,1)S(1)} %get-tuple-element.67.scaled_far, ...), custom_call_target="tpu_custom_call" | custom-call | tf_op jit(solution)/shard_map/pallas_call | solution.py:235
  48.3 2.6 %collective-permute-start.22 = (bf16[192,1152]{1,0:T(8,128)(2,1)}, bf16[192,1152]{1,0:T(8,128)(2,1)}, u32[]{:S(2)}, u32[]{:S(2)}) collective-permute-start(bf16[192,1152]{1,0:T(8,128)(2,1)} %get-tuple-element.70), channel_id=1, source_target_pairs={{0,35},{1,0},{2,1},{3,2},{4,5},{5,6},{6,7},{7,36},{8,43},{9,8},{10... | collective-permute-start | bytes 1327112 | tf_op jit(solution)/shard_map/rz1/ppermute | solution.py:32
  50.8 2.3 %shard_map.109 = (f32[192,1152]{1,0:T(8,128)S(1)}, bf16[192,1152]{1,0:T(8,128)(2,1)}, bf16[192,1152]{1,0:T(8,128)(2,1)}, bf16[192,1152]{1,0:T(8,128)(2,1)}, f32[32,8,128]{2,1,0:T(8,128)}) custom-call(bf16[384,768]{1,0:T(8,128)(2,1)S(1)} %get-tuple-element.54.scaled.scaled_own, f32[8,128]{1,0:T(8,128)S(1)} %get-tuple-element.56.sums, ...), custom_call_target="tpu_custom_call" | custom-call | tf_op jit(solution)/shard_map/pallas_call | solution.py:235
  53.1 1.8 %collective-permute-start.16 = (bf16[192,1152]{1,0:T(8,128)(2,1)}, bf16[192,1152]{1,0:T(8,128)(2,1)S(1)}, u32[]{:S(2)}, u32[]{:S(2)}) collective-permute-start(bf16[192,1152]{1,0:T(8,128)(2,1)} %get-tuple-element.59), channel_id=1, source_target_pairs={{0,192},{1,193},{2,194},{3,195},{4,28},{5,29},{6,30},{7,31},{8,200... | collective-permute-start | bytes 1327112 | tf_op jit(solution)/shard_map/rsecond/ppermute | solution.py:32
  54.9 0.2 collective-permute-start.17
  55.1 2.4 %collective-permute-start.18 = (bf16[192,1152]{1,0:T(8,128)(2,1)}, bf16[192,1152]{1,0:T(8,128)(2,1)S(1)}, u32[]{:S(2)}, u32[]{:S(2)}) collective-permute-start(bf16[192,1152]{1,0:T(8,128)(2,1)} %get-tuple-element.61), channel_id=1, source_target_pairs={{0,128},{1,129},{2,130},{3,131},{4,20},{5,21},{6,22},{7,23},{8,136... | collective-permute-start | bytes 1327112 | tf_op jit(solution)/shard_map/rsecond/ppermute | solution.py:32
  57.5 2.1 %collective-permute-start.23 = (bf16[48,1152]{1,0:T(8,128)(2,1)S(1)}, bf16[48,1152]{1,0:T(8,128)(2,1)S(1)}, u32[]{:S(2)}, u32[]{:S(2)}) collective-permute-start(bf16[48,1152]{1,0:T(8,128)(2,1)S(1)} %get-tuple-element.71), channel_id=1, source_target_pairs={{0,34},{1,35},{2,0},{3,1},{4,6},{5,7},{6,36},{7,37},{8,42},{9,43},... | collective-permute-start | bytes 331784 | tf_op jit(solution)/shard_map/rz4/ppermute | solution.py:32
  59.5 5.1 %all-to-all-start = ((f32[32,8,128]{2,1,0:T(8,128)}), f32[32,8,128]{2,1,0:T(8,128)S(1)}, u32[]{:S(2)}, u32[]{:S(2)}) async-start(f32[32,8,128]{2,1,0:T(8,128)} %get-tuple-element.62), calls=%async_computation | async-start | bytes 262144 | tf_op jit(solution)/shard_map/terms/all_to_all | solution.py:314
  64.7 0.6 copy-done.7
  65.3 0.9 %copy-done.6 = f32[48,1152]{1,0:T(8,128)S(1)} copy-done((f32[48,1152]{1,0:T(8,128)S(1)}, f32[48,1152]{1,0:T(8,128)}, u32[]{:S(2)}) %copy-start.6) | copy-done | bytes 221208
  66.3 0.9 %copy-done.8 = bf16[48,1152]{1,0:T(8,128)(2,1)S(1)} copy-done((bf16[48,1152]{1,0:T(8,128)(2,1)S(1)}, bf16[48,1152]{1,0:T(8,128)(2,1)}, u32[]{:S(2)}) %copy-start.8) | copy-done | bytes 110616
  67.2 1.8 %shard_map.112 = (f32[48,1152]{1,0:T(8,128)S(1)}, f32[48,1152]{1,0:T(8,128)S(1)}, bf16[96,1152]{1,0:T(8,128)(2,1)}) custom-call(f32[48,1152]{1,0:T(8,128)S(1)} %copy-done.6, f32[96,1152]{1,0:T(8,128)S(1)} %get-tuple-element.69.pair, bf16[192,1152]{1,0:T(8,128)(2,1)} %collective-permute-done.22.back, bf16[48,1152]{1,0:T(8,128)(2,1)S(1)} %copy-done.8), custom_call_target="tpu_custom_call" | custom-call | tf_op jit(solution)/shard_map/pallas_call | solution.py:235
  68.9 0.7 copy-done.3
  69.6 3.9 %collective-permute-start.24 = (bf16[96,1152]{1,0:T(8,128)(2,1)}, bf16[96,1152]{1,0:T(8,128)(2,1)S(1)}, u32[]{:S(2)}, u32[]{:S(2)}) collective-permute-start(bf16[96,1152]{1,0:T(8,128)(2,1)} %get-tuple-element.74), channel_id=1, source_target_pairs={{0,34},{1,35},{2,0},{3,1},{4,6},{5,7},{6,36},{7,37},{8,42},{9,43},... | collective-permute-start | bytes 663560 | tf_op jit(solution)/shard_map/rz2/ppermute | solution.py:32
  73.5 1.5 %all-to-all-done.terms = f32[32,8,128]{2,1,0:T(8,128)S(1)} async-done(((f32[32,8,128]{2,1,0:T(8,128)}), f32[32,8,128]{2,1,0:T(8,128)S(1)}, u32[]{:S(2)}, u32[]{:S(2)}) %all-to-all-start) | async-done | bytes 131104 | tf_op jit(solution)/shard_map/terms/all_to_all | solution.py:314
  75.1 0.2 shard_map.110
  75.4 3.2 %collective-permute-start.20 = (bf16[64,1152]{1,0:T(8,128)(2,1)S(1)}, bf16[64,1152]{1,0:T(8,128)(2,1)S(1)}, u32[]{:S(2)}, u32[]{:S(2)}) collective-permute-start(bf16[64,1152]{1,0:T(8,128)(2,1)S(1)} %get-tuple-element.65), channel_id=1, source_target_pairs={{0,8},{1,9},{2,10},{3,11},{4,68},{5,69},{6,70},{7,71},{8,16},{9,17... | collective-permute-start | bytes 442376 | tf_op jit(solution)/shard_map/rfirst/ppermute | solution.py:32
  78.6 1.1 %collective-permute-done.24.back = bf16[96,1152]{1,0:T(8,128)(2,1)S(1)} collective-permute-done((bf16[96,1152]{1,0:T(8,128)(2,1)}, bf16[96,1152]{1,0:T(8,128)(2,1)S(1)}, u32[]{:S(2)}, u32[]{:S(2)}) %collective-permute-start.24) | collective-permute-done | bytes 221216 | tf_op jit(solution)/shard_map/rz2/ppermute | solution.py:32
  79.8 1.3 %collective-permute-done.25.t1 = bf16[48,1152]{1,0:T(8,128)(2,1)S(1)} collective-permute-done((bf16[48,1152]{1,0:T(8,128)(2,1)S(1)}, bf16[48,1152]{1,0:T(8,128)(2,1)S(1)}, u32[]{:S(2)}, u32[]{:S(2)}) %collective-permute-start.25) | collective-permute-done | bytes 110624 | tf_op jit(solution)/shard_map/rpair/ppermute | solution.py:32
  81.1 0.6 collective-permute-done.19.i1
  81.7 1.2 %collective-permute-done.20.i2 = bf16[64,1152]{1,0:T(8,128)(2,1)S(1)} collective-permute-done((bf16[64,1152]{1,0:T(8,128)(2,1)S(1)}, bf16[64,1152]{1,0:T(8,128)(2,1)S(1)}, u32[]{:S(2)}, u32[]{:S(2)}) %collective-permute-start.20) | collective-permute-done | bytes 147488 | tf_op jit(solution)/shard_map/rfirst/ppermute | solution.py:32
  82.9 2.4 %collective-permute-done.21.i3 = bf16[64,1152]{1,0:T(8,128)(2,1)S(1)} collective-permute-done((bf16[64,1152]{1,0:T(8,128)(2,1)S(1)}, bf16[64,1152]{1,0:T(8,128)(2,1)S(1)}, u32[]{:S(2)}, u32[]{:S(2)}) %collective-permute-start.21) | collective-permute-done | bytes 147488 | tf_op jit(solution)/shard_map/rfirst/ppermute | solution.py:32
  85.3 1.5 %shard_map.114 = (f32[48,1152]{1,0:T(8,128)}, f32[48,1152]{1,0:T(8,128)}, f32[1]{0:T(128)}, f32[1]{0:T(128)}, f32[1]{0:T(128)}) custom-call(f32[2]{0:T(128)S(1)} %pad_maximum_fusion.scalars, f32[48,1152]{1,0:T(8,128)S(1)} %copy-done, f32[48,1152]{1,0:T(8,128)S(1)} %get-tuple-element.63.after.image_own, bf16[64,1152]{1,0:T(8,128)(2,1)S(1)} %collective-permute-done.19.i1, ...), custom_call_target="tpu_custom_call" | custom-call | tf_op jit(solution)/shard_map/pallas_call | solution.py:235
  (57 shorter events, 1.2 us)
Async XLA Ops:
  0.6 3.2 %copy-start = (f32[48,1152]{1,0:T(8,128)S(1)}, f32[48,1152]{1,0:T(8,128)}, u32[]{:S(2)}) copy-start(f32[48,1152]{1,0:T(8,128)} %image_raw.1) | copy-start | bytes 663556
  0.6 1.0 %copy-start.1 = (f32[48,1152]{1,0:T(8,128)S(1)}, f32[48,1152]{1,0:T(8,128)}, u32[]{:S(2)}) copy-start(f32[48,1152]{1,0:T(8,128)} %text_raw.1) | copy-start | bytes 663556
  1.6 12.9 %copy-start.9 = (s32[12288]{0:T(1024)S(1)}, s32[12288]{0:T(1024)}, u32[]{:S(2)}) copy-start(s32[12288]{0:T(1024)} %param.8) | copy-start | bytes 147460
  1.8 2.1 %collective-permute-start = (bf16[48,1152]{1,0:T(8,128)(2,1)S(1)}, bf16[48,1152]{1,0:T(8,128)(2,1)S(1)}, u32[]{:S(2)}, u32[]{:S(2)}) collective-permute-start(bf16[48,1152]{1,0:T(8,128)(2,1)S(1)} %get-tuple-element.45), channel_id=1, source_target_pairs={{0,4},{1,5},{2,6},{3,7},{4,0},{5,1},{6,2},{7,3},{8,12},{9,13},{10,... | collective-permute-start | bytes 331784 | tf_op jit(solution)/shard_map/pair/ppermute | solution.py:32
  2.0 13.4 %copy-start.10 = (s32[12288]{0:T(1024)S(1)}, s32[12288]{0:T(1024)}, u32[]{:S(2)}) copy-start(s32[12288]{0:T(1024)} %param.9) | copy-start | bytes 147460
  4.0 8.1 %collective-permute-start.3 = (bf16[48,1152]{1,0:T(8,128)(2,1)S(1)}, bf16[48,1152]{1,0:T(8,128)(2,1)S(1)}, u32[]{:S(2)}, u32[]{:S(2)}) collective-permute-start(bf16[48,1152]{1,0:T(8,128)(2,1)S(1)} %get-tuple-element.47), channel_id=1, source_target_pairs={{0,16},{1,17},{2,18},{3,19},{4,132},{5,133},{6,134},{7,135},{8,24}... | collective-permute-start | bytes 331784 | tf_op jit(solution)/shard_map/first/ppermute | solution.py:32
  5.5 6.6 %collective-permute-start.2 = (bf16[48,1152]{1,0:T(8,128)(2,1)S(1)}, bf16[48,1152]{1,0:T(8,128)(2,1)S(1)}, u32[]{:S(2)}, u32[]{:S(2)}) collective-permute-start(bf16[48,1152]{1,0:T(8,128)(2,1)S(1)} %get-tuple-element.47), channel_id=1, source_target_pairs={{0,24},{1,25},{2,26},{3,27},{4,196},{5,197},{6,198},{7,199},{8,0},... | collective-permute-start | bytes 331784 | tf_op jit(solution)/shard_map/first/ppermute | solution.py:32
  7.1 5.0 %collective-permute-start.1 = (bf16[48,1152]{1,0:T(8,128)(2,1)S(1)}, bf16[48,1152]{1,0:T(8,128)(2,1)S(1)}, u32[]{:S(2)}, u32[]{:S(2)}) collective-permute-start(bf16[48,1152]{1,0:T(8,128)(2,1)S(1)} %get-tuple-element.47), channel_id=1, source_target_pairs={{0,8},{1,9},{2,10},{3,11},{4,68},{5,69},{6,70},{7,71},{8,16},{9,17... | collective-permute-start | bytes 331784 | tf_op jit(solution)/shard_map/first/ppermute | solution.py:32
  8.7 10.9 %collective-permute-start.4 = (bf16[96,1152]{1,0:T(8,128)(2,1)S(1)}, bf16[96,1152]{1,0:T(8,128)(2,1)S(1)}, u32[]{:S(2)}, u32[]{:S(2)}) collective-permute-start(bf16[96,1152]{1,0:T(8,128)(2,1)S(1)} %get-tuple-element.49), channel_id=1, source_target_pairs={{0,2},{1,3},{2,32},{3,33},{4,38},{5,39},{6,4},{7,5},{8,10},{9,11},... | collective-permute-start | bytes 663560 | tf_op jit(solution)/shard_map/z2/ppermute | solution.py:32
  12.1 3.9 %collective-permute-start.5 = (f32[8,128]{1,0:T(8,128)S(1)}, f32[8,128]{1,0:T(8,128)S(1)}, u32[]{:S(2)}, u32[]{:S(2)}) collective-permute-start(f32[8,128]{1,0:T(8,128)S(1)} %shard_map.104), channel_id=1, source_target_pairs={{0,4},{1,5},{2,6},{3,7},{4,0},{5,1},{6,2},{7,3},{8,12},{9,13},{10,... | collective-permute-start | bytes 12296 | tf_op jit(solution)/shard_map/flag/ppermute | solution.py:32
  19.7 9.6 %collective-permute-start.8 = (bf16[192,1152]{1,0:T(8,128)(2,1)S(1)}, bf16[192,1152]{1,0:T(8,128)(2,1)S(1)}, u32[]{:S(2)}, u32[]{:S(2)}) collective-permute-start(bf16[192,1152]{1,0:T(8,128)(2,1)S(1)} %get-tuple-element.53.refs_3_.src.refs_0_), channel_id=1, source_target_pairs={{0,64},{1,65},{2,66},{3,67},{4,12},{5,13},{6,14},{7,15},{8,72},{9,... | collective-permute-start | bytes 1327112 | tf_op jit(solution)/shard_map/second/ppermute | solution.py:32
  21.4 13.9 %collective-permute-start.10 = (bf16[192,1152]{1,0:T(8,128)(2,1)S(1)}, bf16[192,1152]{1,0:T(8,128)(2,1)S(1)}, u32[]{:S(2)}, u32[]{:S(2)}) collective-permute-start(bf16[192,1152]{1,0:T(8,128)(2,1)S(1)} %get-tuple-element.53.refs_3_.src.refs_0_), channel_id=1, source_target_pairs={{0,128},{1,129},{2,130},{3,131},{4,20},{5,21},{6,22},{7,23},{8,136... | collective-permute-start | bytes 1327112 | tf_op jit(solution)/shard_map/second/ppermute | solution.py:32
  24.3 11.0 %collective-permute-start.9 = (bf16[192,1152]{1,0:T(8,128)(2,1)S(1)}, bf16[192,1152]{1,0:T(8,128)(2,1)S(1)}, u32[]{:S(2)}, u32[]{:S(2)}) collective-permute-start(bf16[192,1152]{1,0:T(8,128)(2,1)S(1)} %get-tuple-element.53.refs_3_.src.refs_0_), channel_id=1, source_target_pairs={{0,192},{1,193},{2,194},{3,195},{4,28},{5,29},{6,30},{7,31},{8,200... | collective-permute-start | bytes 1327112 | tf_op jit(solution)/shard_map/second/ppermute | solution.py:32
  25.6 10.2 %collective-permute-start.6 = (bf16[48,1152]{1,0:T(8,128)(2,1)S(1)}, bf16[48,1152]{1,0:T(8,128)(2,1)S(1)}, u32[]{:S(2)}, u32[]{:S(2)}) collective-permute-start(bf16[48,1152]{1,0:T(8,128)(2,1)S(1)} %get-tuple-element.51), channel_id=1, source_target_pairs={{0,2},{1,3},{2,32},{3,33},{4,38},{5,39},{6,4},{7,5},{8,10},{9,11},... | collective-permute-start | bytes 331784 | tf_op jit(solution)/shard_map/z4/ppermute | solution.py:32
  28.3 10.7 %collective-permute-start.7 = (bf16[192,1152]{1,0:T(8,128)(2,1)S(1)}, bf16[192,1152]{1,0:T(8,128)(2,1)S(1)}, u32[]{:S(2)}, u32[]{:S(2)}) collective-permute-start(bf16[192,1152]{1,0:T(8,128)(2,1)S(1)} %get-tuple-element.52), channel_id=1, source_target_pairs={{0,1},{1,2},{2,3},{3,32},{4,39},{5,4},{6,5},{7,6},{8,9},{9,10},{10... | collective-permute-start | bytes 1327112 | tf_op jit(solution)/shard_map/z1/ppermute | solution.py:32
  29.3 12.5 %collective-permute-start.11 = (bf16[192,1152]{1,0:T(8,128)(2,1)S(1)}, bf16[192,1152]{1,0:T(8,128)(2,1)S(1)}, u32[]{:S(2)}, u32[]{:S(2)}) collective-permute-start(bf16[192,1152]{1,0:T(8,128)(2,1)S(1)} %shard_map.107), channel_id=1, source_target_pairs={{0,4},{1,5},{2,6},{3,7},{4,0},{5,1},{6,2},{7,3},{8,12},{9,13},{10,... | collective-permute-start | bytes 1327112 | tf_op jit(solution)/shard_map/swap/ppermute | solution.py:32
  35.3 6.6 %collective-permute-start.14 = (bf16[192,1152]{1,0:T(8,128)(2,1)S(1)}, bf16[192,1152]{1,0:T(8,128)(2,1)S(1)}, u32[]{:S(2)}, u32[]{:S(2)}) collective-permute-start(bf16[192,1152]{1,0:T(8,128)(2,1)S(1)} %collective-permute-done.10.refs_6_.refs_3_), channel_id=1, source_target_pairs={{0,4},{1,5},{2,6},{3,7},{4,0},{5,1},{6,2},{7,3},{8,12},{9,13},{10,... | collective-permute-start | bytes 1327112 | tf_op jit(solution)/shard_map/swap/ppermute | solution.py:32
  35.3 6.6 %collective-permute-start.13 = (bf16[192,1152]{1,0:T(8,128)(2,1)S(1)}, bf16[192,1152]{1,0:T(8,128)(2,1)S(1)}, u32[]{:S(2)}, u32[]{:S(2)}) collective-permute-start(bf16[192,1152]{1,0:T(8,128)(2,1)S(1)} %collective-permute-done.9.refs_5_.refs_2_), channel_id=1, source_target_pairs={{0,4},{1,5},{2,6},{3,7},{4,0},{5,1},{6,2},{7,3},{8,12},{9,13},{10,... | collective-permute-start | bytes 1327112 | tf_op jit(solution)/shard_map/swap/ppermute | solution.py:32
  35.8 6.1 %collective-permute-start.12 = (bf16[192,1152]{1,0:T(8,128)(2,1)S(1)}, bf16[192,1152]{1,0:T(8,128)(2,1)S(1)}, u32[]{:S(2)}, u32[]{:S(2)}) collective-permute-start(bf16[192,1152]{1,0:T(8,128)(2,1)S(1)} %collective-permute-done.8.refs_4_.after.refs_1_), channel_id=1, source_target_pairs={{0,4},{1,5},{2,6},{3,7},{4,0},{5,1},{6,2},{7,3},{8,12},{9,13},{10,... | collective-permute-start | bytes 1327112 | tf_op jit(solution)/shard_map/swap/ppermute | solution.py:32
  45.6 5.2 %collective-permute-start.15 = (bf16[784,1152]{1,0:T(8,128)(2,1)S(1)}, bf16[784,1152]{1,0:T(8,128)(2,1)S(1)}, u32[]{:S(2)}, u32[]{:S(2)}) collective-permute-start(bf16[784,1152]{1,0:T(8,128)(2,1)S(1)} %get-tuple-element.57), channel_id=1, source_target_pairs={{0,4},{1,5},{2,6},{3,7},{4,0},{5,1},{6,2},{7,3},{8,12},{9,13},{10,... | collective-permute-start | bytes 5419016 | tf_op jit(solution)/shard_map/rswap/ppermute | solution.py:32
  48.3 17.1 %copy-start.5 = (f32[48,1152]{1,0:T(8,128)}, f32[48,1152]{1,0:T(8,128)S(1)}, u32[]{:S(2)}) copy-start(f32[48,1152]{1,0:T(8,128)S(1)} %get-tuple-element.68.own) | copy-start | bytes 663556
  48.3 17.1 %collective-permute-start.22 = (bf16[192,1152]{1,0:T(8,128)(2,1)}, bf16[192,1152]{1,0:T(8,128)(2,1)}, u32[]{:S(2)}, u32[]{:S(2)}) collective-permute-start(bf16[192,1152]{1,0:T(8,128)(2,1)} %get-tuple-element.70), channel_id=1, source_target_pairs={{0,35},{1,0},{2,1},{3,2},{4,5},{5,6},{6,7},{7,36},{8,43},{9,8},{10... | collective-permute-start | bytes 1327112 | tf_op jit(solution)/shard_map/rz1/ppermute | solution.py:32
  53.1 22.0 %collective-permute-start.16 = (bf16[192,1152]{1,0:T(8,128)(2,1)}, bf16[192,1152]{1,0:T(8,128)(2,1)S(1)}, u32[]{:S(2)}, u32[]{:S(2)}) collective-permute-start(bf16[192,1152]{1,0:T(8,128)(2,1)} %get-tuple-element.59), channel_id=1, source_target_pairs={{0,192},{1,193},{2,194},{3,195},{4,28},{5,29},{6,30},{7,31},{8,200... | collective-permute-start | bytes 1327112 | tf_op jit(solution)/shard_map/rsecond/ppermute | solution.py:32
  54.9 20.2 %collective-permute-start.17 = (bf16[192,1152]{1,0:T(8,128)(2,1)}, bf16[192,1152]{1,0:T(8,128)(2,1)S(1)}, u32[]{:S(2)}, u32[]{:S(2)}) collective-permute-start(bf16[192,1152]{1,0:T(8,128)(2,1)} %get-tuple-element.60), channel_id=1, source_target_pairs={{0,64},{1,65},{2,66},{3,67},{4,12},{5,13},{6,14},{7,15},{8,72},{9,... | collective-permute-start | bytes 1327112 | tf_op jit(solution)/shard_map/rsecond/ppermute | solution.py:32
  55.1 20.0 %collective-permute-start.18 = (bf16[192,1152]{1,0:T(8,128)(2,1)}, bf16[192,1152]{1,0:T(8,128)(2,1)S(1)}, u32[]{:S(2)}, u32[]{:S(2)}) collective-permute-start(bf16[192,1152]{1,0:T(8,128)(2,1)} %get-tuple-element.61), channel_id=1, source_target_pairs={{0,128},{1,129},{2,130},{3,131},{4,20},{5,21},{6,22},{7,23},{8,136... | collective-permute-start | bytes 1327112 | tf_op jit(solution)/shard_map/rsecond/ppermute | solution.py:32
  57.5 7.2 %collective-permute-start.23 = (bf16[48,1152]{1,0:T(8,128)(2,1)S(1)}, bf16[48,1152]{1,0:T(8,128)(2,1)S(1)}, u32[]{:S(2)}, u32[]{:S(2)}) collective-permute-start(bf16[48,1152]{1,0:T(8,128)(2,1)S(1)} %get-tuple-element.71), channel_id=1, source_target_pairs={{0,34},{1,35},{2,0},{3,1},{4,6},{5,7},{6,36},{7,37},{8,42},{9,43},... | collective-permute-start | bytes 331784 | tf_op jit(solution)/shard_map/rz4/ppermute | solution.py:32
  59.5 15.5 %all-to-all-start = ((f32[32,8,128]{2,1,0:T(8,128)}), f32[32,8,128]{2,1,0:T(8,128)S(1)}, u32[]{:S(2)}, u32[]{:S(2)}) async-start(f32[32,8,128]{2,1,0:T(8,128)} %get-tuple-element.62), calls=%async_computation | async-start | bytes 262144 | tf_op jit(solution)/shard_map/terms/all_to_all | solution.py:314
  64.7 0.6 copy-start.7
  65.3 0.9 %copy-start.6 = (f32[48,1152]{1,0:T(8,128)S(1)}, f32[48,1152]{1,0:T(8,128)}, u32[]{:S(2)}) copy-start(f32[48,1152]{1,0:T(8,128)} %copy-done.5) | copy-start | bytes 663556
  66.3 0.9 %copy-start.8 = (bf16[48,1152]{1,0:T(8,128)(2,1)S(1)}, bf16[48,1152]{1,0:T(8,128)(2,1)}, u32[]{:S(2)}) copy-start(bf16[48,1152]{1,0:T(8,128)(2,1)} %copy-done.7) | copy-start | bytes 331780
  68.9 0.7 copy-start.3
  69.6 15.6 %copy-start.2 = (f32[48,1152]{1,0:T(8,128)S(1)}, f32[48,1152]{1,0:T(8,128)}, u32[]{:S(2)}) copy-start(f32[48,1152]{1,0:T(8,128)} %text_raw.1) | copy-start | bytes 663556
  69.6 10.0 %copy-start.4 = (f32[48,1152]{1,0:T(8,128)S(1)}, f32[48,1152]{1,0:T(8,128)}, u32[]{:S(2)}) copy-start(f32[48,1152]{1,0:T(8,128)} %copy-done.3) | copy-start | bytes 663556
  69.6 10.0 %collective-permute-start.24 = (bf16[96,1152]{1,0:T(8,128)(2,1)}, bf16[96,1152]{1,0:T(8,128)(2,1)S(1)}, u32[]{:S(2)}, u32[]{:S(2)}) collective-permute-start(bf16[96,1152]{1,0:T(8,128)(2,1)} %get-tuple-element.74), channel_id=1, source_target_pairs={{0,34},{1,35},{2,0},{3,1},{4,6},{5,7},{6,36},{7,37},{8,42},{9,43},... | collective-permute-start | bytes 663560 | tf_op jit(solution)/shard_map/rz2/ppermute | solution.py:32
  75.3 6.4 %collective-permute-start.19 = (bf16[64,1152]{1,0:T(8,128)(2,1)S(1)}, bf16[64,1152]{1,0:T(8,128)(2,1)S(1)}, u32[]{:S(2)}, u32[]{:S(2)}) collective-permute-start(bf16[64,1152]{1,0:T(8,128)(2,1)S(1)} %get-tuple-element.64), channel_id=1, source_target_pairs={{0,24},{1,25},{2,26},{3,27},{4,196},{5,197},{6,198},{7,199},{8,0},... | collective-permute-start | bytes 442376 | tf_op jit(solution)/shard_map/rfirst/ppermute | solution.py:32
  75.4 7.5 %collective-permute-start.20 = (bf16[64,1152]{1,0:T(8,128)(2,1)S(1)}, bf16[64,1152]{1,0:T(8,128)(2,1)S(1)}, u32[]{:S(2)}, u32[]{:S(2)}) collective-permute-start(bf16[64,1152]{1,0:T(8,128)(2,1)S(1)} %get-tuple-element.65), channel_id=1, source_target_pairs={{0,8},{1,9},{2,10},{3,11},{4,68},{5,69},{6,70},{7,71},{8,16},{9,17... | collective-permute-start | bytes 442376 | tf_op jit(solution)/shard_map/rfirst/ppermute | solution.py:32
  78.6 6.6 %collective-permute-start.21 = (bf16[64,1152]{1,0:T(8,128)(2,1)S(1)}, bf16[64,1152]{1,0:T(8,128)(2,1)S(1)}, u32[]{:S(2)}, u32[]{:S(2)}) collective-permute-start(bf16[64,1152]{1,0:T(8,128)(2,1)S(1)} %get-tuple-element.66), channel_id=1, source_target_pairs={{0,16},{1,17},{2,18},{3,19},{4,132},{5,133},{6,134},{7,135},{8,24}... | collective-permute-start | bytes 442376 | tf_op jit(solution)/shard_map/rfirst/ppermute | solution.py:32
  79.7 1.4 %collective-permute-start.25 = (bf16[48,1152]{1,0:T(8,128)(2,1)S(1)}, bf16[48,1152]{1,0:T(8,128)(2,1)S(1)}, u32[]{:S(2)}, u32[]{:S(2)}) collective-permute-start(bf16[48,1152]{1,0:T(8,128)(2,1)S(1)} %get-tuple-element.76), channel_id=1, source_target_pairs={{0,4},{1,5},{2,6},{3,7},{4,0},{5,1},{6,2},{7,3},{8,12},{9,13},{10,... | collective-permute-start | bytes 331784 | tf_op jit(solution)/shard_map/rpair/ppermute | solution.py:32

commit v6 on v5

--- a/solution.py
+++ b/solution.py
@@ -1,3 +1,4 @@
+import functools
 import math
 
 import jax
@@ -69,14 +70,11 @@
     kept[...] = out[...]
 
 
-def image_unit_kernel(raw, after, far_after, out, kept):
+def image_unit_kernel(raw, text, text_far, out, kept, pair, pair_kept):
     out[...] = unit(raw[...])
     kept[...] = out[...]
-
-
-def pair_kernel(text, text_far, after, pair, kept):
     stack(pair, (text, text_far))
-    stack(kept, (text, text_far))
+    stack(pair_kept, (text, text_far))
 
 
 def stack(out, sources):
@@ -91,6 +89,11 @@
     stack(message, (pair, pair_2))
     hop[...] = pair_2[:48]
     stack(kept, (own, pair_2))
+
+
+def ids_kernel(image, text, after, image_out, text_out):
+    image_out[...] = image[...]
+    text_out[...] = text[...]
 
 
 def flag_kernel(*refs):
@@ -116,14 +119,19 @@
     return (extra[2:3] + extra[1:2]) + extra[0:1]
 
 
-def terms_kernel(scalars, rows_id, cols_id, before, *refs):
-    pieces, (*far, scaled, sums, text, image) = refs[:7], refs[7:]
-    temp = scalars[0]
-    offset = scalars[1]
-    stack(text, pieces[:3])
-    stack(image, pieces[3:])
+def terms_kernel(first, log_temp, bias, rows_id, cols_id, before, *refs):
+    if first:
+        pieces, (scaled, sums, text, image) = refs[:7], refs[7:]
+        stack(text, pieces[:3])
+        stack(image, pieces[3:])
+        far = ()
+    else:
+        text, pieces, (*far, scaled, sums, image) = refs[0], refs[1:5], refs[5:]
+        stack(image, pieces)
+    temp = jnp.exp(jnp.full((1, 1), log_temp[0], jnp.float32))
+    offset = bias[0]
     totals = [before[n] for n in range(3)]
-    cols = cols_id[...]
+    cols = cols_id[:, :768] if first else cols_id[:, 768:]
     rows = jnp.transpose(jnp.broadcast_to(rows_id[...].astype(jnp.float32), (128, 384)))[:, :1].astype(jnp.int32)
     for tile in range(2):
         at = slice(192 * tile, 192 * (tile + 1))
@@ -156,20 +164,16 @@
     ride(far[0], 768, out)
 
 
-def text_kernel(scaled_own, scaled_far, *refs):
-    pieces, (own, pair, opposite, last, image) = refs[:8], refs[8:]
-    stack(image, pieces[:4])
+def text_kernel(scaled_own, scaled_far, image, image_far, own, pair, opposite, last):
     total = jnp.dot(scaled_own[...], image[...], preferred_element_type=jnp.float32)
-    stack(image, pieces[4:])
-    total = total + jnp.dot(scaled_far[...], image[...], preferred_element_type=jnp.float32)
+    total = total + jnp.dot(scaled_far[...], image_far[...], preferred_element_type=jnp.float32)
     row = 0
     for dst in (own, pair, opposite, last):
         dst[...] = total[row : row + dst.shape[0]].astype(dst.dtype)
         row += dst.shape[0]
 
 
-def image_kernel(scaled, sums, t0, t1, t2, back, own, low1, low2, low3, sums_out, text):
-    stack(text, (t0, t1, t2))
+def image_kernel(scaled, sums, text, back, own, low1, low2, low3, sums_out):
     part = lax.dot_general(
         scaled[...], text[...], (((0,), (0,)), ((), ())), preferred_element_type=jnp.float32
     )
@@ -202,8 +206,9 @@
     low[...] = (far[...] + back[48:].astype(jnp.float32)).astype(low.dtype)
 
 
-def finish_kernel(scalars, image_raw, image_own, i1, i2, i3, text_raw, text_own, t1, sums,
+def finish_kernel(log_temp, image_raw, image_own, i1, i2, i3, text_raw, text_own, t1, sums,
                   image_out, text_out, loss, bias_grad, temp_grad):
+    temp = jnp.exp(jnp.full((1, 1), log_temp[0], jnp.float32))
     for raw, own, parts, out in (
         (image_raw, image_own, (i1, i2, i3), image_out), (text_raw, text_own, (t1,), text_out),
     ):
@@ -212,15 +217,19 @@
         grad = own[...]
         for part in parts:
             grad = grad + part[:48].astype(jnp.float32)
-        grad = grad * scalars[0]
+        grad = grad * temp
         square = jnp.mean(rows * rows, axis=-1, keepdims=True) + 1e-06
         inner = jnp.sum(rows * grad, axis=-1, keepdims=True)
         out[...] = (grad - rows * (inner / (square * width))) / (jnp.sqrt(square) * math.sqrt(width))
     values = [sums[0:1]] + [alight(part, 48) for part in (i1, i2, i3)]
     total = (values[0] + values[3]) + (values[1] + values[2])
     lane = lax.broadcasted_iota(jnp.int32, total.shape, 1)
-    for n, (out, factor) in enumerate(((loss, 1.0), (bias_grad, 1.0), (temp_grad, scalars[0]))):
-        out[0] = jnp.sum(jnp.where(lane == n, total, 0.0)) * factor / (48 * 256)
+    for n, (out, factor) in enumerate(((loss, 1.0), (bias_grad, 1.0), (temp_grad, temp))):
+        out[0] = jnp.sum(jnp.where(lane == n, total * factor, 0.0)) / (48 * 256)
+
+
+def i32(*shape):
+    return jax.ShapeDtypeStruct(shape, jnp.int32)
 
 
 def f32(*shape):
@@ -235,7 +244,7 @@
     return pl.pallas_call(
         kernel,
         out_shape=out_shape,
-        in_specs=[SMEM if a.shape == (2,) else VMEM for a in args] + [ANY] * len(after),
+        in_specs=[SMEM if a.shape == (1,) else VMEM for a in args] + [ANY] * len(after),
         out_specs=tuple(SMEM if o.shape == (1,) else VMEM for o in out_shape),
         scratch_shapes=list(scratch),
         compiler_params=pltpu.CompilerParams(vmem_limit_bytes=grant * 1024 * 1024),
@@ -246,15 +255,6 @@
     pairs, width = image_raw.shape
     x, y, c = lax.axis_index("x"), lax.axis_index("y"), lax.axis_index("core")
     z = lax.axis_index("zh") * 4 + lax.axis_index("zl")
-    text_unit, text_kept = local(text_unit_kernel, (b16(pairs, width),) * 2, text_raw)
-    text_far = send(text_unit, swap, "pair")
-    image_unit, image_kept = local(image_unit_kernel, (b16(pairs, width),) * 2, image_raw, after=(text_kept, text_far))
-    pair, pair_kept = local(
-        pair_kernel, (b16(2 * pairs, width),) * 2, text_kept, text_far, after=(image_kept,),
-    )
-
-    parts = [send(image_unit, along_first(k), "first") for k in OFFSETS]
-    pair_2 = send(pair, apart(2), "z2")
     back = (0,) + OFFSETS
     cols_from = []
     for core in (c, 1 - c):
@@ -267,9 +267,18 @@
     rows_from = [flat(x, y, z, c)]
     for k in (2, 4, 1, 3):
         rows_from += [flat(x, y, (z - k * step) % 8, core) for core in ((c,) if k == 4 else (c, 1 - c))]
+
+    text_unit, text_kept = local(text_unit_kernel, (b16(pairs, width),) * 2, text_raw)
+    image_unit, image_kept, pair, pair_kept = local(
+        image_unit_kernel, (b16(pairs, width),) * 2 + (b16(2 * pairs, width),) * 2,
+        image_raw, text_kept, send(text_unit, swap, "pair"),
+    )
+
+    parts = [send(image_unit, along_first(k), "first") for k in OFFSETS]
+    pair_2 = send(pair, apart(2), "z2")
+    image_ids, text_ids = local(ids_kernel, (i32(256, pairs),) * 2, image_ids.reshape(256, pairs), text_ids.reshape(256, pairs), after=parts[1:2])
     cols_id = image_ids.reshape(256, pairs)[jnp.stack(cols_from)].reshape(1, 32 * pairs)
     rows_id = text_ids.reshape(256, pairs)[jnp.stack(rows_from)].reshape(1, 8 * pairs)
-
     (flag,) = local(flag_kernel, (f32(8, 128),), after=parts)
     flag = send(flag, swap, "flag")
     line, message, hop, kept = local(
@@ -282,27 +291,26 @@
     (line_kept,) = local(copy_kernel, (b16(4 * pairs, width),), line, after=(plane[1],))
     plane_far = [send(p, swap, "swap") for p in [line_kept] + plane[1:]]
 
-    temp = jnp.exp(log_temp[0])
-    scalars = jnp.stack([temp, bias[0]])
-    copies = (pltpu.VMEM((384, width), jnp.bfloat16), pltpu.VMEM((768, width), jnp.bfloat16))
-    scaled_own, sums = local(
-        terms_kernel, (b16(384, 768), f32(3, 8, 768)),
-        scalars, rows_id, cols_id[:, :768], jnp.zeros((3, 8, 768), jnp.float32), *text, *plane, scratch=copies, grant=16,
-    )
-    far, scaled_far, sums = local(
-        terms_kernel, (b16(784, width), b16(384, 768), f32(8, 128)),
-        scalars, rows_id, cols_id[:, 768:], sums, *text, *plane_far, scratch=copies, grant=16,
+    scaled_own, sums, text, image = local(
+        functools.partial(terms_kernel, True),
+        (b16(384, 768), f32(3, 8, 768), b16(384, width), b16(768, width)),
+        log_temp, bias, rows_id, cols_id, jnp.zeros((3, 8, 768), jnp.float32), *text, *plane, grant=16,
+    )
+    far, scaled_far, sums, image_far = local(
+        functools.partial(terms_kernel, False),
+        (b16(784, width), b16(384, 768), f32(8, 128), b16(768, width)),
+        log_temp, bias, rows_id, cols_id, sums, text, *plane_far, grant=16,
     )
     back = send(far, swap, "rswap")
     text_own, text_pair, hop, last = local(
         text_kernel, (f32(pairs, width), f32(2 * pairs, width), b16(pairs, width), b16(4 * pairs, width)),
-        scaled_own, scaled_far, *plane, *plane_far, scratch=copies[1:], grant=16,
+        scaled_own, scaled_far, image, image_far, grant=16,
     )
     last = send(last, apart(-1), "rz1")
     hop = send(hop, apart(-2), "rz4")
     image_own, *lows, spread = local(
         image_kernel, (f32(192, width),) + (b16(192, width),) * 3 + (f32(32, 8, 128),),
-        scaled_own, sums, *text, back, scratch=copies[:1], grant=16,
+        scaled_own, sums, text, back, grant=16,
     )
     image_parts = [send(p, along_second(-k), "rsecond") for p, k in zip(lows, OFFSETS)]
     text_own, text_far, low = local(
@@ -322,7 +330,7 @@
     )
     image_grad, text_grad, loss, bias_grad, temp_grad = local(
         finish_kernel, (f32(pairs, width),) * 2 + (f32(1),) * 3,
-        scalars, image_raw, image_own, *image_parts, text_raw, text_own, send(far_low, swap, "rpair"), sums,
+        log_temp, image_raw, image_own, *image_parts, text_raw, text_own, send(far_low, swap, "rpair"), sums,
     )
     return (loss, image_grad, text_grad, temp_grad, bias_grad)
 

time: 87.2 us -> 85.8 us (0.984); the launches traced: 86.9 us -> 84.6 us
  Pallas kernels: 15.3 us -> 13.6 us
    pallas_call x14, Pallas kernels: 15.3 us -> 13.6 us  [local(): pl.pallas_call(kernel, out_shape=out_shape, in_specs=[SMEM if a.shape ==...]
where the time goes in v6:
time: 85.8 us; the launch traced here: 84.6 us
  starting transfers between devices  41.6 us (48%)
  waiting for transfers between devices  19.4 us (23%)
  Pallas kernels  13.6 us (16%)
  local copies, waits for them, and re-layouts  5.88 us (7%)
  between operations  4.05 us (5%)
    ppermute x26, starting transfers between devices, send(): return lax.ppermute(value, AXES, pairs)  36.5 us
    ppermute x26, waiting for transfers between devices, send(): return lax.ppermute(value, AXES, pairs)  17.3 us
    pallas_call x14, Pallas kernels, local(): pl.pallas_call(kernel, out_shape=out_shape, in_specs=[SMEM if a.shape ==...  13.6 us
    all_to_all x1, starting transfers between devices, body(): lax.all_to_all(spread, AXES, 0, 0, tiled=True, axis_index_groups=across())  5.13 us
    unnamed x22, local copies, waits for them, and re-layouts  4.15 us
    all_to_all x1, waiting for transfers between devices, body(): lax.all_to_all(spread, AXES, 0, 0, tiled=True, axis_index_groups=across())  2.13 us
  transfers between devices with their start and end apart: 27, of which 10 were waited for; matrix products, arithmetic and copies ran while one was open for 2% of the time, Pallas kernels for 11%

profile of v6, /device:TPU:6, one launch (start us, length us, event | category | flops | bytes accessed | tf_op | source)
XLA Modules:
  0.0 84.6 jit_solution(775617666422951104)
XLA Ops:
  0.7 1.0 %copy-done.1 = f32[48,1152]{1,0:T(8,128)S(1)} copy-done((f32[48,1152]{1,0:T(8,128)S(1)}, f32[48,1152]{1,0:T(8,128)}, u32[]{:S(2)}) %copy-start.1) | copy-done | bytes 221208
  1.6 0.1 shard_map.101
  3.7 0.1 stack.167
  3.8 0.1 shard_map.102
  4.0 1.5 %collective-permute-start.3 = (bf16[48,1152]{1,0:T(8,128)(2,1)S(1)}, bf16[48,1152]{1,0:T(8,128)(2,1)S(1)}, u32[]{:S(2)}, u32[]{:S(2)}) collective-permute-start(bf16[48,1152]{1,0:T(8,128)(2,1)S(1)} %get-tuple-element.51), channel_id=1, source_target_pairs={{0,16},{1,17},{2,18},{3,19},{4,132},{5,133},{6,134},{7,135},{8,24}... | collective-permute-start | bytes 331784 | tf_op jit(solution)/shard_map/first/ppermute | solution.py:33
  5.5 2.1 %collective-permute-start.2 = (bf16[48,1152]{1,0:T(8,128)(2,1)S(1)}, bf16[48,1152]{1,0:T(8,128)(2,1)S(1)}, u32[]{:S(2)}, u32[]{:S(2)}) collective-permute-start(bf16[48,1152]{1,0:T(8,128)(2,1)S(1)} %get-tuple-element.51), channel_id=1, source_target_pairs={{0,8},{1,9},{2,10},{3,11},{4,68},{5,69},{6,70},{7,71},{8,16},{9,17... | collective-permute-start | bytes 331784 | tf_op jit(solution)/shard_map/first/ppermute | solution.py:33
  7.6 3.3 %collective-permute-start.4 = (bf16[96,1152]{1,0:T(8,128)(2,1)S(1)}, bf16[96,1152]{1,0:T(8,128)(2,1)S(1)}, u32[]{:S(2)}, u32[]{:S(2)}) collective-permute-start(bf16[96,1152]{1,0:T(8,128)(2,1)S(1)} %get-tuple-element.56), channel_id=1, source_target_pairs={{0,2},{1,3},{2,32},{3,33},{4,38},{5,39},{6,4},{7,5},{8,10},{9,11},... | collective-permute-start | bytes 663560 | tf_op jit(solution)/shard_map/z2/ppermute | solution.py:33
  10.8 0.2 collective-permute-done.2.refs_0_.i1
  11.0 2.5 %collective-permute-done.1.after.refs_1_.i2 = bf16[48,1152]{1,0:T(8,128)(2,1)S(1)} collective-permute-done((bf16[48,1152]{1,0:T(8,128)(2,1)S(1)}, bf16[48,1152]{1,0:T(8,128)(2,1)S(1)}, u32[]{:S(2)}, u32[]{:S(2)}) %collective-permute-start.1) | collective-permute-done | bytes 110624 | tf_op jit(solution)/shard_map/first/ppermute | solution.py:33
  13.5 2.1 %collective-permute-start.5 = (f32[8,128]{1,0:T(8,128)S(1)}, f32[8,128]{1,0:T(8,128)S(1)}, u32[]{:S(2)}, u32[]{:S(2)}) collective-permute-start(f32[8,128]{1,0:T(8,128)S(1)} %shard_map.104), channel_id=1, source_target_pairs={{0,4},{1,5},{2,6},{3,7},{4,0},{5,1},{6,2},{7,3},{8,12},{9,13},{10,... | collective-permute-start | bytes 12296 | tf_op jit(solution)/shard_map/flag/ppermute | solution.py:33
  15.9 0.6 gather_fusion
  16.5 0.6 gather_fusion.1
  17.2 1.2 %collective-permute-done.4.pair_2 = bf16[96,1152]{1,0:T(8,128)(2,1)S(1)} collective-permute-done((bf16[96,1152]{1,0:T(8,128)(2,1)S(1)}, bf16[96,1152]{1,0:T(8,128)(2,1)S(1)}, u32[]{:S(2)}, u32[]{:S(2)}) %collective-permute-start.4) | collective-permute-done | bytes 221216 | tf_op jit(solution)/shard_map/z2/ppermute | solution.py:33
  18.5 1.7 %collective-permute-start.8 = (bf16[192,1152]{1,0:T(8,128)(2,1)S(1)}, bf16[192,1152]{1,0:T(8,128)(2,1)S(1)}, u32[]{:S(2)}, u32[]{:S(2)}) collective-permute-start(bf16[192,1152]{1,0:T(8,128)(2,1)S(1)} %get-tuple-element.60.refs_3_.src), channel_id=1, source_target_pairs={{0,64},{1,65},{2,66},{3,67},{4,12},{5,13},{6,14},{7,15},{8,72},{9,... | collective-permute-start | bytes 1327112 | tf_op jit(solution)/shard_map/second/ppermute | solution.py:33
  20.1 2.9 %collective-permute-start.10 = (bf16[192,1152]{1,0:T(8,128)(2,1)S(1)}, bf16[192,1152]{1,0:T(8,128)(2,1)S(1)}, u32[]{:S(2)}, u32[]{:S(2)}) collective-permute-start(bf16[192,1152]{1,0:T(8,128)(2,1)S(1)} %get-tuple-element.60.refs_3_.src), channel_id=1, source_target_pairs={{0,128},{1,129},{2,130},{3,131},{4,20},{5,21},{6,22},{7,23},{8,136... | collective-permute-start | bytes 1327112 | tf_op jit(solution)/shard_map/second/ppermute | solution.py:33
  23.0 1.3 %collective-permute-start.9 = (bf16[192,1152]{1,0:T(8,128)(2,1)S(1)}, bf16[192,1152]{1,0:T(8,128)(2,1)S(1)}, u32[]{:S(2)}, u32[]{:S(2)}) collective-permute-start(bf16[192,1152]{1,0:T(8,128)(2,1)S(1)} %get-tuple-element.60.refs_3_.src), channel_id=1, source_target_pairs={{0,192},{1,193},{2,194},{3,195},{4,28},{5,29},{6,30},{7,31},{8,200... | collective-permute-start | bytes 1327112 | tf_op jit(solution)/shard_map/second/ppermute | solution.py:33
  24.4 2.7 %collective-permute-start.6 = (bf16[48,1152]{1,0:T(8,128)(2,1)S(1)}, bf16[48,1152]{1,0:T(8,128)(2,1)S(1)}, u32[]{:S(2)}, u32[]{:S(2)}) collective-permute-start(bf16[48,1152]{1,0:T(8,128)(2,1)S(1)} %get-tuple-element.58), channel_id=1, source_target_pairs={{0,2},{1,3},{2,32},{3,33},{4,38},{5,39},{6,4},{7,5},{8,10},{9,11},... | collective-permute-start | bytes 331784 | tf_op jit(solution)/shard_map/z4/ppermute | solution.py:33
  27.0 0.5 collective-permute-start.7
  27.5 0.6 collective-permute-done.8.refs_4_.after
  28.1 0.2 collective-permute-start.11
  28.3 5.7 %collective-permute-done.10.refs_6_ = bf16[192,1152]{1,0:T(8,128)(2,1)S(1)} collective-permute-done((bf16[192,1152]{1,0:T(8,128)(2,1)S(1)}, bf16[192,1152]{1,0:T(8,128)(2,1)S(1)}, u32[]{:S(2)}, u32[]{:S(2)}) %collective-permute-start.10) | collective-permute-done | bytes 442400 | tf_op jit(solution)/shard_map/second/ppermute | solution.py:33
  34.0 0.8 collective-permute-start.13
  34.8 0.1 collective-permute-start.12
  36.2 1.5 %collective-permute-done.7.refs_2_ = bf16[192,1152]{1,0:T(8,128)(2,1)S(1)} collective-permute-done((bf16[192,1152]{1,0:T(8,128)(2,1)S(1)}, bf16[192,1152]{1,0:T(8,128)(2,1)S(1)}, u32[]{:S(2)}, u32[]{:S(2)}) %collective-permute-start.7) | collective-permute-done | bytes 442400 | tf_op jit(solution)/shard_map/z1/ppermute | solution.py:33
  37.8 2.3 %shard_map.106 = (bf16[384,768]{1,0:T(8,128)(2,1)S(1)}, f32[3,8,768]{2,1,0:T(8,128)S(1)}, bf16[384,1152]{1,0:T(8,128)(2,1)S(1)}, bf16[768,1152]{1,0:T(8,128)(2,1)S(1)}) custom-call(f32[1]{0:T(128)S(6)} %copy.11.log_temp, f32[1]{0:T(128)S(6)} %copy.12.bias, s32[1,384]{1,0:T(1,128)S(1)} %reshape.1562.rows_after.rows_id, ...), custom_call_target="tpu_custom_call" | custom-call | tf_op jit(solution)/shard_map/pallas_call | solution.py:244
  40.1 3.1 %shard_map.108 = (bf16[784,1152]{1,0:T(8,128)(2,1)S(1)}, bf16[384,768]{1,0:T(8,128)(2,1)S(1)}, f32[8,128]{1,0:T(8,128)S(1)}, bf16[768,1152]{1,0:T(8,128)(2,1)S(1)}) custom-call(f32[1]{0:T(128)S(6)} %copy.11.log_temp, f32[1]{0:T(128)S(6)} %copy.12.bias, s32[1,384]{1,0:T(1,128)S(1)} %reshape.1562.rows_after.rows_id, ...), custom_call_target="tpu_custom_call" | custom-call | tf_op jit(solution)/shard_map/pallas_call | solution.py:244
  43.4 2.5 %shard_map.111 = (f32[48,1152]{1,0:T(8,128)S(1)}, f32[96,1152]{1,0:T(8,128)S(1)}, bf16[48,1152]{1,0:T(8,128)(2,1)S(1)}, bf16[192,1152]{1,0:T(8,128)(2,1)}) custom-call(bf16[384,768]{1,0:T(8,128)(2,1)S(1)} %get-tuple-element.61.scaled.scaled_own, bf16[384,768]{1,0:T(8,128)(2,1)S(1)} %get-tuple-element.75.scaled_far, ...), custom_call_target="tpu_custom_call" | custom-call | tf_op jit(solution)/shard_map/pallas_call | solution.py:244
  45.8 2.4 %collective-permute-start.22 = (bf16[192,1152]{1,0:T(8,128)(2,1)}, bf16[192,1152]{1,0:T(8,128)(2,1)}, u32[]{:S(2)}, u32[]{:S(2)}) collective-permute-start(bf16[192,1152]{1,0:T(8,128)(2,1)} %get-tuple-element.80), channel_id=1, source_target_pairs={{0,35},{1,0},{2,1},{3,2},{4,5},{5,6},{6,7},{7,36},{8,43},{9,8},{10... | collective-permute-start | bytes 1327112 | tf_op jit(solution)/shard_map/rz1/ppermute | solution.py:33
  48.3 2.3 %shard_map.109 = (f32[192,1152]{1,0:T(8,128)S(1)}, bf16[192,1152]{1,0:T(8,128)(2,1)}, bf16[192,1152]{1,0:T(8,128)(2,1)}, bf16[192,1152]{1,0:T(8,128)(2,1)}, f32[32,8,128]{2,1,0:T(8,128)}) custom-call(bf16[384,768]{1,0:T(8,128)(2,1)S(1)} %get-tuple-element.61.scaled.scaled_own, f32[8,128]{1,0:T(8,128)S(1)} %get-tuple-element.64.sums, ...), custom_call_target="tpu_custom_call" | custom-call | tf_op jit(solution)/shard_map/pallas_call | solution.py:244
  50.6 1.8 %collective-permute-start.16 = (bf16[192,1152]{1,0:T(8,128)(2,1)}, bf16[192,1152]{1,0:T(8,128)(2,1)S(1)}, u32[]{:S(2)}, u32[]{:S(2)}) collective-permute-start(bf16[192,1152]{1,0:T(8,128)(2,1)} %get-tuple-element.67), channel_id=1, source_target_pairs={{0,192},{1,193},{2,194},{3,195},{4,28},{5,29},{6,30},{7,31},{8,200... | collective-permute-start | bytes 1327112 | tf_op jit(solution)/shard_map/rsecond/ppermute | solution.py:33
  52.4 0.2 collective-permute-start.17
  52.6 2.4 %collective-permute-start.18 = (bf16[192,1152]{1,0:T(8,128)(2,1)}, bf16[192,1152]{1,0:T(8,128)(2,1)S(1)}, u32[]{:S(2)}, u32[]{:S(2)}) collective-permute-start(bf16[192,1152]{1,0:T(8,128)(2,1)} %get-tuple-element.69), channel_id=1, source_target_pairs={{0,128},{1,129},{2,130},{3,131},{4,20},{5,21},{6,22},{7,23},{8,136... | collective-permute-start | bytes 1327112 | tf_op jit(solution)/shard_map/rsecond/ppermute | solution.py:33
  55.0 2.2 %collective-permute-start.23 = (bf16[48,1152]{1,0:T(8,128)(2,1)S(1)}, bf16[48,1152]{1,0:T(8,128)(2,1)S(1)}, u32[]{:S(2)}, u32[]{:S(2)}) collective-permute-start(bf16[48,1152]{1,0:T(8,128)(2,1)S(1)} %get-tuple-element.81), channel_id=1, source_target_pairs={{0,34},{1,35},{2,0},{3,1},{4,6},{5,7},{6,36},{7,37},{8,42},{9,43},... | collective-permute-start | bytes 331784 | tf_op jit(solution)/shard_map/rz4/ppermute | solution.py:33
  57.1 5.1 %all-to-all-start = ((f32[32,8,128]{2,1,0:T(8,128)}), f32[32,8,128]{2,1,0:T(8,128)S(1)}, u32[]{:S(2)}, u32[]{:S(2)}) async-start(f32[32,8,128]{2,1,0:T(8,128)} %get-tuple-element.70), calls=%async_computation | async-start | bytes 262144 | tf_op jit(solution)/shard_map/terms/all_to_all | solution.py:322
  62.3 0.6 copy-done.7
  62.9 0.9 %copy-done.6 = f32[48,1152]{1,0:T(8,128)S(1)} copy-done((f32[48,1152]{1,0:T(8,128)S(1)}, f32[48,1152]{1,0:T(8,128)}, u32[]{:S(2)}) %copy-start.6) | copy-done | bytes 221208
  63.8 0.9 %copy-done.8 = bf16[48,1152]{1,0:T(8,128)(2,1)S(1)} copy-done((bf16[48,1152]{1,0:T(8,128)(2,1)S(1)}, bf16[48,1152]{1,0:T(8,128)(2,1)}, u32[]{:S(2)}) %copy-start.8) | copy-done | bytes 110616
  64.7 1.8 %shard_map.112 = (f32[48,1152]{1,0:T(8,128)S(1)}, f32[48,1152]{1,0:T(8,128)S(1)}, bf16[96,1152]{1,0:T(8,128)(2,1)}) custom-call(f32[48,1152]{1,0:T(8,128)S(1)} %copy-done.6, f32[96,1152]{1,0:T(8,128)S(1)} %get-tuple-element.79.pair, bf16[192,1152]{1,0:T(8,128)(2,1)} %collective-permute-done.22.back, bf16[48,1152]{1,0:T(8,128)(2,1)S(1)} %copy-done.8), custom_call_target="tpu_custom_call" | custom-call | tf_op jit(solution)/shard_map/pallas_call | solution.py:244
  66.5 0.7 copy-done.3
  67.2 3.9 %collective-permute-start.24 = (bf16[96,1152]{1,0:T(8,128)(2,1)}, bf16[96,1152]{1,0:T(8,128)(2,1)S(1)}, u32[]{:S(2)}, u32[]{:S(2)}) collective-permute-start(bf16[96,1152]{1,0:T(8,128)(2,1)} %get-tuple-element.84), channel_id=1, source_target_pairs={{0,34},{1,35},{2,0},{3,1},{4,6},{5,7},{6,36},{7,37},{8,42},{9,43},... | collective-permute-start | bytes 663560 | tf_op jit(solution)/shard_map/rz2/ppermute | solution.py:33
  71.1 2.1 %all-to-all-done.terms = f32[32,8,128]{2,1,0:T(8,128)S(1)} async-done(((f32[32,8,128]{2,1,0:T(8,128)}), f32[32,8,128]{2,1,0:T(8,128)S(1)}, u32[]{:S(2)}, u32[]{:S(2)}) %all-to-all-start) | async-done | bytes 131104 | tf_op jit(solution)/shard_map/terms/all_to_all | solution.py:322
  73.2 0.2 shard_map.110
  73.5 3.2 %collective-permute-start.20 = (bf16[64,1152]{1,0:T(8,128)(2,1)S(1)}, bf16[64,1152]{1,0:T(8,128)(2,1)S(1)}, u32[]{:S(2)}, u32[]{:S(2)}) collective-permute-start(bf16[64,1152]{1,0:T(8,128)(2,1)S(1)} %get-tuple-element.73), channel_id=1, source_target_pairs={{0,8},{1,9},{2,10},{3,11},{4,68},{5,69},{6,70},{7,71},{8,16},{9,17... | collective-permute-start | bytes 442376 | tf_op jit(solution)/shard_map/rfirst/ppermute | solution.py:33
  76.8 0.9 %collective-permute-start.21 = (bf16[64,1152]{1,0:T(8,128)(2,1)S(1)}, bf16[64,1152]{1,0:T(8,128)(2,1)S(1)}, u32[]{:S(2)}, u32[]{:S(2)}) collective-permute-start(bf16[64,1152]{1,0:T(8,128)(2,1)S(1)} %get-tuple-element.74), channel_id=1, source_target_pairs={{0,16},{1,17},{2,18},{3,19},{4,132},{5,133},{6,134},{7,135},{8,24}... | collective-permute-start | bytes 442376 | tf_op jit(solution)/shard_map/rfirst/ppermute | solution.py:33
  77.8 1.3 %collective-permute-done.25.t1 = bf16[48,1152]{1,0:T(8,128)(2,1)S(1)} collective-permute-done((bf16[48,1152]{1,0:T(8,128)(2,1)S(1)}, bf16[48,1152]{1,0:T(8,128)(2,1)S(1)}, u32[]{:S(2)}, u32[]{:S(2)}) %collective-permute-start.25) | collective-permute-done | bytes 110624 | tf_op jit(solution)/shard_map/rpair/ppermute | solution.py:33
  79.1 0.8 collective-permute-done.19.i1
  79.9 3.5 %collective-permute-done.21.i3 = bf16[64,1152]{1,0:T(8,128)(2,1)S(1)} collective-permute-done((bf16[64,1152]{1,0:T(8,128)(2,1)S(1)}, bf16[64,1152]{1,0:T(8,128)(2,1)S(1)}, u32[]{:S(2)}, u32[]{:S(2)}) %collective-permute-start.21) | collective-permute-done | bytes 147488 | tf_op jit(solution)/shard_map/rfirst/ppermute | solution.py:33
  83.4 1.0 %shard_map.114 = (f32[48,1152]{1,0:T(8,128)}, f32[48,1152]{1,0:T(8,128)}, f32[1]{0:T(128)}, f32[1]{0:T(128)}, f32[1]{0:T(128)}) custom-call(f32[1]{0:T(128)S(6)} %copy.11.log_temp, f32[48,1152]{1,0:T(8,128)S(1)} %copy-done, f32[48,1152]{1,0:T(8,128)S(1)} %get-tuple-element.71.after.image_own, bf16[64,1152]{1,0:T(8,128)(2,1)S(1)} %collective-permute-done.19.i1, ...), custom_call_target="tpu_custom_call" | custom-call | tf_op jit(solution)/shard_map/pallas_call | solution.py:244
  (55 shorter events, 1.1 us)
Async XLA Ops:
  0.6 3.2 %copy-start = (f32[48,1152]{1,0:T(8,128)S(1)}, f32[48,1152]{1,0:T(8,128)}, u32[]{:S(2)}) copy-start(f32[48,1152]{1,0:T(8,128)} %image_raw.1) | copy-start | bytes 663556
  0.6 1.0 %copy-start.1 = (f32[48,1152]{1,0:T(8,128)S(1)}, f32[48,1152]{1,0:T(8,128)}, u32[]{:S(2)}) copy-start(f32[48,1152]{1,0:T(8,128)} %text_raw.1) | copy-start | bytes 663556
  1.6 14.0 %copy-start.9 = (s32[12288]{0:T(1024)S(1)}, s32[12288]{0:T(1024)}, u32[]{:S(2)}) copy-start(s32[12288]{0:T(1024)} %param.8) | copy-start | bytes 147460
  1.6 14.1 %copy-start.10 = (s32[12288]{0:T(1024)S(1)}, s32[12288]{0:T(1024)}, u32[]{:S(2)}) copy-start(s32[12288]{0:T(1024)} %param.9) | copy-start | bytes 147460
  1.8 2.1 %collective-permute-start = (bf16[48,1152]{1,0:T(8,128)(2,1)S(1)}, bf16[48,1152]{1,0:T(8,128)(2,1)S(1)}, u32[]{:S(2)}, u32[]{:S(2)}) collective-permute-start(bf16[48,1152]{1,0:T(8,128)(2,1)S(1)} %get-tuple-element.50), channel_id=1, source_target_pairs={{0,4},{1,5},{2,6},{3,7},{4,0},{5,1},{6,2},{7,3},{8,12},{9,13},{10,... | collective-permute-start | bytes 331784 | tf_op jit(solution)/shard_map/pair/ppermute | solution.py:33
  4.0 6.9 %collective-permute-start.3 = (bf16[48,1152]{1,0:T(8,128)(2,1)S(1)}, bf16[48,1152]{1,0:T(8,128)(2,1)S(1)}, u32[]{:S(2)}, u32[]{:S(2)}) collective-permute-start(bf16[48,1152]{1,0:T(8,128)(2,1)S(1)} %get-tuple-element.51), channel_id=1, source_target_pairs={{0,16},{1,17},{2,18},{3,19},{4,132},{5,133},{6,134},{7,135},{8,24}... | collective-permute-start | bytes 331784 | tf_op jit(solution)/shard_map/first/ppermute | solution.py:33
  5.5 5.6 %collective-permute-start.2 = (bf16[48,1152]{1,0:T(8,128)(2,1)S(1)}, bf16[48,1152]{1,0:T(8,128)(2,1)S(1)}, u32[]{:S(2)}, u32[]{:S(2)}) collective-permute-start(bf16[48,1152]{1,0:T(8,128)(2,1)S(1)} %get-tuple-element.51), channel_id=1, source_target_pairs={{0,8},{1,9},{2,10},{3,11},{4,68},{5,69},{6,70},{7,71},{8,16},{9,17... | collective-permute-start | bytes 331784 | tf_op jit(solution)/shard_map/first/ppermute | solution.py:33
  7.6 6.0 %collective-permute-start.1 = (bf16[48,1152]{1,0:T(8,128)(2,1)S(1)}, bf16[48,1152]{1,0:T(8,128)(2,1)S(1)}, u32[]{:S(2)}, u32[]{:S(2)}) collective-permute-start(bf16[48,1152]{1,0:T(8,128)(2,1)S(1)} %get-tuple-element.51), channel_id=1, source_target_pairs={{0,24},{1,25},{2,26},{3,27},{4,196},{5,197},{6,198},{7,199},{8,0},... | collective-permute-start | bytes 331784 | tf_op jit(solution)/shard_map/first/ppermute | solution.py:33
  7.6 10.8 %collective-permute-start.4 = (bf16[96,1152]{1,0:T(8,128)(2,1)S(1)}, bf16[96,1152]{1,0:T(8,128)(2,1)S(1)}, u32[]{:S(2)}, u32[]{:S(2)}) collective-permute-start(bf16[96,1152]{1,0:T(8,128)(2,1)S(1)} %get-tuple-element.56), channel_id=1, source_target_pairs={{0,2},{1,3},{2,32},{3,33},{4,38},{5,39},{6,4},{7,5},{8,10},{9,11},... | collective-permute-start | bytes 663560 | tf_op jit(solution)/shard_map/z2/ppermute | solution.py:33
  13.5 3.7 %collective-permute-start.5 = (f32[8,128]{1,0:T(8,128)S(1)}, f32[8,128]{1,0:T(8,128)S(1)}, u32[]{:S(2)}, u32[]{:S(2)}) collective-permute-start(f32[8,128]{1,0:T(8,128)S(1)} %shard_map.104), channel_id=1, source_target_pairs={{0,4},{1,5},{2,6},{3,7},{4,0},{5,1},{6,2},{7,3},{8,12},{9,13},{10,... | collective-permute-start | bytes 12296 | tf_op jit(solution)/shard_map/flag/ppermute | solution.py:33
  18.5 9.6 %collective-permute-start.8 = (bf16[192,1152]{1,0:T(8,128)(2,1)S(1)}, bf16[192,1152]{1,0:T(8,128)(2,1)S(1)}, u32[]{:S(2)}, u32[]{:S(2)}) collective-permute-start(bf16[192,1152]{1,0:T(8,128)(2,1)S(1)} %get-tuple-element.60.refs_3_.src), channel_id=1, source_target_pairs={{0,64},{1,65},{2,66},{3,67},{4,12},{5,13},{6,14},{7,15},{8,72},{9,... | collective-permute-start | bytes 1327112 | tf_op jit(solution)/shard_map/second/ppermute | solution.py:33
  20.1 13.9 %collective-permute-start.10 = (bf16[192,1152]{1,0:T(8,128)(2,1)S(1)}, bf16[192,1152]{1,0:T(8,128)(2,1)S(1)}, u32[]{:S(2)}, u32[]{:S(2)}) collective-permute-start(bf16[192,1152]{1,0:T(8,128)(2,1)S(1)} %get-tuple-element.60.refs_3_.src), channel_id=1, source_target_pairs={{0,128},{1,129},{2,130},{3,131},{4,20},{5,21},{6,22},{7,23},{8,136... | collective-permute-start | bytes 1327112 | tf_op jit(solution)/shard_map/second/ppermute | solution.py:33
  23.0 11.0 %collective-permute-start.9 = (bf16[192,1152]{1,0:T(8,128)(2,1)S(1)}, bf16[192,1152]{1,0:T(8,128)(2,1)S(1)}, u32[]{:S(2)}, u32[]{:S(2)}) collective-permute-start(bf16[192,1152]{1,0:T(8,128)(2,1)S(1)} %get-tuple-element.60.refs_3_.src), channel_id=1, source_target_pairs={{0,192},{1,193},{2,194},{3,195},{4,28},{5,29},{6,30},{7,31},{8,200... | collective-permute-start | bytes 1327112 | tf_op jit(solution)/shard_map/second/ppermute | solution.py:33
  24.4 10.4 %collective-permute-start.6 = (bf16[48,1152]{1,0:T(8,128)(2,1)S(1)}, bf16[48,1152]{1,0:T(8,128)(2,1)S(1)}, u32[]{:S(2)}, u32[]{:S(2)}) collective-permute-start(bf16[48,1152]{1,0:T(8,128)(2,1)S(1)} %get-tuple-element.58), channel_id=1, source_target_pairs={{0,2},{1,3},{2,32},{3,33},{4,38},{5,39},{6,4},{7,5},{8,10},{9,11},... | collective-permute-start | bytes 331784 | tf_op jit(solution)/shard_map/z4/ppermute | solution.py:33
  27.0 10.7 %collective-permute-start.7 = (bf16[192,1152]{1,0:T(8,128)(2,1)S(1)}, bf16[192,1152]{1,0:T(8,128)(2,1)S(1)}, u32[]{:S(2)}, u32[]{:S(2)}) collective-permute-start(bf16[192,1152]{1,0:T(8,128)(2,1)S(1)} %get-tuple-element.59), channel_id=1, source_target_pairs={{0,1},{1,2},{2,3},{3,32},{4,39},{5,4},{6,5},{7,6},{8,9},{9,10},{10... | collective-permute-start | bytes 1327112 | tf_op jit(solution)/shard_map/z1/ppermute | solution.py:33
  28.1 12.0 %collective-permute-start.11 = (bf16[192,1152]{1,0:T(8,128)(2,1)S(1)}, bf16[192,1152]{1,0:T(8,128)(2,1)S(1)}, u32[]{:S(2)}, u32[]{:S(2)}) collective-permute-start(bf16[192,1152]{1,0:T(8,128)(2,1)S(1)} %shard_map.107), channel_id=1, source_target_pairs={{0,4},{1,5},{2,6},{3,7},{4,0},{5,1},{6,2},{7,3},{8,12},{9,13},{10,... | collective-permute-start | bytes 1327112 | tf_op jit(solution)/shard_map/swap/ppermute | solution.py:33
  34.0 6.0 %collective-permute-start.14 = (bf16[192,1152]{1,0:T(8,128)(2,1)S(1)}, bf16[192,1152]{1,0:T(8,128)(2,1)S(1)}, u32[]{:S(2)}, u32[]{:S(2)}) collective-permute-start(bf16[192,1152]{1,0:T(8,128)(2,1)S(1)} %collective-permute-done.10.refs_6_), channel_id=1, source_target_pairs={{0,4},{1,5},{2,6},{3,7},{4,0},{5,1},{6,2},{7,3},{8,12},{9,13},{10,... | collective-permute-start | bytes 1327112 | tf_op jit(solution)/shard_map/swap/ppermute | solution.py:33
  34.0 6.1 %collective-permute-start.13 = (bf16[192,1152]{1,0:T(8,128)(2,1)S(1)}, bf16[192,1152]{1,0:T(8,128)(2,1)S(1)}, u32[]{:S(2)}, u32[]{:S(2)}) collective-permute-start(bf16[192,1152]{1,0:T(8,128)(2,1)S(1)} %collective-permute-done.9.refs_5_), channel_id=1, source_target_pairs={{0,4},{1,5},{2,6},{3,7},{4,0},{5,1},{6,2},{7,3},{8,12},{9,13},{10,... | collective-permute-start | bytes 1327112 | tf_op jit(solution)/shard_map/swap/ppermute | solution.py:33
  34.8 5.3 %collective-permute-start.12 = (bf16[192,1152]{1,0:T(8,128)(2,1)S(1)}, bf16[192,1152]{1,0:T(8,128)(2,1)S(1)}, u32[]{:S(2)}, u32[]{:S(2)}) collective-permute-start(bf16[192,1152]{1,0:T(8,128)(2,1)S(1)} %collective-permute-done.8.refs_4_.after), channel_id=1, source_target_pairs={{0,4},{1,5},{2,6},{3,7},{4,0},{5,1},{6,2},{7,3},{8,12},{9,13},{10,... | collective-permute-start | bytes 1327112 | tf_op jit(solution)/shard_map/swap/ppermute | solution.py:33
  43.3 5.0 %collective-permute-start.15 = (bf16[784,1152]{1,0:T(8,128)(2,1)S(1)}, bf16[784,1152]{1,0:T(8,128)(2,1)S(1)}, u32[]{:S(2)}, u32[]{:S(2)}) collective-permute-start(bf16[784,1152]{1,0:T(8,128)(2,1)S(1)} %get-tuple-element.65), channel_id=1, source_target_pairs={{0,4},{1,5},{2,6},{3,7},{4,0},{5,1},{6,2},{7,3},{8,12},{9,13},{10,... | collective-permute-start | bytes 5419016 | tf_op jit(solution)/shard_map/rswap/ppermute | solution.py:33
  45.8 6.7 %copy-start.5 = (f32[48,1152]{1,0:T(8,128)}, f32[48,1152]{1,0:T(8,128)S(1)}, u32[]{:S(2)}) copy-start(f32[48,1152]{1,0:T(8,128)S(1)} %get-tuple-element.78.own) | copy-start | bytes 663556
  45.8 17.1 %collective-permute-start.22 = (bf16[192,1152]{1,0:T(8,128)(2,1)}, bf16[192,1152]{1,0:T(8,128)(2,1)}, u32[]{:S(2)}, u32[]{:S(2)}) collective-permute-start(bf16[192,1152]{1,0:T(8,128)(2,1)} %get-tuple-element.80), channel_id=1, source_target_pairs={{0,35},{1,0},{2,1},{3,2},{4,5},{5,6},{6,7},{7,36},{8,43},{9,8},{10... | collective-permute-start | bytes 1327112 | tf_op jit(solution)/shard_map/rz1/ppermute | solution.py:33
  50.6 22.7 %collective-permute-start.16 = (bf16[192,1152]{1,0:T(8,128)(2,1)}, bf16[192,1152]{1,0:T(8,128)(2,1)S(1)}, u32[]{:S(2)}, u32[]{:S(2)}) collective-permute-start(bf16[192,1152]{1,0:T(8,128)(2,1)} %get-tuple-element.67), channel_id=1, source_target_pairs={{0,192},{1,193},{2,194},{3,195},{4,28},{5,29},{6,30},{7,31},{8,200... | collective-permute-start | bytes 1327112 | tf_op jit(solution)/shard_map/rsecond/ppermute | solution.py:33
  52.4 20.9 %collective-permute-start.17 = (bf16[192,1152]{1,0:T(8,128)(2,1)}, bf16[192,1152]{1,0:T(8,128)(2,1)S(1)}, u32[]{:S(2)}, u32[]{:S(2)}) collective-permute-start(bf16[192,1152]{1,0:T(8,128)(2,1)} %get-tuple-element.68), channel_id=1, source_target_pairs={{0,64},{1,65},{2,66},{3,67},{4,12},{5,13},{6,14},{7,15},{8,72},{9,... | collective-permute-start | bytes 1327112 | tf_op jit(solution)/shard_map/rsecond/ppermute | solution.py:33
  52.6 20.6 %collective-permute-start.18 = (bf16[192,1152]{1,0:T(8,128)(2,1)}, bf16[192,1152]{1,0:T(8,128)(2,1)S(1)}, u32[]{:S(2)}, u32[]{:S(2)}) collective-permute-start(bf16[192,1152]{1,0:T(8,128)(2,1)} %get-tuple-element.69), channel_id=1, source_target_pairs={{0,128},{1,129},{2,130},{3,131},{4,20},{5,21},{6,22},{7,23},{8,136... | collective-permute-start | bytes 1327112 | tf_op jit(solution)/shard_map/rsecond/ppermute | solution.py:33
  55.0 7.3 %collective-permute-start.23 = (bf16[48,1152]{1,0:T(8,128)(2,1)S(1)}, bf16[48,1152]{1,0:T(8,128)(2,1)S(1)}, u32[]{:S(2)}, u32[]{:S(2)}) collective-permute-start(bf16[48,1152]{1,0:T(8,128)(2,1)S(1)} %get-tuple-element.81), channel_id=1, source_target_pairs={{0,34},{1,35},{2,0},{3,1},{4,6},{5,7},{6,36},{7,37},{8,42},{9,43},... | collective-permute-start | bytes 331784 | tf_op jit(solution)/shard_map/rz4/ppermute | solution.py:33
  57.1 16.1 %all-to-all-start = ((f32[32,8,128]{2,1,0:T(8,128)}), f32[32,8,128]{2,1,0:T(8,128)S(1)}, u32[]{:S(2)}, u32[]{:S(2)}) async-start(f32[32,8,128]{2,1,0:T(8,128)} %get-tuple-element.70), calls=%async_computation | async-start | bytes 262144 | tf_op jit(solution)/shard_map/terms/all_to_all | solution.py:322
  62.3 0.6 copy-start.7
  62.9 0.9 %copy-start.6 = (f32[48,1152]{1,0:T(8,128)S(1)}, f32[48,1152]{1,0:T(8,128)}, u32[]{:S(2)}) copy-start(f32[48,1152]{1,0:T(8,128)} %copy-done.5) | copy-start | bytes 663556
  63.8 0.9 %copy-start.8 = (bf16[48,1152]{1,0:T(8,128)(2,1)S(1)}, bf16[48,1152]{1,0:T(8,128)(2,1)}, u32[]{:S(2)}) copy-start(bf16[48,1152]{1,0:T(8,128)(2,1)} %copy-done.7) | copy-start | bytes 331780
  66.5 0.7 copy-start.3
  67.2 16.2 %copy-start.2 = (f32[48,1152]{1,0:T(8,128)S(1)}, f32[48,1152]{1,0:T(8,128)}, u32[]{:S(2)}) copy-start(f32[48,1152]{1,0:T(8,128)} %text_raw.1) | copy-start | bytes 663556
  67.2 10.5 %copy-start.4 = (f32[48,1152]{1,0:T(8,128)S(1)}, f32[48,1152]{1,0:T(8,128)}, u32[]{:S(2)}) copy-start(f32[48,1152]{1,0:T(8,128)} %copy-done.3) | copy-start | bytes 663556
  67.2 10.4 %collective-permute-start.24 = (bf16[96,1152]{1,0:T(8,128)(2,1)}, bf16[96,1152]{1,0:T(8,128)(2,1)S(1)}, u32[]{:S(2)}, u32[]{:S(2)}) collective-permute-start(bf16[96,1152]{1,0:T(8,128)(2,1)} %get-tuple-element.84), channel_id=1, source_target_pairs={{0,34},{1,35},{2,0},{3,1},{4,6},{5,7},{6,36},{7,37},{8,42},{9,43},... | collective-permute-start | bytes 663560 | tf_op jit(solution)/shard_map/rz2/ppermute | solution.py:33
  73.4 6.4 %collective-permute-start.19 = (bf16[64,1152]{1,0:T(8,128)(2,1)S(1)}, bf16[64,1152]{1,0:T(8,128)(2,1)S(1)}, u32[]{:S(2)}, u32[]{:S(2)}) collective-permute-start(bf16[64,1152]{1,0:T(8,128)(2,1)S(1)} %get-tuple-element.72), channel_id=1, source_target_pairs={{0,24},{1,25},{2,26},{3,27},{4,196},{5,197},{6,198},{7,199},{8,0},... | collective-permute-start | bytes 442376 | tf_op jit(solution)/shard_map/rfirst/ppermute | solution.py:33
  73.5 6.3 %collective-permute-start.20 = (bf16[64,1152]{1,0:T(8,128)(2,1)S(1)}, bf16[64,1152]{1,0:T(8,128)(2,1)S(1)}, u32[]{:S(2)}, u32[]{:S(2)}) collective-permute-start(bf16[64,1152]{1,0:T(8,128)(2,1)S(1)} %get-tuple-element.73), channel_id=1, source_target_pairs={{0,8},{1,9},{2,10},{3,11},{4,68},{5,69},{6,70},{7,71},{8,16},{9,17... | collective-permute-start | bytes 442376 | tf_op jit(solution)/shard_map/rfirst/ppermute | solution.py:33
  76.8 6.6 %collective-permute-start.21 = (bf16[64,1152]{1,0:T(8,128)(2,1)S(1)}, bf16[64,1152]{1,0:T(8,128)(2,1)S(1)}, u32[]{:S(2)}, u32[]{:S(2)}) collective-permute-start(bf16[64,1152]{1,0:T(8,128)(2,1)S(1)} %get-tuple-element.74), channel_id=1, source_target_pairs={{0,16},{1,17},{2,18},{3,19},{4,132},{5,133},{6,134},{7,135},{8,24}... | collective-permute-start | bytes 442376 | tf_op jit(solution)/shard_map/rfirst/ppermute | solution.py:33
  77.7 1.4 %collective-permute-start.25 = (bf16[48,1152]{1,0:T(8,128)(2,1)S(1)}, bf16[48,1152]{1,0:T(8,128)(2,1)S(1)}, u32[]{:S(2)}, u32[]{:S(2)}) collective-permute-start(bf16[48,1152]{1,0:T(8,128)(2,1)S(1)} %get-tuple-element.86), channel_id=1, source_target_pairs={{0,4},{1,5},{2,6},{3,7},{4,0},{5,1},{6,2},{7,3},{8,12},{9,13},{10,... | collective-permute-start | bytes 331784 | tf_op jit(solution)/shard_map/rpair/ppermute | solution.py:33

commit v7 on v6

--- a/solution.py
+++ b/solution.py
@@ -240,7 +240,7 @@
     return jax.ShapeDtypeStruct(shape, jnp.bfloat16)
 
 
-def local(kernel, out_shape, *args, after=(), scratch=(), grant=8):
+def local(kernel, out_shape, *args, after=(), scratch=(), grant=4):
     return pl.pallas_call(
         kernel,
         out_shape=out_shape,
@@ -276,7 +276,7 @@
 
     parts = [send(image_unit, along_first(k), "first") for k in OFFSETS]
     pair_2 = send(pair, apart(2), "z2")
-    image_ids, text_ids = local(ids_kernel, (i32(256, pairs),) * 2, image_ids.reshape(256, pairs), text_ids.reshape(256, pairs), after=parts[1:2])
+    image_ids, text_ids = local(ids_kernel, (i32(256, pairs),) * 2, image_ids.reshape(256, pairs), text_ids.reshape(256, pairs), after=parts[2:3])
     cols_id = image_ids.reshape(256, pairs)[jnp.stack(cols_from)].reshape(1, 32 * pairs)
     rows_id = text_ids.reshape(256, pairs)[jnp.stack(rows_from)].reshape(1, 8 * pairs)
     (flag,) = local(flag_kernel, (f32(8, 128),), after=parts)
@@ -294,23 +294,23 @@
     scaled_own, sums, text, image = local(
         functools.partial(terms_kernel, True),
         (b16(384, 768), f32(3, 8, 768), b16(384, width), b16(768, width)),
-        log_temp, bias, rows_id, cols_id, jnp.zeros((3, 8, 768), jnp.float32), *text, *plane, grant=16,
+        log_temp, bias, rows_id, cols_id, jnp.zeros((3, 8, 768), jnp.float32), *text, *plane, grant=12,
     )
     far, scaled_far, sums, image_far = local(
         functools.partial(terms_kernel, False),
         (b16(784, width), b16(384, 768), f32(8, 128), b16(768, width)),
-        log_temp, bias, rows_id, cols_id, sums, text, *plane_far, grant=16,
+        log_temp, bias, rows_id, cols_id, sums, text, *plane_far, grant=12,
     )
     back = send(far, swap, "rswap")
     text_own, text_pair, hop, last = local(
         text_kernel, (f32(pairs, width), f32(2 * pairs, width), b16(pairs, width), b16(4 * pairs, width)),
-        scaled_own, scaled_far, image, image_far, grant=16,
+        scaled_own, scaled_far, image, image_far, grant=12,
     )
     last = send(last, apart(-1), "rz1")
     hop = send(hop, apart(-2), "rz4")
     image_own, *lows, spread = local(
         image_kernel, (f32(192, width),) + (b16(192, width),) * 3 + (f32(32, 8, 128),),
-        scaled_own, sums, text, back, grant=16,
+        scaled_own, sums, text, back, grant=12,
     )
     image_parts = [send(p, along_second(-k), "rsecond") for p, k in zip(lows, OFFSETS)]
     text_own, text_far, low = local(

time: 85.8 us -> 85 us (level)
  starting transfers between devices: 41.6 us -> 40.7 us
where the time goes in v7:
time: 85 us; the launch traced here: 84.4 us
  starting transfers between devices  40.7 us (48%)
  waiting for transfers between devices  20.1 us (24%)
  Pallas kernels  13.6 us (16%)
  local copies, waits for them, and re-layouts  5.88 us (7%)
  between operations  4.06 us (5%)
    ppermute x26, starting transfers between devices, send(): return lax.ppermute(value, AXES, pairs)  35.6 us
    ppermute x26, waiting for transfers between devices, send(): return lax.ppermute(value, AXES, pairs)  18.1 us
    pallas_call x14, Pallas kernels, local(): pl.pallas_call(kernel, out_shape=out_shape, in_specs=[SMEM if a.shape ==...  13.6 us
    all_to_all x1, starting transfers between devices, body(): lax.all_to_all(spread, AXES, 0, 0, tiled=True, axis_index_groups=across())  5.13 us
    unnamed x22, local copies, waits for them, and re-layouts  4.15 us
    all_to_all x1, waiting for transfers between devices, body(): lax.all_to_all(spread, AXES, 0, 0, tiled=True, axis_index_groups=across())  2.06 us
  transfers between devices with their start and end apart: 27, of which 10 were waited for; matrix products, arithmetic and copies ran while one was open for 2% of the time, Pallas kernels for 11%

profile of v7, /device:TPU:6, one launch (start us, length us, event | category | flops | bytes accessed | tf_op | source)
XLA Modules:
  0.0 84.4 jit_solution(9719837638895895750)
XLA Ops:
  0.7 1.0 %copy-done.1 = f32[48,1152]{1,0:T(8,128)S(1)} copy-done((f32[48,1152]{1,0:T(8,128)S(1)}, f32[48,1152]{1,0:T(8,128)}, u32[]{:S(2)}) %copy-start.1) | copy-done | bytes 221208
  1.6 0.1 shard_map.101
  3.7 0.1 stack.167
  3.8 0.1 shard_map.102
  4.0 0.9 %collective-permute-start.3 = (bf16[48,1152]{1,0:T(8,128)(2,1)S(1)}, bf16[48,1152]{1,0:T(8,128)(2,1)S(1)}, u32[]{:S(2)}, u32[]{:S(2)}) collective-permute-start(bf16[48,1152]{1,0:T(8,128)(2,1)S(1)} %get-tuple-element.51), channel_id=1, source_target_pairs={{0,24},{1,25},{2,26},{3,27},{4,196},{5,197},{6,198},{7,199},{8,0},... | collective-permute-start | bytes 331784 | tf_op jit(solution)/shard_map/first/ppermute | solution.py:33
  4.9 2.4 %collective-permute-start.2 = (bf16[48,1152]{1,0:T(8,128)(2,1)S(1)}, bf16[48,1152]{1,0:T(8,128)(2,1)S(1)}, u32[]{:S(2)}, u32[]{:S(2)}) collective-permute-start(bf16[48,1152]{1,0:T(8,128)(2,1)S(1)} %get-tuple-element.51), channel_id=1, source_target_pairs={{0,8},{1,9},{2,10},{3,11},{4,68},{5,69},{6,70},{7,71},{8,16},{9,17... | collective-permute-start | bytes 331784 | tf_op jit(solution)/shard_map/first/ppermute | solution.py:33
  7.3 0.4 collective-permute-start.1
  7.7 3.0 %collective-permute-start.4 = (bf16[96,1152]{1,0:T(8,128)(2,1)S(1)}, bf16[96,1152]{1,0:T(8,128)(2,1)S(1)}, u32[]{:S(2)}, u32[]{:S(2)}) collective-permute-start(bf16[96,1152]{1,0:T(8,128)(2,1)S(1)} %get-tuple-element.56), channel_id=1, source_target_pairs={{0,2},{1,3},{2,32},{3,33},{4,38},{5,39},{6,4},{7,5},{8,10},{9,11},... | collective-permute-start | bytes 663560 | tf_op jit(solution)/shard_map/z2/ppermute | solution.py:33
  10.8 2.8 %collective-permute-done.1.after.refs_2_.i3 = bf16[48,1152]{1,0:T(8,128)(2,1)S(1)} collective-permute-done((bf16[48,1152]{1,0:T(8,128)(2,1)S(1)}, bf16[48,1152]{1,0:T(8,128)(2,1)S(1)}, u32[]{:S(2)}, u32[]{:S(2)}) %collective-permute-start.1) | collective-permute-done | bytes 110624 | tf_op jit(solution)/shard_map/first/ppermute | solution.py:33
  13.5 0.9 %collective-permute-start.5 = (f32[8,128]{1,0:T(8,128)S(1)}, f32[8,128]{1,0:T(8,128)S(1)}, u32[]{:S(2)}, u32[]{:S(2)}) collective-permute-start(f32[8,128]{1,0:T(8,128)S(1)} %shard_map.104), channel_id=1, source_target_pairs={{0,4},{1,5},{2,6},{3,7},{4,0},{5,1},{6,2},{7,3},{8,12},{9,13},{10,... | collective-permute-start | bytes 12296 | tf_op jit(solution)/shard_map/flag/ppermute | solution.py:33
  14.7 0.6 gather_fusion
  15.3 0.6 gather_fusion.1
  16.0 2.3 %collective-permute-done.4.pair_2 = bf16[96,1152]{1,0:T(8,128)(2,1)S(1)} collective-permute-done((bf16[96,1152]{1,0:T(8,128)(2,1)S(1)}, bf16[96,1152]{1,0:T(8,128)(2,1)S(1)}, u32[]{:S(2)}, u32[]{:S(2)}) %collective-permute-start.4) | collective-permute-done | bytes 221216 | tf_op jit(solution)/shard_map/z2/ppermute | solution.py:33
  18.4 1.7 %collective-permute-start.8 = (bf16[192,1152]{1,0:T(8,128)(2,1)S(1)}, bf16[192,1152]{1,0:T(8,128)(2,1)S(1)}, u32[]{:S(2)}, u32[]{:S(2)}) collective-permute-start(bf16[192,1152]{1,0:T(8,128)(2,1)S(1)} %get-tuple-element.60.refs_3_.src), channel_id=1, source_target_pairs={{0,64},{1,65},{2,66},{3,67},{4,12},{5,13},{6,14},{7,15},{8,72},{9,... | collective-permute-start | bytes 1327112 | tf_op jit(solution)/shard_map/second/ppermute | solution.py:33
  20.0 2.9 %collective-permute-start.10 = (bf16[192,1152]{1,0:T(8,128)(2,1)S(1)}, bf16[192,1152]{1,0:T(8,128)(2,1)S(1)}, u32[]{:S(2)}, u32[]{:S(2)}) collective-permute-start(bf16[192,1152]{1,0:T(8,128)(2,1)S(1)} %get-tuple-element.60.refs_3_.src), channel_id=1, source_target_pairs={{0,128},{1,129},{2,130},{3,131},{4,20},{5,21},{6,22},{7,23},{8,136... | collective-permute-start | bytes 1327112 | tf_op jit(solution)/shard_map/second/ppermute | solution.py:33
  22.9 1.3 %collective-permute-start.9 = (bf16[192,1152]{1,0:T(8,128)(2,1)S(1)}, bf16[192,1152]{1,0:T(8,128)(2,1)S(1)}, u32[]{:S(2)}, u32[]{:S(2)}) collective-permute-start(bf16[192,1152]{1,0:T(8,128)(2,1)S(1)} %get-tuple-element.60.refs_3_.src), channel_id=1, source_target_pairs={{0,192},{1,193},{2,194},{3,195},{4,28},{5,29},{6,30},{7,31},{8,200... | collective-permute-start | bytes 1327112 | tf_op jit(solution)/shard_map/second/ppermute | solution.py:33
  24.3 2.7 %collective-permute-start.6 = (bf16[48,1152]{1,0:T(8,128)(2,1)S(1)}, bf16[48,1152]{1,0:T(8,128)(2,1)S(1)}, u32[]{:S(2)}, u32[]{:S(2)}) collective-permute-start(bf16[48,1152]{1,0:T(8,128)(2,1)S(1)} %get-tuple-element.58), channel_id=1, source_target_pairs={{0,2},{1,3},{2,32},{3,33},{4,38},{5,39},{6,4},{7,5},{8,10},{9,11},... | collective-permute-start | bytes 331784 | tf_op jit(solution)/shard_map/z4/ppermute | solution.py:33
  27.0 0.5 collective-permute-start.7
  27.4 0.6 collective-permute-done.8.refs_4_.after
  28.1 5.8 %collective-permute-done.10.refs_6_ = bf16[192,1152]{1,0:T(8,128)(2,1)S(1)} collective-permute-done((bf16[192,1152]{1,0:T(8,128)(2,1)S(1)}, bf16[192,1152]{1,0:T(8,128)(2,1)S(1)}, u32[]{:S(2)}, u32[]{:S(2)}) %collective-permute-start.10) | collective-permute-done | bytes 442400 | tf_op jit(solution)/shard_map/second/ppermute | solution.py:33
  34.0 0.5 collective-permute-start.13
  34.5 0.3 collective-permute-start.12
  36.0 1.6 %collective-permute-done.7.refs_2_ = bf16[192,1152]{1,0:T(8,128)(2,1)S(1)} collective-permute-done((bf16[192,1152]{1,0:T(8,128)(2,1)S(1)}, bf16[192,1152]{1,0:T(8,128)(2,1)S(1)}, u32[]{:S(2)}, u32[]{:S(2)}) %collective-permute-start.7) | collective-permute-done | bytes 442400 | tf_op jit(solution)/shard_map/z1/ppermute | solution.py:33
  37.7 2.3 %shard_map.106 = (bf16[384,768]{1,0:T(8,128)(2,1)S(1)}, f32[3,8,768]{2,1,0:T(8,128)S(1)}, bf16[384,1152]{1,0:T(8,128)(2,1)S(1)}, bf16[768,1152]{1,0:T(8,128)(2,1)S(1)}) custom-call(f32[1]{0:T(128)S(6)} %copy.11.log_temp, f32[1]{0:T(128)S(6)} %copy.12.bias, s32[1,384]{1,0:T(1,128)S(1)} %reshape.1562.rows_after.rows_id, ...), custom_call_target="tpu_custom_call" | custom-call | tf_op jit(solution)/shard_map/pallas_call | solution.py:244
  40.0 3.1 %shard_map.108 = (bf16[784,1152]{1,0:T(8,128)(2,1)S(1)}, bf16[384,768]{1,0:T(8,128)(2,1)S(1)}, f32[8,128]{1,0:T(8,128)S(1)}, bf16[768,1152]{1,0:T(8,128)(2,1)S(1)}) custom-call(f32[1]{0:T(128)S(6)} %copy.11.log_temp, f32[1]{0:T(128)S(6)} %copy.12.bias, s32[1,384]{1,0:T(1,128)S(1)} %reshape.1562.rows_after.rows_id, ...), custom_call_target="tpu_custom_call" | custom-call | tf_op jit(solution)/shard_map/pallas_call | solution.py:244
  43.3 2.5 %shard_map.111 = (f32[48,1152]{1,0:T(8,128)S(1)}, f32[96,1152]{1,0:T(8,128)S(1)}, bf16[48,1152]{1,0:T(8,128)(2,1)S(1)}, bf16[192,1152]{1,0:T(8,128)(2,1)}) custom-call(bf16[384,768]{1,0:T(8,128)(2,1)S(1)} %get-tuple-element.61.scaled.scaled_own, bf16[384,768]{1,0:T(8,128)(2,1)S(1)} %get-tuple-element.75.scaled_far, ...), custom_call_target="tpu_custom_call" | custom-call | tf_op jit(solution)/shard_map/pallas_call | solution.py:244
  45.8 2.4 %collective-permute-start.22 = (bf16[192,1152]{1,0:T(8,128)(2,1)}, bf16[192,1152]{1,0:T(8,128)(2,1)}, u32[]{:S(2)}, u32[]{:S(2)}) collective-permute-start(bf16[192,1152]{1,0:T(8,128)(2,1)} %get-tuple-element.80), channel_id=1, source_target_pairs={{0,35},{1,0},{2,1},{3,2},{4,5},{5,6},{6,7},{7,36},{8,43},{9,8},{10... | collective-permute-start | bytes 1327112 | tf_op jit(solution)/shard_map/rz1/ppermute | solution.py:33
  48.2 2.3 %shard_map.109 = (f32[192,1152]{1,0:T(8,128)S(1)}, bf16[192,1152]{1,0:T(8,128)(2,1)}, bf16[192,1152]{1,0:T(8,128)(2,1)}, bf16[192,1152]{1,0:T(8,128)(2,1)}, f32[32,8,128]{2,1,0:T(8,128)}) custom-call(bf16[384,768]{1,0:T(8,128)(2,1)S(1)} %get-tuple-element.61.scaled.scaled_own, f32[8,128]{1,0:T(8,128)S(1)} %get-tuple-element.64.sums, ...), custom_call_target="tpu_custom_call" | custom-call | tf_op jit(solution)/shard_map/pallas_call | solution.py:244
  50.5 1.8 %collective-permute-start.16 = (bf16[192,1152]{1,0:T(8,128)(2,1)}, bf16[192,1152]{1,0:T(8,128)(2,1)S(1)}, u32[]{:S(2)}, u32[]{:S(2)}) collective-permute-start(bf16[192,1152]{1,0:T(8,128)(2,1)} %get-tuple-element.67), channel_id=1, source_target_pairs={{0,192},{1,193},{2,194},{3,195},{4,28},{5,29},{6,30},{7,31},{8,200... | collective-permute-start | bytes 1327112 | tf_op jit(solution)/shard_map/rsecond/ppermute | solution.py:33
  52.3 0.2 collective-permute-start.17
  52.5 2.4 %collective-permute-start.18 = (bf16[192,1152]{1,0:T(8,128)(2,1)}, bf16[192,1152]{1,0:T(8,128)(2,1)S(1)}, u32[]{:S(2)}, u32[]{:S(2)}) collective-permute-start(bf16[192,1152]{1,0:T(8,128)(2,1)} %get-tuple-element.69), channel_id=1, source_target_pairs={{0,128},{1,129},{2,130},{3,131},{4,20},{5,21},{6,22},{7,23},{8,136... | collective-permute-start | bytes 1327112 | tf_op jit(solution)/shard_map/rsecond/ppermute | solution.py:33
  54.9 2.2 %collective-permute-start.23 = (bf16[48,1152]{1,0:T(8,128)(2,1)S(1)}, bf16[48,1152]{1,0:T(8,128)(2,1)S(1)}, u32[]{:S(2)}, u32[]{:S(2)}) collective-permute-start(bf16[48,1152]{1,0:T(8,128)(2,1)S(1)} %get-tuple-element.81), channel_id=1, source_target_pairs={{0,34},{1,35},{2,0},{3,1},{4,6},{5,7},{6,36},{7,37},{8,42},{9,43},... | collective-permute-start | bytes 331784 | tf_op jit(solution)/shard_map/rz4/ppermute | solution.py:33
  57.0 5.1 %all-to-all-start = ((f32[32,8,128]{2,1,0:T(8,128)}), f32[32,8,128]{2,1,0:T(8,128)S(1)}, u32[]{:S(2)}, u32[]{:S(2)}) async-start(f32[32,8,128]{2,1,0:T(8,128)} %get-tuple-element.70), calls=%async_computation | async-start | bytes 262144 | tf_op jit(solution)/shard_map/terms/all_to_all | solution.py:322
  62.2 0.6 copy-done.7
  62.8 0.9 %copy-done.6 = f32[48,1152]{1,0:T(8,128)S(1)} copy-done((f32[48,1152]{1,0:T(8,128)S(1)}, f32[48,1152]{1,0:T(8,128)}, u32[]{:S(2)}) %copy-start.6) | copy-done | bytes 221208
  63.8 0.9 %copy-done.8 = bf16[48,1152]{1,0:T(8,128)(2,1)S(1)} copy-done((bf16[48,1152]{1,0:T(8,128)(2,1)S(1)}, bf16[48,1152]{1,0:T(8,128)(2,1)}, u32[]{:S(2)}) %copy-start.8) | copy-done | bytes 110616
  64.7 1.8 %shard_map.112 = (f32[48,1152]{1,0:T(8,128)S(1)}, f32[48,1152]{1,0:T(8,128)S(1)}, bf16[96,1152]{1,0:T(8,128)(2,1)}) custom-call(f32[48,1152]{1,0:T(8,128)S(1)} %copy-done.6, f32[96,1152]{1,0:T(8,128)S(1)} %get-tuple-element.79.pair, bf16[192,1152]{1,0:T(8,128)(2,1)} %collective-permute-done.22.back, bf16[48,1152]{1,0:T(8,128)(2,1)S(1)} %copy-done.8), custom_call_target="tpu_custom_call" | custom-call | tf_op jit(solution)/shard_map/pallas_call | solution.py:244
  66.4 0.7 copy-done.3
  67.1 3.9 %collective-permute-start.24 = (bf16[96,1152]{1,0:T(8,128)(2,1)}, bf16[96,1152]{1,0:T(8,128)(2,1)S(1)}, u32[]{:S(2)}, u32[]{:S(2)}) collective-permute-start(bf16[96,1152]{1,0:T(8,128)(2,1)} %get-tuple-element.84), channel_id=1, source_target_pairs={{0,34},{1,35},{2,0},{3,1},{4,6},{5,7},{6,36},{7,37},{8,42},{9,43},... | collective-permute-start | bytes 663560 | tf_op jit(solution)/shard_map/rz2/ppermute | solution.py:33
  71.0 2.1 %all-to-all-done.terms = f32[32,8,128]{2,1,0:T(8,128)S(1)} async-done(((f32[32,8,128]{2,1,0:T(8,128)}), f32[32,8,128]{2,1,0:T(8,128)S(1)}, u32[]{:S(2)}, u32[]{:S(2)}) %all-to-all-start) | async-done | bytes 131104 | tf_op jit(solution)/shard_map/terms/all_to_all | solution.py:322
  73.1 0.2 shard_map.110
  73.3 0.7 collective-permute-start.19
  74.0 2.6 %collective-permute-start.20 = (bf16[64,1152]{1,0:T(8,128)(2,1)S(1)}, bf16[64,1152]{1,0:T(8,128)(2,1)S(1)}, u32[]{:S(2)}, u32[]{:S(2)}) collective-permute-start(bf16[64,1152]{1,0:T(8,128)(2,1)S(1)} %get-tuple-element.73), channel_id=1, source_target_pairs={{0,8},{1,9},{2,10},{3,11},{4,68},{5,69},{6,70},{7,71},{8,16},{9,17... | collective-permute-start | bytes 442376 | tf_op jit(solution)/shard_map/rfirst/ppermute | solution.py:33
  76.6 1.6 %collective-permute-start.21 = (bf16[64,1152]{1,0:T(8,128)(2,1)S(1)}, bf16[64,1152]{1,0:T(8,128)(2,1)S(1)}, u32[]{:S(2)}, u32[]{:S(2)}) collective-permute-start(bf16[64,1152]{1,0:T(8,128)(2,1)S(1)} %get-tuple-element.74), channel_id=1, source_target_pairs={{0,16},{1,17},{2,18},{3,19},{4,132},{5,133},{6,134},{7,135},{8,24}... | collective-permute-start | bytes 442376 | tf_op jit(solution)/shard_map/rfirst/ppermute | solution.py:33
  78.3 1.3 %collective-permute-done.25.t1 = bf16[48,1152]{1,0:T(8,128)(2,1)S(1)} collective-permute-done((bf16[48,1152]{1,0:T(8,128)(2,1)S(1)}, bf16[48,1152]{1,0:T(8,128)(2,1)S(1)}, u32[]{:S(2)}, u32[]{:S(2)}) %collective-permute-start.25) | collective-permute-done | bytes 110624 | tf_op jit(solution)/shard_map/rpair/ppermute | solution.py:33
  79.7 1.2 %collective-permute-done.20.i2 = bf16[64,1152]{1,0:T(8,128)(2,1)S(1)} collective-permute-done((bf16[64,1152]{1,0:T(8,128)(2,1)S(1)}, bf16[64,1152]{1,0:T(8,128)(2,1)S(1)}, u32[]{:S(2)}, u32[]{:S(2)}) %collective-permute-start.20) | collective-permute-done | bytes 147488 | tf_op jit(solution)/shard_map/rfirst/ppermute | solution.py:33
  80.9 2.4 %collective-permute-done.21.i3 = bf16[64,1152]{1,0:T(8,128)(2,1)S(1)} collective-permute-done((bf16[64,1152]{1,0:T(8,128)(2,1)S(1)}, bf16[64,1152]{1,0:T(8,128)(2,1)S(1)}, u32[]{:S(2)}, u32[]{:S(2)}) %collective-permute-start.21) | collective-permute-done | bytes 147488 | tf_op jit(solution)/shard_map/rfirst/ppermute | solution.py:33
  83.3 1.0 %shard_map.114 = (f32[48,1152]{1,0:T(8,128)}, f32[48,1152]{1,0:T(8,128)}, f32[1]{0:T(128)}, f32[1]{0:T(128)}, f32[1]{0:T(128)}) custom-call(f32[1]{0:T(128)S(6)} %copy.11.log_temp, f32[48,1152]{1,0:T(8,128)S(1)} %copy-done, f32[48,1152]{1,0:T(8,128)S(1)} %get-tuple-element.71.after.image_own, bf16[64,1152]{1,0:T(8,128)(2,1)S(1)} %collective-permute-done.19.i1, ...), custom_call_target="tpu_custom_call" | custom-call | tf_op jit(solution)/shard_map/pallas_call | solution.py:244
  (55 shorter events, 1.2 us)
Async XLA Ops:
  0.6 3.2 %copy-start = (f32[48,1152]{1,0:T(8,128)S(1)}, f32[48,1152]{1,0:T(8,128)}, u32[]{:S(2)}) copy-start(f32[48,1152]{1,0:T(8,128)} %image_raw.1) | copy-start | bytes 663556
  0.6 1.0 %copy-start.1 = (f32[48,1152]{1,0:T(8,128)S(1)}, f32[48,1152]{1,0:T(8,128)}, u32[]{:S(2)}) copy-start(f32[48,1152]{1,0:T(8,128)} %text_raw.1) | copy-start | bytes 663556
  1.6 12.8 %copy-start.9 = (s32[12288]{0:T(1024)S(1)}, s32[12288]{0:T(1024)}, u32[]{:S(2)}) copy-start(s32[12288]{0:T(1024)} %param.8) | copy-start | bytes 147460
  1.6 12.9 %copy-start.10 = (s32[12288]{0:T(1024)S(1)}, s32[12288]{0:T(1024)}, u32[]{:S(2)}) copy-start(s32[12288]{0:T(1024)} %param.9) | copy-start | bytes 147460
  1.8 2.1 %collective-permute-start = (bf16[48,1152]{1,0:T(8,128)(2,1)S(1)}, bf16[48,1152]{1,0:T(8,128)(2,1)S(1)}, u32[]{:S(2)}, u32[]{:S(2)}) collective-permute-start(bf16[48,1152]{1,0:T(8,128)(2,1)S(1)} %get-tuple-element.50), channel_id=1, source_target_pairs={{0,4},{1,5},{2,6},{3,7},{4,0},{5,1},{6,2},{7,3},{8,12},{9,13},{10,... | collective-permute-start | bytes 331784 | tf_op jit(solution)/shard_map/pair/ppermute | solution.py:33
  4.0 6.8 %collective-permute-start.3 = (bf16[48,1152]{1,0:T(8,128)(2,1)S(1)}, bf16[48,1152]{1,0:T(8,128)(2,1)S(1)}, u32[]{:S(2)}, u32[]{:S(2)}) collective-permute-start(bf16[48,1152]{1,0:T(8,128)(2,1)S(1)} %get-tuple-element.51), channel_id=1, source_target_pairs={{0,24},{1,25},{2,26},{3,27},{4,196},{5,197},{6,198},{7,199},{8,0},... | collective-permute-start | bytes 331784 | tf_op jit(solution)/shard_map/first/ppermute | solution.py:33
  4.9 5.9 %collective-permute-start.2 = (bf16[48,1152]{1,0:T(8,128)(2,1)S(1)}, bf16[48,1152]{1,0:T(8,128)(2,1)S(1)}, u32[]{:S(2)}, u32[]{:S(2)}) collective-permute-start(bf16[48,1152]{1,0:T(8,128)(2,1)S(1)} %get-tuple-element.51), channel_id=1, source_target_pairs={{0,8},{1,9},{2,10},{3,11},{4,68},{5,69},{6,70},{7,71},{8,16},{9,17... | collective-permute-start | bytes 331784 | tf_op jit(solution)/shard_map/first/ppermute | solution.py:33
  7.3 6.3 %collective-permute-start.1 = (bf16[48,1152]{1,0:T(8,128)(2,1)S(1)}, bf16[48,1152]{1,0:T(8,128)(2,1)S(1)}, u32[]{:S(2)}, u32[]{:S(2)}) collective-permute-start(bf16[48,1152]{1,0:T(8,128)(2,1)S(1)} %get-tuple-element.51), channel_id=1, source_target_pairs={{0,16},{1,17},{2,18},{3,19},{4,132},{5,133},{6,134},{7,135},{8,24}... | collective-permute-start | bytes 331784 | tf_op jit(solution)/shard_map/first/ppermute | solution.py:33
  7.7 10.6 %collective-permute-start.4 = (bf16[96,1152]{1,0:T(8,128)(2,1)S(1)}, bf16[96,1152]{1,0:T(8,128)(2,1)S(1)}, u32[]{:S(2)}, u32[]{:S(2)}) collective-permute-start(bf16[96,1152]{1,0:T(8,128)(2,1)S(1)} %get-tuple-element.56), channel_id=1, source_target_pairs={{0,2},{1,3},{2,32},{3,33},{4,38},{5,39},{6,4},{7,5},{8,10},{9,11},... | collective-permute-start | bytes 663560 | tf_op jit(solution)/shard_map/z2/ppermute | solution.py:33
  13.5 2.4 %collective-permute-start.5 = (f32[8,128]{1,0:T(8,128)S(1)}, f32[8,128]{1,0:T(8,128)S(1)}, u32[]{:S(2)}, u32[]{:S(2)}) collective-permute-start(f32[8,128]{1,0:T(8,128)S(1)} %shard_map.104), channel_id=1, source_target_pairs={{0,4},{1,5},{2,6},{3,7},{4,0},{5,1},{6,2},{7,3},{8,12},{9,13},{10,... | collective-permute-start | bytes 12296 | tf_op jit(solution)/shard_map/flag/ppermute | solution.py:33
  18.4 9.6 %collective-permute-start.8 = (bf16[192,1152]{1,0:T(8,128)(2,1)S(1)}, bf16[192,1152]{1,0:T(8,128)(2,1)S(1)}, u32[]{:S(2)}, u32[]{:S(2)}) collective-permute-start(bf16[192,1152]{1,0:T(8,128)(2,1)S(1)} %get-tuple-element.60.refs_3_.src), channel_id=1, source_target_pairs={{0,64},{1,65},{2,66},{3,67},{4,12},{5,13},{6,14},{7,15},{8,72},{9,... | collective-permute-start | bytes 1327112 | tf_op jit(solution)/shard_map/second/ppermute | solution.py:33
  20.0 13.9 %collective-permute-start.10 = (bf16[192,1152]{1,0:T(8,128)(2,1)S(1)}, bf16[192,1152]{1,0:T(8,128)(2,1)S(1)}, u32[]{:S(2)}, u32[]{:S(2)}) collective-permute-start(bf16[192,1152]{1,0:T(8,128)(2,1)S(1)} %get-tuple-element.60.refs_3_.src), channel_id=1, source_target_pairs={{0,128},{1,129},{2,130},{3,131},{4,20},{5,21},{6,22},{7,23},{8,136... | collective-permute-start | bytes 1327112 | tf_op jit(solution)/shard_map/second/ppermute | solution.py:33
  22.9 11.0 %collective-permute-start.9 = (bf16[192,1152]{1,0:T(8,128)(2,1)S(1)}, bf16[192,1152]{1,0:T(8,128)(2,1)S(1)}, u32[]{:S(2)}, u32[]{:S(2)}) collective-permute-start(bf16[192,1152]{1,0:T(8,128)(2,1)S(1)} %get-tuple-element.60.refs_3_.src), channel_id=1, source_target_pairs={{0,192},{1,193},{2,194},{3,195},{4,28},{5,29},{6,30},{7,31},{8,200... | collective-permute-start | bytes 1327112 | tf_op jit(solution)/shard_map/second/ppermute | solution.py:33
  24.3 10.2 %collective-permute-start.6 = (bf16[48,1152]{1,0:T(8,128)(2,1)S(1)}, bf16[48,1152]{1,0:T(8,128)(2,1)S(1)}, u32[]{:S(2)}, u32[]{:S(2)}) collective-permute-start(bf16[48,1152]{1,0:T(8,128)(2,1)S(1)} %get-tuple-element.58), channel_id=1, source_target_pairs={{0,2},{1,3},{2,32},{3,33},{4,38},{5,39},{6,4},{7,5},{8,10},{9,11},... | collective-permute-start | bytes 331784 | tf_op jit(solution)/shard_map/z4/ppermute | solution.py:33
  27.0 10.7 %collective-permute-start.7 = (bf16[192,1152]{1,0:T(8,128)(2,1)S(1)}, bf16[192,1152]{1,0:T(8,128)(2,1)S(1)}, u32[]{:S(2)}, u32[]{:S(2)}) collective-permute-start(bf16[192,1152]{1,0:T(8,128)(2,1)S(1)} %get-tuple-element.59), channel_id=1, source_target_pairs={{0,1},{1,2},{2,3},{3,32},{4,39},{5,4},{6,5},{7,6},{8,9},{9,10},{10... | collective-permute-start | bytes 1327112 | tf_op jit(solution)/shard_map/z1/ppermute | solution.py:33
  28.0 12.0 %collective-permute-start.11 = (bf16[192,1152]{1,0:T(8,128)(2,1)S(1)}, bf16[192,1152]{1,0:T(8,128)(2,1)S(1)}, u32[]{:S(2)}, u32[]{:S(2)}) collective-permute-start(bf16[192,1152]{1,0:T(8,128)(2,1)S(1)} %shard_map.107), channel_id=1, source_target_pairs={{0,4},{1,5},{2,6},{3,7},{4,0},{5,1},{6,2},{7,3},{8,12},{9,13},{10,... | collective-permute-start | bytes 1327112 | tf_op jit(solution)/shard_map/swap/ppermute | solution.py:33
  34.0 6.0 %collective-permute-start.14 = (bf16[192,1152]{1,0:T(8,128)(2,1)S(1)}, bf16[192,1152]{1,0:T(8,128)(2,1)S(1)}, u32[]{:S(2)}, u32[]{:S(2)}) collective-permute-start(bf16[192,1152]{1,0:T(8,128)(2,1)S(1)} %collective-permute-done.10.refs_6_), channel_id=1, source_target_pairs={{0,4},{1,5},{2,6},{3,7},{4,0},{5,1},{6,2},{7,3},{8,12},{9,13},{10,... | collective-permute-start | bytes 1327112 | tf_op jit(solution)/shard_map/swap/ppermute | solution.py:33
  34.0 6.0 %collective-permute-start.13 = (bf16[192,1152]{1,0:T(8,128)(2,1)S(1)}, bf16[192,1152]{1,0:T(8,128)(2,1)S(1)}, u32[]{:S(2)}, u32[]{:S(2)}) collective-permute-start(bf16[192,1152]{1,0:T(8,128)(2,1)S(1)} %collective-permute-done.9.refs_5_), channel_id=1, source_target_pairs={{0,4},{1,5},{2,6},{3,7},{4,0},{5,1},{6,2},{7,3},{8,12},{9,13},{10,... | collective-permute-start | bytes 1327112 | tf_op jit(solution)/shard_map/swap/ppermute | solution.py:33
  34.5 5.6 %collective-permute-start.12 = (bf16[192,1152]{1,0:T(8,128)(2,1)S(1)}, bf16[192,1152]{1,0:T(8,128)(2,1)S(1)}, u32[]{:S(2)}, u32[]{:S(2)}) collective-permute-start(bf16[192,1152]{1,0:T(8,128)(2,1)S(1)} %collective-permute-done.8.refs_4_.after), channel_id=1, source_target_pairs={{0,4},{1,5},{2,6},{3,7},{4,0},{5,1},{6,2},{7,3},{8,12},{9,13},{10,... | collective-permute-start | bytes 1327112 | tf_op jit(solution)/shard_map/swap/ppermute | solution.py:33
  43.2 5.0 %collective-permute-start.15 = (bf16[784,1152]{1,0:T(8,128)(2,1)S(1)}, bf16[784,1152]{1,0:T(8,128)(2,1)S(1)}, u32[]{:S(2)}, u32[]{:S(2)}) collective-permute-start(bf16[784,1152]{1,0:T(8,128)(2,1)S(1)} %get-tuple-element.65), channel_id=1, source_target_pairs={{0,4},{1,5},{2,6},{3,7},{4,0},{5,1},{6,2},{7,3},{8,12},{9,13},{10,... | collective-permute-start | bytes 5419016 | tf_op jit(solution)/shard_map/rswap/ppermute | solution.py:33
  45.8 6.7 %copy-start.5 = (f32[48,1152]{1,0:T(8,128)}, f32[48,1152]{1,0:T(8,128)S(1)}, u32[]{:S(2)}) copy-start(f32[48,1152]{1,0:T(8,128)S(1)} %get-tuple-element.78.own) | copy-start | bytes 663556
  45.8 17.1 %collective-permute-start.22 = (bf16[192,1152]{1,0:T(8,128)(2,1)}, bf16[192,1152]{1,0:T(8,128)(2,1)}, u32[]{:S(2)}, u32[]{:S(2)}) collective-permute-start(bf16[192,1152]{1,0:T(8,128)(2,1)} %get-tuple-element.80), channel_id=1, source_target_pairs={{0,35},{1,0},{2,1},{3,2},{4,5},{5,6},{6,7},{7,36},{8,43},{9,8},{10... | collective-permute-start | bytes 1327112 | tf_op jit(solution)/shard_map/rz1/ppermute | solution.py:33
  50.5 22.6 %collective-permute-start.16 = (bf16[192,1152]{1,0:T(8,128)(2,1)}, bf16[192,1152]{1,0:T(8,128)(2,1)S(1)}, u32[]{:S(2)}, u32[]{:S(2)}) collective-permute-start(bf16[192,1152]{1,0:T(8,128)(2,1)} %get-tuple-element.67), channel_id=1, source_target_pairs={{0,192},{1,193},{2,194},{3,195},{4,28},{5,29},{6,30},{7,31},{8,200... | collective-permute-start | bytes 1327112 | tf_op jit(solution)/shard_map/rsecond/ppermute | solution.py:33
  52.3 20.8 %collective-permute-start.17 = (bf16[192,1152]{1,0:T(8,128)(2,1)}, bf16[192,1152]{1,0:T(8,128)(2,1)S(1)}, u32[]{:S(2)}, u32[]{:S(2)}) collective-permute-start(bf16[192,1152]{1,0:T(8,128)(2,1)} %get-tuple-element.68), channel_id=1, source_target_pairs={{0,64},{1,65},{2,66},{3,67},{4,12},{5,13},{6,14},{7,15},{8,72},{9,... | collective-permute-start | bytes 1327112 | tf_op jit(solution)/shard_map/rsecond/ppermute | solution.py:33
  52.5 20.6 %collective-permute-start.18 = (bf16[192,1152]{1,0:T(8,128)(2,1)}, bf16[192,1152]{1,0:T(8,128)(2,1)S(1)}, u32[]{:S(2)}, u32[]{:S(2)}) collective-permute-start(bf16[192,1152]{1,0:T(8,128)(2,1)} %get-tuple-element.69), channel_id=1, source_target_pairs={{0,128},{1,129},{2,130},{3,131},{4,20},{5,21},{6,22},{7,23},{8,136... | collective-permute-start | bytes 1327112 | tf_op jit(solution)/shard_map/rsecond/ppermute | solution.py:33
  54.9 7.3 %collective-permute-start.23 = (bf16[48,1152]{1,0:T(8,128)(2,1)S(1)}, bf16[48,1152]{1,0:T(8,128)(2,1)S(1)}, u32[]{:S(2)}, u32[]{:S(2)}) collective-permute-start(bf16[48,1152]{1,0:T(8,128)(2,1)S(1)} %get-tuple-element.81), channel_id=1, source_target_pairs={{0,34},{1,35},{2,0},{3,1},{4,6},{5,7},{6,36},{7,37},{8,42},{9,43},... | collective-permute-start | bytes 331784 | tf_op jit(solution)/shard_map/rz4/ppermute | solution.py:33
  57.0 16.1 %all-to-all-start = ((f32[32,8,128]{2,1,0:T(8,128)}), f32[32,8,128]{2,1,0:T(8,128)S(1)}, u32[]{:S(2)}, u32[]{:S(2)}) async-start(f32[32,8,128]{2,1,0:T(8,128)} %get-tuple-element.70), calls=%async_computation | async-start | bytes 262144 | tf_op jit(solution)/shard_map/terms/all_to_all | solution.py:322
  62.2 0.6 copy-start.7
  62.8 0.9 %copy-start.6 = (f32[48,1152]{1,0:T(8,128)S(1)}, f32[48,1152]{1,0:T(8,128)}, u32[]{:S(2)}) copy-start(f32[48,1152]{1,0:T(8,128)} %copy-done.5) | copy-start | bytes 663556
  63.8 0.9 %copy-start.8 = (bf16[48,1152]{1,0:T(8,128)(2,1)S(1)}, bf16[48,1152]{1,0:T(8,128)(2,1)}, u32[]{:S(2)}) copy-start(bf16[48,1152]{1,0:T(8,128)(2,1)} %copy-done.7) | copy-start | bytes 331780
  66.4 0.7 copy-start.3
  67.1 16.2 %copy-start.2 = (f32[48,1152]{1,0:T(8,128)S(1)}, f32[48,1152]{1,0:T(8,128)}, u32[]{:S(2)}) copy-start(f32[48,1152]{1,0:T(8,128)} %text_raw.1) | copy-start | bytes 663556
  67.1 11.1 %copy-start.4 = (f32[48,1152]{1,0:T(8,128)S(1)}, f32[48,1152]{1,0:T(8,128)}, u32[]{:S(2)}) copy-start(f32[48,1152]{1,0:T(8,128)} %copy-done.3) | copy-start | bytes 663556
  67.1 11.1 %collective-permute-start.24 = (bf16[96,1152]{1,0:T(8,128)(2,1)}, bf16[96,1152]{1,0:T(8,128)(2,1)S(1)}, u32[]{:S(2)}, u32[]{:S(2)}) collective-permute-start(bf16[96,1152]{1,0:T(8,128)(2,1)} %get-tuple-element.84), channel_id=1, source_target_pairs={{0,34},{1,35},{2,0},{3,1},{4,6},{5,7},{6,36},{7,37},{8,42},{9,43},... | collective-permute-start | bytes 663560 | tf_op jit(solution)/shard_map/rz2/ppermute | solution.py:33
  73.3 6.4 %collective-permute-start.19 = (bf16[64,1152]{1,0:T(8,128)(2,1)S(1)}, bf16[64,1152]{1,0:T(8,128)(2,1)S(1)}, u32[]{:S(2)}, u32[]{:S(2)}) collective-permute-start(bf16[64,1152]{1,0:T(8,128)(2,1)S(1)} %get-tuple-element.72), channel_id=1, source_target_pairs={{0,24},{1,25},{2,26},{3,27},{4,196},{5,197},{6,198},{7,199},{8,0},... | collective-permute-start | bytes 442376 | tf_op jit(solution)/shard_map/rfirst/ppermute | solution.py:33
  74.0 6.8 %collective-permute-start.20 = (bf16[64,1152]{1,0:T(8,128)(2,1)S(1)}, bf16[64,1152]{1,0:T(8,128)(2,1)S(1)}, u32[]{:S(2)}, u32[]{:S(2)}) collective-permute-start(bf16[64,1152]{1,0:T(8,128)(2,1)S(1)} %get-tuple-element.73), channel_id=1, source_target_pairs={{0,8},{1,9},{2,10},{3,11},{4,68},{5,69},{6,70},{7,71},{8,16},{9,17... | collective-permute-start | bytes 442376 | tf_op jit(solution)/shard_map/rfirst/ppermute | solution.py:33
  76.6 6.6 %collective-permute-start.21 = (bf16[64,1152]{1,0:T(8,128)(2,1)S(1)}, bf16[64,1152]{1,0:T(8,128)(2,1)S(1)}, u32[]{:S(2)}, u32[]{:S(2)}) collective-permute-start(bf16[64,1152]{1,0:T(8,128)(2,1)S(1)} %get-tuple-element.74), channel_id=1, source_target_pairs={{0,16},{1,17},{2,18},{3,19},{4,132},{5,133},{6,134},{7,135},{8,24}... | collective-permute-start | bytes 442376 | tf_op jit(solution)/shard_map/rfirst/ppermute | solution.py:33
  78.2 1.4 %collective-permute-start.25 = (bf16[48,1152]{1,0:T(8,128)(2,1)S(1)}, bf16[48,1152]{1,0:T(8,128)(2,1)S(1)}, u32[]{:S(2)}, u32[]{:S(2)}) collective-permute-start(bf16[48,1152]{1,0:T(8,128)(2,1)S(1)} %get-tuple-element.86), channel_id=1, source_target_pairs={{0,4},{1,5},{2,6},{3,7},{4,0},{5,1},{6,2},{7,3},{8,12},{9,13},{10,... | collective-permute-start | bytes 331784 | tf_op jit(solution)/shard_map/rpair/ppermute | solution.py:33

commit v8 on v7

--- a/solution.py
+++ b/solution.py
@@ -123,7 +123,7 @@
     if first:
         pieces, (scaled, sums, text, image) = refs[:7], refs[7:]
         stack(text, pieces[:3])
-        stack(image, pieces[3:])
+        stack(image, (pieces[3], pieces[5], pieces[6], pieces[4]))
         far = ()
     else:
         text, pieces, (*far, scaled, sums, image) = refs[0], refs[1:5], refs[5:]
@@ -294,7 +294,7 @@
     scaled_own, sums, text, image = local(
         functools.partial(terms_kernel, True),
         (b16(384, 768), f32(3, 8, 768), b16(384, width), b16(768, width)),
-        log_temp, bias, rows_id, cols_id, jnp.zeros((3, 8, 768), jnp.float32), *text, *plane, grant=12,
+        log_temp, bias, rows_id, cols_id, jnp.zeros((3, 8, 768), jnp.float32), *text, plane[0], plane[3], *plane[1:3], grant=12,
     )
     far, scaled_far, sums, image_far = local(
         functools.partial(terms_kernel, False),

time: 85 us -> 84.9 us (level)
  waiting for transfers between devices: 20.1 us -> 15 us
  starting transfers between devices: 40.7 us -> 45.4 us
    ppermute x26, waiting for transfers between devices: 18.1 us -> 13.4 us  [send(): return lax.ppermute(value, AXES, pairs)]
    ppermute x26, starting transfers between devices: 35.6 us -> 39.1 us  [send(): return lax.ppermute(value, AXES, pairs)]
    all_to_all x1, starting transfers between devices: 5.13 us -> 6.25 us  [body(): lax.all_to_all(spread, AXES, 0, 0, tiled=True, axis_index_groups=across())]
where the time goes in v8:
time: 84.9 us; the launch traced here: 83.9 us
  starting transfers between devices  45.4 us (53%)
  waiting for transfers between devices  15 us (18%)
  Pallas kernels  13.6 us (16%)
  local copies, waits for them, and re-layouts  5.88 us (7%)
  between operations  4.06 us (5%)
    ppermute x26, starting transfers between devices, send(): return lax.ppermute(value, AXES, pairs)  39.1 us
    pallas_call x14, Pallas kernels, local(): pl.pallas_call(kernel, out_shape=out_shape, in_specs=[SMEM if a.shape ==...  13.6 us
    ppermute x26, waiting for transfers between devices, send(): return lax.ppermute(value, AXES, pairs)  13.4 us
    all_to_all x1, starting transfers between devices, body(): lax.all_to_all(spread, AXES, 0, 0, tiled=True, axis_index_groups=across())  6.25 us
    unnamed x22, local copies, waits for them, and re-layouts  4.15 us
  transfers between devices with their start and end apart: 27, of which 10 were waited for; matrix products, arithmetic and copies ran while one was open for 2% of the time, Pallas kernels for 11%

profile of v8, /device:TPU:6, one launch (start us, length us, event | category | flops | bytes accessed | tf_op | source)
XLA Modules:
  0.0 83.9 jit_solution(6500707699804430561)
XLA Ops:
  0.7 1.0 %copy-done.1 = f32[48,1152]{1,0:T(8,128)S(1)} copy-done((f32[48,1152]{1,0:T(8,128)S(1)}, f32[48,1152]{1,0:T(8,128)}, u32[]{:S(2)}) %copy-start.1) | copy-done | bytes 221208
  1.6 0.1 shard_map.101
  3.6 0.1 stack.134
  3.7 0.1 stack.167
  3.8 0.1 shard_map.102
  4.0 0.9 %collective-permute-start.3 = (bf16[48,1152]{1,0:T(8,128)(2,1)S(1)}, bf16[48,1152]{1,0:T(8,128)(2,1)S(1)}, u32[]{:S(2)}, u32[]{:S(2)}) collective-permute-start(bf16[48,1152]{1,0:T(8,128)(2,1)S(1)} %get-tuple-element.51), channel_id=1, source_target_pairs={{0,24},{1,25},{2,26},{3,27},{4,196},{5,197},{6,198},{7,199},{8,0},... | collective-permute-start | bytes 331784 | tf_op jit(solution)/shard_map/first/ppermute | solution.py:33
  4.9 2.4 %collective-permute-start.2 = (bf16[48,1152]{1,0:T(8,128)(2,1)S(1)}, bf16[48,1152]{1,0:T(8,128)(2,1)S(1)}, u32[]{:S(2)}, u32[]{:S(2)}) collective-permute-start(bf16[48,1152]{1,0:T(8,128)(2,1)S(1)} %get-tuple-element.51), channel_id=1, source_target_pairs={{0,8},{1,9},{2,10},{3,11},{4,68},{5,69},{6,70},{7,71},{8,16},{9,17... | collective-permute-start | bytes 331784 | tf_op jit(solution)/shard_map/first/ppermute | solution.py:33
  7.3 0.4 collective-permute-start.1
  7.7 3.0 %collective-permute-start.4 = (bf16[96,1152]{1,0:T(8,128)(2,1)S(1)}, bf16[96,1152]{1,0:T(8,128)(2,1)S(1)}, u32[]{:S(2)}, u32[]{:S(2)}) collective-permute-start(bf16[96,1152]{1,0:T(8,128)(2,1)S(1)} %get-tuple-element.56), channel_id=1, source_target_pairs={{0,2},{1,3},{2,32},{3,33},{4,38},{5,39},{6,4},{7,5},{8,10},{9,11},... | collective-permute-start | bytes 663560 | tf_op jit(solution)/shard_map/z2/ppermute | solution.py:33
  10.8 2.8 %collective-permute-done.1.after.refs_2_.i3 = bf16[48,1152]{1,0:T(8,128)(2,1)S(1)} collective-permute-done((bf16[48,1152]{1,0:T(8,128)(2,1)S(1)}, bf16[48,1152]{1,0:T(8,128)(2,1)S(1)}, u32[]{:S(2)}, u32[]{:S(2)}) %collective-permute-start.1) | collective-permute-done | bytes 110624 | tf_op jit(solution)/shard_map/first/ppermute | solution.py:33
  13.5 0.9 %collective-permute-start.5 = (f32[8,128]{1,0:T(8,128)S(1)}, f32[8,128]{1,0:T(8,128)S(1)}, u32[]{:S(2)}, u32[]{:S(2)}) collective-permute-start(f32[8,128]{1,0:T(8,128)S(1)} %shard_map.104), channel_id=1, source_target_pairs={{0,4},{1,5},{2,6},{3,7},{4,0},{5,1},{6,2},{7,3},{8,12},{9,13},{10,... | collective-permute-start | bytes 12296 | tf_op jit(solution)/shard_map/flag/ppermute | solution.py:33
  14.7 0.6 gather_fusion
  15.3 0.6 gather_fusion.1
  16.0 2.3 %collective-permute-done.4.pair_2 = bf16[96,1152]{1,0:T(8,128)(2,1)S(1)} collective-permute-done((bf16[96,1152]{1,0:T(8,128)(2,1)S(1)}, bf16[96,1152]{1,0:T(8,128)(2,1)S(1)}, u32[]{:S(2)}, u32[]{:S(2)}) %collective-permute-start.4) | collective-permute-done | bytes 221216 | tf_op jit(solution)/shard_map/z2/ppermute | solution.py:33
  18.4 1.7 %collective-permute-start.9 = (bf16[192,1152]{1,0:T(8,128)(2,1)S(1)}, bf16[192,1152]{1,0:T(8,128)(2,1)S(1)}, u32[]{:S(2)}, u32[]{:S(2)}) collective-permute-start(bf16[192,1152]{1,0:T(8,128)(2,1)S(1)} %get-tuple-element.60.refs_3_.src), channel_id=1, source_target_pairs={{0,64},{1,65},{2,66},{3,67},{4,12},{5,13},{6,14},{7,15},{8,72},{9,... | collective-permute-start | bytes 1327112 | tf_op jit(solution)/shard_map/second/ppermute | solution.py:33
  20.0 1.7 %collective-permute-start.10 = (bf16[192,1152]{1,0:T(8,128)(2,1)S(1)}, bf16[192,1152]{1,0:T(8,128)(2,1)S(1)}, u32[]{:S(2)}, u32[]{:S(2)}) collective-permute-start(bf16[192,1152]{1,0:T(8,128)(2,1)S(1)} %get-tuple-element.60.refs_3_.src), channel_id=1, source_target_pairs={{0,192},{1,193},{2,194},{3,195},{4,28},{5,29},{6,30},{7,31},{8,200... | collective-permute-start | bytes 1327112 | tf_op jit(solution)/shard_map/second/ppermute | solution.py:33
  21.7 2.0 %collective-permute-start.8 = (bf16[192,1152]{1,0:T(8,128)(2,1)S(1)}, bf16[192,1152]{1,0:T(8,128)(2,1)S(1)}, u32[]{:S(2)}, u32[]{:S(2)}) collective-permute-start(bf16[192,1152]{1,0:T(8,128)(2,1)S(1)} %get-tuple-element.60.refs_3_.src), channel_id=1, source_target_pairs={{0,128},{1,129},{2,130},{3,131},{4,20},{5,21},{6,22},{7,23},{8,136... | collective-permute-start | bytes 1327112 | tf_op jit(solution)/shard_map/second/ppermute | solution.py:33
  23.7 2.7 %collective-permute-start.6 = (bf16[48,1152]{1,0:T(8,128)(2,1)S(1)}, bf16[48,1152]{1,0:T(8,128)(2,1)S(1)}, u32[]{:S(2)}, u32[]{:S(2)}) collective-permute-start(bf16[48,1152]{1,0:T(8,128)(2,1)S(1)} %get-tuple-element.58), channel_id=1, source_target_pairs={{0,2},{1,3},{2,32},{3,33},{4,38},{5,39},{6,4},{7,5},{8,10},{9,11},... | collective-permute-start | bytes 331784 | tf_op jit(solution)/shard_map/z4/ppermute | solution.py:33
  26.3 0.5 collective-permute-start.7
  26.8 1.2 %collective-permute-done.9.refs_5_.after = bf16[192,1152]{1,0:T(8,128)(2,1)S(1)} collective-permute-done((bf16[192,1152]{1,0:T(8,128)(2,1)S(1)}, bf16[192,1152]{1,0:T(8,128)(2,1)S(1)}, u32[]{:S(2)}, u32[]{:S(2)}) %collective-permute-start.9) | collective-permute-done | bytes 442400 | tf_op jit(solution)/shard_map/second/ppermute | solution.py:33
  28.1 0.2 collective-permute-done.10.refs_6_
  28.3 5.0 %collective-permute-start.13 = (bf16[192,1152]{1,0:T(8,128)(2,1)S(1)}, bf16[192,1152]{1,0:T(8,128)(2,1)S(1)}, u32[]{:S(2)}, u32[]{:S(2)}) collective-permute-start(bf16[192,1152]{1,0:T(8,128)(2,1)S(1)} %collective-permute-done.10.refs_6_), channel_id=1, source_target_pairs={{0,4},{1,5},{2,6},{3,7},{4,0},{5,1},{6,2},{7,3},{8,12},{9,13},{10,... | collective-permute-start | bytes 1327112 | tf_op jit(solution)/shard_map/swap/ppermute | solution.py:33
  33.3 0.6 collective-permute-done.8.refs_4_
  35.3 1.8 %collective-permute-done.7.refs_2_ = bf16[192,1152]{1,0:T(8,128)(2,1)S(1)} collective-permute-done((bf16[192,1152]{1,0:T(8,128)(2,1)S(1)}, bf16[192,1152]{1,0:T(8,128)(2,1)S(1)}, u32[]{:S(2)}, u32[]{:S(2)}) %collective-permute-start.7) | collective-permute-done | bytes 442400 | tf_op jit(solution)/shard_map/z1/ppermute | solution.py:33
  37.1 2.3 %shard_map.106 = (bf16[384,768]{1,0:T(8,128)(2,1)S(1)}, f32[3,8,768]{2,1,0:T(8,128)S(1)}, bf16[384,1152]{1,0:T(8,128)(2,1)S(1)}, bf16[768,1152]{1,0:T(8,128)(2,1)S(1)}) custom-call(f32[1]{0:T(128)S(6)} %copy.11.log_temp, f32[1]{0:T(128)S(6)} %copy.12.bias, s32[1,384]{1,0:T(1,128)S(1)} %reshape.1562.rows_after.rows_id, ...), custom_call_target="tpu_custom_call" | custom-call | tf_op jit(solution)/shard_map/pallas_call | solution.py:244
  39.4 3.1 %shard_map.108 = (bf16[784,1152]{1,0:T(8,128)(2,1)S(1)}, bf16[384,768]{1,0:T(8,128)(2,1)S(1)}, f32[8,128]{1,0:T(8,128)S(1)}, bf16[768,1152]{1,0:T(8,128)(2,1)S(1)}) custom-call(f32[1]{0:T(128)S(6)} %copy.11.log_temp, f32[1]{0:T(128)S(6)} %copy.12.bias, s32[1,384]{1,0:T(1,128)S(1)} %reshape.1562.rows_after.rows_id, ...), custom_call_target="tpu_custom_call" | custom-call | tf_op jit(solution)/shard_map/pallas_call | solution.py:244
  42.7 2.5 %shard_map.111 = (f32[48,1152]{1,0:T(8,128)S(1)}, f32[96,1152]{1,0:T(8,128)S(1)}, bf16[48,1152]{1,0:T(8,128)(2,1)S(1)}, bf16[192,1152]{1,0:T(8,128)(2,1)}) custom-call(bf16[384,768]{1,0:T(8,128)(2,1)S(1)} %get-tuple-element.61.scaled.scaled_own, bf16[384,768]{1,0:T(8,128)(2,1)S(1)} %get-tuple-element.75.scaled_far, ...), custom_call_target="tpu_custom_call" | custom-call | tf_op jit(solution)/shard_map/pallas_call | solution.py:244
  45.2 2.5 %collective-permute-start.22 = (bf16[192,1152]{1,0:T(8,128)(2,1)}, bf16[192,1152]{1,0:T(8,128)(2,1)}, u32[]{:S(2)}, u32[]{:S(2)}) collective-permute-start(bf16[192,1152]{1,0:T(8,128)(2,1)} %get-tuple-element.80), channel_id=1, source_target_pairs={{0,35},{1,0},{2,1},{3,2},{4,5},{5,6},{6,7},{7,36},{8,43},{9,8},{10... | collective-permute-start | bytes 1327112 | tf_op jit(solution)/shard_map/rz1/ppermute | solution.py:33
  47.7 2.3 %shard_map.109 = (f32[192,1152]{1,0:T(8,128)S(1)}, bf16[192,1152]{1,0:T(8,128)(2,1)}, bf16[192,1152]{1,0:T(8,128)(2,1)}, bf16[192,1152]{1,0:T(8,128)(2,1)}, f32[32,8,128]{2,1,0:T(8,128)}) custom-call(bf16[384,768]{1,0:T(8,128)(2,1)S(1)} %get-tuple-element.61.scaled.scaled_own, f32[8,128]{1,0:T(8,128)S(1)} %get-tuple-element.64.sums, ...), custom_call_target="tpu_custom_call" | custom-call | tf_op jit(solution)/shard_map/pallas_call | solution.py:244
  50.0 2.5 %collective-permute-start.16 = (bf16[192,1152]{1,0:T(8,128)(2,1)}, bf16[192,1152]{1,0:T(8,128)(2,1)S(1)}, u32[]{:S(2)}, u32[]{:S(2)}) collective-permute-start(bf16[192,1152]{1,0:T(8,128)(2,1)} %get-tuple-element.67), channel_id=1, source_target_pairs={{0,192},{1,193},{2,194},{3,195},{4,28},{5,29},{6,30},{7,31},{8,200... | collective-permute-start | bytes 1327112 | tf_op jit(solution)/shard_map/rsecond/ppermute | solution.py:33
  52.5 1.5 %collective-permute-start.18 = (bf16[192,1152]{1,0:T(8,128)(2,1)}, bf16[192,1152]{1,0:T(8,128)(2,1)S(1)}, u32[]{:S(2)}, u32[]{:S(2)}) collective-permute-start(bf16[192,1152]{1,0:T(8,128)(2,1)} %get-tuple-element.69), channel_id=1, source_target_pairs={{0,128},{1,129},{2,130},{3,131},{4,20},{5,21},{6,22},{7,23},{8,136... | collective-permute-start | bytes 1327112 | tf_op jit(solution)/shard_map/rsecond/ppermute | solution.py:33
  53.9 1.9 %collective-permute-start.23 = (bf16[48,1152]{1,0:T(8,128)(2,1)S(1)}, bf16[48,1152]{1,0:T(8,128)(2,1)S(1)}, u32[]{:S(2)}, u32[]{:S(2)}) collective-permute-start(bf16[48,1152]{1,0:T(8,128)(2,1)S(1)} %get-tuple-element.81), channel_id=1, source_target_pairs={{0,34},{1,35},{2,0},{3,1},{4,6},{5,7},{6,36},{7,37},{8,42},{9,43},... | collective-permute-start | bytes 331784 | tf_op jit(solution)/shard_map/rz4/ppermute | solution.py:33
  55.9 6.2 %all-to-all-start = ((f32[32,8,128]{2,1,0:T(8,128)}), f32[32,8,128]{2,1,0:T(8,128)S(1)}, u32[]{:S(2)}, u32[]{:S(2)}) async-start(f32[32,8,128]{2,1,0:T(8,128)} %get-tuple-element.70), calls=%async_computation | async-start | bytes 262144 | tf_op jit(solution)/shard_map/terms/all_to_all | solution.py:322
  62.2 0.6 copy-done.7
  62.8 0.9 %copy-done.6 = f32[48,1152]{1,0:T(8,128)S(1)} copy-done((f32[48,1152]{1,0:T(8,128)S(1)}, f32[48,1152]{1,0:T(8,128)}, u32[]{:S(2)}) %copy-start.6) | copy-done | bytes 221208
  63.7 0.9 %copy-done.8 = bf16[48,1152]{1,0:T(8,128)(2,1)S(1)} copy-done((bf16[48,1152]{1,0:T(8,128)(2,1)S(1)}, bf16[48,1152]{1,0:T(8,128)(2,1)}, u32[]{:S(2)}) %copy-start.8) | copy-done | bytes 110616
  64.6 1.8 %shard_map.112 = (f32[48,1152]{1,0:T(8,128)S(1)}, f32[48,1152]{1,0:T(8,128)S(1)}, bf16[96,1152]{1,0:T(8,128)(2,1)}) custom-call(f32[48,1152]{1,0:T(8,128)S(1)} %copy-done.6, f32[96,1152]{1,0:T(8,128)S(1)} %get-tuple-element.79.pair, bf16[192,1152]{1,0:T(8,128)(2,1)} %collective-permute-done.22.back, bf16[48,1152]{1,0:T(8,128)(2,1)S(1)} %copy-done.8), custom_call_target="tpu_custom_call" | custom-call | tf_op jit(solution)/shard_map/pallas_call | solution.py:244
  66.4 0.7 copy-done.3
  67.1 3.9 %collective-permute-start.24 = (bf16[96,1152]{1,0:T(8,128)(2,1)}, bf16[96,1152]{1,0:T(8,128)(2,1)S(1)}, u32[]{:S(2)}, u32[]{:S(2)}) collective-permute-start(bf16[96,1152]{1,0:T(8,128)(2,1)} %get-tuple-element.84), channel_id=1, source_target_pairs={{0,34},{1,35},{2,0},{3,1},{4,6},{5,7},{6,36},{7,37},{8,42},{9,43},... | collective-permute-start | bytes 663560 | tf_op jit(solution)/shard_map/rz2/ppermute | solution.py:33
  71.0 1.5 %all-to-all-done.terms = f32[32,8,128]{2,1,0:T(8,128)S(1)} async-done(((f32[32,8,128]{2,1,0:T(8,128)}), f32[32,8,128]{2,1,0:T(8,128)S(1)}, u32[]{:S(2)}, u32[]{:S(2)}) %all-to-all-start) | async-done | bytes 131104 | tf_op jit(solution)/shard_map/terms/all_to_all | solution.py:322
  72.5 0.2 shard_map.110
  72.8 0.8 collective-permute-start.19
  73.6 2.5 %collective-permute-start.20 = (bf16[64,1152]{1,0:T(8,128)(2,1)S(1)}, bf16[64,1152]{1,0:T(8,128)(2,1)S(1)}, u32[]{:S(2)}, u32[]{:S(2)}) collective-permute-start(bf16[64,1152]{1,0:T(8,128)(2,1)S(1)} %get-tuple-element.73), channel_id=1, source_target_pairs={{0,8},{1,9},{2,10},{3,11},{4,68},{5,69},{6,70},{7,71},{8,16},{9,17... | collective-permute-start | bytes 442376 | tf_op jit(solution)/shard_map/rfirst/ppermute | solution.py:33
  76.1 2.0 %collective-permute-start.21 = (bf16[64,1152]{1,0:T(8,128)(2,1)S(1)}, bf16[64,1152]{1,0:T(8,128)(2,1)S(1)}, u32[]{:S(2)}, u32[]{:S(2)}) collective-permute-start(bf16[64,1152]{1,0:T(8,128)(2,1)S(1)} %get-tuple-element.74), channel_id=1, source_target_pairs={{0,16},{1,17},{2,18},{3,19},{4,132},{5,133},{6,134},{7,135},{8,24}... | collective-permute-start | bytes 442376 | tf_op jit(solution)/shard_map/rfirst/ppermute | solution.py:33
  78.3 1.3 %collective-permute-done.25.t1 = bf16[48,1152]{1,0:T(8,128)(2,1)S(1)} collective-permute-done((bf16[48,1152]{1,0:T(8,128)(2,1)S(1)}, bf16[48,1152]{1,0:T(8,128)(2,1)S(1)}, u32[]{:S(2)}, u32[]{:S(2)}) %collective-permute-start.25) | collective-permute-done | bytes 110624 | tf_op jit(solution)/shard_map/rpair/ppermute | solution.py:33
  79.6 0.8 collective-permute-done.20.i2
  80.3 2.4 %collective-permute-done.21.i3 = bf16[64,1152]{1,0:T(8,128)(2,1)S(1)} collective-permute-done((bf16[64,1152]{1,0:T(8,128)(2,1)S(1)}, bf16[64,1152]{1,0:T(8,128)(2,1)S(1)}, u32[]{:S(2)}, u32[]{:S(2)}) %collective-permute-start.21) | collective-permute-done | bytes 147488 | tf_op jit(solution)/shard_map/rfirst/ppermute | solution.py:33
  82.7 1.0 %shard_map.114 = (f32[48,1152]{1,0:T(8,128)}, f32[48,1152]{1,0:T(8,128)}, f32[1]{0:T(128)}, f32[1]{0:T(128)}, f32[1]{0:T(128)}) custom-call(f32[1]{0:T(128)S(6)} %copy.11.log_temp, f32[48,1152]{1,0:T(8,128)S(1)} %copy-done, f32[48,1152]{1,0:T(8,128)S(1)} %get-tuple-element.71.after.image_own, bf16[64,1152]{1,0:T(8,128)(2,1)S(1)} %collective-permute-done.19.i1, ...), custom_call_target="tpu_custom_call" | custom-call | tf_op jit(solution)/shard_map/pallas_call | solution.py:244
  (55 shorter events, 1.1 us)
Async XLA Ops:
  0.6 3.2 %copy-start = (f32[48,1152]{1,0:T(8,128)S(1)}, f32[48,1152]{1,0:T(8,128)}, u32[]{:S(2)}) copy-start(f32[48,1152]{1,0:T(8,128)} %image_raw.1) | copy-start | bytes 663556
  0.6 1.0 %copy-start.1 = (f32[48,1152]{1,0:T(8,128)S(1)}, f32[48,1152]{1,0:T(8,128)}, u32[]{:S(2)}) copy-start(f32[48,1152]{1,0:T(8,128)} %text_raw.1) | copy-start | bytes 663556
  1.6 12.8 %copy-start.9 = (s32[12288]{0:T(1024)S(1)}, s32[12288]{0:T(1024)}, u32[]{:S(2)}) copy-start(s32[12288]{0:T(1024)} %param.8) | copy-start | bytes 147460
  1.6 12.9 %copy-start.10 = (s32[12288]{0:T(1024)S(1)}, s32[12288]{0:T(1024)}, u32[]{:S(2)}) copy-start(s32[12288]{0:T(1024)} %param.9) | copy-start | bytes 147460
  1.8 2.1 %collective-permute-start = (bf16[48,1152]{1,0:T(8,128)(2,1)S(1)}, bf16[48,1152]{1,0:T(8,128)(2,1)S(1)}, u32[]{:S(2)}, u32[]{:S(2)}) collective-permute-start(bf16[48,1152]{1,0:T(8,128)(2,1)S(1)} %get-tuple-element.50), channel_id=1, source_target_pairs={{0,4},{1,5},{2,6},{3,7},{4,0},{5,1},{6,2},{7,3},{8,12},{9,13},{10,... | collective-permute-start | bytes 331784 | tf_op jit(solution)/shard_map/pair/ppermute | solution.py:33
  4.0 6.8 %collective-permute-start.3 = (bf16[48,1152]{1,0:T(8,128)(2,1)S(1)}, bf16[48,1152]{1,0:T(8,128)(2,1)S(1)}, u32[]{:S(2)}, u32[]{:S(2)}) collective-permute-start(bf16[48,1152]{1,0:T(8,128)(2,1)S(1)} %get-tuple-element.51), channel_id=1, source_target_pairs={{0,24},{1,25},{2,26},{3,27},{4,196},{5,197},{6,198},{7,199},{8,0},... | collective-permute-start | bytes 331784 | tf_op jit(solution)/shard_map/first/ppermute | solution.py:33
  4.9 5.9 %collective-permute-start.2 = (bf16[48,1152]{1,0:T(8,128)(2,1)S(1)}, bf16[48,1152]{1,0:T(8,128)(2,1)S(1)}, u32[]{:S(2)}, u32[]{:S(2)}) collective-permute-start(bf16[48,1152]{1,0:T(8,128)(2,1)S(1)} %get-tuple-element.51), channel_id=1, source_target_pairs={{0,8},{1,9},{2,10},{3,11},{4,68},{5,69},{6,70},{7,71},{8,16},{9,17... | collective-permute-start | bytes 331784 | tf_op jit(solution)/shard_map/first/ppermute | solution.py:33
  7.3 6.3 %collective-permute-start.1 = (bf16[48,1152]{1,0:T(8,128)(2,1)S(1)}, bf16[48,1152]{1,0:T(8,128)(2,1)S(1)}, u32[]{:S(2)}, u32[]{:S(2)}) collective-permute-start(bf16[48,1152]{1,0:T(8,128)(2,1)S(1)} %get-tuple-element.51), channel_id=1, source_target_pairs={{0,16},{1,17},{2,18},{3,19},{4,132},{5,133},{6,134},{7,135},{8,24}... | collective-permute-start | bytes 331784 | tf_op jit(solution)/shard_map/first/ppermute | solution.py:33
  7.7 10.6 %collective-permute-start.4 = (bf16[96,1152]{1,0:T(8,128)(2,1)S(1)}, bf16[96,1152]{1,0:T(8,128)(2,1)S(1)}, u32[]{:S(2)}, u32[]{:S(2)}) collective-permute-start(bf16[96,1152]{1,0:T(8,128)(2,1)S(1)} %get-tuple-element.56), channel_id=1, source_target_pairs={{0,2},{1,3},{2,32},{3,33},{4,38},{5,39},{6,4},{7,5},{8,10},{9,11},... | collective-permute-start | bytes 663560 | tf_op jit(solution)/shard_map/z2/ppermute | solution.py:33
  13.5 2.4 %collective-permute-start.5 = (f32[8,128]{1,0:T(8,128)S(1)}, f32[8,128]{1,0:T(8,128)S(1)}, u32[]{:S(2)}, u32[]{:S(2)}) collective-permute-start(f32[8,128]{1,0:T(8,128)S(1)} %shard_map.104), channel_id=1, source_target_pairs={{0,4},{1,5},{2,6},{3,7},{4,0},{5,1},{6,2},{7,3},{8,12},{9,13},{10,... | collective-permute-start | bytes 12296 | tf_op jit(solution)/shard_map/flag/ppermute | solution.py:33
  18.4 9.6 %collective-permute-start.9 = (bf16[192,1152]{1,0:T(8,128)(2,1)S(1)}, bf16[192,1152]{1,0:T(8,128)(2,1)S(1)}, u32[]{:S(2)}, u32[]{:S(2)}) collective-permute-start(bf16[192,1152]{1,0:T(8,128)(2,1)S(1)} %get-tuple-element.60.refs_3_.src), channel_id=1, source_target_pairs={{0,64},{1,65},{2,66},{3,67},{4,12},{5,13},{6,14},{7,15},{8,72},{9,... | collective-permute-start | bytes 1327112 | tf_op jit(solution)/shard_map/second/ppermute | solution.py:33
  20.0 8.3 %collective-permute-start.10 = (bf16[192,1152]{1,0:T(8,128)(2,1)S(1)}, bf16[192,1152]{1,0:T(8,128)(2,1)S(1)}, u32[]{:S(2)}, u32[]{:S(2)}) collective-permute-start(bf16[192,1152]{1,0:T(8,128)(2,1)S(1)} %get-tuple-element.60.refs_3_.src), channel_id=1, source_target_pairs={{0,192},{1,193},{2,194},{3,195},{4,28},{5,29},{6,30},{7,31},{8,200... | collective-permute-start | bytes 1327112 | tf_op jit(solution)/shard_map/second/ppermute | solution.py:33
  21.7 12.3 %collective-permute-start.8 = (bf16[192,1152]{1,0:T(8,128)(2,1)S(1)}, bf16[192,1152]{1,0:T(8,128)(2,1)S(1)}, u32[]{:S(2)}, u32[]{:S(2)}) collective-permute-start(bf16[192,1152]{1,0:T(8,128)(2,1)S(1)} %get-tuple-element.60.refs_3_.src), channel_id=1, source_target_pairs={{0,128},{1,129},{2,130},{3,131},{4,20},{5,21},{6,22},{7,23},{8,136... | collective-permute-start | bytes 1327112 | tf_op jit(solution)/shard_map/second/ppermute | solution.py:33
  23.7 9.6 %collective-permute-start.6 = (bf16[48,1152]{1,0:T(8,128)(2,1)S(1)}, bf16[48,1152]{1,0:T(8,128)(2,1)S(1)}, u32[]{:S(2)}, u32[]{:S(2)}) collective-permute-start(bf16[48,1152]{1,0:T(8,128)(2,1)S(1)} %get-tuple-element.58), channel_id=1, source_target_pairs={{0,2},{1,3},{2,32},{3,33},{4,38},{5,39},{6,4},{7,5},{8,10},{9,11},... | collective-permute-start | bytes 331784 | tf_op jit(solution)/shard_map/z4/ppermute | solution.py:33
  26.3 10.7 %collective-permute-start.7 = (bf16[192,1152]{1,0:T(8,128)(2,1)S(1)}, bf16[192,1152]{1,0:T(8,128)(2,1)S(1)}, u32[]{:S(2)}, u32[]{:S(2)}) collective-permute-start(bf16[192,1152]{1,0:T(8,128)(2,1)S(1)} %get-tuple-element.59), channel_id=1, source_target_pairs={{0,1},{1,2},{2,3},{3,32},{4,39},{5,4},{6,5},{7,6},{8,9},{9,10},{10... | collective-permute-start | bytes 1327112 | tf_op jit(solution)/shard_map/z1/ppermute | solution.py:33
  28.0 11.4 %collective-permute-start.11 = (bf16[192,1152]{1,0:T(8,128)(2,1)S(1)}, bf16[192,1152]{1,0:T(8,128)(2,1)S(1)}, u32[]{:S(2)}, u32[]{:S(2)}) collective-permute-start(bf16[192,1152]{1,0:T(8,128)(2,1)S(1)} %shard_map.107), channel_id=1, source_target_pairs={{0,4},{1,5},{2,6},{3,7},{4,0},{5,1},{6,2},{7,3},{8,12},{9,13},{10,... | collective-permute-start | bytes 1327112 | tf_op jit(solution)/shard_map/swap/ppermute | solution.py:33
  28.3 11.1 %collective-permute-start.13 = (bf16[192,1152]{1,0:T(8,128)(2,1)S(1)}, bf16[192,1152]{1,0:T(8,128)(2,1)S(1)}, u32[]{:S(2)}, u32[]{:S(2)}) collective-permute-start(bf16[192,1152]{1,0:T(8,128)(2,1)S(1)} %collective-permute-done.10.refs_6_), channel_id=1, source_target_pairs={{0,4},{1,5},{2,6},{3,7},{4,0},{5,1},{6,2},{7,3},{8,12},{9,13},{10,... | collective-permute-start | bytes 1327112 | tf_op jit(solution)/shard_map/swap/ppermute | solution.py:33
  33.3 6.1 %collective-permute-start.12 = (bf16[192,1152]{1,0:T(8,128)(2,1)S(1)}, bf16[192,1152]{1,0:T(8,128)(2,1)S(1)}, u32[]{:S(2)}, u32[]{:S(2)}) collective-permute-start(bf16[192,1152]{1,0:T(8,128)(2,1)S(1)} %collective-permute-done.9.refs_5_.after), channel_id=1, source_target_pairs={{0,4},{1,5},{2,6},{3,7},{4,0},{5,1},{6,2},{7,3},{8,12},{9,13},{10,... | collective-permute-start | bytes 1327112 | tf_op jit(solution)/shard_map/swap/ppermute | solution.py:33
  34.0 5.5 %collective-permute-start.14 = (bf16[192,1152]{1,0:T(8,128)(2,1)S(1)}, bf16[192,1152]{1,0:T(8,128)(2,1)S(1)}, u32[]{:S(2)}, u32[]{:S(2)}) collective-permute-start(bf16[192,1152]{1,0:T(8,128)(2,1)S(1)} %collective-permute-done.8.refs_4_), channel_id=1, source_target_pairs={{0,4},{1,5},{2,6},{3,7},{4,0},{5,1},{6,2},{7,3},{8,12},{9,13},{10,... | collective-permute-start | bytes 1327112 | tf_op jit(solution)/shard_map/swap/ppermute | solution.py:33
  42.6 5.1 %collective-permute-start.15 = (bf16[784,1152]{1,0:T(8,128)(2,1)S(1)}, bf16[784,1152]{1,0:T(8,128)(2,1)S(1)}, u32[]{:S(2)}, u32[]{:S(2)}) collective-permute-start(bf16[784,1152]{1,0:T(8,128)(2,1)S(1)} %get-tuple-element.65), channel_id=1, source_target_pairs={{0,4},{1,5},{2,6},{3,7},{4,0},{5,1},{6,2},{7,3},{8,12},{9,13},{10,... | collective-permute-start | bytes 5419016 | tf_op jit(solution)/shard_map/rswap/ppermute | solution.py:33
  45.1 7.3 %copy-start.5 = (f32[48,1152]{1,0:T(8,128)}, f32[48,1152]{1,0:T(8,128)S(1)}, u32[]{:S(2)}) copy-start(f32[48,1152]{1,0:T(8,128)S(1)} %get-tuple-element.78.own) | copy-start | bytes 663556
  45.2 17.6 %collective-permute-start.22 = (bf16[192,1152]{1,0:T(8,128)(2,1)}, bf16[192,1152]{1,0:T(8,128)(2,1)}, u32[]{:S(2)}, u32[]{:S(2)}) collective-permute-start(bf16[192,1152]{1,0:T(8,128)(2,1)} %get-tuple-element.80), channel_id=1, source_target_pairs={{0,35},{1,0},{2,1},{3,2},{4,5},{5,6},{6,7},{7,36},{8,43},{9,8},{10... | collective-permute-start | bytes 1327112 | tf_op jit(solution)/shard_map/rz1/ppermute | solution.py:33
  50.0 22.6 %collective-permute-start.16 = (bf16[192,1152]{1,0:T(8,128)(2,1)}, bf16[192,1152]{1,0:T(8,128)(2,1)S(1)}, u32[]{:S(2)}, u32[]{:S(2)}) collective-permute-start(bf16[192,1152]{1,0:T(8,128)(2,1)} %get-tuple-element.67), channel_id=1, source_target_pairs={{0,192},{1,193},{2,194},{3,195},{4,28},{5,29},{6,30},{7,31},{8,200... | collective-permute-start | bytes 1327112 | tf_op jit(solution)/shard_map/rsecond/ppermute | solution.py:33
  52.5 20.1 %collective-permute-start.17 = (bf16[192,1152]{1,0:T(8,128)(2,1)}, bf16[192,1152]{1,0:T(8,128)(2,1)S(1)}, u32[]{:S(2)}, u32[]{:S(2)}) collective-permute-start(bf16[192,1152]{1,0:T(8,128)(2,1)} %get-tuple-element.68), channel_id=1, source_target_pairs={{0,64},{1,65},{2,66},{3,67},{4,12},{5,13},{6,14},{7,15},{8,72},{9,... | collective-permute-start | bytes 1327112 | tf_op jit(solution)/shard_map/rsecond/ppermute | solution.py:33
  52.5 20.1 %collective-permute-start.18 = (bf16[192,1152]{1,0:T(8,128)(2,1)}, bf16[192,1152]{1,0:T(8,128)(2,1)S(1)}, u32[]{:S(2)}, u32[]{:S(2)}) collective-permute-start(bf16[192,1152]{1,0:T(8,128)(2,1)} %get-tuple-element.69), channel_id=1, source_target_pairs={{0,128},{1,129},{2,130},{3,131},{4,20},{5,21},{6,22},{7,23},{8,136... | collective-permute-start | bytes 1327112 | tf_op jit(solution)/shard_map/rsecond/ppermute | solution.py:33
  53.9 8.2 %collective-permute-start.23 = (bf16[48,1152]{1,0:T(8,128)(2,1)S(1)}, bf16[48,1152]{1,0:T(8,128)(2,1)S(1)}, u32[]{:S(2)}, u32[]{:S(2)}) collective-permute-start(bf16[48,1152]{1,0:T(8,128)(2,1)S(1)} %get-tuple-element.81), channel_id=1, source_target_pairs={{0,34},{1,35},{2,0},{3,1},{4,6},{5,7},{6,36},{7,37},{8,42},{9,43},... | collective-permute-start | bytes 331784 | tf_op jit(solution)/shard_map/rz4/ppermute | solution.py:33
  55.9 16.7 %all-to-all-start = ((f32[32,8,128]{2,1,0:T(8,128)}), f32[32,8,128]{2,1,0:T(8,128)S(1)}, u32[]{:S(2)}, u32[]{:S(2)}) async-start(f32[32,8,128]{2,1,0:T(8,128)} %get-tuple-element.70), calls=%async_computation | async-start | bytes 262144 | tf_op jit(solution)/shard_map/terms/all_to_all | solution.py:322
  62.1 0.6 copy-start.7
  62.8 0.9 %copy-start.6 = (f32[48,1152]{1,0:T(8,128)S(1)}, f32[48,1152]{1,0:T(8,128)}, u32[]{:S(2)}) copy-start(f32[48,1152]{1,0:T(8,128)} %copy-done.5) | copy-start | bytes 663556
  63.7 0.9 %copy-start.8 = (bf16[48,1152]{1,0:T(8,128)(2,1)S(1)}, bf16[48,1152]{1,0:T(8,128)(2,1)}, u32[]{:S(2)}) copy-start(bf16[48,1152]{1,0:T(8,128)(2,1)} %copy-done.7) | copy-start | bytes 331780
  66.4 0.7 copy-start.3
  67.1 15.6 %copy-start.2 = (f32[48,1152]{1,0:T(8,128)S(1)}, f32[48,1152]{1,0:T(8,128)}, u32[]{:S(2)}) copy-start(f32[48,1152]{1,0:T(8,128)} %text_raw.1) | copy-start | bytes 663556
  67.1 11.0 %copy-start.4 = (f32[48,1152]{1,0:T(8,128)S(1)}, f32[48,1152]{1,0:T(8,128)}, u32[]{:S(2)}) copy-start(f32[48,1152]{1,0:T(8,128)} %copy-done.3) | copy-start | bytes 663556
  67.1 11.0 %collective-permute-start.24 = (bf16[96,1152]{1,0:T(8,128)(2,1)}, bf16[96,1152]{1,0:T(8,128)(2,1)S(1)}, u32[]{:S(2)}, u32[]{:S(2)}) collective-permute-start(bf16[96,1152]{1,0:T(8,128)(2,1)} %get-tuple-element.84), channel_id=1, source_target_pairs={{0,34},{1,35},{2,0},{3,1},{4,6},{5,7},{6,36},{7,37},{8,42},{9,43},... | collective-permute-start | bytes 663560 | tf_op jit(solution)/shard_map/rz2/ppermute | solution.py:33
  72.8 6.8 %collective-permute-start.19 = (bf16[64,1152]{1,0:T(8,128)(2,1)S(1)}, bf16[64,1152]{1,0:T(8,128)(2,1)S(1)}, u32[]{:S(2)}, u32[]{:S(2)}) collective-permute-start(bf16[64,1152]{1,0:T(8,128)(2,1)S(1)} %get-tuple-element.72), channel_id=1, source_target_pairs={{0,24},{1,25},{2,26},{3,27},{4,196},{5,197},{6,198},{7,199},{8,0},... | collective-permute-start | bytes 442376 | tf_op jit(solution)/shard_map/rfirst/ppermute | solution.py:33
  73.6 6.8 %collective-permute-start.20 = (bf16[64,1152]{1,0:T(8,128)(2,1)S(1)}, bf16[64,1152]{1,0:T(8,128)(2,1)S(1)}, u32[]{:S(2)}, u32[]{:S(2)}) collective-permute-start(bf16[64,1152]{1,0:T(8,128)(2,1)S(1)} %get-tuple-element.73), channel_id=1, source_target_pairs={{0,8},{1,9},{2,10},{3,11},{4,68},{5,69},{6,70},{7,71},{8,16},{9,17... | collective-permute-start | bytes 442376 | tf_op jit(solution)/shard_map/rfirst/ppermute | solution.py:33
  76.1 6.6 %collective-permute-start.21 = (bf16[64,1152]{1,0:T(8,128)(2,1)S(1)}, bf16[64,1152]{1,0:T(8,128)(2,1)S(1)}, u32[]{:S(2)}, u32[]{:S(2)}) collective-permute-start(bf16[64,1152]{1,0:T(8,128)(2,1)S(1)} %get-tuple-element.74), channel_id=1, source_target_pairs={{0,16},{1,17},{2,18},{3,19},{4,132},{5,133},{6,134},{7,135},{8,24}... | collective-permute-start | bytes 442376 | tf_op jit(solution)/shard_map/rfirst/ppermute | solution.py:33
  78.2 1.4 %collective-permute-start.25 = (bf16[48,1152]{1,0:T(8,128)(2,1)S(1)}, bf16[48,1152]{1,0:T(8,128)(2,1)S(1)}, u32[]{:S(2)}, u32[]{:S(2)}) collective-permute-start(bf16[48,1152]{1,0:T(8,128)(2,1)S(1)} %get-tuple-element.86), channel_id=1, source_target_pairs={{0,4},{1,5},{2,6},{3,7},{4,0},{5,1},{6,2},{7,3},{8,12},{9,13},{10,... | collective-permute-start | bytes 331784 | tf_op jit(solution)/shard_map/rpair/ppermute | solution.py:33
